TPU v7x, 512 devices: a whole 4x4x16 slice. The times are simulated.
512 devices in a mesh: tm: 32 (over x, z_lo), clip: 16 (over z_hi, y, core).
Axes of the slice: x: 4, y: 4, z: 16 (z_hi: 2, z_lo: 8; z = z_hi * 8 + z_lo), core: 2. Of those that a mesh axis runs over, the one named last changes fastest.
Arguments:
- video: float32 [16, 32, 16, 32, 320], P('clip', 'tm'), may hold values from -6 to 6
- spatial_w: bfloat16 [9, 320, 320], P(None, 'clip'), may hold values from -0.109375 to 0.109375
- spatial_b: float32 [320], replicated, may hold values from -3 to 3
- temporal_w: float32 [3, 320, 320], P(None, 'clip'), may hold values from -0.1875 to 0.1875
- cotangent: float32 [16, 32, 16, 32, 320], P('clip', 'tm'), may hold values from -6 to 6
Outputs:
- output: float32 [16, 32, 16, 32, 320], P('clip', 'tm')
- grad_video: float32 [16, 32, 16, 32, 320], P('clip', 'tm')
- grad_temporal: float32 [3, 320, 320], P(None, 'clip')
All inputs are finite; a program needn't handle non-finite values.
Results may differ from a plain program's by a relative error of at most 0.0049.
Values may be sent and summed in bfloat16 or wider, within the bound.
No kernel may reach another device: no remote copies, remote signals or barrier semaphores. Data moves between devices by JAX's collectives and lax.ppermute only.
A program may use at most 64 MiB of HBM per device.

v0:
```python
import math

import jax
import jax.numpy as jnp
from jax import lax
from jax.sharding import Mesh
from jax.sharding import PartitionSpec as P

CLIP = ("clip_0", "clip_1", "clip_2")


def from_everyone(array, axis):
    peers = lax.axis_size(axis)
    return lax.all_to_all(
        jnp.broadcast_to(array[None], (peers, *array.shape)), axis, 0, 0, tiled=True
    )


def joined_along(blocks, dim):
    blocks = jnp.moveaxis(blocks, 0, dim)
    shape = blocks.shape
    return blocks.reshape(*shape[:dim], shape[dim] * shape[dim + 1], *shape[dim + 2 :])


def gather_axes(array, axes, dim):
    far, near = axes
    blocks = from_everyone(from_everyone(array, far), near)
    return joined_along(blocks.swapaxes(0, 1).reshape(-1, *array.shape), dim)


def in_one_piece(arrays, axis, dim, along):
    widths = [a.shape[along] for a in arrays]
    both = jnp.concatenate(arrays, axis=along)
    whole = gather_axes(both, axis, dim)
    return tuple(jnp.split(whole, [sum(widths[:k]) for k in range(1, len(widths))], axis=along))


def padded_2(cells, sides, width):
    for axis, dim in sides:
        count = lax.axis_size(axis)
        ends = count - 1
        head = lax.slice_in_dim(cells, 0, width, axis=dim)
        tail = lax.slice_in_dim(cells, cells.shape[dim] - width, cells.shape[dim], axis=dim)
        cells = jnp.concatenate(
            [
                lax.ppermute(tail, axis, [(i, (i + 1) % count) for i in range(ends)]),
                cells,
                lax.ppermute(head, axis, [((i + 1) % count, i) for i in range(ends)]),
            ],
            axis=dim,
        )
    return cells


def cut_along(array, dim, peers):
    before, after = (array.shape[:dim], array.shape[dim + 1 :])
    return jnp.moveaxis(array.reshape(*before, peers, -1, *after), dim, 0)


def summed_on_arrival(array, axis, dim):
    peers = lax.axis_size(axis)
    blocks = lax.all_to_all(cut_along(array, dim, peers), axis, 0, 0, tiled=True)
    return jnp.sum(blocks, axis=0)


def rows_for(lines, peers):
    spare = -lines.shape[0] % peers
    if not spare:
        return lines
    return jnp.concatenate([lines, jnp.zeros((spare, *lines.shape[1:]), lines.dtype)])


def collect(array, axis, dim):
    return joined_along(from_everyone(array, axis), dim)


def sum_by_parts(array, axes):
    lines = array.reshape(-1)
    padded = rows_for(lines, lax.axis_size(axes))
    whole = collect(summed_on_arrival(padded, axes, 0), axes, 0)
    return lax.slice_in_dim(whole, 0, len(lines)).reshape(array.shape)


def outer_dot(left, right):
    return lax.dot_general(
        left, right, (((0,), (0,)), ((), ())), preferred_element_type=jnp.float32
    )


def transpose_dot(left, right):
    return lax.dot_general(
        left, right, (((1,), (1,)), ((), ())), preferred_element_type=jnp.float32
    )


def on_device(video, spatial_w, spatial_b, temporal_w, cotangent):
    clips, frames, height, width, chans = video.shape
    row_count = clips * frames * height * width
    video_b = video.astype(jnp.bfloat16)
    padded = jnp.pad(video_b, ((0, 0), (0, 0), (1, 1), (1, 1), (0, 0)))
    temporal_b = temporal_w.astype(jnp.bfloat16)
    spatial_all, temporal_all = in_one_piece(
        (spatial_w, temporal_b), (("clip_0", "clip_1"), "clip_2"), 1, 0
    )
    spatial = jnp.zeros((row_count, chans), jnp.float32)
    for shift_y in range(3):
        for shift_x in range(3):
            window = padded[:, :, shift_y : shift_y + height, shift_x : shift_x + width, :].reshape(
                row_count, chans
            )
            spatial = spatial + jnp.dot(
                window, spatial_all[3 * shift_y + shift_x], preferred_element_type=jnp.float32
            )
    spatial = spatial + spatial_b
    sigmoid_s = jax.nn.sigmoid(spatial)
    hidden = (spatial * sigmoid_s).astype(jnp.bfloat16).reshape(clips, frames, height, width, chans)
    hidden_pad = padded_2(hidden, (("tm", 1),), 1)
    temporal = jnp.zeros((row_count, chans), jnp.float32)
    for kernel_tap in range(3):
        shifted = hidden_pad[:, kernel_tap : kernel_tap + frames].reshape(row_count, chans)
        temporal = temporal + jnp.dot(
            shifted, temporal_all[kernel_tap], preferred_element_type=jnp.float32
        )
    output = video + temporal.reshape(video.shape)
    cot_b = cotangent.astype(jnp.bfloat16)
    cot_flat = cot_b.reshape(row_count, chans)
    cot_pad = padded_2(cot_b, (("tm", 1),), 1)
    grad_hidden = jnp.zeros((row_count, chans), jnp.float32)
    grads = []
    for kernel_tap in range(3):
        shifted_cot = cot_pad[:, 2 - kernel_tap : 2 - kernel_tap + frames].reshape(row_count, chans)
        grad_hidden = grad_hidden + transpose_dot(shifted_cot, temporal_all[kernel_tap])
        shifted_hid = hidden_pad[:, kernel_tap : kernel_tap + frames].reshape(row_count, chans)
        grads.append(outer_dot(shifted_hid, cot_flat))
    local_grad = jnp.stack(grads)
    total_rows = row_count * lax.axis_size("tm") * lax.axis_size(CLIP)
    shared = summed_on_arrival(local_grad, CLIP, 1)
    owned = sum_by_parts(shared, "tm")
    grad_temporal = owned * (1.0 / math.sqrt(total_rows))
    grad_spatial = (grad_hidden * sigmoid_s * (1.0 + spatial * (1.0 - sigmoid_s))).astype(
        jnp.bfloat16
    )
    grad_frames = jnp.pad(
        grad_spatial.reshape(clips, frames, height, width, chans),
        ((0, 0), (0, 0), (1, 1), (1, 1), (0, 0)),
    )
    grad_acc = cotangent.reshape(row_count, chans)
    for shift_y in range(3):
        for shift_x in range(3):
            window = grad_frames[
                :, :, 2 - shift_y : 2 - shift_y + height, 2 - shift_x : 2 - shift_x + width, :
            ].reshape(row_count, chans)
            grad_acc = grad_acc + transpose_dot(window, spatial_all[3 * shift_y + shift_x])
    grad_video = grad_acc.reshape(video.shape)
    return (output, grad_video, grad_temporal)


def solution(mesh):
    finer = Mesh(
        mesh.devices.reshape(mesh.shape["tm"], 2, 4, 2), ("tm", "clip_0", "clip_1", "clip_2")
    )
    placed = (
        P(CLIP, "tm", None, None, None),
        P(None, CLIP, None),
        P(),
        P(None, CLIP, None),
        P(CLIP, "tm", None, None, None),
    )
    return jax.shard_map(
        on_device,
        mesh=finer,
        in_specs=placed,
        out_specs=(
            P(CLIP, "tm", None, None, None),
            P(CLIP, "tm", None, None, None),
            P(None, CLIP, None),
        ),
        check_vma=False,
    )
```

profile of v0, /device:TPU:8, one launch (start us, length us, event | category | flops | bytes accessed | tf_op | source)
XLA Modules:
  0.0 336.7 jit_solution(4406146921070608351)
XLA Ops:
  2.5 1.4 broadcast_in_dim.6
  3.9 18.3 %all-to-all-start = ((bf16[8,12,20,320]{3,2,1,0:T(8,128)(2,1)}), bf16[8,12,20,320]{3,2,1,0:T(8,128)(2,1)S(1)}, u32[]{:S(2)}, u32[]{:S(2)}) async-start(bf16[8,12,20,320]{3,2,1,0:T(8,128)(2,1)} %broadcast_in_dim.6), calls=%async_computation | async-start | bytes 3538944 | tf_op jit(solution)/shard_map/all_to_all | solution.py:14
  24.2 1.7 pad_slice_fusion.12
  25.9 40.8 %all-to-all-done = bf16[8,12,20,320]{3,2,1,0:T(8,128)(2,1)S(1)} async-done(((bf16[8,12,20,320]{3,2,1,0:T(8,128)(2,1)}), bf16[8,12,20,320]{3,2,1,0:T(8,128)(2,1)S(1)}, u32[]{:S(2)}, u32[]{:S(2)}) %all-to-all-start) | async-done | bytes 1228832 | tf_op jit(solution)/shard_map/all_to_all | solution.py:14
  67.5 6.1 %all_to_all.30 = bf16[2,8,12,20,320]{4,1,3,2,0:T(8,128)(2,1)S(1)} all-to-all(bf16[2,8,12,20,320]{4,1,3,2,0:T(8,128)(2,1)S(1)} %broadcast_in_dim.7), channel_id=1, replica_groups=mesh['tm'=32,'clip_0'=2,'clip_1'=4,'clip_2'=2] {'clip_2'}, dimensions={0} | all-to-all | bytes 4915200 | tf_op jit(solution)/shard_map/all_to_all | solution.py:14
  73.6 6.2 %copy.33 = bf16[8,2,12,20,320]{4,1,0,3,2:T(2,128)(2,1)} copy(bf16[8,2,12,20,320]{4,0,3,2,1:T(8,128)(2,1)S(1)} %bitcast.164) | data formatting | bytes 4915200 | tf_op jit(solution)/shard_map/transpose | solution.py:28
  79.8 6.0 %reshape.173 = bf16[16,12,20,320]{3,0,2,1:T(8,128)(2,1)S(1)} reshape(bf16[8,2,12,20,320]{4,1,0,3,2:T(2,128)(2,1)} %copy.33) | data formatting | bytes 4915200 | tf_op jit(solution)/shard_map/reshape | solution.py:28
  85.8 1.6 fusion.29
  94.4 1.4 fusion.33
  98.2 1.5 multiply_convert_fusion.1
  100.6 44.6 %collective-permute-start = (bf16[1,1,16,32,320]{4,3,2,1,0:T(8,128)(2,1)}, bf16[1,1,16,32,320]{4,3,2,1,0:T(8,128)(2,1)}, u32[]{:S(2)}, u32[]{:S(2)}) collective-permute-start(bf16[1,1,16,32,320]{4,3,2,1,0:T(8,128)(2,1)} %bitcast.188), channel_id=1, source_target_pairs={{0,16},{16,32},{32,48},{48,64},{64,80},{80,96},{96,112},{112,128},... | collective-permute-start | bytes 983048 | tf_op jit(solution)/shard_map/ppermute | solution.py:46
  145.2 1.5 collective-permute-start.1
  146.7 2.3 multiply_convert_fusion
  150.5 3.0 collective-permute-done
  153.5 3.8 %reshape.201 = bf16[16,20,16,32]{1,0,3,2:T(8,128)(2,1)S(1)} reshape(bf16[320,16,32]{0,2,1:T(8,128)(2,1)} %bitcast.32) | data formatting | bytes 655360 | tf_op jit(solution)/shard_map/reshape.90
  157.3 1.5 fusion.13
  158.9 6.3 %collective-permute-done.1 = bf16[1,1,16,32,320]{4,3,2,1,0:T(8,128)(2,1)} collective-permute-done((bf16[1,1,16,32,320]{4,3,2,1,0:T(8,128)(2,1)}, bf16[1,1,16,32,320]{4,3,2,1,0:T(8,128)(2,1)}, u32[]{:S(2)}, u32[]{:S(2)}) %collective-permute-start.1) | collective-permute-done | bytes 327712 | tf_op jit(solution)/shard_map/ppermute | solution.py:48
  165.1 3.8 %reshape.205 = bf16[16,20,16,32]{1,0,3,2:T(8,128)(2,1)S(1)} reshape(bf16[320,16,32]{0,2,1:T(8,128)(2,1)} %bitcast.46) | data formatting | bytes 655360 | tf_op jit(solution)/shard_map/reshape.94
  170.2 1.3 copy.54
  171.6 4.1 %all-to-all-start.2 = ((f32[16,3,20,320]{3,2,1,0:T(8,128)}), f32[16,3,20,320]{3,2,1,0:T(8,128)S(1)}, u32[]{:S(2)}, u32[]{:S(2)}) async-start(f32[16,3,20,320]{3,2,1,0:T(8,128)} %copy.54), calls=%async_computation.2 | async-start | bytes 3538944 | tf_op jit(solution)/shard_map/all_to_all | solution.py:62
  175.6 3.1 collective-permute-start.3
  181.3 80.8 %collective-permute-done.3 = bf16[1,1,16,32,320]{4,3,2,1,0:T(8,128)(2,1)} collective-permute-done((bf16[1,1,16,32,320]{4,3,2,1,0:T(8,128)(2,1)S(1)}, bf16[1,1,16,32,320]{4,3,2,1,0:T(8,128)(2,1)}, u32[]{:S(2)}, u32[]{:S(2)}) %collective-permute-start.3) | collective-permute-done | bytes 327712 | tf_op jit(solution)/shard_map/ppermute | solution.py:46
  262.1 2.2 fusion.38
  267.7 2.8 collective-permute-done.2
  270.4 2.7 fusion.19
  282.5 22.2 %all-to-all-start.3 = ((f32[32,1,600]{2,1,0:T(1,128)}), f32[32,1,600]{2,1,0:T(1,128)S(1)}, u32[]{:S(2)}, u32[]{:S(2)}) async-start(f32[32,1,600]{2,1,0:T(1,128)} %all_to_all.22), calls=%async_computation.3 | async-start | bytes 163840 | tf_op jit(solution)/shard_map/all_to_all | solution.py:62
  304.7 2.3 fusion.7
  308.6 8.9 %all-to-all-done.3 = f32[32,1,600]{2,1,0:T(1,128)S(1)} async-done(((f32[32,1,600]{2,1,0:T(1,128)}), f32[32,1,600]{2,1,0:T(1,128)S(1)}, u32[]{:S(2)}, u32[]{:S(2)}) %all-to-all-start.3) | async-done | bytes 76832 | tf_op jit(solution)/shard_map/all_to_all | solution.py:62
  318.2 4.8 %all-to-all-start.4 = ((f32[32,1,600]{2,1,0:T(1,128)}), f32[32,1,600]{2,1,0:T(1,128)S(1)}, u32[]{:S(2)}, u32[]{:S(2)}) async-start(f32[32,1,600]{2,1,0:T(1,128)} %broadcast_in_dim.8), calls=%async_computation.4 | async-start | bytes 163840 | tf_op jit(solution)/shard_map/all_to_all | solution.py:14
  323.0 1.4 fusion.36
  324.4 1.4 fusion.12
  327.1 8.6 %all-to-all-done.4 = f32[32,1,600]{2,1,0:T(1,128)S(1)} async-done(((f32[32,1,600]{2,1,0:T(1,128)}), f32[32,1,600]{2,1,0:T(1,128)S(1)}, u32[]{:S(2)}, u32[]{:S(2)}) %all-to-all-start.4) | async-done | bytes 76832 | tf_op jit(solution)/shard_map/all_to_all | solution.py:14
  (154 shorter events, 36.7 us)
Async XLA Ops:
  3.9 19.5 %copy-start.3 = (f32[1,1,16,32,320]{4,3,2,1,0:T(8,128)S(1)}, f32[1,1,16,32,320]{4,3,2,1,0:T(8,128)}, u32[]{:S(2)}) copy-start(f32[1,1,16,32,320]{4,3,2,1,0:T(8,128)} %param.9) | copy-start | bytes 1966084
  3.9 62.8 %all-to-all-start = ((bf16[8,12,20,320]{3,2,1,0:T(8,128)(2,1)}), bf16[8,12,20,320]{3,2,1,0:T(8,128)(2,1)S(1)}, u32[]{:S(2)}, u32[]{:S(2)}) async-start(bf16[8,12,20,320]{3,2,1,0:T(8,128)(2,1)} %broadcast_in_dim.6), calls=%async_computation | async-start | bytes 3538944 | tf_op jit(solution)/shard_map/all_to_all | solution.py:14
  87.3 2.2 copy-start.42
  87.3 3.1 copy-start.41
  87.3 4.0 %copy-start.40 = (bf16[1,16,20,320]{3,1,2,0:T(8,128)(2,1)S(1)}, bf16[1,16,20,320]{3,1,2,0:T(8,128)(2,1)}, u32[]{:S(2)}) copy-start(bf16[1,16,20,320]{3,1,2,0:T(8,128)(2,1)} %get-tuple-element.14) | copy-start | bytes 614404
  87.5 6.0 %copy-start.17 = (bf16[320,320]{1,0:T(8,128)(2,1)}, bf16[320,320]{1,0:T(8,128)(2,1)S(1)}, u32[]{:S(2)}) copy-start(bf16[320,320]{1,0:T(8,128)(2,1)S(1)} %squeeze.48) | copy-start | bytes 614404
  87.5 4.0 %copy-start.39 = (bf16[1,16,20,320]{3,1,2,0:T(8,128)(2,1)S(1)}, bf16[1,16,20,320]{3,1,2,0:T(8,128)(2,1)}, u32[]{:S(2)}) copy-start(bf16[1,16,20,320]{3,1,2,0:T(8,128)(2,1)} %get-tuple-element.13) | copy-start | bytes 614404
  91.5 2.5 copy-start.8
  91.6 2.7 copy-start.10
  91.7 2.2 copy-start.29
  91.8 4.0 %copy-start.12 = (bf16[320,320]{1,0:T(8,128)(2,1)}, bf16[320,320]{1,0:T(8,128)(2,1)S(1)}, u32[]{:S(2)}) copy-start(bf16[320,320]{1,0:T(8,128)(2,1)S(1)} %squeeze.55) | copy-start | bytes 614404
  92.7 3.1 copy-start.28
  93.9 2.3 copy-start.2
  93.9 2.3 copy-start.16
  94.4 2.3 copy-start.23
  94.4 2.3 copy-start.33
  100.6 52.8 %collective-permute-start = (bf16[1,1,16,32,320]{4,3,2,1,0:T(8,128)(2,1)}, bf16[1,1,16,32,320]{4,3,2,1,0:T(8,128)(2,1)}, u32[]{:S(2)}, u32[]{:S(2)}) collective-permute-start(bf16[1,1,16,32,320]{4,3,2,1,0:T(8,128)(2,1)} %bitcast.188), channel_id=1, source_target_pairs={{0,16},{16,32},{32,48},{48,64},{64,80},{80,96},{96,112},{112,128},... | collective-permute-start | bytes 983048 | tf_op jit(solution)/shard_map/ppermute | solution.py:46
  145.2 19.9 %collective-permute-start.1 = (bf16[1,1,16,32,320]{4,3,2,1,0:T(8,128)(2,1)}, bf16[1,1,16,32,320]{4,3,2,1,0:T(8,128)(2,1)}, u32[]{:S(2)}, u32[]{:S(2)}) collective-permute-start(bf16[1,1,16,32,320]{4,3,2,1,0:T(8,128)(2,1)} %bitcast.189), channel_id=1, source_target_pairs={{16,0},{32,16},{48,32},{64,48},{80,64},{96,80},{112,96},{128,112},... | collective-permute-start | bytes 983048 | tf_op jit(solution)/shard_map/ppermute | solution.py:48
  171.6 8.5 %copy-start.4 = (f32[1,1,16,32,320]{4,3,2,1,0:T(8,128)S(1)}, f32[1,1,16,32,320]{4,3,2,1,0:T(8,128)}, u32[]{:S(2)}) copy-start(f32[1,1,16,32,320]{4,3,2,1,0:T(8,128)} %param.9) | copy-start | bytes 1966084
  171.6 9.6 %copy-start.34 = (bf16[1,16,20,320]{3,1,2,0:T(8,128)(2,1)S(1)}, bf16[1,16,20,320]{3,1,2,0:T(8,128)(2,1)}, u32[]{:S(2)}) copy-start(bf16[1,16,20,320]{3,1,2,0:T(8,128)(2,1)} %get-tuple-element.9) | copy-start | bytes 614404
  171.6 110.0 %all-to-all-start.2 = ((f32[16,3,20,320]{3,2,1,0:T(8,128)}), f32[16,3,20,320]{3,2,1,0:T(8,128)S(1)}, u32[]{:S(2)}, u32[]{:S(2)}) async-start(f32[16,3,20,320]{3,2,1,0:T(8,128)} %copy.54), calls=%async_computation.2 | async-start | bytes 3538944 | tf_op jit(solution)/shard_map/all_to_all | solution.py:62
  175.6 86.5 %collective-permute-start.3 = (bf16[1,1,16,32,320]{4,3,2,1,0:T(8,128)(2,1)S(1)}, bf16[1,1,16,32,320]{4,3,2,1,0:T(8,128)(2,1)}, u32[]{:S(2)}, u32[]{:S(2)}) collective-permute-start(bf16[1,1,16,32,320]{4,3,2,1,0:T(8,128)(2,1)S(1)} %convert_element_type.24), channel_id=1, source_target_pairs={{0,16},{16,32},{32,48},{48,64},{64,80},{80,96},{96,112},{112,128},... | collective-permute-start | bytes 983048 | tf_op jit(solution)/shard_map/ppermute | solution.py:46
  178.8 91.7 %collective-permute-start.2 = (bf16[1,1,16,32,320]{4,3,2,1,0:T(8,128)(2,1)S(1)}, bf16[1,1,16,32,320]{4,3,2,1,0:T(8,128)(2,1)}, u32[]{:S(2)}, u32[]{:S(2)}) collective-permute-start(bf16[1,1,16,32,320]{4,3,2,1,0:T(8,128)(2,1)S(1)} %convert_element_type.24), channel_id=1, source_target_pairs={{16,0},{32,16},{48,32},{64,48},{80,64},{96,80},{112,96},{128,112},... | collective-permute-start | bytes 983048 | tf_op jit(solution)/shard_map/ppermute | solution.py:48
  265.4 7.8 %copy-start.14 = (bf16[320,320]{1,0:T(8,128)(2,1)}, bf16[320,320]{1,0:T(8,128)(2,1)S(1)}, u32[]{:S(2)}) copy-start(bf16[320,320]{1,0:T(8,128)(2,1)S(1)} %squeeze.58) | copy-start | bytes 614404
  274.8 3.0 copy-start.20
  275.2 3.8 %copy-start.6 = (f32[512,320]{0,1:T(8,128)S(1)}, f32[512,320]{0,1:T(8,128)}, u32[]{:S(2)}) copy-start(f32[512,320]{0,1:T(8,128)} %copy.49) | copy-start | bytes 1966084
  275.2 3.8 %copy-start.18 = (bf16[320,320]{1,0:T(8,128)(2,1)S(1)}, bf16[320,320]{1,0:T(8,128)(2,1)}, u32[]{:S(2)}) copy-start(bf16[320,320]{1,0:T(8,128)(2,1)} %copy-done.17) | copy-start | bytes 614404
  276.6 2.8 copy-start.24
  282.5 34.9 %all-to-all-start.3 = ((f32[32,1,600]{2,1,0:T(1,128)}), f32[32,1,600]{2,1,0:T(1,128)S(1)}, u32[]{:S(2)}, u32[]{:S(2)}) async-start(f32[32,1,600]{2,1,0:T(1,128)} %all_to_all.22), calls=%async_computation.3 | async-start | bytes 163840 | tf_op jit(solution)/shard_map/all_to_all | solution.py:62
  304.7 3.5 %copy-start.15 = (bf16[320,320]{1,0:T(8,128)(2,1)S(1)}, bf16[320,320]{1,0:T(8,128)(2,1)}, u32[]{:S(2)}) copy-start(bf16[320,320]{1,0:T(8,128)(2,1)} %copy-done.14) | copy-start | bytes 614404
  307.0 17.4 %copy-start.35 = (bf16[320,320]{1,0:T(8,128)(2,1)S(1)}, bf16[320,320]{1,0:T(8,128)(2,1)}, u32[]{:S(2)}) copy-start(bf16[320,320]{1,0:T(8,128)(2,1)} %squeeze.57) | copy-start | bytes 614404
  318.2 17.5 %all-to-all-start.4 = ((f32[32,1,600]{2,1,0:T(1,128)}), f32[32,1,600]{2,1,0:T(1,128)S(1)}, u32[]{:S(2)}, u32[]{:S(2)}) async-start(f32[32,1,600]{2,1,0:T(1,128)} %broadcast_in_dim.8), calls=%async_computation.4 | async-start | bytes 163840 | tf_op jit(solution)/shard_map/all_to_all | solution.py:14
  (20 other events, 26.3 us)
where the time goes:
time: 338 us; the launch traced here: 337 us
  waiting for transfers between devices  151 us (45%)
  starting transfers between devices  99.8 us (30%)
  local copies, waits for them, and re-layouts  45.9 us (14%)
  matrix products  25.2 us (7%)
  other arithmetic  6.96 us (2%)
  blocking collectives  6.1 us (2%)
    ppermute x2, waiting for transfers between devices, padded_2(): lax.ppermute(tail, axis, [(i, (i + 1) % count) for i in range(ends)])  83.8 us
    all_to_all x2, waiting for transfers between devices, from_everyone(): lax.all_to_all(jnp.broadcast_to(array[None], (peers, *array.shape)), axis...  49.4 us
    ppermute x2, starting transfers between devices, padded_2(): lax.ppermute(tail, axis, [(i, (i + 1) % count) for i in range(ends)])  47.7 us
    all_to_all x2, starting transfers between devices, summed_on_arrival(): lax.all_to_all(cut_along(array, dim, peers), axis, 0, 0, tiled=True)  26.2 us
    all_to_all x2, starting transfers between devices, from_everyone(): lax.all_to_all(jnp.broadcast_to(array[None], (peers, *array.shape)), axis...  23.1 us
    dot_general x12, matrix products, transpose_dot(): lax.dot_general(left, right, (((1,), (1,)), ((), ())), preferred_element_...  13.9 us
    ppermute x2, waiting for transfers between devices, padded_2(): lax.ppermute(head, axis, [((i + 1) % count, i) for i in range(ends)])  9.05 us
    all_to_all x2, waiting for transfers between devices, summed_on_arrival(): lax.all_to_all(cut_along(array, dim, peers), axis, 0, 0, tiled=True)  8.86 us
  transfers between devices with their start and end apart: 8, of which 7 were waited for; matrix products, arithmetic and copies ran while one was open for 11% of the time, Pallas kernels for 0%

commit v1 on v0

v1 whole, which is shorter than its diff:
```python
import math

import jax
import jax.numpy as jnp
from jax import lax
from jax.experimental import pallas as pl
from jax.experimental.pallas import tpu as pltpu
from jax.sharding import Mesh
from jax.sharding import PartitionSpec as P

AXES = ("x", "m", "k", "h", "y", "c")
SIZES = (4, 2, 4, 2, 4, 2)
TM = ("x", "m", "k")
Z_LO = ("m", "k")
CLIP = ("h", "y", "c")
PLANE = ("x", "y")
H, W, C = 16, 32, 320
ROWS = H * W
HALF, PART, OWN = 160, 40, 20
TAPS = 12
PIECE = 64
BF = jnp.bfloat16
F32 = jnp.float32


def pairs_across():
    def place(z):
        return (z % 8) * 2 + z // 8

    there = [(z - 4) % 16 if z % 8 < 4 else (z + 4) % 16 for z in range(16)]
    return [(place(z), place(there[z])) for z in range(16)]


ACROSS = pairs_across()
FRAMES_UP = [(t, t + 1) for t in range(31)]
FRAMES_DOWN = [(t + 1, t) for t in range(31)]


def across(a):
    return lax.ppermute(a, ("m", "k", "h"), ACROSS)


def core_swap(a):
    return lax.ppermute(a, "c", [(0, 1), (1, 0)])


def to_all(a, axes):
    n = lax.axis_size(axes)
    return lax.all_to_all(jnp.broadcast_to(a[None], (n, *a.shape)), axes, 0, 0, tiled=True)


def start_of(x):
    return min(PIECE * x, 6 * PART - PIECE)


def dot(a, b):
    return lax.dot_general(a, b, (((1,), (0,)), ((), ())), preferred_element_type=F32)


def dot_nt(a, b):
    return lax.dot_general(a, b, (((1,), (1,)), ((), ())), preferred_element_type=F32)


def dot_tn(a, b):
    return lax.dot_general(a, b, (((0,), (0,)), ((), ())), preferred_element_type=F32)


def fill_windows(windows, value):
    col = lax.broadcasted_iota(jnp.int32, (ROWS, 1), 0) % W
    edge = jnp.zeros((W, C), BF)
    for d in range(3):
        windows[d, 0:W, :] = edge
        windows[d, W + ROWS : 2 * W + ROWS, :] = edge
    windows[1, W : W + ROWS, :] = value.astype(BF)
    left = jnp.where(col == 0, 0.0, pltpu.roll(value, 1, 0))
    windows[0, W : W + ROWS, :] = left.astype(BF)
    right = jnp.where(col == W - 1, 0.0, pltpu.roll(value, ROWS - 1, 0))
    windows[2, W : W + ROWS, :] = right.astype(BF)


def tap(w_ref, t):
    return w_ref[t].reshape(C, C)


def forward_kernel(
    place, own_m, own_t, oth_m, oth_t, video, bias, cot, cot_prev, cot_next,
    w_ref, hidden_ref, slope_ref, mine_ref, theirs_ref, windows,
):
    c, h = place[0], place[1]
    for source, first, half in (
        (own_m, 6 * c, h), (own_t, 6 * (1 - c), h),
    ):
        for y in range(4):
            for t in range(6):
                w_ref[first + t, half, y * PART : (y + 1) * PART, :] = source[y, t * PART : (t + 1) * PART, :]
    for source, first, half in (
        (oth_m, 6 * c, 1 - h), (oth_t, 6 * (1 - c), 1 - h),
    ):
        for x in range(4):
            for y in range(4):
                at, stop = PIECE * x, min(PIECE * (x + 1), 6 * PART)
                while at < stop:
                    t, r = divmod(at, PART)
                    n = min(PART - r, stop - at)
                    s = at - start_of(x)
                    w_ref[first + t, half, y * PART + r : y * PART + r + n, :] = source[x * 4 + y, s : s + n, :]
                    at += n
    fill_windows(windows, video[...])
    spatial = jnp.zeros((ROWS, C), F32) + bias[...]
    for a in range(3):
        for b in range(3):
            spatial = spatial + dot(windows[b, a * W : a * W + ROWS, :], tap(w_ref, 3 * a + b))
    sig = jax.nn.sigmoid(spatial)
    hidden = (spatial * sig).astype(BF)
    hidden_ref[...] = hidden
    slope_ref[...] = sig * (1.0 + spatial * (1.0 - sig))
    grads = [
        dot_tn(hidden, other)
        for other in (cot_next[...], cot[...].astype(BF), cot_prev[...])
    ]
    pad = jnp.zeros((4, C), F32)
    for half in range(2):
        for y in range(4):
            both = []
            for core in range(2):
                r = half * HALF + y * PART + core * OWN
                both.append(jnp.concatenate([g[r : r + OWN, :] for g in grads] + [pad], axis=0))
            mine = jnp.where(c == 0, both[0], both[1])
            theirs = jnp.where(c == 0, both[1], both[0])
            for x in range(4):
                mine_ref[x, y, half] = mine[16 * x : 16 * x + 16, :]
                theirs_ref[x, y, half] = theirs[16 * x : 16 * x + 16, :]


def backward_kernel(w_ref, slope, cot, cot_prev, cot_next, grad_ref, windows):
    gh = dot_nt(cot_next[...], tap(w_ref, 9))
    gh = gh + dot_nt(cot[...].astype(BF), tap(w_ref, 10))
    gh = gh + dot_nt(cot_prev[...], tap(w_ref, 11))
    gs = (gh * slope[...]).astype(BF).astype(F32)
    fill_windows(windows, gs)
    acc = cot[...]
    for a in range(3):
        for b in range(3):
            acc = acc + dot_nt(windows[2 - b, (2 - a) * W : (2 - a) * W + ROWS, :], tap(w_ref, 3 * a + b))
    grad_ref[...] = acc


def output_kernel(w_ref, video, hidden, prev, after, out_ref):
    acc = video[...] + dot(hidden[...], tap(w_ref, 1))
    acc = acc + dot(prev[...], tap(w_ref, 0))
    out_ref[...] = acc + dot(after[...], tap(w_ref, 2))


def vmem(n):
    return [pl.BlockSpec(memory_space=pltpu.VMEM)] * n


def params():
    return pltpu.CompilerParams(vmem_limit_bytes=48 * 1024 * 1024)


def cost(dots, read):
    return pl.CostEstimate(flops=dots * 2 * ROWS * C * C, bytes_accessed=read, transcendentals=0)


def on_device(video, spatial_w, spatial_b, temporal_w, cotangent):
    c, h, x = lax.axis_index("c"), lax.axis_index("h"), lax.axis_index("x")
    shape = video.shape
    video_f = video.reshape(ROWS, C)
    cot_f = cotangent.reshape(ROWS, C)
    cot_b = cot_f.astype(BF)

    w = jnp.concatenate([spatial_w, temporal_w.astype(BF)], axis=0)
    w = lax.all_to_all(w, "c", 0, 1, tiled=True).reshape(6 * PART, C)
    quarter = lax.dynamic_slice_in_dim(w, jnp.minimum(PIECE * x, 6 * PART - PIECE), PIECE, 0)
    other = across(quarter)
    other, w = lax.optimization_barrier((other, w))
    own_m = to_all(w, "y")
    oth_m = to_all(other, PLANE)
    cot_next = lax.ppermute(cot_b, TM, FRAMES_DOWN)
    cot_prev = lax.ppermute(cot_b, TM, FRAMES_UP)
    own_t, oth_t = core_swap(own_m), core_swap(oth_m)

    place = jnp.stack([c, h]).astype(jnp.int32)
    w_all, hidden, slope, mine, theirs = pl.pallas_call(
        forward_kernel,
        out_shape=(
            jax.ShapeDtypeStruct((TAPS, 2, HALF, C), BF),
            jax.ShapeDtypeStruct((ROWS, C), BF),
            jax.ShapeDtypeStruct((ROWS, C), F32),
            jax.ShapeDtypeStruct((4, 4, 2, 16, C), F32),
            jax.ShapeDtypeStruct((4, 4, 2, 16, C), F32),
        ),
        in_specs=[pl.BlockSpec(memory_space=pltpu.SMEM)] + vmem(9),
        out_specs=vmem(5),
        scratch_shapes=[pltpu.VMEM((3, ROWS + 2 * W, C), BF)],
        compiler_params=params(),
        cost_estimate=cost(12, 8_000_000),
        name="forward",
    )(place, own_m, own_t, oth_m, oth_t, video_f, spatial_b.reshape(1, C), cot_f, cot_prev, cot_next)

    part = mine + core_swap(theirs)
    part = lax.all_to_all(part.reshape(16, 2, 16, C), PLANE, 0, 0, tiled=True)

    prev = lax.ppermute(hidden, TM, FRAMES_UP)
    after = lax.ppermute(hidden, TM, FRAMES_DOWN)
    grad_video = pl.pallas_call(
        backward_kernel,
        out_shape=jax.ShapeDtypeStruct((ROWS, C), F32),
        in_specs=vmem(5),
        out_specs=vmem(1)[0],
        scratch_shapes=[pltpu.VMEM((3, ROWS + 2 * W, C), BF)],
        compiler_params=params(),
        cost_estimate=cost(12, 5_000_000),
        name="backward",
    )(w_all, slope, cot_f, cot_prev, cot_next)

    part = jnp.sum(part, axis=0)
    keep = jnp.where(h == 0, part[0], part[1])
    give = jnp.where(h == 0, part[1], part[0])
    part = keep + across(give)
    part = jnp.sum(to_all(part, Z_LO), axis=0)
    part = to_all(part, "x").reshape(4 * 16, C)
    output = pl.pallas_call(
        output_kernel,
        out_shape=jax.ShapeDtypeStruct((ROWS, C), F32),
        in_specs=vmem(5),
        out_specs=vmem(1)[0],
        compiler_params=params(),
        cost_estimate=cost(3, 3_000_000),
        name="output",
    )(w_all[9:], video_f, hidden, prev, after)
    total_rows = ROWS * lax.axis_size(TM) * lax.axis_size(CLIP)
    grad_temporal = part[: 3 * OWN].reshape(3, OWN, C) * (1.0 / math.sqrt(total_rows))
    return output.reshape(shape), grad_video.reshape(shape), grad_temporal


def solution(mesh):
    finer = Mesh(mesh.devices.reshape(SIZES), AXES)
    placed = (
        P(CLIP, TM, None, None, None),
        P(None, CLIP, None),
        P(),
        P(None, CLIP, None),
        P(CLIP, TM, None, None, None),
    )
    return jax.shard_map(
        on_device,
        mesh=finer,
        in_specs=placed,
        out_specs=(
            P(CLIP, TM, None, None, None),
            P(CLIP, TM, None, None, None),
            P(None, CLIP, None),
        ),
        check_vma=False,
    )
```

time: 338 us -> 167 us (0.49)
  the two profiles are of different devices: /device:TPU:8 before, /device:TPU:2 now
where the time goes in v1:
time: 167 us; the launch traced here: 166 us
  starting transfers between devices  77.5 us (46%)
  waiting for transfers between devices  60.1 us (36%)
  Pallas kernels  13.6 us (8%)
  local copies, waits for them, and re-layouts  8.7 us (5%)
  other arithmetic  4.88 us (3%)
    all_to_all x4, starting transfers between devices, to_all(): lax.all_to_all(jnp.broadcast_to(a[None], (n, *a.shape)), axes, 0, 0, tile...  19.3 us
    ppermute x2, starting transfers between devices, across(): return lax.ppermute(a, ('m', 'k', 'h'), ACROSS)  19 us
    all_to_all x4, waiting for transfers between devices, to_all(): lax.all_to_all(jnp.broadcast_to(a[None], (n, *a.shape)), axes, 0, 0, tile...  16.1 us
    ppermute x1, starting transfers between devices, on_device(): after = lax.ppermute(hidden, TM, FRAMES_DOWN)  12.5 us
    all_to_all x1, waiting for transfers between devices, on_device(): part = lax.all_to_all(part.reshape(16, 2, 16, C), PLANE, 0, 0, tiled=True)  12.2 us
    ppermute x1, waiting for transfers between devices, on_device(): cot_prev = lax.ppermute(cot_b, TM, FRAMES_UP)  11.2 us
    ppermute x1, starting transfers between devices, on_device(): cot_next = lax.ppermute(cot_b, TM, FRAMES_DOWN)  9.52 us
    ppermute x2, waiting for transfers between devices, across(): return lax.ppermute(a, ('m', 'k', 'h'), ACROSS)  7.85 us
  transfers between devices with their start and end apart: 15, of which 10 were waited for; matrix products, arithmetic and copies ran while one was open for 2% of the time, Pallas kernels for 4%

profile of v1, /device:TPU:2, one launch (start us, length us, event | category | flops | bytes accessed | tf_op | source)
XLA Modules:
  0.0 165.6 jit_solution(13774000758864951749)
XLA Ops:
  1.5 1.7 pad_maximum_fusion
  3.2 3.4 %all-to-all-start = ((bf16[12,20,320]{2,1,0:T(8,128)(2,1)}), bf16[12,20,320]{2,1,0:T(8,128)(2,1)S(1)}, u32[]{:S(2)}, u32[]{:S(2)}) async-start(bf16[12,20,320]{2,1,0:T(8,128)(2,1)} %pad_maximum_fusion), calls=%async_computation | async-start | bytes 442368 | tf_op jit(solution)/shard_map/all_to_all | solution.py:174
  6.7 1.5 all-to-all-done
  8.3 12.7 %collective-permute-start = (bf16[64,320]{1,0:T(8,128)(2,1)S(1)}, bf16[64,320]{1,0:T(8,128)(2,1)S(1)}, u32[]{:S(2)}, u32[]{:S(2)}) collective-permute-start(bf16[64,320]{1,0:T(8,128)(2,1)S(1)} %constant_dynamic-slice_fusion), channel_id=1, source_target_pairs={{0,72},{16,88},{32,104},{48,120},{64,8},{80,24},{96,40},{112,56},{... | collective-permute-start | bytes 122888 | tf_op jit(solution)/shard_map/ppermute | solution.py:40
  21.0 4.5 %collective-permute-done = bf16[64,320]{1,0:T(8,128)(2,1)S(1)} collective-permute-done((bf16[64,320]{1,0:T(8,128)(2,1)S(1)}, bf16[64,320]{1,0:T(8,128)(2,1)S(1)}, u32[]{:S(2)}, u32[]{:S(2)}) %collective-permute-start) | collective-permute-done | bytes 40992 | tf_op jit(solution)/shard_map/ppermute | solution.py:40
  26.5 7.5 %all-to-all-start.2 = ((bf16[16,64,320]{2,1,0:T(8,128)(2,1)}), bf16[16,64,320]{2,1,0:T(8,128)(2,1)S(1)}, u32[]{:S(2)}, u32[]{:S(2)}) async-start(bf16[16,64,320]{2,1,0:T(8,128)(2,1)} %broadcast_in_dim.9), calls=%async_computation.2 | async-start | bytes 1572864 | tf_op jit(solution)/shard_map/all_to_all | solution.py:49
  34.1 9.3 %all-to-all-done.2.oth_m = bf16[16,64,320]{2,1,0:T(8,128)(2,1)S(1)} async-done(((bf16[16,64,320]{2,1,0:T(8,128)(2,1)}), bf16[16,64,320]{2,1,0:T(8,128)(2,1)S(1)}, u32[]{:S(2)}, u32[]{:S(2)}) %all-to-all-start.2) | async-done | bytes 655392 | tf_op jit(solution)/shard_map/all_to_all | solution.py:49
  44.3 3.5 %all-to-all-start.1 = ((bf16[4,240,320]{1,2,0:T(8,128)(2,1)}), bf16[4,240,320]{1,2,0:T(8,128)(2,1)S(1)}, u32[]{:S(2)}, u32[]{:S(2)}) async-start(bf16[4,240,320]{1,2,0:T(8,128)(2,1)} %broadcast_in_dim.8), calls=%async_computation.1 | async-start | bytes 1310720 | tf_op jit(solution)/shard_map/all_to_all | solution.py:49
  47.8 1.9 %collective-permute-start.2 = (bf16[16,64,320]{2,1,0:T(8,128)(2,1)S(1)}, bf16[16,64,320]{2,1,0:T(8,128)(2,1)}, u32[]{:S(2)}, u32[]{:S(2)}) collective-permute-start(bf16[16,64,320]{2,1,0:T(8,128)(2,1)S(1)} %all-to-all-done.2.oth_m), channel_id=1, source_target_pairs={{0,1},{1,0},{2,3},{3,2},{4,5},{5,4},{6,7},{7,6},{8,9},{9,8},{10,11... | collective-permute-start | bytes 1966088 | tf_op jit(solution)/shard_map/ppermute | solution.py:44
  49.7 6.8 %all-to-all-done.1 = bf16[4,240,320]{1,2,0:T(8,128)(2,1)S(1)} async-done(((bf16[4,240,320]{1,2,0:T(8,128)(2,1)}), bf16[4,240,320]{1,2,0:T(8,128)(2,1)S(1)}, u32[]{:S(2)}, u32[]{:S(2)}) %all-to-all-start.1) | async-done | bytes 614432 | tf_op jit(solution)/shard_map/all_to_all | solution.py:49
  56.5 1.9 %collective-permute-start.1 = (bf16[4,240,320]{1,2,0:T(8,128)(2,1)S(1)}, bf16[4,240,320]{1,2,0:T(8,128)(2,1)}, u32[]{:S(2)}, u32[]{:S(2)}) collective-permute-start(bf16[4,240,320]{1,2,0:T(8,128)(2,1)S(1)} %all-to-all-done.1), channel_id=1, source_target_pairs={{0,1},{1,0},{2,3},{3,2},{4,5},{5,4},{6,7},{7,6},{8,9},{9,8},{10,11... | collective-permute-start | bytes 1843208 | tf_op jit(solution)/shard_map/ppermute | solution.py:44
  58.5 9.5 %collective-permute-start.4 = (bf16[512,320]{1,0:T(8,128)(2,1)S(1)}, bf16[512,320]{1,0:T(8,128)(2,1)S(1)}, u32[]{:S(2)}, u32[]{:S(2)}) collective-permute-start(bf16[512,320]{1,0:T(8,128)(2,1)S(1)} %bitcast_convert_fusion), channel_id=1, source_target_pairs={{16,0},{32,16},{48,32},{64,48},{80,64},{96,80},{112,96},{128,112},... | collective-permute-start | bytes 983048 | tf_op jit(solution)/shard_map/ppermute | solution.py:180
  68.0 1.9 %collective-permute-start.3 = (bf16[512,320]{1,0:T(8,128)(2,1)S(1)}, bf16[512,320]{1,0:T(8,128)(2,1)S(1)}, u32[]{:S(2)}, u32[]{:S(2)}) collective-permute-start(bf16[512,320]{1,0:T(8,128)(2,1)S(1)} %bitcast_convert_fusion), channel_id=1, source_target_pairs={{0,16},{16,32},{32,48},{48,64},{64,80},{80,96},{96,112},{112,128},... | collective-permute-start | bytes 983048 | tf_op jit(solution)/shard_map/ppermute | solution.py:181
  70.4 1.4 copy.17.own_t
  71.9 5.6 %collective-permute-done.4.cot_next = bf16[512,320]{1,0:T(8,128)(2,1)S(1)} collective-permute-done((bf16[512,320]{1,0:T(8,128)(2,1)S(1)}, bf16[512,320]{1,0:T(8,128)(2,1)S(1)}, u32[]{:S(2)}, u32[]{:S(2)}) %collective-permute-start.4) | collective-permute-done | bytes 327712 | tf_op jit(solution)/shard_map/ppermute | solution.py:180
  77.5 11.2 %collective-permute-done.3.cot_prev = bf16[512,320]{1,0:T(8,128)(2,1)S(1)} collective-permute-done((bf16[512,320]{1,0:T(8,128)(2,1)S(1)}, bf16[512,320]{1,0:T(8,128)(2,1)S(1)}, u32[]{:S(2)}, u32[]{:S(2)}) %collective-permute-start.3) | collective-permute-done | bytes 327712 | tf_op jit(solution)/shard_map/ppermute | solution.py:181
  88.7 6.2 %forward.1 = (bf16[12,2,160,320]{3,2,1,0:T(8,128)(2,1)}, bf16[512,320]{1,0:T(8,128)(2,1)S(1)}, f32[512,320]{1,0:T(8,128)S(1)}, f32[4,4,2,16,320]{4,3,2,1,0:T(8,128)S(1)}, f32[4,4,2,16,320]{4,3,2,1,0:T(8,128)S(1)}) custom-call(s32[2]{0:T(128)S(1)} %pad_add_fusion.place, bf16[4,240,320]{2,1,0:T(8,128)(2,1)S(1)} %copy.16.own_m, ...), custom_call_target="tpu_custom_call" | custom-call | flops 1258291200 | bytes 8000000 | tf_op jit(solution)/shard_map/forward/pallas_call | solution.py:185
  95.7 1.9 %collective-permute-start.7 = (f32[4,4,2,16,320]{4,3,2,1,0:T(8,128)S(1)}, f32[4,4,2,16,320]{4,3,2,1,0:T(8,128)S(1)}, u32[]{:S(2)}, u32[]{:S(2)}) collective-permute-start(f32[4,4,2,16,320]{4,3,2,1,0:T(8,128)S(1)} %get-tuple-element.16), channel_id=1, source_target_pairs={{0,1},{1,0},{2,3},{3,2},{4,5},{5,4},{6,7},{7,6},{8,9},{9,8},{10,11... | collective-permute-start | bytes 1966088 | tf_op jit(solution)/shard_map/ppermute | solution.py:44
  97.6 2.3 %collective-permute-done.7 = f32[4,4,2,16,320]{4,3,2,1,0:T(8,128)S(1)} collective-permute-done((f32[4,4,2,16,320]{4,3,2,1,0:T(8,128)S(1)}, f32[4,4,2,16,320]{4,3,2,1,0:T(8,128)S(1)}, u32[]{:S(2)}, u32[]{:S(2)}) %collective-permute-start.7) | collective-permute-done | bytes 655392 | tf_op jit(solution)/shard_map/ppermute | solution.py:44
  100.9 4.2 %all-to-all-start.3 = ((f32[16,2,16,320]{3,2,1,0:T(8,128)}), f32[16,2,16,320]{3,2,1,0:T(8,128)}, u32[]{:S(2)}, u32[]{:S(2)}) async-start(f32[16,2,16,320]{3,2,1,0:T(8,128)} %bitcast.8), calls=%async_computation.3 | async-start | bytes 1572864 | tf_op jit(solution)/shard_map/all_to_all | solution.py:203
  105.1 12.2 %all-to-all-done.3 = f32[16,2,16,320]{3,2,1,0:T(8,128)} async-done(((f32[16,2,16,320]{3,2,1,0:T(8,128)}), f32[16,2,16,320]{3,2,1,0:T(8,128)}, u32[]{:S(2)}, u32[]{:S(2)}) %all-to-all-start.3) | async-done | bytes 655392 | tf_op jit(solution)/shard_map/all_to_all | solution.py:203
  117.3 1.2 reduce_sum.18
  118.5 6.3 %collective-permute-start.8 = (f32[16,320]{1,0:T(8,128)S(1)}, f32[16,320]{1,0:T(8,128)S(1)}, u32[]{:S(2)}, u32[]{:S(2)}) collective-permute-start(f32[16,320]{1,0:T(8,128)S(1)} %select_bitcast_fusion), channel_id=1, source_target_pairs={{0,72},{16,88},{32,104},{48,120},{64,8},{80,24},{96,40},{112,56},{... | collective-permute-start | bytes 61448 | tf_op jit(solution)/shard_map/ppermute | solution.py:40
  124.7 3.4 %collective-permute-done.8 = f32[16,320]{1,0:T(8,128)S(1)} collective-permute-done((f32[16,320]{1,0:T(8,128)S(1)}, f32[16,320]{1,0:T(8,128)S(1)}, u32[]{:S(2)}, u32[]{:S(2)}) %collective-permute-start.8) | collective-permute-done | bytes 20512 | tf_op jit(solution)/shard_map/ppermute | solution.py:40
  128.8 3.4 %all-to-all-start.4 = ((f32[8,16,320]{2,1,0:T(8,128)}), f32[8,16,320]{2,1,0:T(8,128)S(1)}, u32[]{:S(2)}, u32[]{:S(2)}) async-start(f32[8,16,320]{2,1,0:T(8,128)} %broadcast_in_dim.10), calls=%async_computation.4 | async-start | bytes 393216 | tf_op jit(solution)/shard_map/all_to_all | solution.py:49
  132.2 12.5 %collective-permute-start.6 = (bf16[512,320]{1,0:T(8,128)(2,1)S(1)}, bf16[512,320]{1,0:T(8,128)(2,1)S(1)}, u32[]{:S(2)}, u32[]{:S(2)}) collective-permute-start(bf16[512,320]{1,0:T(8,128)(2,1)S(1)} %get-tuple-element.13.hidden), channel_id=1, source_target_pairs={{16,0},{32,16},{48,32},{64,48},{80,64},{96,80},{112,96},{128,112},... | collective-permute-start | bytes 983048 | tf_op jit(solution)/shard_map/ppermute | solution.py:206
  144.7 1.9 %collective-permute-start.5 = (bf16[512,320]{1,0:T(8,128)(2,1)S(1)}, bf16[512,320]{1,0:T(8,128)(2,1)}, u32[]{:S(2)}, u32[]{:S(2)}) collective-permute-start(bf16[512,320]{1,0:T(8,128)(2,1)S(1)} %get-tuple-element.13.hidden), channel_id=1, source_target_pairs={{0,16},{16,32},{32,48},{48,64},{64,80},{80,96},{96,112},{112,128},... | collective-permute-start | bytes 983048 | tf_op jit(solution)/shard_map/ppermute | solution.py:205
  147.3 5.0 %all-to-all-start.5 = ((f32[4,16,320]{2,1,0:T(8,128)}), f32[4,16,320]{2,1,0:T(8,128)S(1)}, u32[]{:S(2)}, u32[]{:S(2)}) async-start(f32[4,16,320]{2,1,0:T(8,128)} %broadcast_in_dim.11), calls=%async_computation.5 | async-start | bytes 196608 | tf_op jit(solution)/shard_map/all_to_all | solution.py:49
  152.3 1.8 %copy-done.2 = bf16[12,2,160,320]{3,2,1,0:T(8,128)(2,1)S(1)} copy-done((bf16[12,2,160,320]{3,2,1,0:T(8,128)(2,1)S(1)}, bf16[12,2,160,320]{3,2,1,0:T(8,128)(2,1)}, u32[]{:S(2)}) %copy-start.2) | copy-done | bytes 2457624
  154.1 4.6 %backward.1 = f32[512,320]{1,0:T(8,128)} custom-call(bf16[12,2,160,320]{3,2,1,0:T(8,128)(2,1)S(1)} %copy-done.2, f32[512,320]{1,0:T(8,128)S(1)} %copy-done.5, f32[512,320]{1,0:T(8,128)S(1)} %bitcast.18, bf16[512,320]{1,0:T(8,128)(2,1)S(1)} %collective-permute-done.3.cot_prev, bf16[512,320]{1,0:T(8,128)(2,1)S(1)} %collective-permute-done.4.cot_next), custom_call_target="tpu_custom_call" | custom-call | flops 1258291200 | bytes 5000000 | tf_op jit(solution)/shard_map/backward/pallas_call | solution.py:207
  158.8 3.3 %collective-permute-done.5.prev = bf16[512,320]{1,0:T(8,128)(2,1)} collective-permute-done((bf16[512,320]{1,0:T(8,128)(2,1)S(1)}, bf16[512,320]{1,0:T(8,128)(2,1)}, u32[]{:S(2)}, u32[]{:S(2)}) %collective-permute-start.5) | collective-permute-done | bytes 327712 | tf_op jit(solution)/shard_map/ppermute | solution.py:205
  162.2 2.8 %output.1 = f32[512,320]{1,0:T(8,128)} custom-call(bf16[3,2,160,320]{3,2,1,0:T(8,128)(2,1)S(1)} %slice.14.w_ref, f32[512,320]{1,0:T(8,128)S(1)} %bitcast.20, bf16[512,320]{1,0:T(8,128)(2,1)S(1)} %get-tuple-element.13.hidden, bf16[512,320]{1,0:T(8,128)(2,1)} %collective-permute-done.5.prev, bf16[512,320]{1,0:T(8,128)(2,1)S(1)} %collective-permute-done.6.after), custom_call_target="tpu_custom_call" | custom-call | flops 314572800 | bytes 3000000 | tf_op jit(solution)/shard_map/output/pallas_call | solution.py:224
  (38 shorter events, 7.5 us)
Async XLA Ops:
  3.2 5.0 %all-to-all-start = ((bf16[12,20,320]{2,1,0:T(8,128)(2,1)}), bf16[12,20,320]{2,1,0:T(8,128)(2,1)S(1)}, u32[]{:S(2)}, u32[]{:S(2)}) async-start(bf16[12,20,320]{2,1,0:T(8,128)(2,1)} %pad_maximum_fusion), calls=%async_computation | async-start | bytes 442368 | tf_op jit(solution)/shard_map/all_to_all | solution.py:174
  6.6 51.8 %copy-start = (f32[1,1,16,32,320]{4,3,2,1,0:T(8,128)S(1)}, f32[1,1,16,32,320]{4,3,2,1,0:T(8,128)}, u32[]{:S(2)}) copy-start(f32[1,1,16,32,320]{4,3,2,1,0:T(8,128)} %param.9) | copy-start | bytes 1966084
  8.3 61.7 %copy-start.6 = (f32[320]{0:T(512)S(1)}, f32[320]{0:T(512)}, u32[]{:S(2)}) copy-start(f32[320]{0:T(512)} %param.7) | copy-start | bytes 3844
  8.3 17.2 %collective-permute-start = (bf16[64,320]{1,0:T(8,128)(2,1)S(1)}, bf16[64,320]{1,0:T(8,128)(2,1)S(1)}, u32[]{:S(2)}, u32[]{:S(2)}) collective-permute-start(bf16[64,320]{1,0:T(8,128)(2,1)S(1)} %constant_dynamic-slice_fusion), channel_id=1, source_target_pairs={{0,72},{16,88},{32,104},{48,120},{64,8},{80,24},{96,40},{112,56},{... | collective-permute-start | bytes 122888 | tf_op jit(solution)/shard_map/ppermute | solution.py:40
  26.5 16.9 %all-to-all-start.2 = ((bf16[16,64,320]{2,1,0:T(8,128)(2,1)}), bf16[16,64,320]{2,1,0:T(8,128)(2,1)S(1)}, u32[]{:S(2)}, u32[]{:S(2)}) async-start(bf16[16,64,320]{2,1,0:T(8,128)(2,1)} %broadcast_in_dim.9), calls=%async_computation.2 | async-start | bytes 1572864 | tf_op jit(solution)/shard_map/all_to_all | solution.py:49
  44.3 12.2 %all-to-all-start.1 = ((bf16[4,240,320]{1,2,0:T(8,128)(2,1)}), bf16[4,240,320]{1,2,0:T(8,128)(2,1)S(1)}, u32[]{:S(2)}, u32[]{:S(2)}) async-start(bf16[4,240,320]{1,2,0:T(8,128)(2,1)} %broadcast_in_dim.8), calls=%async_computation.1 | async-start | bytes 1310720 | tf_op jit(solution)/shard_map/all_to_all | solution.py:49
  47.8 40.9 %collective-permute-start.2 = (bf16[16,64,320]{2,1,0:T(8,128)(2,1)S(1)}, bf16[16,64,320]{2,1,0:T(8,128)(2,1)}, u32[]{:S(2)}, u32[]{:S(2)}) collective-permute-start(bf16[16,64,320]{2,1,0:T(8,128)(2,1)S(1)} %all-to-all-done.2.oth_m), channel_id=1, source_target_pairs={{0,1},{1,0},{2,3},{3,2},{4,5},{5,4},{6,7},{7,6},{8,9},{9,8},{10,11... | collective-permute-start | bytes 1966088 | tf_op jit(solution)/shard_map/ppermute | solution.py:44
  56.5 13.9 %collective-permute-start.1 = (bf16[4,240,320]{1,2,0:T(8,128)(2,1)S(1)}, bf16[4,240,320]{1,2,0:T(8,128)(2,1)}, u32[]{:S(2)}, u32[]{:S(2)}) collective-permute-start(bf16[4,240,320]{1,2,0:T(8,128)(2,1)S(1)} %all-to-all-done.1), channel_id=1, source_target_pairs={{0,1},{1,0},{2,3},{3,2},{4,5},{5,4},{6,7},{7,6},{8,9},{9,8},{10,11... | collective-permute-start | bytes 1843208 | tf_op jit(solution)/shard_map/ppermute | solution.py:44
  58.5 19.0 %collective-permute-start.4 = (bf16[512,320]{1,0:T(8,128)(2,1)S(1)}, bf16[512,320]{1,0:T(8,128)(2,1)S(1)}, u32[]{:S(2)}, u32[]{:S(2)}) collective-permute-start(bf16[512,320]{1,0:T(8,128)(2,1)S(1)} %bitcast_convert_fusion), channel_id=1, source_target_pairs={{16,0},{32,16},{48,32},{64,48},{80,64},{96,80},{112,96},{128,112},... | collective-permute-start | bytes 983048 | tf_op jit(solution)/shard_map/ppermute | solution.py:180
  68.0 20.6 %collective-permute-start.3 = (bf16[512,320]{1,0:T(8,128)(2,1)S(1)}, bf16[512,320]{1,0:T(8,128)(2,1)S(1)}, u32[]{:S(2)}, u32[]{:S(2)}) collective-permute-start(bf16[512,320]{1,0:T(8,128)(2,1)S(1)} %bitcast_convert_fusion), channel_id=1, source_target_pairs={{0,16},{16,32},{32,48},{48,64},{64,80},{80,96},{96,112},{112,128},... | collective-permute-start | bytes 983048 | tf_op jit(solution)/shard_map/ppermute | solution.py:181
  94.8 0.9 copy-start.4
  95.7 4.2 %collective-permute-start.7 = (f32[4,4,2,16,320]{4,3,2,1,0:T(8,128)S(1)}, f32[4,4,2,16,320]{4,3,2,1,0:T(8,128)S(1)}, u32[]{:S(2)}, u32[]{:S(2)}) collective-permute-start(f32[4,4,2,16,320]{4,3,2,1,0:T(8,128)S(1)} %get-tuple-element.16), channel_id=1, source_target_pairs={{0,1},{1,0},{2,3},{3,2},{4,5},{5,4},{6,7},{7,6},{8,9},{9,8},{10,11... | collective-permute-start | bytes 1966088 | tf_op jit(solution)/shard_map/ppermute | solution.py:44
  99.9 52.4 %copy-start.1 = (f32[1,1,16,32,320]{4,3,2,1,0:T(8,128)S(1)}, f32[1,1,16,32,320]{4,3,2,1,0:T(8,128)}, u32[]{:S(2)}) copy-start(f32[1,1,16,32,320]{4,3,2,1,0:T(8,128)} %param.9) | copy-start | bytes 1966084
  99.9 52.4 %copy-start.5 = (f32[512,320]{1,0:T(8,128)S(1)}, f32[512,320]{1,0:T(8,128)}, u32[]{:S(2)}) copy-start(f32[512,320]{1,0:T(8,128)} %copy-done.4) | copy-start | bytes 1966084
  100.9 16.4 %all-to-all-start.3 = ((f32[16,2,16,320]{3,2,1,0:T(8,128)}), f32[16,2,16,320]{3,2,1,0:T(8,128)}, u32[]{:S(2)}, u32[]{:S(2)}) async-start(f32[16,2,16,320]{3,2,1,0:T(8,128)} %bitcast.8), calls=%async_computation.3 | async-start | bytes 1572864 | tf_op jit(solution)/shard_map/all_to_all | solution.py:203
  118.5 9.6 %collective-permute-start.8 = (f32[16,320]{1,0:T(8,128)S(1)}, f32[16,320]{1,0:T(8,128)S(1)}, u32[]{:S(2)}, u32[]{:S(2)}) collective-permute-start(f32[16,320]{1,0:T(8,128)S(1)} %select_bitcast_fusion), channel_id=1, source_target_pairs={{0,72},{16,88},{32,104},{48,120},{64,8},{80,24},{96,40},{112,56},{... | collective-permute-start | bytes 61448 | tf_op jit(solution)/shard_map/ppermute | solution.py:40
  128.8 17.8 %all-to-all-start.4 = ((f32[8,16,320]{2,1,0:T(8,128)}), f32[8,16,320]{2,1,0:T(8,128)S(1)}, u32[]{:S(2)}, u32[]{:S(2)}) async-start(f32[8,16,320]{2,1,0:T(8,128)} %broadcast_in_dim.10), calls=%async_computation.4 | async-start | bytes 393216 | tf_op jit(solution)/shard_map/all_to_all | solution.py:49
  132.2 26.6 %collective-permute-start.6 = (bf16[512,320]{1,0:T(8,128)(2,1)S(1)}, bf16[512,320]{1,0:T(8,128)(2,1)S(1)}, u32[]{:S(2)}, u32[]{:S(2)}) collective-permute-start(bf16[512,320]{1,0:T(8,128)(2,1)S(1)} %get-tuple-element.13.hidden), channel_id=1, source_target_pairs={{16,0},{32,16},{48,32},{64,48},{80,64},{96,80},{112,96},{128,112},... | collective-permute-start | bytes 983048 | tf_op jit(solution)/shard_map/ppermute | solution.py:206
  144.7 17.5 %collective-permute-start.5 = (bf16[512,320]{1,0:T(8,128)(2,1)S(1)}, bf16[512,320]{1,0:T(8,128)(2,1)}, u32[]{:S(2)}, u32[]{:S(2)}) collective-permute-start(bf16[512,320]{1,0:T(8,128)(2,1)S(1)} %get-tuple-element.13.hidden), channel_id=1, source_target_pairs={{0,16},{16,32},{32,48},{48,64},{64,80},{80,96},{96,112},{112,128},... | collective-permute-start | bytes 983048 | tf_op jit(solution)/shard_map/ppermute | solution.py:205
  147.3 17.7 %all-to-all-start.5 = ((f32[4,16,320]{2,1,0:T(8,128)}), f32[4,16,320]{2,1,0:T(8,128)S(1)}, u32[]{:S(2)}, u32[]{:S(2)}) async-start(f32[4,16,320]{2,1,0:T(8,128)} %broadcast_in_dim.11), calls=%async_computation.5 | async-start | bytes 196608 | tf_op jit(solution)/shard_map/all_to_all | solution.py:49
  152.3 1.8 %copy-start.2 = (bf16[12,2,160,320]{3,2,1,0:T(8,128)(2,1)S(1)}, bf16[12,2,160,320]{3,2,1,0:T(8,128)(2,1)}, u32[]{:S(2)}) copy-start(bf16[12,2,160,320]{3,2,1,0:T(8,128)(2,1)} %get-tuple-element.12.w_ref) | copy-start | bytes 7372804
  154.1 8.1 %copy-start.3 = (f32[1,1,16,32,320]{4,3,2,1,0:T(8,128)S(1)}, f32[1,1,16,32,320]{4,3,2,1,0:T(8,128)}, u32[]{:S(2)}) copy-start(f32[1,1,16,32,320]{4,3,2,1,0:T(8,128)} %param.5) | copy-start | bytes 1966084

commit v2 on v1

v2 whole, which is shorter than its diff:
```python
import math

import jax
import jax.numpy as jnp
from jax import lax
from jax.experimental import pallas as pl
from jax.experimental.pallas import tpu as pltpu
from jax.sharding import Mesh
from jax.sharding import PartitionSpec as P

AXES = ("x", "m", "k", "h", "y", "c")
SIZES = (4, 2, 4, 2, 4, 2)
TM = ("x", "m", "k")
Z_LO = ("m", "k")
CLIP = ("h", "y", "c")
PLANE = ("x", "y")
H, W, C = 16, 32, 320
ROWS = H * W
HALF, PART, OWN = 160, 40, 20
TAPS = 12
BF = jnp.bfloat16
F32 = jnp.float32


def pairs_across():
    def place(z):
        return (z % 8) * 2 + z // 8

    there = [(z - 4) % 16 if z % 8 < 4 else (z + 4) % 16 for z in range(16)]
    return [(place(z), place(there[z])) for z in range(16)]


ACROSS = pairs_across()
FRAMES_UP = [(t, t + 1) for t in range(31)]
FRAMES_DOWN = [(t + 1, t) for t in range(31)]


def across(a):
    return lax.ppermute(a, ("m", "k", "h"), ACROSS)


def core_swap(a):
    return lax.ppermute(a, "c", [(0, 1), (1, 0)])


def to_all(a, axes):
    n = lax.axis_size(axes)
    return lax.all_to_all(jnp.broadcast_to(a[None], (n, *a.shape)), axes, 0, 0, tiled=True)


def dot(a, b):
    return lax.dot_general(a, b, (((1,), (0,)), ((), ())), preferred_element_type=F32)


def dot_nt(a, b):
    return lax.dot_general(a, b, (((1,), (1,)), ((), ())), preferred_element_type=F32)


def dot_tn(a, b):
    return lax.dot_general(a, b, (((0,), (0,)), ((), ())), preferred_element_type=F32)


def fill_windows(windows, value):
    col = lax.broadcasted_iota(jnp.int32, (ROWS, 1), 0) % W
    edge = jnp.zeros((W, C), BF)
    for d in range(3):
        windows[d, 0:W, :] = edge
        windows[d, W + ROWS : 2 * W + ROWS, :] = edge
    windows[1, W : W + ROWS, :] = value.astype(BF)
    left = jnp.where(col == 0, 0.0, pltpu.roll(value, 1, 0))
    windows[0, W : W + ROWS, :] = left.astype(BF)
    right = jnp.where(col == W - 1, 0.0, pltpu.roll(value, ROWS - 1, 0))
    windows[2, W : W + ROWS, :] = right.astype(BF)


def tap(w_ref, t):
    return w_ref[t].reshape(C, C)


def join(w_ref, t, half, y, mine, theirs, c):
    low = jnp.where(c == 0, mine, theirs)
    high = jnp.where(c == 0, theirs, mine)
    w_ref[t, half, y * PART : (y + 1) * PART, :] = jnp.concatenate([low, high], axis=0)


def prepare_kernel(place, own_m, own_t, video, w_ref, windows):
    c = place[0]
    for t in range(TAPS):
        for y in range(4):
            join(w_ref, t, 0, y, own_m[y, t], own_t[y, t], c)
    fill_windows(windows, video[...])


def forward_kernel(
    place, own, oth_m, oth_t, windows, bias, cot, cot_prev, cot_next,
    w_ref, hidden_ref, slope_ref, mine_ref, theirs_ref,
):
    c, h = place[0], place[1]
    for t in range(TAPS):
        w_ref[t, h] = own[t, 0]
        for y in range(4):
            source = (t // 3) * 4 + y
            join(w_ref, t, 1 - h, y, oth_m[source, t % 3], oth_t[source, t % 3], c)
    spatial = jnp.zeros((ROWS, C), F32) + bias[...]
    for a in range(3):
        for b in range(3):
            spatial = spatial + dot(windows[b, a * W : a * W + ROWS, :], tap(w_ref, 3 * a + b))
    sig = jax.nn.sigmoid(spatial)
    hidden = (spatial * sig).astype(BF)
    hidden_ref[...] = hidden
    slope_ref[...] = sig * (1.0 + spatial * (1.0 - sig))
    grads = [
        dot_tn(hidden, other)
        for other in (cot_next[...], cot[...].astype(BF), cot_prev[...])
    ]
    pad = jnp.zeros((4, C), F32)
    for half in range(2):
        for y in range(4):
            both = []
            for core in range(2):
                r = half * HALF + y * PART + core * OWN
                both.append(jnp.concatenate([g[r : r + OWN, :] for g in grads] + [pad], axis=0))
            mine = jnp.where(c == 0, both[0], both[1])
            theirs = jnp.where(c == 0, both[1], both[0])
            for x in range(4):
                mine_ref[x, y, half] = mine[16 * x : 16 * x + 16, :]
                theirs_ref[x, y, half] = theirs[16 * x : 16 * x + 16, :]


def split_kernel(place, parts, keep_ref, give_ref):
    h = place[1]
    total = parts[0]
    for i in range(1, 16):
        total = total + parts[i]
    keep_ref[...] = jnp.where(h == 0, total[0], total[1])
    give_ref[...] = jnp.where(h == 0, total[1], total[0])


def backward_kernel(w_ref, slope, cot, cot_prev, cot_next, grad_ref, windows):
    gh = dot_nt(cot_next[...], tap(w_ref, 9))
    gh = gh + dot_nt(cot[...].astype(BF), tap(w_ref, 10))
    gh = gh + dot_nt(cot_prev[...], tap(w_ref, 11))
    gs = (gh * slope[...]).astype(BF).astype(F32)
    fill_windows(windows, gs)
    acc = cot[...]
    for a in range(3):
        for b in range(3):
            acc = acc + dot_nt(windows[2 - b, (2 - a) * W : (2 - a) * W + ROWS, :], tap(w_ref, 3 * a + b))
    grad_ref[...] = acc


def output_kernel(w_ref, video, hidden, prev, after, out_ref):
    acc = video[...] + dot(hidden[...], tap(w_ref, 10))
    acc = acc + dot(prev[...], tap(w_ref, 9))
    out_ref[...] = acc + dot(after[...], tap(w_ref, 11))


def kernel_call(body, outs, ins, scratch, micros, name):
    whole = pl.BlockSpec(memory_space=pltpu.VMEM)
    specs = [pl.BlockSpec(memory_space=pltpu.SMEM) if a.shape == (2,) else whole for a in ins]
    return pl.pallas_call(
        body,
        out_shape=tuple(jax.ShapeDtypeStruct(*o) for o in outs),
        in_specs=specs,
        out_specs=tuple(whole for _ in outs),
        scratch_shapes=scratch,
        compiler_params=pltpu.CompilerParams(vmem_limit_bytes=48 * 1024 * 1024),
        cost_estimate=pl.CostEstimate(flops=int(micros * 1.0e9), bytes_accessed=1_000_000, transcendentals=0),
        name=name,
    )(*ins)


def on_device(video, spatial_w, spatial_b, temporal_w, cotangent):
    tie = lax.optimization_barrier
    c, h, x = lax.axis_index("c"), lax.axis_index("h"), lax.axis_index("x")
    place = jnp.stack([c, h]).astype(jnp.int32)
    shape = video.shape
    video_f = video.reshape(ROWS, C)
    cot_f = cotangent.reshape(ROWS, C)
    cot_b = cot_f.astype(BF)

    w = jnp.concatenate([spatial_w, temporal_w.astype(BF)], axis=0)
    other = across(lax.dynamic_slice_in_dim(w, 3 * x, 3, 0))
    own_m = lax.all_gather(w, "y")
    other, own_m, cot_b = tie((other, own_m, cot_b))
    oth_m = to_all(other, PLANE)
    own_t = core_swap(own_m)
    cot_next = lax.ppermute(cot_b, TM, FRAMES_DOWN)
    cot_prev = lax.ppermute(cot_b, TM, FRAMES_UP)
    own, windows = kernel_call(
        prepare_kernel,
        [((TAPS, 1, HALF, C), BF), ((3, ROWS + 2 * W, C), BF)],
        (place, own_m, own_t, video_f), [], 100, "prepare",
    )
    oth_m, own, windows = tie((oth_m, own, windows))
    oth_t = core_swap(oth_m)

    w_all, hidden, slope, mine, theirs = kernel_call(
        forward_kernel,
        [
            ((TAPS, 2, HALF, C), BF), ((ROWS, C), BF), ((ROWS, C), F32),
            ((4, 4, 2, 16, C), F32), ((4, 4, 2, 16, C), F32),
        ],
        (place, own, oth_m, oth_t, windows, spatial_b.reshape(1, C), cot_f, cot_prev, cot_next),
        [], 6, "forward",
    )

    part = mine + core_swap(theirs)
    part = lax.all_to_all(part.reshape(16, 2, 16, C), PLANE, 0, 0, tiled=True)
    prev = lax.ppermute(hidden, TM, FRAMES_UP)
    after = lax.ppermute(hidden, TM, FRAMES_DOWN)
    keep, give = kernel_call(
        split_kernel, [((16, C), F32), ((16, C), F32)], (place, part), [], 100, "split",
    )
    part = keep + across(give)
    part, slope = tie((part, slope))
    part = to_all(part, Z_LO)
    (grad_video,) = kernel_call(
        backward_kernel, [((ROWS, C), F32)], (w_all, slope, cot_f, cot_prev, cot_next),
        [pltpu.VMEM((3, ROWS + 2 * W, C), BF)], 5, "backward",
    )
    part, grad_video = tie((part, grad_video))
    part = jnp.sum(part, axis=0)
    part, video_f = tie((part, video_f))
    part = to_all(part, "x").reshape(4 * 16, C)
    (output,) = kernel_call(
        output_kernel, [((ROWS, C), F32)], (w_all, video_f, hidden, prev, after), [], 3, "output",
    )
    total_rows = ROWS * lax.axis_size(TM) * lax.axis_size(CLIP)
    grad_temporal = part[: 3 * OWN].reshape(3, OWN, C) * (1.0 / math.sqrt(total_rows))
    return output.reshape(shape), grad_video.reshape(shape), grad_temporal


def solution(mesh):
    finer = Mesh(mesh.devices.reshape(SIZES), AXES)
    placed = (
        P(CLIP, TM, None, None, None),
        P(None, CLIP, None),
        P(),
        P(None, CLIP, None),
        P(CLIP, TM, None, None, None),
    )
    return jax.shard_map(
        on_device,
        mesh=finer,
        in_specs=placed,
        out_specs=(
            P(CLIP, TM, None, None, None),
            P(CLIP, TM, None, None, None),
            P(None, CLIP, None),
        ),
        check_vma=False,
    )
```

time: 167 us -> 167 us (level)
  blocking collectives: 0 us -> 30.8 us
  waiting for transfers between devices: 60.1 us -> 41.9 us
  starting transfers between devices: 77.5 us -> 59.8 us
  local copies, waits for them, and re-layouts: 8.7 us -> 12.8 us
    all_to_all x0 -> x1, blocking collectives: none -> 16.6 us  [on_device(): part = lax.all_to_all(part.reshape(16, 2, 16, C), PLANE, 0, 0, tiled=True)]
    all_gather x0 -> x1, blocking collectives: none -> 14.2 us  [on_device(): own_m = lax.all_gather(w, 'y')]
    all_to_all x2 -> x0, waiting for transfers between devices: 13.7 us -> none  [the longest x1 12.2 us: on_device(): part = lax.all_to_all(part.reshape(16, 2, 16, C), PLANE, 0, 0, tiled=True)]
    all_to_all x2 -> x0, starting transfers between devices: 7.62 us -> none  [the longest x1 4.18 us: on_device(): part = lax.all_to_all(part.reshape(16, 2, 16, C), PLANE, 0, 0, tiled=True)]
    all_to_all x4 -> x3, waiting for transfers between devices: 16.1 us -> 9.36 us  [to_all(): lax.all_to_all(jnp.broadcast_to(a[None], (n, *a.shape)), axes, 0, 0, tile...]
    all_to_all x4 -> x3, starting transfers between devices: 19.3 us -> 14.9 us  [to_all(): lax.all_to_all(jnp.broadcast_to(a[None], (n, *a.shape)), axes, 0, 0, tile...]
    ppermute x2, starting transfers between devices: 19 us -> 14.7 us  [across(): return lax.ppermute(a, ('m', 'k', 'h'), ACROSS)]
    unnamed x14 -> x24, local copies, waits for them, and re-layouts: 2.73 us -> 7.05 us
  transfers between devices with their start and end apart: 15 -> 12, of which waited for: 10 -> 6; matrix products, arithmetic and copies ran while one was open for 2% -> 4% of each run, Pallas kernels for 4% -> 5%
where the time goes in v2:
time: 167 us; the launch traced here: 166 us
  starting transfers between devices  59.8 us (36%)
  waiting for transfers between devices  41.9 us (25%)
  blocking collectives  30.8 us (18%)
  Pallas kernels  15.1 us (9%)
  local copies, waits for them, and re-layouts  12.8 us (8%)
  other arithmetic  4.85 us (3%)
    all_to_all x1, blocking collectives, on_device(): part = lax.all_to_all(part.reshape(16, 2, 16, C), PLANE, 0, 0, tiled=True)  16.6 us
    pallas_call x5, Pallas kernels, kernel_call(): pl.pallas_call(body, out_shape=tuple((jax.ShapeDtypeStruct(*o) for o in o...  15.1 us
    all_to_all x3, starting transfers between devices, to_all(): lax.all_to_all(jnp.broadcast_to(a[None], (n, *a.shape)), axes, 0, 0, tile...  14.9 us
    ppermute x2, starting transfers between devices, across(): return lax.ppermute(a, ('m', 'k', 'h'), ACROSS)  14.7 us
    all_gather x1, blocking collectives, on_device(): own_m = lax.all_gather(w, 'y')  14.2 us
    ppermute x1, starting transfers between devices, on_device(): after = lax.ppermute(hidden, TM, FRAMES_DOWN)  11.7 us
    ppermute x1, waiting for transfers between devices, on_device(): cot_prev = lax.ppermute(cot_b, TM, FRAMES_UP)  11.2 us
    all_to_all x3, waiting for transfers between devices, to_all(): lax.all_to_all(jnp.broadcast_to(a[None], (n, *a.shape)), axes, 0, 0, tile...  9.36 us
  transfers between devices with their start and end apart: 12, of which 6 were waited for; matrix products, arithmetic and copies ran while one was open for 4% of the time, Pallas kernels for 5%

profile of v2, /device:TPU:2, one launch (start us, length us, event | category | flops | bytes accessed | tf_op | source)
XLA Modules:
  0.0 166.1 jit_solution(12166348805076289748)
XLA Ops:
  2.4 12.7 %collective-permute-start = (bf16[3,20,320]{2,1,0:T(8,128)(2,1)S(1)}, bf16[3,20,320]{2,1,0:T(8,128)(2,1)S(1)}, u32[]{:S(2)}, u32[]{:S(2)}) collective-permute-start(bf16[3,20,320]{2,1,0:T(8,128)(2,1)S(1)} %fusion), channel_id=1, source_target_pairs={{0,72},{16,88},{32,104},{48,120},{64,8},{80,24},{96,40},{112,56},{... | collective-permute-start | bytes 115208 | tf_op jit(solution)/shard_map/ppermute | solution.py:39
  16.1 1.9 %bitcast_convert_fusion = bf16[512,320]{1,0:T(8,128)(2,1)} fusion(f32[1,1,16,32,320]{4,3,2,1,0:T(8,128)} %param.9), kind=kLoop, calls=%fused_computation.6 | loop fusion | flops 163840 | bytes 983040 | tf_op jit(solution)/shard_map/convert_element_type | solution.py:180
  18.0 14.2 %all-gather = bf16[48,20,320]{2,1,0:T(8,128)(2,1)S(1)} all-gather(bf16[12,20,320]{2,1,0:T(8,128)(2,1)S(1)} %pad_maximum_fusion), channel_id=2, replica_groups=mesh['x'=4,'m'=2,'k'=4,'h'=2,'y'=4,'c'=2] {'y'}, dimensions={0}, use_global_device_ids=true | all-gather | bytes 768000 | tf_op jit(solution)/shard_map/all_gather | solution.py:184
  32.2 1.2 copy.8
  33.5 1.9 %collective-permute-start.1 = (bf16[4,12,20,320]{3,0,2,1:T(4,128)(2,1)}, bf16[4,12,20,320]{3,0,2,1:T(4,128)(2,1)}, u32[]{:S(2)}, u32[]{:S(2)}) collective-permute-start(bf16[4,12,20,320]{3,0,2,1:T(4,128)(2,1)} %copy.8), channel_id=1, source_target_pairs={{0,1},{1,0},{2,3},{3,2},{4,5},{5,4},{6,7},{7,6},{8,9},{9,8},{10,11... | collective-permute-start | bytes 1843208 | tf_op jit(solution)/shard_map/ppermute | solution.py:43
  36.5 7.9 %all-to-all-start = ((bf16[16,3,20,320]{3,2,1,0:T(8,128)(2,1)}), bf16[16,3,20,320]{3,2,1,0:T(8,128)(2,1)S(1)}, u32[]{:S(2)}, u32[]{:S(2)}) async-start(bf16[16,3,20,320]{3,2,1,0:T(8,128)(2,1)} %broadcast_in_dim.6), calls=%async_computation | async-start | bytes 1769472 | tf_op jit(solution)/shard_map/all_to_all | solution.py:48
  44.4 1.2 copy.9.own_t
  45.7 1.1 prepare.1
  46.8 1.1 copy-done.6
  47.9 1.1 copy-done.7
  49.0 9.4 %all-to-all-done.oth_m = bf16[16,3,20,320]{3,2,1,0:T(8,128)(2,1)S(1)} async-done(((bf16[16,3,20,320]{3,2,1,0:T(8,128)(2,1)}), bf16[16,3,20,320]{3,2,1,0:T(8,128)(2,1)S(1)}, u32[]{:S(2)}, u32[]{:S(2)}) %all-to-all-start) | async-done | bytes 614432 | tf_op jit(solution)/shard_map/all_to_all | solution.py:48
  58.5 2.1 %collective-permute-start.2 = (bf16[16,3,20,320]{3,0,2,1:T(8,128)(2,1)S(1)}, bf16[16,3,20,320]{3,0,2,1:T(8,128)(2,1)S(1)}, u32[]{:S(2)}, u32[]{:S(2)}) collective-permute-start(bf16[16,3,20,320]{3,0,2,1:T(8,128)(2,1)S(1)} %copy.10), channel_id=1, source_target_pairs={{0,1},{1,0},{2,3},{3,2},{4,5},{5,4},{6,7},{7,6},{8,9},{9,8},{10,11... | collective-permute-start | bytes 1843208 | tf_op jit(solution)/shard_map/ppermute | solution.py:43
  60.6 8.8 %collective-permute-start.4 = (bf16[512,320]{1,0:T(8,128)(2,1)S(1)}, bf16[512,320]{1,0:T(8,128)(2,1)S(1)}, u32[]{:S(2)}, u32[]{:S(2)}) collective-permute-start(bf16[512,320]{1,0:T(8,128)(2,1)S(1)} %copy-done.10), channel_id=1, source_target_pairs={{16,0},{32,16},{48,32},{64,48},{80,64},{96,80},{112,96},{128,112},... | collective-permute-start | bytes 983048 | tf_op jit(solution)/shard_map/ppermute | solution.py:188
  69.4 1.9 %collective-permute-start.3 = (bf16[512,320]{1,0:T(8,128)(2,1)S(1)}, bf16[512,320]{1,0:T(8,128)(2,1)S(1)}, u32[]{:S(2)}, u32[]{:S(2)}) collective-permute-start(bf16[512,320]{1,0:T(8,128)(2,1)S(1)} %copy-done.10), channel_id=1, source_target_pairs={{0,16},{16,32},{32,48},{48,64},{64,80},{80,96},{96,112},{112,128},... | collective-permute-start | bytes 983048 | tf_op jit(solution)/shard_map/ppermute | solution.py:189
  71.5 7.3 %collective-permute-done.4.cot_next = bf16[512,320]{1,0:T(8,128)(2,1)S(1)} collective-permute-done((bf16[512,320]{1,0:T(8,128)(2,1)S(1)}, bf16[512,320]{1,0:T(8,128)(2,1)S(1)}, u32[]{:S(2)}, u32[]{:S(2)}) %collective-permute-start.4) | collective-permute-done | bytes 327712 | tf_op jit(solution)/shard_map/ppermute | solution.py:188
  78.9 11.2 %collective-permute-done.3.cot_prev = bf16[512,320]{1,0:T(8,128)(2,1)S(1)} collective-permute-done((bf16[512,320]{1,0:T(8,128)(2,1)S(1)}, bf16[512,320]{1,0:T(8,128)(2,1)S(1)}, u32[]{:S(2)}, u32[]{:S(2)}) %collective-permute-start.3) | collective-permute-done | bytes 327712 | tf_op jit(solution)/shard_map/ppermute | solution.py:189
  90.0 5.9 %forward.1 = (bf16[12,2,160,320]{3,2,1,0:T(8,128)(2,1)}, bf16[512,320]{1,0:T(8,128)(2,1)S(1)}, f32[512,320]{1,0:T(8,128)S(1)}, f32[4,4,2,16,320]{4,3,2,1,0:T(8,128)S(1)}, f32[4,4,2,16,320]{4,3,2,1,0:T(8,128)S(1)}) custom-call(s32[2]{0:T(128)S(1)} %pad_add_fusion.place, bf16[12,1,160,320]{3,2,1,0:T(8,128)(2,1)} %copy-done.6, ...), custom_call_target="tpu_custom_call" | custom-call | flops 6000000000 | bytes 1000000 | tf_op jit(solution)/shard_map/forward/pallas_call | solution.py:161
  96.0 1.9 %collective-permute-start.5 = (f32[4,4,2,16,320]{4,3,2,1,0:T(8,128)S(1)}, f32[4,4,2,16,320]{4,3,2,1,0:T(8,128)S(1)}, u32[]{:S(2)}, u32[]{:S(2)}) collective-permute-start(f32[4,4,2,16,320]{4,3,2,1,0:T(8,128)S(1)} %get-tuple-element.34), channel_id=1, source_target_pairs={{0,1},{1,0},{2,3},{3,2},{4,5},{5,4},{6,7},{7,6},{8,9},{9,8},{10,11... | collective-permute-start | bytes 1966088 | tf_op jit(solution)/shard_map/ppermute | solution.py:43
  98.0 2.3 %collective-permute-done.5 = f32[4,4,2,16,320]{4,3,2,1,0:T(8,128)S(1)} collective-permute-done((f32[4,4,2,16,320]{4,3,2,1,0:T(8,128)S(1)}, f32[4,4,2,16,320]{4,3,2,1,0:T(8,128)S(1)}, u32[]{:S(2)}, u32[]{:S(2)}) %collective-permute-start.5) | collective-permute-done | bytes 655392 | tf_op jit(solution)/shard_map/ppermute | solution.py:43
  100.3 16.6 %all_to_all.20.parts = f32[16,2,16,320]{3,2,1,0:T(8,128)S(1)} all-to-all(f32[16,2,16,320]{3,2,1,0:T(8,128)S(1)} %bitcast.16), channel_id=1, replica_groups=mesh['x'=4,'m'=2,'k'=4,'h'=2,'y'=4,'c'=2] {'x','y'}, dimensions={0} | all-to-all | bytes 1310720 | tf_op jit(solution)/shard_map/all_to_all | solution.py:209
  117.5 1.9 %collective-permute-start.6 = (f32[16,320]{1,0:T(8,128)S(1)}, f32[16,320]{1,0:T(8,128)S(1)}, u32[]{:S(2)}, u32[]{:S(2)}) collective-permute-start(f32[16,320]{1,0:T(8,128)S(1)} %get-tuple-element.36), channel_id=1, source_target_pairs={{0,72},{16,88},{32,104},{48,120},{64,8},{80,24},{96,40},{112,56},{... | collective-permute-start | bytes 61448 | tf_op jit(solution)/shard_map/ppermute | solution.py:39
  119.4 7.7 %collective-permute-done.6 = f32[16,320]{1,0:T(8,128)S(1)} collective-permute-done((f32[16,320]{1,0:T(8,128)S(1)}, f32[16,320]{1,0:T(8,128)S(1)}, u32[]{:S(2)}, u32[]{:S(2)}) %collective-permute-start.6) | collective-permute-done | bytes 20512 | tf_op jit(solution)/shard_map/ppermute | solution.py:39
  127.8 3.4 %all-to-all-start.2 = ((f32[8,16,320]{2,1,0:T(8,128)}), f32[8,16,320]{2,1,0:T(8,128)S(1)}, u32[]{:S(2)}, u32[]{:S(2)}) async-start(f32[8,16,320]{2,1,0:T(8,128)} %broadcast_in_dim.7), calls=%async_computation.2 | async-start | bytes 393216 | tf_op jit(solution)/shard_map/all_to_all | solution.py:48
  131.2 11.7 %collective-permute-start.8 = (bf16[512,320]{1,0:T(8,128)(2,1)S(1)}, bf16[512,320]{1,0:T(8,128)(2,1)S(1)}, u32[]{:S(2)}, u32[]{:S(2)}) collective-permute-start(bf16[512,320]{1,0:T(8,128)(2,1)S(1)} %get-tuple-element.42.hidden), channel_id=1, source_target_pairs={{16,0},{32,16},{48,32},{64,48},{80,64},{96,80},{112,96},{128,112},... | collective-permute-start | bytes 983048 | tf_op jit(solution)/shard_map/ppermute | solution.py:211
  142.9 1.9 %collective-permute-start.7 = (bf16[512,320]{1,0:T(8,128)(2,1)S(1)}, bf16[512,320]{1,0:T(8,128)(2,1)}, u32[]{:S(2)}, u32[]{:S(2)}) collective-permute-start(bf16[512,320]{1,0:T(8,128)(2,1)S(1)} %get-tuple-element.42.hidden), channel_id=1, source_target_pairs={{0,16},{16,32},{32,48},{48,64},{64,80},{80,96},{96,112},{112,128},... | collective-permute-start | bytes 983048 | tf_op jit(solution)/shard_map/ppermute | solution.py:210
  144.9 1.8 %copy-done.4 = bf16[12,2,160,320]{3,2,1,0:T(8,128)(2,1)S(1)} copy-done((bf16[12,2,160,320]{3,2,1,0:T(8,128)(2,1)S(1)}, bf16[12,2,160,320]{3,2,1,0:T(8,128)(2,1)}, u32[]{:S(2)}) %copy-start.4) | copy-done | bytes 2457624
  146.7 1.1 copy-done.9
  147.8 4.7 %backward.1 = f32[512,320]{1,0:T(8,128)} custom-call(bf16[12,2,160,320]{3,2,1,0:T(8,128)(2,1)S(1)} %copy-done.4, f32[512,320]{1,0:T(8,128)S(1)} %copy-done.9, f32[512,320]{1,0:T(8,128)S(1)} %bitcast.13, bf16[512,320]{1,0:T(8,128)(2,1)S(1)} %copy-done.3, bf16[512,320]{1,0:T(8,128)(2,1)S(1)} %collective-permute-done.4.cot_next), custom_call_target="tpu_custom_call" | custom-call | flops 5000000000 | bytes 1000000 | tf_op jit(solution)/shard_map/backward/pallas_call | solution.py:161
  153.2 3.5 %all-to-all-start.3 = ((f32[4,16,320]{2,1,0:T(8,128)}), f32[4,16,320]{2,1,0:T(8,128)S(1)}, u32[]{:S(2)}, u32[]{:S(2)}) async-start(f32[4,16,320]{2,1,0:T(8,128)} %broadcast_in_dim.8), calls=%async_computation.3 | async-start | bytes 196608 | tf_op jit(solution)/shard_map/all_to_all | solution.py:48
  156.7 4.1 %collective-permute-done.7.prev = bf16[512,320]{1,0:T(8,128)(2,1)} collective-permute-done((bf16[512,320]{1,0:T(8,128)(2,1)S(1)}, bf16[512,320]{1,0:T(8,128)(2,1)}, u32[]{:S(2)}, u32[]{:S(2)}) %collective-permute-start.7) | collective-permute-done | bytes 327712 | tf_op jit(solution)/shard_map/ppermute | solution.py:210
  160.8 1.8 %copy-done.5 = bf16[12,2,160,320]{3,2,1,0:T(8,128)(2,1)S(1)} copy-done((bf16[12,2,160,320]{3,2,1,0:T(8,128)(2,1)S(1)}, bf16[12,2,160,320]{3,2,1,0:T(8,128)(2,1)}, u32[]{:S(2)}) %copy-start.5) | copy-done | bytes 2457624
  162.6 2.8 %output.1 = f32[512,320]{1,0:T(8,128)} custom-call(bf16[12,2,160,320]{3,2,1,0:T(8,128)(2,1)S(1)} %copy-done.5, f32[512,320]{1,0:T(8,128)S(1)} %bitcast.15, bf16[512,320]{1,0:T(8,128)(2,1)S(1)} %get-tuple-element.42.hidden, bf16[512,320]{1,0:T(8,128)(2,1)} %collective-permute-done.7.prev, bf16[512,320]{1,0:T(8,128)(2,1)S(1)} %collective-permute-done.8.after), custom_call_target="tpu_custom_call" | custom-call | flops 3000000000 | bytes 1000000 | tf_op jit(solution)/shard_map/output/pallas_call | solution.py:161
  (41 shorter events, 6.8 us)
Async XLA Ops:
  2.4 29.8 %collective-permute-start = (bf16[3,20,320]{2,1,0:T(8,128)(2,1)S(1)}, bf16[3,20,320]{2,1,0:T(8,128)(2,1)S(1)}, u32[]{:S(2)}, u32[]{:S(2)}) collective-permute-start(bf16[3,20,320]{2,1,0:T(8,128)(2,1)S(1)} %fusion), channel_id=1, source_target_pairs={{0,72},{16,88},{32,104},{48,120},{64,8},{80,24},{96,40},{112,56},{... | collective-permute-start | bytes 115208 | tf_op jit(solution)/shard_map/ppermute | solution.py:39
  33.5 11.0 %collective-permute-start.1 = (bf16[4,12,20,320]{3,0,2,1:T(4,128)(2,1)}, bf16[4,12,20,320]{3,0,2,1:T(4,128)(2,1)}, u32[]{:S(2)}, u32[]{:S(2)}) collective-permute-start(bf16[4,12,20,320]{3,0,2,1:T(4,128)(2,1)} %copy.8), channel_id=1, source_target_pairs={{0,1},{1,0},{2,3},{3,2},{4,5},{5,4},{6,7},{7,6},{8,9},{9,8},{10,11... | collective-permute-start | bytes 1843208 | tf_op jit(solution)/shard_map/ppermute | solution.py:43
  36.5 9.2 %copy-start.1 = (f32[1,1,16,32,320]{4,3,2,1,0:T(8,128)S(1)}, f32[1,1,16,32,320]{4,3,2,1,0:T(8,128)}, u32[]{:S(2)}) copy-start(f32[1,1,16,32,320]{4,3,2,1,0:T(8,128)} %param.5) | copy-start | bytes 1966084
  36.5 21.9 %all-to-all-start = ((bf16[16,3,20,320]{3,2,1,0:T(8,128)(2,1)}), bf16[16,3,20,320]{3,2,1,0:T(8,128)(2,1)S(1)}, u32[]{:S(2)}, u32[]{:S(2)}) async-start(bf16[16,3,20,320]{3,2,1,0:T(8,128)(2,1)} %broadcast_in_dim.6), calls=%async_computation | async-start | bytes 1769472 | tf_op jit(solution)/shard_map/all_to_all | solution.py:48
  46.8 1.1 copy-start.6
  47.9 1.1 copy-start.7
  49.0 11.5 %copy-start.10 = (bf16[512,320]{1,0:T(8,128)(2,1)S(1)}, bf16[512,320]{1,0:T(8,128)(2,1)}, u32[]{:S(2)}) copy-start(bf16[512,320]{1,0:T(8,128)(2,1)} %bitcast_convert_fusion) | copy-start | bytes 983044
  49.0 22.3 %copy-start.11 = (f32[320]{0:T(512)S(1)}, f32[320]{0:T(512)}, u32[]{:S(2)}) copy-start(f32[320]{0:T(512)} %param.7) | copy-start | bytes 3844
  58.4 31.7 %copy-start = (f32[1,1,16,32,320]{4,3,2,1,0:T(8,128)S(1)}, f32[1,1,16,32,320]{4,3,2,1,0:T(8,128)}, u32[]{:S(2)}) copy-start(f32[1,1,16,32,320]{4,3,2,1,0:T(8,128)} %param.9) | copy-start | bytes 1966084
  58.5 12.9 %collective-permute-start.2 = (bf16[16,3,20,320]{3,0,2,1:T(8,128)(2,1)S(1)}, bf16[16,3,20,320]{3,0,2,1:T(8,128)(2,1)S(1)}, u32[]{:S(2)}, u32[]{:S(2)}) collective-permute-start(bf16[16,3,20,320]{3,0,2,1:T(8,128)(2,1)S(1)} %copy.10), channel_id=1, source_target_pairs={{0,1},{1,0},{2,3},{3,2},{4,5},{5,4},{6,7},{7,6},{8,9},{9,8},{10,11... | collective-permute-start | bytes 1843208 | tf_op jit(solution)/shard_map/ppermute | solution.py:43
  60.6 18.3 %collective-permute-start.4 = (bf16[512,320]{1,0:T(8,128)(2,1)S(1)}, bf16[512,320]{1,0:T(8,128)(2,1)S(1)}, u32[]{:S(2)}, u32[]{:S(2)}) collective-permute-start(bf16[512,320]{1,0:T(8,128)(2,1)S(1)} %copy-done.10), channel_id=1, source_target_pairs={{16,0},{32,16},{48,32},{64,48},{80,64},{96,80},{112,96},{128,112},... | collective-permute-start | bytes 983048 | tf_op jit(solution)/shard_map/ppermute | solution.py:188
  69.4 20.6 %collective-permute-start.3 = (bf16[512,320]{1,0:T(8,128)(2,1)S(1)}, bf16[512,320]{1,0:T(8,128)(2,1)S(1)}, u32[]{:S(2)}, u32[]{:S(2)}) collective-permute-start(bf16[512,320]{1,0:T(8,128)(2,1)S(1)} %copy-done.10), channel_id=1, source_target_pairs={{0,16},{16,32},{32,48},{48,64},{64,80},{80,96},{96,112},{112,128},... | collective-permute-start | bytes 983048 | tf_op jit(solution)/shard_map/ppermute | solution.py:189
  90.0 6.0 %copy-start.2 = (bf16[512,320]{1,0:T(8,128)(2,1)}, bf16[512,320]{1,0:T(8,128)(2,1)S(1)}, u32[]{:S(2)}) copy-start(bf16[512,320]{1,0:T(8,128)(2,1)S(1)} %collective-permute-done.3.cot_prev) | copy-start | bytes 983044
  96.0 20.9 %copy-start.8 = (f32[512,320]{1,0:T(8,128)}, f32[512,320]{1,0:T(8,128)S(1)}, u32[]{:S(2)}) copy-start(f32[512,320]{1,0:T(8,128)S(1)} %get-tuple-element.39.slope) | copy-start | bytes 1966084
  96.0 4.2 %collective-permute-start.5 = (f32[4,4,2,16,320]{4,3,2,1,0:T(8,128)S(1)}, f32[4,4,2,16,320]{4,3,2,1,0:T(8,128)S(1)}, u32[]{:S(2)}, u32[]{:S(2)}) collective-permute-start(f32[4,4,2,16,320]{4,3,2,1,0:T(8,128)S(1)} %get-tuple-element.34), channel_id=1, source_target_pairs={{0,1},{1,0},{2,3},{3,2},{4,5},{5,4},{6,7},{7,6},{8,9},{9,8},{10,11... | collective-permute-start | bytes 1966088 | tf_op jit(solution)/shard_map/ppermute | solution.py:43
  116.9 28.0 %copy-start.3 = (bf16[512,320]{1,0:T(8,128)(2,1)S(1)}, bf16[512,320]{1,0:T(8,128)(2,1)}, u32[]{:S(2)}) copy-start(bf16[512,320]{1,0:T(8,128)(2,1)} %copy-done.2) | copy-start | bytes 983044
  117.5 9.6 %collective-permute-start.6 = (f32[16,320]{1,0:T(8,128)S(1)}, f32[16,320]{1,0:T(8,128)S(1)}, u32[]{:S(2)}, u32[]{:S(2)}) collective-permute-start(f32[16,320]{1,0:T(8,128)S(1)} %get-tuple-element.36), channel_id=1, source_target_pairs={{0,72},{16,88},{32,104},{48,120},{64,8},{80,24},{96,40},{112,56},{... | collective-permute-start | bytes 61448 | tf_op jit(solution)/shard_map/ppermute | solution.py:39
  127.8 24.7 %all-to-all-start.2 = ((f32[8,16,320]{2,1,0:T(8,128)}), f32[8,16,320]{2,1,0:T(8,128)S(1)}, u32[]{:S(2)}, u32[]{:S(2)}) async-start(f32[8,16,320]{2,1,0:T(8,128)} %broadcast_in_dim.7), calls=%async_computation.2 | async-start | bytes 393216 | tf_op jit(solution)/shard_map/all_to_all | solution.py:48
  131.2 25.5 %collective-permute-start.8 = (bf16[512,320]{1,0:T(8,128)(2,1)S(1)}, bf16[512,320]{1,0:T(8,128)(2,1)S(1)}, u32[]{:S(2)}, u32[]{:S(2)}) collective-permute-start(bf16[512,320]{1,0:T(8,128)(2,1)S(1)} %get-tuple-element.42.hidden), channel_id=1, source_target_pairs={{16,0},{32,16},{48,32},{64,48},{80,64},{96,80},{112,96},{128,112},... | collective-permute-start | bytes 983048 | tf_op jit(solution)/shard_map/ppermute | solution.py:211
  142.9 17.9 %collective-permute-start.7 = (bf16[512,320]{1,0:T(8,128)(2,1)S(1)}, bf16[512,320]{1,0:T(8,128)(2,1)}, u32[]{:S(2)}, u32[]{:S(2)}) collective-permute-start(bf16[512,320]{1,0:T(8,128)(2,1)S(1)} %get-tuple-element.42.hidden), channel_id=1, source_target_pairs={{0,16},{16,32},{32,48},{48,64},{64,80},{80,96},{96,112},{112,128},... | collective-permute-start | bytes 983048 | tf_op jit(solution)/shard_map/ppermute | solution.py:210
  144.9 1.8 %copy-start.4 = (bf16[12,2,160,320]{3,2,1,0:T(8,128)(2,1)S(1)}, bf16[12,2,160,320]{3,2,1,0:T(8,128)(2,1)}, u32[]{:S(2)}) copy-start(bf16[12,2,160,320]{3,2,1,0:T(8,128)(2,1)} %get-tuple-element.32.w_ref) | copy-start | bytes 7372804
  146.7 1.1 copy-start.9
  153.2 12.2 %all-to-all-start.3 = ((f32[4,16,320]{2,1,0:T(8,128)}), f32[4,16,320]{2,1,0:T(8,128)S(1)}, u32[]{:S(2)}, u32[]{:S(2)}) async-start(f32[4,16,320]{2,1,0:T(8,128)} %broadcast_in_dim.8), calls=%async_computation.3 | async-start | bytes 196608 | tf_op jit(solution)/shard_map/all_to_all | solution.py:48
  160.8 1.8 %copy-start.5 = (bf16[12,2,160,320]{3,2,1,0:T(8,128)(2,1)S(1)}, bf16[12,2,160,320]{3,2,1,0:T(8,128)(2,1)}, u32[]{:S(2)}) copy-start(bf16[12,2,160,320]{3,2,1,0:T(8,128)(2,1)} %get-tuple-element.32.w_ref) | copy-start | bytes 7372804

commit v3 on v2

--- a/solution.py
+++ b/solution.py
@@ -31,8 +31,9 @@
 
 
 ACROSS = pairs_across()
-FRAMES_UP = [(t, t + 1) for t in range(31)]
-FRAMES_DOWN = [(t + 1, t) for t in range(31)]
+FRAMES_UP = [(t, t + 1) for t in range(31) if t % 8 != 7]
+FRAMES_DOWN = [(u, t) for t, u in FRAMES_UP]
+FRAMES_FAR = [p for t in (7, 15, 23) for p in ((t, t + 1), (t + 1, t))]
 
 
 def across(a):
@@ -83,6 +84,19 @@
     w_ref[t, half, y * PART : (y + 1) * PART, :] = jnp.concatenate([low, high], axis=0)
 
 
+def sides(place, before, after, far):
+    first, last = place[2] == 0, place[2] == 7
+    return jnp.where(first, far, before), jnp.where(last, far, after)
+
+
+def conv(windows, w_ref, bias):
+    acc = jnp.zeros((ROWS, C), F32) + bias
+    for a in range(3):
+        for b in range(3):
+            acc = acc + dot(windows[b, a * W : a * W + ROWS, :], tap(w_ref, 3 * a + b))
+    return acc
+
+
 def prepare_kernel(place, own_m, own_t, video, w_ref, windows):
     c = place[0]
     for t in range(TAPS):
@@ -92,7 +106,7 @@
 
 
 def forward_kernel(
-    place, own, oth_m, oth_t, windows, bias, cot, cot_prev, cot_next,
+    place, own, oth_m, oth_t, windows, bias, cot, cot_prev, cot_next, far,
     w_ref, hidden_ref, slope_ref, mine_ref, theirs_ref,
 ):
     c, h = place[0], place[1]
@@ -101,18 +115,13 @@
         for y in range(4):
             source = (t // 3) * 4 + y
             join(w_ref, t, 1 - h, y, oth_m[source, t % 3], oth_t[source, t % 3], c)
-    spatial = jnp.zeros((ROWS, C), F32) + bias[...]
-    for a in range(3):
-        for b in range(3):
-            spatial = spatial + dot(windows[b, a * W : a * W + ROWS, :], tap(w_ref, 3 * a + b))
+    spatial = conv(windows, w_ref, bias[...])
     sig = jax.nn.sigmoid(spatial)
     hidden = (spatial * sig).astype(BF)
     hidden_ref[...] = hidden
     slope_ref[...] = sig * (1.0 + spatial * (1.0 - sig))
-    grads = [
-        dot_tn(hidden, other)
-        for other in (cot_next[...], cot[...].astype(BF), cot_prev[...])
-    ]
+    before, after = sides(place, cot_prev[...], cot_next[...], far[0])
+    grads = [dot_tn(hidden, other) for other in (after, cot[...].astype(BF), before)]
     pad = jnp.zeros((4, C), F32)
     for half in range(2):
         for y in range(4):
@@ -136,10 +145,11 @@
     give_ref[...] = jnp.where(h == 0, total[1], total[0])
 
 
-def backward_kernel(w_ref, slope, cot, cot_prev, cot_next, grad_ref, windows):
-    gh = dot_nt(cot_next[...], tap(w_ref, 9))
+def backward_kernel(place, w_ref, slope, cot, cot_prev, cot_next, far, grad_ref, windows):
+    before, after = sides(place, cot_prev[...], cot_next[...], far[0])
+    gh = dot_nt(after, tap(w_ref, 9))
     gh = gh + dot_nt(cot[...].astype(BF), tap(w_ref, 10))
-    gh = gh + dot_nt(cot_prev[...], tap(w_ref, 11))
+    gh = gh + dot_nt(before, tap(w_ref, 11))
     gs = (gh * slope[...]).astype(BF).astype(F32)
     fill_windows(windows, gs)
     acc = cot[...]
@@ -149,15 +159,23 @@
     grad_ref[...] = acc
 
 
-def output_kernel(w_ref, video, hidden, prev, after, out_ref):
+def far_kernel(place, w_ref, far, bias, hidden_ref, windows):
+    fill_windows(windows, far[1].astype(F32))
+    spatial = conv(windows, w_ref, bias[...])
+    hidden = (spatial * jax.nn.sigmoid(spatial)).astype(BF)
+    hidden_ref[...] = jnp.where(place[3] == 1, hidden, jnp.zeros_like(hidden))
+
+
+def output_kernel(place, w_ref, video, hidden, prev, after, far, out_ref):
+    before, behind = sides(place, prev[...], after[...], far[...])
     acc = video[...] + dot(hidden[...], tap(w_ref, 10))
-    acc = acc + dot(prev[...], tap(w_ref, 9))
-    out_ref[...] = acc + dot(after[...], tap(w_ref, 11))
+    acc = acc + dot(before, tap(w_ref, 9))
+    out_ref[...] = acc + dot(behind, tap(w_ref, 11))
 
 
 def kernel_call(body, outs, ins, scratch, micros, name):
     whole = pl.BlockSpec(memory_space=pltpu.VMEM)
-    specs = [pl.BlockSpec(memory_space=pltpu.SMEM) if a.shape == (2,) else whole for a in ins]
+    specs = [pl.BlockSpec(memory_space=pltpu.SMEM) if a.shape == (4,) else whole for a in ins]
     return pl.pallas_call(
         body,
         out_shape=tuple(jax.ShapeDtypeStruct(*o) for o in outs),
@@ -172,27 +190,31 @@
 
 def on_device(video, spatial_w, spatial_b, temporal_w, cotangent):
     tie = lax.optimization_barrier
-    c, h, x = lax.axis_index("c"), lax.axis_index("h"), lax.axis_index("x")
-    place = jnp.stack([c, h]).astype(jnp.int32)
+    c, h, x, z = (lax.axis_index(a) for a in ("c", "h", "x", Z_LO))
+    wrapped = ((z == 0) & (x > 0)) | ((z == 7) & (x < 3))
+    place = jnp.stack([c, h, z, wrapped.astype(jnp.int32)]).astype(jnp.int32)
     shape = video.shape
     video_f = video.reshape(ROWS, C)
     cot_f = cotangent.reshape(ROWS, C)
-    cot_b = cot_f.astype(BF)
-
+    bias = spatial_b.reshape(1, C)
+
+    both = jnp.stack([cot_f, video_f]).astype(BF)
+    cot_b = both[0]
+    far = lax.ppermute(both, TM, FRAMES_FAR)
     w = jnp.concatenate([spatial_w, temporal_w.astype(BF)], axis=0)
     other = across(lax.dynamic_slice_in_dim(w, 3 * x, 3, 0))
     own_m = lax.all_gather(w, "y")
-    other, own_m, cot_b = tie((other, own_m, cot_b))
+    cot_next = lax.ppermute(cot_b, TM, FRAMES_DOWN)
+    cot_prev = lax.ppermute(cot_b, TM, FRAMES_UP)
+    other, own_m, cot_next, cot_prev = tie((other, own_m, cot_next, cot_prev))
     oth_m = to_all(other, PLANE)
     own_t = core_swap(own_m)
-    cot_next = lax.ppermute(cot_b, TM, FRAMES_DOWN)
-    cot_prev = lax.ppermute(cot_b, TM, FRAMES_UP)
     own, windows = kernel_call(
         prepare_kernel,
         [((TAPS, 1, HALF, C), BF), ((3, ROWS + 2 * W, C), BF)],
-        (place, own_m, own_t, video_f), [], 100, "prepare",
-    )
-    oth_m, own, windows = tie((oth_m, own, windows))
+        (place, own_m, own_t, video_f), [], 0.01, "prepare",
+    )
+    oth_m, own, windows, far = tie((oth_m, own, windows, far))
     oth_t = core_swap(oth_m)
 
     w_all, hidden, slope, mine, theirs = kernel_call(
@@ -201,7 +223,7 @@
             ((TAPS, 2, HALF, C), BF), ((ROWS, C), BF), ((ROWS, C), F32),
             ((4, 4, 2, 16, C), F32), ((4, 4, 2, 16, C), F32),
         ],
-        (place, own, oth_m, oth_t, windows, spatial_b.reshape(1, C), cot_f, cot_prev, cot_next),
+        (place, own, oth_m, oth_t, windows, bias, cot_f, cot_prev, cot_next, far),
         [], 6, "forward",
     )
 
@@ -209,14 +231,19 @@
     part = lax.all_to_all(part.reshape(16, 2, 16, C), PLANE, 0, 0, tiled=True)
     prev = lax.ppermute(hidden, TM, FRAMES_UP)
     after = lax.ppermute(hidden, TM, FRAMES_DOWN)
+    (hidden_far,) = kernel_call(
+        far_kernel, [((ROWS, C), BF)], (place, w_all, far, bias),
+        [pltpu.VMEM((3, ROWS + 2 * W, C), BF)], 5, "far",
+    )
+    part, prev, after, hidden_far = tie((part, prev, after, hidden_far))
     keep, give = kernel_call(
-        split_kernel, [((16, C), F32), ((16, C), F32)], (place, part), [], 100, "split",
+        split_kernel, [((16, C), F32), ((16, C), F32)], (place, part), [], 0.01, "split",
     )
     part = keep + across(give)
     part, slope = tie((part, slope))
     part = to_all(part, Z_LO)
     (grad_video,) = kernel_call(
-        backward_kernel, [((ROWS, C), F32)], (w_all, slope, cot_f, cot_prev, cot_next),
+        backward_kernel, [((ROWS, C), F32)], (place, w_all, slope, cot_f, cot_prev, cot_next, far),
         [pltpu.VMEM((3, ROWS + 2 * W, C), BF)], 5, "backward",
     )
     part, grad_video = tie((part, grad_video))
@@ -224,7 +251,7 @@
     part, video_f = tie((part, video_f))
     part = to_all(part, "x").reshape(4 * 16, C)
     (output,) = kernel_call(
-        output_kernel, [((ROWS, C), F32)], (w_all, video_f, hidden, prev, after), [], 3, "output",
+        output_kernel, [((ROWS, C), F32)], (place, w_all, video_f, hidden, prev, after, hidden_far), [], 3, "output",
     )
     total_rows = ROWS * lax.axis_size(TM) * lax.axis_size(CLIP)
     grad_temporal = part[: 3 * OWN].reshape(3, OWN, C) * (1.0 / math.sqrt(total_rows))

time: 167 us -> 153 us (0.916)
  waiting for transfers between devices: 41.9 us -> 25 us
  blocking collectives: 30.8 us -> 14.8 us
  local copies, waits for them, and re-layouts: 12.8 us -> 25.3 us
  Pallas kernels: 15.1 us -> 18.9 us
  starting transfers between devices: 59.8 us -> 63.5 us
    all_to_all x1 -> x0, blocking collectives: 16.6 us -> none  [on_device(): part = lax.all_to_all(part.reshape(16, 2, 16, C), PLANE, 0, 0, tiled=True)]
    ppermute x1, waiting for transfers between devices: 11.2 us -> 0.01 us  [on_device(): cot_prev = lax.ppermute(cot_b, TM, FRAMES_UP)]
    ppermute x1, starting transfers between devices: 11.7 us -> 1.28 us  [on_device(): after = lax.ppermute(hidden, TM, FRAMES_DOWN)]
    unnamed x24 -> x54, local copies, waits for them, and re-layouts: 7.05 us -> 15.1 us
    ppermute x1, starting transfers between devices: 8.84 us -> 1.29 us  [on_device(): cot_next = lax.ppermute(cot_b, TM, FRAMES_DOWN)]
    ppermute x1, waiting for transfers between devices: 7.31 us -> 0.01 us  [on_device(): cot_next = lax.ppermute(cot_b, TM, FRAMES_DOWN)]
    all_to_all x0 -> x1, starting transfers between devices: none -> 6.06 us  [on_device(): part = lax.all_to_all(part.reshape(16, 2, 16, C), PLANE, 0, 0, tiled=True)]
    ppermute x0 -> x1, starting transfers between devices: none -> 5.57 us  [on_device(): far = lax.ppermute(both, TM, FRAMES_FAR)]
  transfers between devices with their start and end apart: 12 -> 14, of which waited for: 6 -> 7; matrix products, arithmetic and copies ran while one was open for 4% -> 4% of each run, Pallas kernels for 5% -> 8%
where the time goes in v3:
time: 153 us; the launch traced here: 152 us
  starting transfers between devices  63.5 us (42%)
  local copies, waits for them, and re-layouts  25.3 us (17%)
  waiting for transfers between devices  25 us (16%)
  Pallas kernels  18.9 us (12%)
  blocking collectives  14.8 us (10%)
  other arithmetic  3.57 us (2%)
    pallas_call x6, Pallas kernels, kernel_call(): pl.pallas_call(body, out_shape=tuple((jax.ShapeDtypeStruct(*o) for o in o...  18.9 us
    all_to_all x3, starting transfers between devices, to_all(): lax.all_to_all(jnp.broadcast_to(a[None], (n, *a.shape)), axes, 0, 0, tile...  18.3 us
    ppermute x2, starting transfers between devices, across(): return lax.ppermute(a, ('m', 'k', 'h'), ACROSS)  16.8 us
    unnamed x54, local copies, waits for them, and re-layouts  15.1 us
    all_gather x1, blocking collectives, on_device(): own_m = lax.all_gather(w, 'y')  14.8 us
    all_to_all x3, waiting for transfers between devices, to_all(): lax.all_to_all(jnp.broadcast_to(a[None], (n, *a.shape)), axes, 0, 0, tile...  12.3 us
    ppermute x2, waiting for transfers between devices, across(): return lax.ppermute(a, ('m', 'k', 'h'), ACROSS)  7.53 us
    all_to_all x1, starting transfers between devices, on_device(): part = lax.all_to_all(part.reshape(16, 2, 16, C), PLANE, 0, 0, tiled=True)  6.06 us
  transfers between devices with their start and end apart: 14, of which 7 were waited for; matrix products, arithmetic and copies ran while one was open for 4% of the time, Pallas kernels for 8%

profile of v3, /device:TPU:2, one launch (start us, length us, event | category | flops | bytes accessed | tf_op | source)
XLA Modules:
  0.0 152.1 jit_solution(55366368583460689)
XLA Ops:
  0.6 1.3 convert.9
  1.9 3.8 %collective-permute-start.2 = (bf16[512,320]{1,0:T(8,128)(2,1)S(1)}, bf16[512,320]{1,0:T(8,128)(2,1)S(1)}, u32[]{:S(2)}, u32[]{:S(2)}) collective-permute-start(bf16[512,320]{1,0:T(8,128)(2,1)S(1)} %bitcast.21), channel_id=1, source_target_pairs={{0,16},{16,32},{32,48},{48,64},{64,80},{80,96},{96,112},{128,144},... | collective-permute-start | bytes 983048 | tf_op jit(solution)/shard_map/ppermute | solution.py:208
  5.8 1.3 collective-permute-start.1
  8.0 14.7 %collective-permute-start = (bf16[3,20,320]{2,1,0:T(8,128)(2,1)S(1)}, bf16[3,20,320]{2,1,0:T(8,128)(2,1)S(1)}, u32[]{:S(2)}, u32[]{:S(2)}) collective-permute-start(bf16[3,20,320]{2,1,0:T(8,128)(2,1)S(1)} %fusion), channel_id=1, source_target_pairs={{0,72},{16,88},{32,104},{48,120},{64,8},{80,24},{96,40},{112,56},{... | collective-permute-start | bytes 115208 | tf_op jit(solution)/shard_map/ppermute | solution.py:40
  24.0 5.6 %collective-permute-start.4 = (bf16[2,512,320]{1,2,0:T(8,128)(2,1)}, bf16[2,512,320]{1,2,0:T(8,128)(2,1)}, u32[]{:S(2)}, u32[]{:S(2)}) collective-permute-start(bf16[2,512,320]{1,2,0:T(8,128)(2,1)} %copy.19), channel_id=1, source_target_pairs={{112,128},{128,112},{240,256},{256,240},{368,384},{384,368},{113,1... | collective-permute-start | bytes 1966088 | tf_op jit(solution)/shard_map/ppermute | solution.py:203
  29.7 14.8 %all-gather = bf16[48,20,320]{2,1,0:T(8,128)(2,1)S(1)} all-gather(bf16[12,20,320]{2,1,0:T(8,128)(2,1)S(1)} %pad_maximum_fusion.1), channel_id=2, replica_groups=mesh['x'=4,'m'=2,'k'=4,'h'=2,'y'=4,'c'=2] {'y'}, dimensions={0}, use_global_device_ids=true | all-gather | bytes 768000 | tf_op jit(solution)/shard_map/all_gather | solution.py:206
  44.5 1.2 copy.17
  45.8 1.9 %collective-permute-start.3 = (bf16[4,12,20,320]{3,0,2,1:T(4,128)(2,1)}, bf16[4,12,20,320]{3,0,2,1:T(4,128)(2,1)S(1)}, u32[]{:S(2)}, u32[]{:S(2)}) collective-permute-start(bf16[4,12,20,320]{3,0,2,1:T(4,128)(2,1)} %copy.17), channel_id=1, source_target_pairs={{0,1},{1,0},{2,3},{3,2},{4,5},{5,4},{6,7},{7,6},{8,9},{9,8},{10,11... | collective-permute-start | bytes 1843208 | tf_op jit(solution)/shard_map/ppermute | solution.py:44
  48.7 6.7 %all-to-all-start = ((bf16[16,3,20,320]{3,2,1,0:T(8,128)(2,1)}), bf16[16,3,20,320]{3,2,1,0:T(8,128)(2,1)S(1)}, u32[]{:S(2)}, u32[]{:S(2)}) async-start(bf16[16,3,20,320]{3,2,1,0:T(8,128)(2,1)} %broadcast_in_dim.6), calls=%async_computation | async-start | bytes 1769472 | tf_op jit(solution)/shard_map/all_to_all | solution.py:49
  55.6 1.1 prepare.1
  58.9 10.4 %all-to-all-done.oth_m = bf16[16,3,20,320]{3,2,1,0:T(8,128)(2,1)S(1)} async-done(((bf16[16,3,20,320]{3,2,1,0:T(8,128)(2,1)}), bf16[16,3,20,320]{3,2,1,0:T(8,128)(2,1)S(1)}, u32[]{:S(2)}, u32[]{:S(2)}) %all-to-all-start) | async-done | bytes 614432 | tf_op jit(solution)/shard_map/all_to_all | solution.py:49
  70.3 1.9 %collective-permute-start.5 = (bf16[16,3,20,320]{3,0,2,1:T(8,128)(2,1)}, bf16[16,3,20,320]{3,0,2,1:T(8,128)(2,1)}, u32[]{:S(2)}, u32[]{:S(2)}) collective-permute-start(bf16[16,3,20,320]{3,0,2,1:T(8,128)(2,1)} %copy.20), channel_id=1, source_target_pairs={{0,1},{1,0},{2,3},{3,2},{4,5},{5,4},{6,7},{7,6},{8,9},{9,8},{10,11... | collective-permute-start | bytes 1843208 | tf_op jit(solution)/shard_map/ppermute | solution.py:44
  72.2 1.5 copy.22.far
  74.7 2.2 %copy.21.oth_t = bf16[16,3,20,320]{3,2,1,0:T(8,128)(2,1)} copy(bf16[16,3,20,320]{3,0,2,1:T(8,128)(2,1)} %collective-permute-done.5) | data formatting | bytes 1228800 | tf_op jit(solution)/shard_map/ppermute | solution.py:44
  77.0 6.8 %forward.1 = (bf16[12,2,160,320]{3,2,1,0:T(8,128)(2,1)}, bf16[512,320]{1,0:T(8,128)(2,1)S(1)}, f32[512,320]{1,0:T(8,128)S(1)}, f32[4,4,2,16,320]{4,3,2,1,0:T(8,128)S(1)}, f32[4,4,2,16,320]{4,3,2,1,0:T(8,128)S(1)}) custom-call(s32[4]{0:T(128)S(1)} %pad_add_fusion.place, bf16[12,1,160,320]{3,2,1,0:T(8,128)(2,1)} %copy-done.4, ...), custom_call_target="tpu_custom_call" | custom-call | flops 6000000000 | bytes 1000000 | tf_op jit(solution)/shard_map/forward/pallas_call | solution.py:179
  83.7 2.0 %collective-permute-start.6 = (f32[4,4,2,16,320]{4,3,2,1,0:T(8,128)S(1)}, f32[4,4,2,16,320]{4,3,2,1,0:T(8,128)S(1)}, u32[]{:S(2)}, u32[]{:S(2)}) collective-permute-start(f32[4,4,2,16,320]{4,3,2,1,0:T(8,128)S(1)} %get-tuple-element.42), channel_id=1, source_target_pairs={{0,1},{1,0},{2,3},{3,2},{4,5},{5,4},{6,7},{7,6},{8,9},{9,8},{10,11... | collective-permute-start | bytes 1966088 | tf_op jit(solution)/shard_map/ppermute | solution.py:44
  85.8 2.1 %collective-permute-done.6 = f32[4,4,2,16,320]{4,3,2,1,0:T(8,128)S(1)} collective-permute-done((f32[4,4,2,16,320]{4,3,2,1,0:T(8,128)S(1)}, f32[4,4,2,16,320]{4,3,2,1,0:T(8,128)S(1)}, u32[]{:S(2)}, u32[]{:S(2)}) %collective-permute-start.6) | collective-permute-done | bytes 655392 | tf_op jit(solution)/shard_map/ppermute | solution.py:44
  88.9 6.1 %all-to-all-start.1 = ((f32[16,2,16,320]{3,2,1,0:T(8,128)}), f32[16,2,16,320]{3,2,1,0:T(8,128)S(1)}, u32[]{:S(2)}, u32[]{:S(2)}) async-start(f32[16,2,16,320]{3,2,1,0:T(8,128)} %bitcast.20), calls=%async_computation.1 | async-start | bytes 1572864 | tf_op jit(solution)/shard_map/all_to_all | solution.py:231
  95.0 1.3 collective-permute-start.8
  96.3 4.6 %collective-permute-start.7 = (bf16[512,320]{1,0:T(8,128)(2,1)}, bf16[512,320]{1,0:T(8,128)(2,1)S(1)}, u32[]{:S(2)}, u32[]{:S(2)}) collective-permute-start(bf16[512,320]{1,0:T(8,128)(2,1)} %copy-done.12), channel_id=1, source_target_pairs={{0,16},{16,32},{32,48},{48,64},{64,80},{80,96},{96,112},{128,144},... | collective-permute-start | bytes 983048 | tf_op jit(solution)/shard_map/ppermute | solution.py:232
  100.9 1.8 %copy-done.18 = bf16[12,2,160,320]{3,2,1,0:T(8,128)(2,1)S(1)} copy-done((bf16[12,2,160,320]{3,2,1,0:T(8,128)(2,1)S(1)}, bf16[12,2,160,320]{3,2,1,0:T(8,128)(2,1)}, u32[]{:S(2)}) %copy-start.18) | copy-done | bytes 2457624
  102.7 2.9 %far.1 = bf16[512,320]{1,0:T(8,128)(2,1)S(1)} custom-call(s32[4]{0:T(128)S(1)} %pad_add_fusion.place, bf16[12,2,160,320]{3,2,1,0:T(8,128)(2,1)S(1)} %copy-done.18, bf16[2,512,320]{2,1,0:T(8,128)(2,1)S(1)} %copy-done.3, f32[1,320]{1,0:T(1,128)S(1)} %reshape.35.bias), custom_call_target="tpu_custom_call" | custom-call | flops 5000000000 | bytes 1000000 | tf_op jit(solution)/shard_map/far/pallas_call | solution.py:179
  106.4 1.5 %collective-permute-done.8.after = bf16[512,320]{1,0:T(8,128)(2,1)S(1)} collective-permute-done((bf16[512,320]{1,0:T(8,128)(2,1)}, bf16[512,320]{1,0:T(8,128)(2,1)S(1)}, u32[]{:S(2)}, u32[]{:S(2)}) %collective-permute-start.8) | collective-permute-done | bytes 327712 | tf_op jit(solution)/shard_map/ppermute | solution.py:233
  110.5 2.1 %collective-permute-start.9 = (f32[16,320]{1,0:T(8,128)S(1)}, f32[16,320]{1,0:T(8,128)S(1)}, u32[]{:S(2)}, u32[]{:S(2)}) collective-permute-start(f32[16,320]{1,0:T(8,128)S(1)} %get-tuple-element.46), channel_id=1, source_target_pairs={{0,72},{16,88},{32,104},{48,120},{64,8},{80,24},{96,40},{112,56},{... | collective-permute-start | bytes 61448 | tf_op jit(solution)/shard_map/ppermute | solution.py:40
  112.6 7.5 %collective-permute-done.9 = f32[16,320]{1,0:T(8,128)S(1)} collective-permute-done((f32[16,320]{1,0:T(8,128)S(1)}, f32[16,320]{1,0:T(8,128)S(1)}, u32[]{:S(2)}, u32[]{:S(2)}) %collective-permute-start.9) | collective-permute-done | bytes 20512 | tf_op jit(solution)/shard_map/ppermute | solution.py:40
  120.9 6.9 %all-to-all-start.2 = ((f32[8,16,320]{2,1,0:T(8,128)}), f32[8,16,320]{2,1,0:T(8,128)S(1)}, u32[]{:S(2)}, u32[]{:S(2)}) async-start(f32[8,16,320]{2,1,0:T(8,128)} %broadcast_in_dim.7), calls=%async_computation.2 | async-start | bytes 393216 | tf_op jit(solution)/shard_map/all_to_all | solution.py:49
  129.7 1.8 %copy-done.19 = bf16[12,2,160,320]{3,2,1,0:T(8,128)(2,1)S(1)} copy-done((bf16[12,2,160,320]{3,2,1,0:T(8,128)(2,1)S(1)}, bf16[12,2,160,320]{3,2,1,0:T(8,128)(2,1)}, u32[]{:S(2)}) %copy-start.19) | copy-done | bytes 2457624
  132.7 5.2 %backward.1 = f32[512,320]{1,0:T(8,128)} custom-call(s32[4]{0:T(128)S(1)} %pad_add_fusion.place, bf16[12,2,160,320]{3,2,1,0:T(8,128)(2,1)S(1)} %copy-done.19, f32[512,320]{1,0:T(8,128)S(1)} %copy-done.24, f32[512,320]{1,0:T(8,128)S(1)} %bitcast.19, bf16[512,320]{1,0:T(8,128)(2,1)S(1)} %copy-done.8, bf16[512,320]{1,0:T(8,128)(2,1)S(1)} %copy-done.11, ...), custom_call_target="tpu_custom_call" | custom-call | flops 5000000000 | bytes 1000000 | tf_op jit(solution)/shard_map/backward/pallas_call | solution.py:179
  137.9 1.9 %all-to-all-done.2 = f32[8,16,320]{2,1,0:T(8,128)S(1)} async-done(((f32[8,16,320]{2,1,0:T(8,128)}), f32[8,16,320]{2,1,0:T(8,128)S(1)}, u32[]{:S(2)}, u32[]{:S(2)}) %all-to-all-start.2) | async-done | bytes 163872 | tf_op jit(solution)/shard_map/all_to_all | solution.py:49
  140.5 4.8 %all-to-all-start.3 = ((f32[4,16,320]{2,1,0:T(8,128)}), f32[4,16,320]{2,1,0:T(8,128)S(1)}, u32[]{:S(2)}, u32[]{:S(2)}) async-start(f32[4,16,320]{2,1,0:T(8,128)} %broadcast_in_dim.8), calls=%async_computation.3 | async-start | bytes 196608 | tf_op jit(solution)/shard_map/all_to_all | solution.py:49
  146.3 1.8 %copy-done.20 = bf16[12,2,160,320]{3,2,1,0:T(8,128)(2,1)S(1)} copy-done((bf16[12,2,160,320]{3,2,1,0:T(8,128)(2,1)S(1)}, bf16[12,2,160,320]{3,2,1,0:T(8,128)(2,1)}, u32[]{:S(2)}) %copy-start.20) | copy-done | bytes 2457624
  149.1 2.3 %output.1 = f32[512,320]{1,0:T(8,128)} custom-call(s32[4]{0:T(128)S(1)} %pad_add_fusion.place, bf16[12,2,160,320]{3,2,1,0:T(8,128)(2,1)S(1)} %copy-done.20, f32[512,320]{1,0:T(8,128)S(1)} %bitcast.17, bf16[512,320]{1,0:T(8,128)(2,1)S(1)} %copy-done.13, bf16[512,320]{1,0:T(8,128)(2,1)S(1)} %copy-done.17, bf16[512,320]{1,0:T(8,128)(2,1)S(1)} %copy-done.15, ...), custom_call_target="tpu_custom_call" | custom-call | flops 3000000000 | bytes 1000000 | tf_op jit(solution)/shard_map/output/pallas_call | solution.py:179
  (79 shorter events, 19.2 us)
Async XLA Ops:
  0.6 7.4 %copy-start.25 = (bf16[9,20,320]{2,1,0:T(8,128)(2,1)S(1)}, bf16[9,20,320]{2,1,0:T(8,128)(2,1)}, u32[]{:S(2)}) copy-start(bf16[9,20,320]{2,1,0:T(8,128)(2,1)} %param.6) | copy-start | bytes 345604
  0.6 22.1 %copy-start = (f32[1,1,16,32,320]{4,3,2,1,0:T(8,128)S(1)}, f32[1,1,16,32,320]{4,3,2,1,0:T(8,128)}, u32[]{:S(2)}) copy-start(f32[1,1,16,32,320]{4,3,2,1,0:T(8,128)} %param.5) | copy-start | bytes 1966084
  1.9 42.6 %collective-permute-start.2 = (bf16[512,320]{1,0:T(8,128)(2,1)S(1)}, bf16[512,320]{1,0:T(8,128)(2,1)S(1)}, u32[]{:S(2)}, u32[]{:S(2)}) collective-permute-start(bf16[512,320]{1,0:T(8,128)(2,1)S(1)} %bitcast.21), channel_id=1, source_target_pairs={{0,16},{16,32},{32,48},{48,64},{64,80},{80,96},{96,112},{128,144},... | collective-permute-start | bytes 983048 | tf_op jit(solution)/shard_map/ppermute | solution.py:208
  5.8 38.7 %collective-permute-start.1 = (bf16[512,320]{1,0:T(8,128)(2,1)S(1)}, bf16[512,320]{1,0:T(8,128)(2,1)S(1)}, u32[]{:S(2)}, u32[]{:S(2)}) collective-permute-start(bf16[512,320]{1,0:T(8,128)(2,1)S(1)} %bitcast.22), channel_id=1, source_target_pairs={{16,0},{32,16},{48,32},{64,48},{80,64},{96,80},{112,96},{144,128},... | collective-permute-start | bytes 983048 | tf_op jit(solution)/shard_map/ppermute | solution.py:207
  8.0 36.5 %collective-permute-start = (bf16[3,20,320]{2,1,0:T(8,128)(2,1)S(1)}, bf16[3,20,320]{2,1,0:T(8,128)(2,1)S(1)}, u32[]{:S(2)}, u32[]{:S(2)}) collective-permute-start(bf16[3,20,320]{2,1,0:T(8,128)(2,1)S(1)} %fusion), channel_id=1, source_target_pairs={{0,72},{16,88},{32,104},{48,120},{64,8},{80,24},{96,40},{112,56},{... | collective-permute-start | bytes 115208 | tf_op jit(solution)/shard_map/ppermute | solution.py:40
  24.0 34.9 %collective-permute-start.4 = (bf16[2,512,320]{1,2,0:T(8,128)(2,1)}, bf16[2,512,320]{1,2,0:T(8,128)(2,1)}, u32[]{:S(2)}, u32[]{:S(2)}) collective-permute-start(bf16[2,512,320]{1,2,0:T(8,128)(2,1)} %copy.19), channel_id=1, source_target_pairs={{112,128},{128,112},{240,256},{256,240},{368,384},{384,368},{113,1... | collective-permute-start | bytes 1966088 | tf_op jit(solution)/shard_map/ppermute | solution.py:203
  44.5 4.2 %copy-start.6 = (bf16[512,320]{1,0:T(8,128)(2,1)}, bf16[512,320]{1,0:T(8,128)(2,1)S(1)}, u32[]{:S(2)}) copy-start(bf16[512,320]{1,0:T(8,128)(2,1)S(1)} %collective-permute-done.2.cot_prev) | copy-start | bytes 983044
  44.5 4.2 %copy-start.9 = (bf16[512,320]{1,0:T(8,128)(2,1)}, bf16[512,320]{1,0:T(8,128)(2,1)S(1)}, u32[]{:S(2)}) copy-start(bf16[512,320]{1,0:T(8,128)(2,1)S(1)} %collective-permute-done.1.cot_next) | copy-start | bytes 983044
  45.8 9.7 %collective-permute-start.3 = (bf16[4,12,20,320]{3,0,2,1:T(4,128)(2,1)}, bf16[4,12,20,320]{3,0,2,1:T(4,128)(2,1)S(1)}, u32[]{:S(2)}, u32[]{:S(2)}) collective-permute-start(bf16[4,12,20,320]{3,0,2,1:T(4,128)(2,1)} %copy.17), channel_id=1, source_target_pairs={{0,1},{1,0},{2,3},{3,2},{4,5},{5,4},{6,7},{7,6},{8,9},{9,8},{10,11... | collective-permute-start | bytes 1843208 | tf_op jit(solution)/shard_map/ppermute | solution.py:44
  48.7 20.6 %all-to-all-start = ((bf16[16,3,20,320]{3,2,1,0:T(8,128)(2,1)}), bf16[16,3,20,320]{3,2,1,0:T(8,128)(2,1)S(1)}, u32[]{:S(2)}, u32[]{:S(2)}) async-start(bf16[16,3,20,320]{3,2,1,0:T(8,128)(2,1)} %broadcast_in_dim.6), calls=%async_computation | async-start | bytes 1769472 | tf_op jit(solution)/shard_map/all_to_all | solution.py:49
  55.6 16.6 %copy-start.26 = (f32[320]{0:T(512)S(1)}, f32[320]{0:T(512)}, u32[]{:S(2)}) copy-start(f32[320]{0:T(512)} %param.7) | copy-start | bytes 3844
  70.3 4.4 %collective-permute-start.5 = (bf16[16,3,20,320]{3,0,2,1:T(8,128)(2,1)}, bf16[16,3,20,320]{3,0,2,1:T(8,128)(2,1)}, u32[]{:S(2)}, u32[]{:S(2)}) collective-permute-start(bf16[16,3,20,320]{3,0,2,1:T(8,128)(2,1)} %copy.20), channel_id=1, source_target_pairs={{0,1},{1,0},{2,3},{3,2},{4,5},{5,4},{6,7},{7,6},{8,9},{9,8},{10,11... | collective-permute-start | bytes 1843208 | tf_op jit(solution)/shard_map/ppermute | solution.py:44
  72.2 4.7 %copy-start.1 = (f32[1,1,16,32,320]{4,3,2,1,0:T(8,128)S(1)}, f32[1,1,16,32,320]{4,3,2,1,0:T(8,128)}, u32[]{:S(2)}) copy-start(f32[1,1,16,32,320]{4,3,2,1,0:T(8,128)} %param.9) | copy-start | bytes 1966084
  73.8 10.0 %copy-start.2 = (bf16[2,512,320]{2,1,0:T(8,128)(2,1)}, bf16[2,512,320]{2,1,0:T(8,128)(2,1)S(1)}, u32[]{:S(2)}) copy-start(bf16[2,512,320]{2,1,0:T(8,128)(2,1)S(1)} %copy.22.far) | copy-start | bytes 1966084
  73.8 3.2 %copy-start.7 = (bf16[512,320]{1,0:T(8,128)(2,1)S(1)}, bf16[512,320]{1,0:T(8,128)(2,1)}, u32[]{:S(2)}) copy-start(bf16[512,320]{1,0:T(8,128)(2,1)} %copy-done.6) | copy-start | bytes 983044
  73.8 3.2 %copy-start.10 = (bf16[512,320]{1,0:T(8,128)(2,1)S(1)}, bf16[512,320]{1,0:T(8,128)(2,1)}, u32[]{:S(2)}) copy-start(bf16[512,320]{1,0:T(8,128)(2,1)} %copy-done.9) | copy-start | bytes 983044
  83.7 5.2 %copy-start.12 = (bf16[512,320]{1,0:T(8,128)(2,1)}, bf16[512,320]{1,0:T(8,128)(2,1)S(1)}, u32[]{:S(2)}) copy-start(bf16[512,320]{1,0:T(8,128)(2,1)S(1)} %get-tuple-element.43.hidden) | copy-start | bytes 983044
  83.7 5.2 %copy-start.23 = (f32[512,320]{1,0:T(8,128)}, f32[512,320]{1,0:T(8,128)S(1)}, u32[]{:S(2)}) copy-start(f32[512,320]{1,0:T(8,128)S(1)} %get-tuple-element.49.slope) | copy-start | bytes 1966084
  83.7 4.2 %collective-permute-start.6 = (f32[4,4,2,16,320]{4,3,2,1,0:T(8,128)S(1)}, f32[4,4,2,16,320]{4,3,2,1,0:T(8,128)S(1)}, u32[]{:S(2)}, u32[]{:S(2)}) collective-permute-start(f32[4,4,2,16,320]{4,3,2,1,0:T(8,128)S(1)} %get-tuple-element.42), channel_id=1, source_target_pairs={{0,1},{1,0},{2,3},{3,2},{4,5},{5,4},{6,7},{7,6},{8,9},{9,8},{10,11... | collective-permute-start | bytes 1966088 | tf_op jit(solution)/shard_map/ppermute | solution.py:44
  87.9 12.9 %copy-start.3 = (bf16[2,512,320]{2,1,0:T(8,128)(2,1)S(1)}, bf16[2,512,320]{2,1,0:T(8,128)(2,1)}, u32[]{:S(2)}) copy-start(bf16[2,512,320]{2,1,0:T(8,128)(2,1)} %copy-done.2) | copy-start | bytes 1966084
  88.9 21.0 %all-to-all-start.1 = ((f32[16,2,16,320]{3,2,1,0:T(8,128)}), f32[16,2,16,320]{3,2,1,0:T(8,128)S(1)}, u32[]{:S(2)}, u32[]{:S(2)}) async-start(f32[16,2,16,320]{3,2,1,0:T(8,128)} %bitcast.20), calls=%async_computation.1 | async-start | bytes 1572864 | tf_op jit(solution)/shard_map/all_to_all | solution.py:231
  95.0 12.9 %collective-permute-start.8 = (bf16[512,320]{1,0:T(8,128)(2,1)}, bf16[512,320]{1,0:T(8,128)(2,1)S(1)}, u32[]{:S(2)}, u32[]{:S(2)}) collective-permute-start(bf16[512,320]{1,0:T(8,128)(2,1)} %copy-done.12), channel_id=1, source_target_pairs={{16,0},{32,16},{48,32},{64,48},{80,64},{96,80},{112,96},{144,128},... | collective-permute-start | bytes 983048 | tf_op jit(solution)/shard_map/ppermute | solution.py:233
  96.3 12.9 %collective-permute-start.7 = (bf16[512,320]{1,0:T(8,128)(2,1)}, bf16[512,320]{1,0:T(8,128)(2,1)S(1)}, u32[]{:S(2)}, u32[]{:S(2)}) collective-permute-start(bf16[512,320]{1,0:T(8,128)(2,1)} %copy-done.12), channel_id=1, source_target_pairs={{0,16},{16,32},{32,48},{48,64},{64,80},{80,96},{96,112},{128,144},... | collective-permute-start | bytes 983048 | tf_op jit(solution)/shard_map/ppermute | solution.py:232
  100.9 1.8 %copy-start.18 = (bf16[12,2,160,320]{3,2,1,0:T(8,128)(2,1)S(1)}, bf16[12,2,160,320]{3,2,1,0:T(8,128)(2,1)}, u32[]{:S(2)}) copy-start(bf16[12,2,160,320]{3,2,1,0:T(8,128)(2,1)} %get-tuple-element.40.w_ref) | copy-start | bytes 7372804
  110.5 9.6 %collective-permute-start.9 = (f32[16,320]{1,0:T(8,128)S(1)}, f32[16,320]{1,0:T(8,128)S(1)}, u32[]{:S(2)}, u32[]{:S(2)}) collective-permute-start(f32[16,320]{1,0:T(8,128)S(1)} %get-tuple-element.46), channel_id=1, source_target_pairs={{0,72},{16,88},{32,104},{48,120},{64,8},{80,24},{96,40},{112,56},{... | collective-permute-start | bytes 61448 | tf_op jit(solution)/shard_map/ppermute | solution.py:40
  120.9 19.0 %all-to-all-start.2 = ((f32[8,16,320]{2,1,0:T(8,128)}), f32[8,16,320]{2,1,0:T(8,128)S(1)}, u32[]{:S(2)}, u32[]{:S(2)}) async-start(f32[8,16,320]{2,1,0:T(8,128)} %broadcast_in_dim.7), calls=%async_computation.2 | async-start | bytes 393216 | tf_op jit(solution)/shard_map/all_to_all | solution.py:49
  129.7 1.8 %copy-start.19 = (bf16[12,2,160,320]{3,2,1,0:T(8,128)(2,1)S(1)}, bf16[12,2,160,320]{3,2,1,0:T(8,128)(2,1)}, u32[]{:S(2)}) copy-start(bf16[12,2,160,320]{3,2,1,0:T(8,128)(2,1)} %get-tuple-element.40.w_ref) | copy-start | bytes 7372804
  131.6 1.1 copy-start.24
  132.7 12.6 %copy-start.13 = (bf16[512,320]{1,0:T(8,128)(2,1)S(1)}, bf16[512,320]{1,0:T(8,128)(2,1)}, u32[]{:S(2)}) copy-start(bf16[512,320]{1,0:T(8,128)(2,1)} %copy-done.12) | copy-start | bytes 983044
  132.7 12.6 %copy-start.15 = (bf16[512,320]{1,0:T(8,128)(2,1)S(1)}, bf16[512,320]{1,0:T(8,128)(2,1)}, u32[]{:S(2)}) copy-start(bf16[512,320]{1,0:T(8,128)(2,1)} %copy-done.14) | copy-start | bytes 983044
  140.5 10.9 %all-to-all-start.3 = ((f32[4,16,320]{2,1,0:T(8,128)}), f32[4,16,320]{2,1,0:T(8,128)S(1)}, u32[]{:S(2)}, u32[]{:S(2)}) async-start(f32[4,16,320]{2,1,0:T(8,128)} %broadcast_in_dim.8), calls=%async_computation.3 | async-start | bytes 196608 | tf_op jit(solution)/shard_map/all_to_all | solution.py:49
  146.3 1.8 %copy-start.20 = (bf16[12,2,160,320]{3,2,1,0:T(8,128)(2,1)S(1)}, bf16[12,2,160,320]{3,2,1,0:T(8,128)(2,1)}, u32[]{:S(2)}) copy-start(bf16[12,2,160,320]{3,2,1,0:T(8,128)(2,1)} %get-tuple-element.40.w_ref) | copy-start | bytes 7372804
  (9 other events, 8.5 us)

commit v4 on v3

--- a/solution.py
+++ b/solution.py
@@ -18,6 +18,9 @@
 ROWS = H * W
 HALF, PART, OWN = 160, 40, 20
 TAPS = 12
+SPACE = 9
+WIDE = 384
+SLOT = 64
 BF = jnp.bfloat16
 F32 = jnp.float32
 
@@ -97,30 +100,52 @@
     return acc
 
 
-def prepare_kernel(place, own_m, own_t, video, w_ref, windows):
-    c = place[0]
+def copies(sems, *pairs):
+    started = [pltpu.make_async_copy(src, dst, sems.at[i]) for i, (src, dst) in enumerate(pairs)]
+    for one in started:
+        one.start()
+    return started
+
+
+def prepare_kernel(video, out, windows, sems):
+    fill_windows(windows, video[...])
+    for one in copies(sems, (windows, out)):
+        one.wait()
+
+
+def forward_kernel(
+    place, w_mine_h, w_theirs_h, windows_h, bias, cot_h, prev_h, next_h, far_h,
+    w_h, hidden_h, slope_h, mine_ref, theirs_ref,
+    w_mine, w_theirs, windows, cot, cot_prev, cot_next, far, w_ref, hidden_ref, slope_ref, sems,
+):
+    c, h = place[0], place[1]
+    arrive = copies(
+        sems, (w_mine_h, w_mine), (w_theirs_h, w_theirs), (windows_h, windows),
+        (cot_h, cot), (prev_h, cot_prev), (next_h, cot_next), (far_h, far),
+    )
+    leave = [
+        pltpu.make_async_copy(src, dst, sems.at[7 + i])
+        for i, (src, dst) in enumerate(((w_ref, w_h), (hidden_ref, hidden_h), (slope_ref, slope_h)))
+    ]
+    arrive[0].wait()
+    arrive[1].wait()
     for t in range(TAPS):
         for y in range(4):
-            join(w_ref, t, 0, y, own_m[y, t], own_t[y, t], c)
-    fill_windows(windows, video[...])
-
-
-def forward_kernel(
-    place, own, oth_m, oth_t, windows, bias, cot, cot_prev, cot_next, far,
-    w_ref, hidden_ref, slope_ref, mine_ref, theirs_ref,
-):
-    c, h = place[0], place[1]
-    for t in range(TAPS):
-        w_ref[t, h] = own[t, 0]
-        for y in range(4):
             source = (t // 3) * 4 + y
-            join(w_ref, t, 1 - h, y, oth_m[source, t % 3], oth_t[source, t % 3], c)
+            for i, half in ((0, h), (1, 1 - h)):
+                at = i * SLOT + (t % 3) * OWN
+                join(w_ref, t, half, y, w_mine[source, at : at + OWN, 0:C], w_theirs[source, at : at + OWN, 0:C], c)
+    leave[0].start()
+    for one in arrive[2:]:
+        one.wait()
     spatial = conv(windows, w_ref, bias[...])
     sig = jax.nn.sigmoid(spatial)
     hidden = (spatial * sig).astype(BF)
     hidden_ref[...] = hidden
     slope_ref[...] = sig * (1.0 + spatial * (1.0 - sig))
-    before, after = sides(place, cot_prev[...], cot_next[...], far[0])
+    leave[1].start()
+    leave[2].start()
+    before, after = sides(place, cot_prev[...], cot_next[...], far[...])
     grads = [dot_tn(hidden, other) for other in (after, cot[...].astype(BF), before)]
     pad = jnp.zeros((4, C), F32)
     for half in range(2):
@@ -134,6 +159,8 @@
             for x in range(4):
                 mine_ref[x, y, half] = mine[16 * x : 16 * x + 16, :]
                 theirs_ref[x, y, half] = theirs[16 * x : 16 * x + 16, :]
+    for one in leave:
+        one.wait()
 
 
 def split_kernel(place, parts, keep_ref, give_ref):
@@ -145,13 +172,24 @@
     give_ref[...] = jnp.where(h == 0, total[1], total[0])
 
 
-def backward_kernel(place, w_ref, slope, cot, cot_prev, cot_next, far, grad_ref, windows):
-    before, after = sides(place, cot_prev[...], cot_next[...], far[0])
+def backward_kernel(
+    place, w_h, slope_h, cot_h, prev_h, next_h, far_h, grad_ref,
+    w_ref, slope, cot, cot_prev, cot_next, far, windows, sems,
+):
+    arrive = copies(
+        sems, (w_h.at[SPACE:TAPS], w_ref.at[SPACE:TAPS]), (cot_h, cot), (prev_h, cot_prev), (next_h, cot_next),
+        (far_h, far), (slope_h, slope), (w_h.at[0:SPACE], w_ref.at[0:SPACE]),
+    )
+    for one in arrive[:5]:
+        one.wait()
+    before, after = sides(place, cot_prev[...], cot_next[...], far[...])
     gh = dot_nt(after, tap(w_ref, 9))
     gh = gh + dot_nt(cot[...].astype(BF), tap(w_ref, 10))
     gh = gh + dot_nt(before, tap(w_ref, 11))
+    arrive[5].wait()
     gs = (gh * slope[...]).astype(BF).astype(F32)
     fill_windows(windows, gs)
+    arrive[6].wait()
     acc = cot[...]
     for a in range(3):
         for b in range(3):
@@ -159,33 +197,54 @@
     grad_ref[...] = acc
 
 
-def far_kernel(place, w_ref, far, bias, hidden_ref, windows):
-    fill_windows(windows, far[1].astype(F32))
+def far_kernel(place, w_h, far_h, bias, hidden_h, w_ref, far, hidden_ref, windows, sems):
+    arrive = copies(sems, (far_h, far), (w_h.at[0:SPACE], w_ref))
+    arrive[0].wait()
+    fill_windows(windows, far[...].astype(F32))
+    arrive[1].wait()
     spatial = conv(windows, w_ref, bias[...])
     hidden = (spatial * jax.nn.sigmoid(spatial)).astype(BF)
     hidden_ref[...] = jnp.where(place[3] == 1, hidden, jnp.zeros_like(hidden))
-
-
-def output_kernel(place, w_ref, video, hidden, prev, after, far, out_ref):
+    for one in copies(sems, (hidden_ref, hidden_h)):
+        one.wait()
+
+
+def output_kernel(
+    place, w_h, video_h, hidden_h, prev_h, after_h, far_h, out_ref,
+    w_ref, video, hidden, prev, after, far, sems,
+):
+    for one in copies(
+        sems, (w_h.at[SPACE:TAPS], w_ref), (video_h, video), (hidden_h, hidden), (prev_h, prev), (after_h, after), (far_h, far),
+    ):
+        one.wait()
     before, behind = sides(place, prev[...], after[...], far[...])
-    acc = video[...] + dot(hidden[...], tap(w_ref, 10))
-    acc = acc + dot(before, tap(w_ref, 9))
-    out_ref[...] = acc + dot(behind, tap(w_ref, 11))
-
-
-def kernel_call(body, outs, ins, scratch, micros, name):
-    whole = pl.BlockSpec(memory_space=pltpu.VMEM)
-    specs = [pl.BlockSpec(memory_space=pltpu.SMEM) if a.shape == (4,) else whole for a in ins]
+    acc = video[...] + dot(hidden[...], tap(w_ref, 1))
+    acc = acc + dot(before, tap(w_ref, 0))
+    out_ref[...] = acc + dot(behind, tap(w_ref, 2))
+
+
+FRAME_B = (ROWS, C), BF
+FRAME_F = (ROWS, C), F32
+WINDOWS = (3, ROWS + 2 * W, C), BF
+WEIGHTS = (TAPS, 2, HALF, C), BF
+PIECES = (16, 2 * SLOT, WIDE), BF
+SUMS = (4, 4, 2, 16, C), F32
+SHARE = (16, C), F32
+
+
+def kernel_call(body, ins, outs, scratch, copied, micros, name):
+    spaces = {"s": pltpu.SMEM, "v": pltpu.VMEM, "h": pltpu.HBM}
+    specs = [[pl.BlockSpec(memory_space=spaces[o[-1]]) for o in group] for group in (ins, outs)]
     return pl.pallas_call(
         body,
-        out_shape=tuple(jax.ShapeDtypeStruct(*o) for o in outs),
-        in_specs=specs,
-        out_specs=tuple(whole for _ in outs),
-        scratch_shapes=scratch,
-        compiler_params=pltpu.CompilerParams(vmem_limit_bytes=48 * 1024 * 1024),
+        out_shape=tuple(jax.ShapeDtypeStruct(*o[0]) for o in outs),
+        in_specs=specs[0],
+        out_specs=tuple(specs[1]),
+        scratch_shapes=[pltpu.VMEM(*o) for o in scratch] + [pltpu.SemaphoreType.DMA((copied,))] * (copied > 0),
+        compiler_params=pltpu.CompilerParams(vmem_limit_bytes=(60 if copied else 8) * 1024 * 1024),
         cost_estimate=pl.CostEstimate(flops=int(micros * 1.0e9), bytes_accessed=1_000_000, transcendentals=0),
         name=name,
-    )(*ins)
+    )(*(a for a, _ in ins))
 
 
 def on_device(video, spatial_w, spatial_b, temporal_w, cotangent):
@@ -198,33 +257,30 @@
     cot_f = cotangent.reshape(ROWS, C)
     bias = spatial_b.reshape(1, C)
 
-    both = jnp.stack([cot_f, video_f]).astype(BF)
-    cot_b = both[0]
-    far = lax.ppermute(both, TM, FRAMES_FAR)
+    cot_b, video_b = cot_f.astype(BF), video_f.astype(BF)
+    far = lax.ppermute(cot_b, TM, FRAMES_FAR)
+    video_far = lax.ppermute(video_b, TM, FRAMES_FAR)
     w = jnp.concatenate([spatial_w, temporal_w.astype(BF)], axis=0)
-    other = across(lax.dynamic_slice_in_dim(w, 3 * x, 3, 0))
-    own_m = lax.all_gather(w, "y")
+    quarter = lax.dynamic_slice_in_dim(w, 3 * x, 3, 0).reshape(3 * OWN, C)
+    quarter = jnp.pad(quarter, ((0, SLOT - 3 * OWN), (0, WIDE - C)))
+    other = across(quarter)
     cot_next = lax.ppermute(cot_b, TM, FRAMES_DOWN)
     cot_prev = lax.ppermute(cot_b, TM, FRAMES_UP)
-    other, own_m, cot_next, cot_prev = tie((other, own_m, cot_next, cot_prev))
-    oth_m = to_all(other, PLANE)
-    own_t = core_swap(own_m)
-    own, windows = kernel_call(
-        prepare_kernel,
-        [((TAPS, 1, HALF, C), BF), ((3, ROWS + 2 * W, C), BF)],
-        (place, own_m, own_t, video_f), [], 0.01, "prepare",
-    )
-    oth_m, own, windows, far = tie((oth_m, own, windows, far))
-    oth_t = core_swap(oth_m)
+    other, cot_next, cot_prev = tie((other, cot_next, cot_prev))
+    w_mine = to_all(jnp.concatenate([quarter, other], axis=0), PLANE)
+    (windows,) = kernel_call(prepare_kernel, [(video_f, "v")], [(WINDOWS, "h")], [WINDOWS], 1, 0.01, "prepare")
+    w_mine, windows, far, video_far = tie((w_mine, windows, far, video_far))
+    w_theirs = core_swap(w_mine)
 
     w_all, hidden, slope, mine, theirs = kernel_call(
         forward_kernel,
         [
-            ((TAPS, 2, HALF, C), BF), ((ROWS, C), BF), ((ROWS, C), F32),
-            ((4, 4, 2, 16, C), F32), ((4, 4, 2, 16, C), F32),
+            (place, "s"), (w_mine, "h"), (w_theirs, "h"), (windows, "h"), (bias, "v"),
+            (cot_f, "h"), (cot_prev, "h"), (cot_next, "h"), (far, "h"),
         ],
-        (place, own, oth_m, oth_t, windows, bias, cot_f, cot_prev, cot_next, far),
-        [], 6, "forward",
+        [(WEIGHTS, "h"), (FRAME_B, "h"), (FRAME_F, "h"), (SUMS, "v"), (SUMS, "v")],
+        [PIECES, PIECES, WINDOWS, FRAME_F, FRAME_B, FRAME_B, FRAME_B, WEIGHTS, FRAME_B, FRAME_F],
+        10, 6, "forward",
     )
 
     part = mine + core_swap(theirs)
@@ -232,26 +288,31 @@
     prev = lax.ppermute(hidden, TM, FRAMES_UP)
     after = lax.ppermute(hidden, TM, FRAMES_DOWN)
     (hidden_far,) = kernel_call(
-        far_kernel, [((ROWS, C), BF)], (place, w_all, far, bias),
-        [pltpu.VMEM((3, ROWS + 2 * W, C), BF)], 5, "far",
+        far_kernel, [(place, "s"), (w_all, "h"), (video_far, "h"), (bias, "v")], [(FRAME_B, "h")],
+        [((SPACE, 2, HALF, C), BF), FRAME_B, FRAME_B, WINDOWS], 2, 5, "far",
     )
     part, prev, after, hidden_far = tie((part, prev, after, hidden_far))
     keep, give = kernel_call(
-        split_kernel, [((16, C), F32), ((16, C), F32)], (place, part), [], 0.01, "split",
+        split_kernel, [(place, "s"), (part, "v")], [(SHARE, "v"), (SHARE, "v")], [], 0, 0.01, "split",
     )
     part = keep + across(give)
     part, slope = tie((part, slope))
     part = to_all(part, Z_LO)
     (grad_video,) = kernel_call(
-        backward_kernel, [((ROWS, C), F32)], (place, w_all, slope, cot_f, cot_prev, cot_next, far),
-        [pltpu.VMEM((3, ROWS + 2 * W, C), BF)], 5, "backward",
+        backward_kernel,
+        [(place, "s"), (w_all, "h"), (slope, "h"), (cot_f, "h"), (cot_prev, "h"), (cot_next, "h"), (far, "h")],
+        [(FRAME_F, "v")],
+        [WEIGHTS, FRAME_F, FRAME_F, FRAME_B, FRAME_B, FRAME_B, WINDOWS], 7, 5, "backward",
     )
     part, grad_video = tie((part, grad_video))
     part = jnp.sum(part, axis=0)
     part, video_f = tie((part, video_f))
     part = to_all(part, "x").reshape(4 * 16, C)
     (output,) = kernel_call(
-        output_kernel, [((ROWS, C), F32)], (place, w_all, video_f, hidden, prev, after, hidden_far), [], 3, "output",
+        output_kernel,
+        [(place, "s"), (w_all, "h"), (video_f, "h"), (hidden, "h"), (prev, "h"), (after, "h"), (hidden_far, "h")],
+        [(FRAME_F, "v")],
+        [((3, 2, HALF, C), BF), FRAME_F, FRAME_B, FRAME_B, FRAME_B, FRAME_B], 6, 3, "output",
     )
     total_rows = ROWS * lax.axis_size(TM) * lax.axis_size(CLIP)
     grad_temporal = part[: 3 * OWN].reshape(3, OWN, C) * (1.0 / math.sqrt(total_rows))

time: 153 us -> 156 us (1.020)
  the two profiles are of different devices: /device:TPU:2 before, /device:TPU:8 now
where the time goes in v4:
time: 156 us; the launch traced here: 155 us
  starting transfers between devices  58.4 us (37%)
  waiting for transfers between devices  55.6 us (36%)
  Pallas kernels  29 us (19%)
  other arithmetic  5.74 us (4%)
  local copies, waits for them, and re-layouts  4.79 us (3%)
    all_to_all x3, waiting for transfers between devices, to_all(): lax.all_to_all(jnp.broadcast_to(a[None], (n, *a.shape)), axes, 0, 0, tile...  38 us
    pallas_call x6, Pallas kernels, kernel_call(): pl.pallas_call(body, out_shape=tuple((jax.ShapeDtypeStruct(*o[0]) for o i...  29 us
    all_to_all x3, starting transfers between devices, to_all(): lax.all_to_all(jnp.broadcast_to(a[None], (n, *a.shape)), axes, 0, 0, tile...  19.7 us
    ppermute x2, starting transfers between devices, across(): return lax.ppermute(a, ('m', 'k', 'h'), ACROSS)  16.6 us
    ppermute x2, waiting for transfers between devices, across(): return lax.ppermute(a, ('m', 'k', 'h'), ACROSS)  10.7 us
    all_to_all x1, starting transfers between devices, on_device(): part = lax.all_to_all(part.reshape(16, 2, 16, C), PLANE, 0, 0, tiled=True)  5.86 us
    ppermute x2, waiting for transfers between devices, core_swap(): return lax.ppermute(a, 'c', [(0, 1), (1, 0)])  4.7 us
    ppermute x1, starting transfers between devices, on_device(): prev = lax.ppermute(hidden, TM, FRAMES_UP)  4.57 us
  transfers between devices with their start and end apart: 14, of which 9 were waited for; matrix products, arithmetic and copies ran while one was open for 2% of the time, Pallas kernels for 13%

profile of v4, /device:TPU:8, one launch (start us, length us, event | category | flops | bytes accessed | tf_op | source)
XLA Modules:
  0.0 154.5 jit_solution(14086611194902621184)
XLA Ops:
  0.6 1.2 bitcast_convert_fusion.1
  1.8 3.8 %collective-permute-start.2 = (bf16[512,320]{1,0:T(8,128)(2,1)S(1)}, bf16[512,320]{1,0:T(8,128)(2,1)S(1)}, u32[]{:S(2)}, u32[]{:S(2)}) collective-permute-start(bf16[512,320]{1,0:T(8,128)(2,1)S(1)} %bitcast_convert_fusion.1), channel_id=1, source_target_pairs={{0,16},{16,32},{32,48},{48,64},{64,80},{80,96},{96,112},{128,144},... | collective-permute-start | bytes 983048 | tf_op jit(solution)/shard_map/ppermute | solution.py:268
  5.7 1.3 collective-permute-start.1
  7.0 0.9 convert_element_type.12
  7.9 0.8 fusion
  8.8 14.7 %collective-permute-start = (bf16[64,384]{1,0:T(8,128)(2,1)S(1)}, bf16[64,384]{1,0:T(8,128)(2,1)S(1)}, u32[]{:S(2)}, u32[]{:S(2)}) collective-permute-start(bf16[64,384]{1,0:T(8,128)(2,1)S(1)} %pad.4), channel_id=1, source_target_pairs={{0,72},{16,88},{32,104},{48,120},{64,8},{80,24},{96,40},{112,56},{... | collective-permute-start | bytes 147464 | tf_op jit(solution)/shard_map/ppermute | solution.py:43
  23.4 2.9 %collective-permute-done = bf16[64,384]{1,0:T(8,128)(2,1)S(1)} collective-permute-done((bf16[64,384]{1,0:T(8,128)(2,1)S(1)}, bf16[64,384]{1,0:T(8,128)(2,1)S(1)}, u32[]{:S(2)}, u32[]{:S(2)}) %collective-permute-start) | collective-permute-done | bytes 49184 | tf_op jit(solution)/shard_map/ppermute | solution.py:43
  26.3 0.8 copy-done.5
  27.1 1.4 broadcast_in_dim.6
  28.5 7.5 %all-to-all-start = ((bf16[16,128,384]{2,1,0:T(8,128)(2,1)}), bf16[16,128,384]{2,1,0:T(8,128)(2,1)S(1)}, u32[]{:S(2)}, u32[]{:S(2)}) async-start(bf16[16,128,384]{2,1,0:T(8,128)(2,1)} %broadcast_in_dim.6), calls=%async_computation | async-start | bytes 3145728 | tf_op jit(solution)/shard_map/all_to_all | solution.py:52
  37.5 2.5 %prepare.1.windows_h = bf16[3,576,320]{2,1,0:T(8,128)(2,1)} custom-call(f32[512,320]{1,0:T(8,128)} %bitcast.12), custom_call_target="tpu_custom_call" | custom-call | flops 10000000 | bytes 1000000 | tf_op jit(solution)/shard_map/prepare/pallas_call | solution.py:238
  40.0 32.0 %all-to-all-done.w_mine_h = bf16[16,128,384]{2,1,0:T(8,128)(2,1)S(1)} async-done(((bf16[16,128,384]{2,1,0:T(8,128)(2,1)}), bf16[16,128,384]{2,1,0:T(8,128)(2,1)S(1)}, u32[]{:S(2)}, u32[]{:S(2)}) %all-to-all-start) | async-done | bytes 1572896 | tf_op jit(solution)/shard_map/all_to_all | solution.py:52
  72.0 1.9 %collective-permute-start.5 = (bf16[16,128,384]{2,1,0:T(8,128)(2,1)S(1)}, bf16[16,128,384]{2,1,0:T(8,128)(2,1)}, u32[]{:S(2)}, u32[]{:S(2)}) collective-permute-start(bf16[16,128,384]{2,1,0:T(8,128)(2,1)S(1)} %all-to-all-done.w_mine_h), channel_id=1, source_target_pairs={{0,1},{1,0},{2,3},{3,2},{4,5},{5,4},{6,7},{7,6},{8,9},{9,8},{10,11... | collective-permute-start | bytes 4718600 | tf_op jit(solution)/shard_map/ppermute | solution.py:47
  75.1 2.3 %collective-permute-done.5.w_theirs_h = bf16[16,128,384]{2,1,0:T(8,128)(2,1)} collective-permute-done((bf16[16,128,384]{2,1,0:T(8,128)(2,1)S(1)}, bf16[16,128,384]{2,1,0:T(8,128)(2,1)}, u32[]{:S(2)}, u32[]{:S(2)}) %collective-permute-start.5) | collective-permute-done | bytes 1572896 | tf_op jit(solution)/shard_map/ppermute | solution.py:47
  77.4 8.6 %forward.1 = (bf16[12,2,160,320]{3,2,1,0:T(8,128)(2,1)}, bf16[512,320]{1,0:T(8,128)(2,1)}, f32[512,320]{1,0:T(8,128)}, f32[4,4,2,16,320]{4,3,2,1,0:T(8,128)}, f32[4,4,2,16,320]{4,3,2,1,0:T(8,128)}) custom-call(s32[4]{0:T(128)} %pad_add_fusion.place, bf16[16,128,384]{2,1,0:T(8,128)(2,1)} %copy-done.2, ...), custom_call_target="tpu_custom_call" | custom-call | flops 6000000000 | bytes 1000000 | tf_op jit(solution)/shard_map/forward/pallas_call | solution.py:238
  86.0 2.0 %collective-permute-start.6 = (f32[4,4,2,16,320]{4,3,2,1,0:T(8,128)}, f32[4,4,2,16,320]{4,3,2,1,0:T(8,128)S(1)}, u32[]{:S(2)}, u32[]{:S(2)}) collective-permute-start(f32[4,4,2,16,320]{4,3,2,1,0:T(8,128)} %get-tuple-element.35), channel_id=1, source_target_pairs={{0,1},{1,0},{2,3},{3,2},{4,5},{5,4},{6,7},{7,6},{8,9},{9,8},{10,11... | collective-permute-start | bytes 1966088 | tf_op jit(solution)/shard_map/ppermute | solution.py:47
  88.0 2.3 %collective-permute-done.6 = f32[4,4,2,16,320]{4,3,2,1,0:T(8,128)S(1)} collective-permute-done((f32[4,4,2,16,320]{4,3,2,1,0:T(8,128)}, f32[4,4,2,16,320]{4,3,2,1,0:T(8,128)S(1)}, u32[]{:S(2)}, u32[]{:S(2)}) %collective-permute-start.6) | collective-permute-done | bytes 655392 | tf_op jit(solution)/shard_map/ppermute | solution.py:47
  90.4 2.2 %add.16 = f32[4,4,2,16,320]{4,3,2,1,0:T(8,128)} add(f32[4,4,2,16,320]{4,3,2,1,0:T(8,128)} %get-tuple-element.34, f32[4,4,2,16,320]{4,3,2,1,0:T(8,128)S(1)} %collective-permute-done.6) | non-fusion elementwise | flops 163840 | bytes 1966080 | tf_op jit(solution)/shard_map/add | solution.py:286
  92.6 5.9 %all-to-all-start.1 = ((f32[16,2,16,320]{3,2,1,0:T(8,128)}), f32[16,2,16,320]{3,2,1,0:T(8,128)S(1)}, u32[]{:S(2)}, u32[]{:S(2)}) async-start(f32[16,2,16,320]{3,2,1,0:T(8,128)} %bitcast.6), calls=%async_computation.1 | async-start | bytes 1572864 | tf_op jit(solution)/shard_map/all_to_all | solution.py:287
  98.4 1.3 collective-permute-start.8
  99.7 4.6 %collective-permute-start.7 = (bf16[512,320]{1,0:T(8,128)(2,1)S(1)}, bf16[512,320]{1,0:T(8,128)(2,1)S(1)}, u32[]{:S(2)}, u32[]{:S(2)}) collective-permute-start(bf16[512,320]{1,0:T(8,128)(2,1)S(1)} %copy-done.8), channel_id=1, source_target_pairs={{0,16},{16,32},{32,48},{48,64},{64,80},{80,96},{96,112},{128,144},... | collective-permute-start | bytes 983048 | tf_op jit(solution)/shard_map/ppermute | solution.py:288
  104.3 5.6 %far.1.far_h = bf16[512,320]{1,0:T(8,128)(2,1)} custom-call(s32[4]{0:T(128)} %pad_add_fusion.place, bf16[12,2,160,320]{3,2,1,0:T(8,128)(2,1)} %get-tuple-element.33.w_h, bf16[512,320]{1,0:T(8,128)(2,1)} %copy-done.7, f32[1,320]{1,0:T(1,128)} %reshape.39.bias), custom_call_target="tpu_custom_call" | custom-call | flops 5000000000 | bytes 1000000 | tf_op jit(solution)/shard_map/far/pallas_call | solution.py:238
  109.9 1.0 collective-permute-done.8.after_h
  110.9 1.2 collective-permute-done.7.prev_h
  112.7 1.9 %collective-permute-start.9 = (f32[16,320]{1,0:T(8,128)S(1)}, f32[16,320]{1,0:T(8,128)S(1)}, u32[]{:S(2)}, u32[]{:S(2)}) collective-permute-start(f32[16,320]{1,0:T(8,128)S(1)} %get-tuple-element.40), channel_id=1, source_target_pairs={{0,72},{16,88},{32,104},{48,120},{64,8},{80,24},{96,40},{112,56},{... | collective-permute-start | bytes 61448 | tf_op jit(solution)/shard_map/ppermute | solution.py:43
  114.6 7.8 %collective-permute-done.9 = f32[16,320]{1,0:T(8,128)S(1)} collective-permute-done((f32[16,320]{1,0:T(8,128)S(1)}, f32[16,320]{1,0:T(8,128)S(1)}, u32[]{:S(2)}, u32[]{:S(2)}) %collective-permute-start.9) | collective-permute-done | bytes 20512 | tf_op jit(solution)/shard_map/ppermute | solution.py:43
  123.1 7.9 %all-to-all-start.2 = ((f32[8,16,320]{2,1,0:T(8,128)}), f32[8,16,320]{2,1,0:T(8,128)S(1)}, u32[]{:S(2)}, u32[]{:S(2)}) async-start(f32[8,16,320]{2,1,0:T(8,128)} %broadcast_in_dim.7), calls=%async_computation.2 | async-start | bytes 393216 | tf_op jit(solution)/shard_map/all_to_all | solution.py:52
  131.0 7.5 %backward.1 = f32[512,320]{1,0:T(8,128)} custom-call(s32[4]{0:T(128)} %pad_add_fusion.place, bf16[12,2,160,320]{3,2,1,0:T(8,128)(2,1)} %get-tuple-element.33.w_h, f32[512,320]{1,0:T(8,128)} %get-tuple-element.43.slope_h, f32[512,320]{1,0:T(8,128)} %bitcast.15, bf16[512,320]{1,0:T(8,128)(2,1)} %copy-done.4, bf16[512,320]{1,0:T(8,128)(2,1)} %copy-done.5, ...), custom_call_target="tpu_custom_call" | custom-call | flops 5000000000 | bytes 1000000 | tf_op jit(solution)/shard_map/backward/pallas_call | solution.py:238
  138.6 4.6 %all-to-all-done.2 = f32[8,16,320]{2,1,0:T(8,128)S(1)} async-done(((f32[8,16,320]{2,1,0:T(8,128)}), f32[8,16,320]{2,1,0:T(8,128)S(1)}, u32[]{:S(2)}, u32[]{:S(2)}) %all-to-all-start.2) | async-done | bytes 163872 | tf_op jit(solution)/shard_map/all_to_all | solution.py:52
  143.8 4.2 %all-to-all-start.3 = ((f32[4,16,320]{2,1,0:T(8,128)}), f32[4,16,320]{2,1,0:T(8,128)S(1)}, u32[]{:S(2)}, u32[]{:S(2)}) async-start(f32[4,16,320]{2,1,0:T(8,128)} %broadcast_in_dim.8), calls=%async_computation.3 | async-start | bytes 196608 | tf_op jit(solution)/shard_map/all_to_all | solution.py:52
  148.1 4.3 %output.1 = f32[512,320]{1,0:T(8,128)} custom-call(s32[4]{0:T(128)} %pad_add_fusion.place, bf16[12,2,160,320]{3,2,1,0:T(8,128)(2,1)} %get-tuple-element.33.w_h, f32[512,320]{1,0:T(8,128)} %bitcast.13, bf16[512,320]{1,0:T(8,128)(2,1)} %get-tuple-element.36.hidden_h, bf16[512,320]{1,0:T(8,128)(2,1)} %copy-done.10, bf16[512,320]{1,0:T(8,128)(2,1)} %copy-done.9, ...), custom_call_target="tpu_custom_call" | custom-call | flops 3000000000 | bytes 1000000 | tf_op jit(solution)/shard_map/output/pallas_call | solution.py:238
  152.3 1.5 all-to-all-done.3
  (41 shorter events, 5.2 us)
Async XLA Ops:
  1.8 24.5 %collective-permute-start.2 = (bf16[512,320]{1,0:T(8,128)(2,1)S(1)}, bf16[512,320]{1,0:T(8,128)(2,1)S(1)}, u32[]{:S(2)}, u32[]{:S(2)}) collective-permute-start(bf16[512,320]{1,0:T(8,128)(2,1)S(1)} %bitcast_convert_fusion.1), channel_id=1, source_target_pairs={{0,16},{16,32},{32,48},{48,64},{64,80},{80,96},{96,112},{128,144},... | collective-permute-start | bytes 983048 | tf_op jit(solution)/shard_map/ppermute | solution.py:268
  5.7 20.6 %collective-permute-start.1 = (bf16[512,320]{1,0:T(8,128)(2,1)S(1)}, bf16[512,320]{1,0:T(8,128)(2,1)S(1)}, u32[]{:S(2)}, u32[]{:S(2)}) collective-permute-start(bf16[512,320]{1,0:T(8,128)(2,1)S(1)} %bitcast_convert_fusion.1), channel_id=1, source_target_pairs={{16,0},{32,16},{48,32},{64,48},{80,64},{96,80},{112,96},{144,128},... | collective-permute-start | bytes 983048 | tf_op jit(solution)/shard_map/ppermute | solution.py:267
  8.8 17.5 %collective-permute-start = (bf16[64,384]{1,0:T(8,128)(2,1)S(1)}, bf16[64,384]{1,0:T(8,128)(2,1)S(1)}, u32[]{:S(2)}, u32[]{:S(2)}) collective-permute-start(bf16[64,384]{1,0:T(8,128)(2,1)S(1)} %pad.4), channel_id=1, source_target_pairs={{0,72},{16,88},{32,104},{48,120},{64,8},{80,24},{96,40},{112,56},{... | collective-permute-start | bytes 147464 | tf_op jit(solution)/shard_map/ppermute | solution.py:43
  26.3 2.2 %copy-start.4 = (bf16[512,320]{1,0:T(8,128)(2,1)}, bf16[512,320]{1,0:T(8,128)(2,1)S(1)}, u32[]{:S(2)}) copy-start(bf16[512,320]{1,0:T(8,128)(2,1)S(1)} %collective-permute-done.2.prev_h) | copy-start | bytes 983044
  26.3 0.8 copy-start.5
  28.5 7.5 %copy-start.1 = (f32[1,1,16,32,320]{4,3,2,1,0:T(8,128)S(1)}, f32[1,1,16,32,320]{4,3,2,1,0:T(8,128)}, u32[]{:S(2)}) copy-start(f32[1,1,16,32,320]{4,3,2,1,0:T(8,128)} %param.5) | copy-start | bytes 1966084
  28.5 43.5 %all-to-all-start = ((bf16[16,128,384]{2,1,0:T(8,128)(2,1)}), bf16[16,128,384]{2,1,0:T(8,128)(2,1)S(1)}, u32[]{:S(2)}, u32[]{:S(2)}) async-start(bf16[16,128,384]{2,1,0:T(8,128)(2,1)} %broadcast_in_dim.6), calls=%async_computation | async-start | bytes 3145728 | tf_op jit(solution)/shard_map/all_to_all | solution.py:52
  36.0 37.9 %copy-start.3 = (f32[320]{0:T(512)S(1)}, f32[320]{0:T(512)}, u32[]{:S(2)}) copy-start(f32[320]{0:T(512)} %param.7) | copy-start | bytes 3844
  36.1 3.9 %collective-permute-start.4 = (bf16[512,320]{1,0:T(8,128)(2,1)S(1)}, bf16[512,320]{1,0:T(8,128)(2,1)S(1)}, u32[]{:S(2)}, u32[]{:S(2)}) collective-permute-start(bf16[512,320]{1,0:T(8,128)(2,1)S(1)} %bitcast_convert_fusion), channel_id=1, source_target_pairs={{112,128},{128,112},{240,256},{256,240},{368,384},{384,368},{113,1... | collective-permute-start | bytes 983048 | tf_op jit(solution)/shard_map/ppermute | solution.py:262
  36.8 3.2 %collective-permute-start.3 = (bf16[512,320]{1,0:T(8,128)(2,1)S(1)}, bf16[512,320]{1,0:T(8,128)(2,1)S(1)}, u32[]{:S(2)}, u32[]{:S(2)}) collective-permute-start(bf16[512,320]{1,0:T(8,128)(2,1)S(1)} %bitcast_convert_fusion.1), channel_id=1, source_target_pairs={{112,128},{128,112},{240,256},{256,240},{368,384},{384,368},{113,1... | collective-permute-start | bytes 983048 | tf_op jit(solution)/shard_map/ppermute | solution.py:261
  40.0 46.0 %copy-start.7 = (bf16[512,320]{1,0:T(8,128)(2,1)}, bf16[512,320]{1,0:T(8,128)(2,1)S(1)}, u32[]{:S(2)}) copy-start(bf16[512,320]{1,0:T(8,128)(2,1)S(1)} %collective-permute-done.4.far_h) | copy-start | bytes 983044
  40.0 37.4 %copy-start.6 = (bf16[512,320]{1,0:T(8,128)(2,1)}, bf16[512,320]{1,0:T(8,128)(2,1)S(1)}, u32[]{:S(2)}) copy-start(bf16[512,320]{1,0:T(8,128)(2,1)S(1)} %collective-permute-done.3.far_h) | copy-start | bytes 983044
  72.0 5.4 %copy-start.2 = (bf16[16,128,384]{2,1,0:T(8,128)(2,1)}, bf16[16,128,384]{2,1,0:T(8,128)(2,1)S(1)}, u32[]{:S(2)}) copy-start(bf16[16,128,384]{2,1,0:T(8,128)(2,1)S(1)} %all-to-all-done.w_mine_h) | copy-start | bytes 4718596
  72.0 5.4 %collective-permute-start.5 = (bf16[16,128,384]{2,1,0:T(8,128)(2,1)S(1)}, bf16[16,128,384]{2,1,0:T(8,128)(2,1)}, u32[]{:S(2)}, u32[]{:S(2)}) collective-permute-start(bf16[16,128,384]{2,1,0:T(8,128)(2,1)S(1)} %all-to-all-done.w_mine_h), channel_id=1, source_target_pairs={{0,1},{1,0},{2,3},{3,2},{4,5},{5,4},{6,7},{7,6},{8,9},{9,8},{10,11... | collective-permute-start | bytes 4718600 | tf_op jit(solution)/shard_map/ppermute | solution.py:47
  86.0 4.4 %collective-permute-start.6 = (f32[4,4,2,16,320]{4,3,2,1,0:T(8,128)}, f32[4,4,2,16,320]{4,3,2,1,0:T(8,128)S(1)}, u32[]{:S(2)}, u32[]{:S(2)}) collective-permute-start(f32[4,4,2,16,320]{4,3,2,1,0:T(8,128)} %get-tuple-element.35), channel_id=1, source_target_pairs={{0,1},{1,0},{2,3},{3,2},{4,5},{5,4},{6,7},{7,6},{8,9},{9,8},{10,11... | collective-permute-start | bytes 1966088 | tf_op jit(solution)/shard_map/ppermute | solution.py:47
  90.4 8.0 %copy-start.8 = (bf16[512,320]{1,0:T(8,128)(2,1)S(1)}, bf16[512,320]{1,0:T(8,128)(2,1)}, u32[]{:S(2)}) copy-start(bf16[512,320]{1,0:T(8,128)(2,1)} %get-tuple-element.36.hidden_h) | copy-start | bytes 983044
  92.6 19.6 %all-to-all-start.1 = ((f32[16,2,16,320]{3,2,1,0:T(8,128)}), f32[16,2,16,320]{3,2,1,0:T(8,128)S(1)}, u32[]{:S(2)}, u32[]{:S(2)}) async-start(f32[16,2,16,320]{3,2,1,0:T(8,128)} %bitcast.6), calls=%async_computation.1 | async-start | bytes 1572864 | tf_op jit(solution)/shard_map/all_to_all | solution.py:287
  98.4 12.5 %collective-permute-start.8 = (bf16[512,320]{1,0:T(8,128)(2,1)S(1)}, bf16[512,320]{1,0:T(8,128)(2,1)S(1)}, u32[]{:S(2)}, u32[]{:S(2)}) collective-permute-start(bf16[512,320]{1,0:T(8,128)(2,1)S(1)} %copy-done.8), channel_id=1, source_target_pairs={{16,0},{32,16},{48,32},{64,48},{80,64},{96,80},{112,96},{144,128},... | collective-permute-start | bytes 983048 | tf_op jit(solution)/shard_map/ppermute | solution.py:289
  99.7 12.4 %collective-permute-start.7 = (bf16[512,320]{1,0:T(8,128)(2,1)S(1)}, bf16[512,320]{1,0:T(8,128)(2,1)S(1)}, u32[]{:S(2)}, u32[]{:S(2)}) collective-permute-start(bf16[512,320]{1,0:T(8,128)(2,1)S(1)} %copy-done.8), channel_id=1, source_target_pairs={{0,16},{16,32},{32,48},{48,64},{64,80},{80,96},{96,112},{128,144},... | collective-permute-start | bytes 983048 | tf_op jit(solution)/shard_map/ppermute | solution.py:288
  104.3 7.8 %copy-start = (s32[4]{0:T(128)S(1)}, s32[4]{0:T(128)}, u32[]{:S(2)}) copy-start(s32[4]{0:T(128)} %pad_add_fusion.place) | copy-start | bytes 52
  110.9 27.6 %copy-start.9 = (bf16[512,320]{1,0:T(8,128)(2,1)}, bf16[512,320]{1,0:T(8,128)(2,1)S(1)}, u32[]{:S(2)}) copy-start(bf16[512,320]{1,0:T(8,128)(2,1)S(1)} %collective-permute-done.8.after_h) | copy-start | bytes 983044
  112.1 26.4 %copy-start.10 = (bf16[512,320]{1,0:T(8,128)(2,1)}, bf16[512,320]{1,0:T(8,128)(2,1)S(1)}, u32[]{:S(2)}) copy-start(bf16[512,320]{1,0:T(8,128)(2,1)S(1)} %collective-permute-done.7.prev_h) | copy-start | bytes 983044
  112.7 9.7 %collective-permute-start.9 = (f32[16,320]{1,0:T(8,128)S(1)}, f32[16,320]{1,0:T(8,128)S(1)}, u32[]{:S(2)}, u32[]{:S(2)}) collective-permute-start(f32[16,320]{1,0:T(8,128)S(1)} %get-tuple-element.40), channel_id=1, source_target_pairs={{0,72},{16,88},{32,104},{48,120},{64,8},{80,24},{96,40},{112,56},{... | collective-permute-start | bytes 61448 | tf_op jit(solution)/shard_map/ppermute | solution.py:43
  123.1 20.0 %all-to-all-start.2 = ((f32[8,16,320]{2,1,0:T(8,128)}), f32[8,16,320]{2,1,0:T(8,128)S(1)}, u32[]{:S(2)}, u32[]{:S(2)}) async-start(f32[8,16,320]{2,1,0:T(8,128)} %broadcast_in_dim.7), calls=%async_computation.2 | async-start | bytes 393216 | tf_op jit(solution)/shard_map/all_to_all | solution.py:52
  143.8 10.0 %all-to-all-start.3 = ((f32[4,16,320]{2,1,0:T(8,128)}), f32[4,16,320]{2,1,0:T(8,128)S(1)}, u32[]{:S(2)}, u32[]{:S(2)}) async-start(f32[4,16,320]{2,1,0:T(8,128)} %broadcast_in_dim.8), calls=%async_computation.3 | async-start | bytes 196608 | tf_op jit(solution)/shard_map/all_to_all | solution.py:52

commit v5 on v4

--- a/solution.py
+++ b/solution.py
@@ -20,6 +20,7 @@
 TAPS = 12
 SPACE = 9
 WIDE = 384
+LIMIT = 48
 SLOT = 64
 BF = jnp.bfloat16
 F32 = jnp.float32
@@ -114,37 +115,22 @@
 
 
 def forward_kernel(
-    place, w_mine_h, w_theirs_h, windows_h, bias, cot_h, prev_h, next_h, far_h,
-    w_h, hidden_h, slope_h, mine_ref, theirs_ref,
-    w_mine, w_theirs, windows, cot, cot_prev, cot_next, far, w_ref, hidden_ref, slope_ref, sems,
+    place, own_m, own_t, oth_m, oth_t, windows, bias, cot, cot_prev, cot_next, far,
+    w_h, hidden_ref, slope_ref, mine_ref, theirs_ref, w_ref, sems,
 ):
     c, h = place[0], place[1]
-    arrive = copies(
-        sems, (w_mine_h, w_mine), (w_theirs_h, w_theirs), (windows_h, windows),
-        (cot_h, cot), (prev_h, cot_prev), (next_h, cot_next), (far_h, far),
-    )
-    leave = [
-        pltpu.make_async_copy(src, dst, sems.at[7 + i])
-        for i, (src, dst) in enumerate(((w_ref, w_h), (hidden_ref, hidden_h), (slope_ref, slope_h)))
-    ]
-    arrive[0].wait()
-    arrive[1].wait()
     for t in range(TAPS):
         for y in range(4):
-            source = (t // 3) * 4 + y
-            for i, half in ((0, h), (1, 1 - h)):
-                at = i * SLOT + (t % 3) * OWN
-                join(w_ref, t, half, y, w_mine[source, at : at + OWN, 0:C], w_theirs[source, at : at + OWN, 0:C], c)
-    leave[0].start()
-    for one in arrive[2:]:
-        one.wait()
+            at = t * OWN
+            join(w_ref, t, h, y, own_m[y, at : at + OWN, 0:C], own_t[y, at : at + OWN, 0:C], c)
+            x, at = t // 3, y * SLOT + (t % 3) * OWN
+            join(w_ref, t, 1 - h, y, oth_m[x, at : at + OWN, 0:C], oth_t[x, at : at + OWN, 0:C], c)
+    leave = copies(sems, (w_ref, w_h))
     spatial = conv(windows, w_ref, bias[...])
     sig = jax.nn.sigmoid(spatial)
     hidden = (spatial * sig).astype(BF)
     hidden_ref[...] = hidden
     slope_ref[...] = sig * (1.0 + spatial * (1.0 - sig))
-    leave[1].start()
-    leave[2].start()
     before, after = sides(place, cot_prev[...], cot_next[...], far[...])
     grads = [dot_tn(hidden, other) for other in (after, cot[...].astype(BF), before)]
     pad = jnp.zeros((4, C), F32)
@@ -197,18 +183,6 @@
     grad_ref[...] = acc
 
 
-def far_kernel(place, w_h, far_h, bias, hidden_h, w_ref, far, hidden_ref, windows, sems):
-    arrive = copies(sems, (far_h, far), (w_h.at[0:SPACE], w_ref))
-    arrive[0].wait()
-    fill_windows(windows, far[...].astype(F32))
-    arrive[1].wait()
-    spatial = conv(windows, w_ref, bias[...])
-    hidden = (spatial * jax.nn.sigmoid(spatial)).astype(BF)
-    hidden_ref[...] = jnp.where(place[3] == 1, hidden, jnp.zeros_like(hidden))
-    for one in copies(sems, (hidden_ref, hidden_h)):
-        one.wait()
-
-
 def output_kernel(
     place, w_h, video_h, hidden_h, prev_h, after_h, far_h, out_ref,
     w_ref, video, hidden, prev, after, far, sems,
@@ -227,12 +201,11 @@
 FRAME_F = (ROWS, C), F32
 WINDOWS = (3, ROWS + 2 * W, C), BF
 WEIGHTS = (TAPS, 2, HALF, C), BF
-PIECES = (16, 2 * SLOT, WIDE), BF
 SUMS = (4, 4, 2, 16, C), F32
 SHARE = (16, C), F32
 
 
-def kernel_call(body, ins, outs, scratch, copied, micros, name):
+def kernel_call(body, ins, outs, scratch, copied, micros, name, limit=60):
     spaces = {"s": pltpu.SMEM, "v": pltpu.VMEM, "h": pltpu.HBM}
     specs = [[pl.BlockSpec(memory_space=spaces[o[-1]]) for o in group] for group in (ins, outs)]
     return pl.pallas_call(
@@ -241,7 +214,7 @@
         in_specs=specs[0],
         out_specs=tuple(specs[1]),
         scratch_shapes=[pltpu.VMEM(*o) for o in scratch] + [pltpu.SemaphoreType.DMA((copied,))] * (copied > 0),
-        compiler_params=pltpu.CompilerParams(vmem_limit_bytes=(60 if copied else 8) * 1024 * 1024),
+        compiler_params=pltpu.CompilerParams(vmem_limit_bytes=limit * 1024 * 1024),
         cost_estimate=pl.CostEstimate(flops=int(micros * 1.0e9), bytes_accessed=1_000_000, transcendentals=0),
         name=name,
     )(*(a for a, _ in ins))
@@ -257,46 +230,42 @@
     cot_f = cotangent.reshape(ROWS, C)
     bias = spatial_b.reshape(1, C)
 
-    cot_b, video_b = cot_f.astype(BF), video_f.astype(BF)
-    far = lax.ppermute(cot_b, TM, FRAMES_FAR)
-    video_far = lax.ppermute(video_b, TM, FRAMES_FAR)
+    cot_b = cot_f.astype(BF)
     w = jnp.concatenate([spatial_w, temporal_w.astype(BF)], axis=0)
     quarter = lax.dynamic_slice_in_dim(w, 3 * x, 3, 0).reshape(3 * OWN, C)
-    quarter = jnp.pad(quarter, ((0, SLOT - 3 * OWN), (0, WIDE - C)))
-    other = across(quarter)
+    other = across(jnp.pad(quarter, ((0, SLOT - 3 * OWN), (0, WIDE - C))))
+    w = jnp.pad(w.reshape(TAPS * OWN, C), ((0, 0), (0, WIDE - C)))
+    other, cot_b, w = tie((other, cot_b, w))
     cot_next = lax.ppermute(cot_b, TM, FRAMES_DOWN)
     cot_prev = lax.ppermute(cot_b, TM, FRAMES_UP)
-    other, cot_next, cot_prev = tie((other, cot_next, cot_prev))
-    w_mine = to_all(jnp.concatenate([quarter, other], axis=0), PLANE)
+    far = lax.ppermute(cot_b, TM, FRAMES_FAR)
+    own_m = lax.all_gather(jnp.concatenate([w, other], axis=0), "y")
+    oth_m = own_m[:, TAPS * OWN :].reshape(4 * SLOT, WIDE)
+    oth_m, cot_next, cot_prev, far = tie((oth_m, cot_next, cot_prev, far))
+    oth_m = lax.all_gather(oth_m, "x")
     (windows,) = kernel_call(prepare_kernel, [(video_f, "v")], [(WINDOWS, "h")], [WINDOWS], 1, 0.01, "prepare")
-    w_mine, windows, far, video_far = tie((w_mine, windows, far, video_far))
-    w_theirs = core_swap(w_mine)
+    oth_m, own_m, windows = tie((oth_m, own_m, windows))
+    own_t, oth_t = core_swap(own_m), core_swap(oth_m)
 
     w_all, hidden, slope, mine, theirs = kernel_call(
         forward_kernel,
         [
-            (place, "s"), (w_mine, "h"), (w_theirs, "h"), (windows, "h"), (bias, "v"),
-            (cot_f, "h"), (cot_prev, "h"), (cot_next, "h"), (far, "h"),
+            (place, "s"), (own_m, "v"), (own_t, "v"), (oth_m, "v"), (oth_t, "v"), (windows, "v"), (bias, "v"),
+            (cot_f, "v"), (cot_prev, "v"), (cot_next, "v"), (far, "v"),
         ],
-        [(WEIGHTS, "h"), (FRAME_B, "h"), (FRAME_F, "h"), (SUMS, "v"), (SUMS, "v")],
-        [PIECES, PIECES, WINDOWS, FRAME_F, FRAME_B, FRAME_B, FRAME_B, WEIGHTS, FRAME_B, FRAME_F],
-        10, 6, "forward",
-    )
-
+        [(WEIGHTS, "h"), (FRAME_B, "v"), (FRAME_F, "v"), (SUMS, "v"), (SUMS, "v")],
+        [WEIGHTS], 1, 0.01, "forward", LIMIT,
+    )
     part = mine + core_swap(theirs)
     part = lax.all_to_all(part.reshape(16, 2, 16, C), PLANE, 0, 0, tiled=True)
     prev = lax.ppermute(hidden, TM, FRAMES_UP)
     after = lax.ppermute(hidden, TM, FRAMES_DOWN)
-    (hidden_far,) = kernel_call(
-        far_kernel, [(place, "s"), (w_all, "h"), (video_far, "h"), (bias, "v")], [(FRAME_B, "h")],
-        [((SPACE, 2, HALF, C), BF), FRAME_B, FRAME_B, WINDOWS], 2, 5, "far",
-    )
-    part, prev, after, hidden_far = tie((part, prev, after, hidden_far))
+    hidden_far = lax.ppermute(hidden, TM, FRAMES_FAR)
     keep, give = kernel_call(
-        split_kernel, [(place, "s"), (part, "v")], [(SHARE, "v"), (SHARE, "v")], [], 0, 0.01, "split",
+        split_kernel, [(place, "s"), (part, "v")], [(SHARE, "v"), (SHARE, "v")], [], 0, 1000, "split", 8,
     )
     part = keep + across(give)
-    part, slope = tie((part, slope))
+    part, slope, prev, after, hidden_far = tie((part, slope, prev, after, hidden_far))
     part = to_all(part, Z_LO)
     (grad_video,) = kernel_call(
         backward_kernel,

time: 156 us -> 151 us (0.968)
  blocking collectives: 0 us -> 32.8 us
  waiting for transfers between devices: 55.6 us -> 25.5 us
  Pallas kernels: 29 us -> 22.5 us
  local copies, waits for them, and re-layouts: 4.79 us -> 3.1 us
    all_gather x0 -> x2, blocking collectives: none -> 32.8 us  [the longest x1 17 us: on_device(): oth_m = lax.all_gather(oth_m, 'x')]
    all_to_all x3 -> x2, waiting for transfers between devices: 38 us -> 7.02 us  [to_all(): lax.all_to_all(jnp.broadcast_to(a[None], (n, *a.shape)), axes, 0, 0, tile...]
    pallas_call x6 -> x5, Pallas kernels: 29 us -> 22.5 us  [kernel_call(): pl.pallas_call(body, out_shape=tuple((jax.ShapeDtypeStruct(*o[0]) for o i...]
    all_to_all x1, waiting for transfers between devices: 0.01 us -> 5.79 us  [on_device(): part = lax.all_to_all(part.reshape(16, 2, 16, C), PLANE, 0, 0, tiled=True)]
    ppermute x2, waiting for transfers between devices: 10.7 us -> 6.37 us  [across(): return lax.ppermute(a, ('m', 'k', 'h'), ACROSS)]
    ppermute x2 -> x3, starting transfers between devices: 3.94 us -> 6.6 us  [core_swap(): return lax.ppermute(a, 'c', [(0, 1), (1, 0)])]
    all_to_all x3 -> x2, starting transfers between devices: 19.7 us -> 17.1 us  [to_all(): lax.all_to_all(jnp.broadcast_to(a[None], (n, *a.shape)), axes, 0, 0, tile...]
    ppermute x1, waiting for transfers between devices: 0.01 us -> 2.49 us  [on_device(): cot_next = lax.ppermute(cot_b, TM, FRAMES_DOWN)]
  transfers between devices with their start and end apart: 14 -> 14, of which waited for: 9 -> 8; matrix products, arithmetic and copies ran while one was open for 2% -> 2% of each run, Pallas kernels for 13% -> 10%
where the time goes in v5:
time: 151 us; the launch traced here: 150 us
  starting transfers between devices  59.9 us (40%)
  blocking collectives  32.8 us (22%)
  waiting for transfers between devices  25.5 us (17%)
  Pallas kernels  22.5 us (15%)
  other arithmetic  5.02 us (3%)
  local copies, waits for them, and re-layouts  3.1 us (2%)
    pallas_call x5, Pallas kernels, kernel_call(): pl.pallas_call(body, out_shape=tuple((jax.ShapeDtypeStruct(*o[0]) for o i...  22.5 us
    all_to_all x2, starting transfers between devices, to_all(): lax.all_to_all(jnp.broadcast_to(a[None], (n, *a.shape)), axes, 0, 0, tile...  17.1 us
    all_gather x1, blocking collectives, on_device(): oth_m = lax.all_gather(oth_m, 'x')  17 us
    ppermute x2, starting transfers between devices, across(): return lax.ppermute(a, ('m', 'k', 'h'), ACROSS)  16 us
    all_gather x1, blocking collectives, on_device(): own_m = lax.all_gather(jnp.concatenate([w, other], axis=0), 'y')  15.8 us
    all_to_all x1, starting transfers between devices, on_device(): part = lax.all_to_all(part.reshape(16, 2, 16, C), PLANE, 0, 0, tiled=True)  7.29 us
    all_to_all x2, waiting for transfers between devices, to_all(): lax.all_to_all(jnp.broadcast_to(a[None], (n, *a.shape)), axes, 0, 0, tile...  7.02 us
    ppermute x3, starting transfers between devices, core_swap(): return lax.ppermute(a, 'c', [(0, 1), (1, 0)])  6.6 us
  transfers between devices with their start and end apart: 14, of which 8 were waited for; matrix products, arithmetic and copies ran while one was open for 2% of the time, Pallas kernels for 10%

profile of v5, /device:TPU:8, one launch (start us, length us, event | category | flops | bytes accessed | tf_op | source)
XLA Modules:
  0.0 149.8 jit_solution(7622509347088137099)
XLA Ops:
  0.6 0.9 convert_element_type.11
  1.5 0.8 fusion
  2.4 12.7 %collective-permute-start = (bf16[64,384]{1,0:T(8,128)(2,1)S(1)}, bf16[64,384]{1,0:T(8,128)(2,1)S(1)}, u32[]{:S(2)}, u32[]{:S(2)}) collective-permute-start(bf16[64,384]{1,0:T(8,128)(2,1)S(1)} %pad.8), channel_id=1, source_target_pairs={{0,72},{16,88},{32,104},{48,120},{64,8},{80,24},{96,40},{112,56},{... | collective-permute-start | bytes 147464 | tf_op jit(solution)/shard_map/ppermute | solution.py:44
  15.2 1.2 bitcast_convert_fusion
  16.4 1.0 pad_maximum_fusion
  17.4 2.5 %prepare.1.windows = bf16[3,576,320]{2,1,0:T(8,128)(2,1)} custom-call(f32[512,320]{1,0:T(8,128)} %bitcast.18), custom_call_target="tpu_custom_call" | custom-call | flops 10000000 | bytes 1000000 | tf_op jit(solution)/shard_map/prepare/pallas_call | solution.py:211
  20.7 2.9 %collective-permute-start.2 = (bf16[512,320]{1,0:T(8,128)(2,1)S(1)}, bf16[512,320]{1,0:T(8,128)(2,1)S(1)}, u32[]{:S(2)}, u32[]{:S(2)}) collective-permute-start(bf16[512,320]{1,0:T(8,128)(2,1)S(1)} %bitcast_convert_fusion), channel_id=1, source_target_pairs={{0,16},{16,32},{32,48},{48,64},{64,80},{80,96},{96,112},{128,144},... | collective-permute-start | bytes 983048 | tf_op jit(solution)/shard_map/ppermute | solution.py:240
  23.6 1.3 collective-permute-start.1
  24.9 15.8 %all-gather = bf16[1216,384]{1,0:T(8,128)(2,1)} all-gather(bf16[304,384]{1,0:T(8,128)(2,1)S(1)} %pad_maximum_fusion.1), channel_id=2, replica_groups=mesh['x'=4,'m'=2,'k'=4,'h'=2,'y'=4,'c'=2] {'y'}, dimensions={0}, use_global_device_ids=true | all-gather | bytes 1167360 | tf_op jit(solution)/shard_map/all_gather | solution.py:242
  40.7 0.9 slice.8
  41.7 2.5 %collective-permute-done.1.cot_next.next_h = bf16[512,320]{1,0:T(8,128)(2,1)S(1)} collective-permute-done((bf16[512,320]{1,0:T(8,128)(2,1)S(1)}, bf16[512,320]{1,0:T(8,128)(2,1)S(1)}, u32[]{:S(2)}, u32[]{:S(2)}) %collective-permute-start.1) | collective-permute-done | bytes 327712 | tf_op jit(solution)/shard_map/ppermute | solution.py:239
  44.2 17.0 %all-gather.1 = bf16[1024,384]{1,0:T(8,128)(2,1)S(1)} all-gather(bf16[256,384]{1,0:T(8,128)(2,1)S(1)} %bitcast.20), channel_id=3, replica_groups=mesh['x'=4,'m'=2,'k'=4,'h'=2,'y'=4,'c'=2] {'x'}, dimensions={0}, use_global_device_ids=true | all-gather | bytes 983040 | tf_op jit(solution)/shard_map/all_gather | solution.py:245
  61.2 1.9 %collective-permute-start.4 = (bf16[4,304,384]{2,1,0:T(8,128)(2,1)}, bf16[4,304,384]{2,1,0:T(8,128)(2,1)}, u32[]{:S(2)}, u32[]{:S(2)}) collective-permute-start(bf16[4,304,384]{2,1,0:T(8,128)(2,1)} %bitcast.5.own_m), channel_id=1, source_target_pairs={{0,1},{1,0},{2,3},{3,2},{4,5},{5,4},{6,7},{7,6},{8,9},{9,8},{10,11... | collective-permute-start | bytes 2801672 | tf_op jit(solution)/shard_map/ppermute | solution.py:48
  63.2 2.4 %collective-permute-start.5 = (bf16[4,256,384]{2,1,0:T(8,128)(2,1)S(1)}, bf16[4,256,384]{2,1,0:T(8,128)(2,1)S(1)}, u32[]{:S(2)}, u32[]{:S(2)}) collective-permute-start(bf16[4,256,384]{2,1,0:T(8,128)(2,1)S(1)} %bitcast.14), channel_id=1, source_target_pairs={{0,1},{1,0},{2,3},{3,2},{4,5},{5,4},{6,7},{7,6},{8,9},{9,8},{10,11... | collective-permute-start | bytes 2359304 | tf_op jit(solution)/shard_map/ppermute | solution.py:48
  65.7 1.8 %collective-permute-done.5.oth_t = bf16[4,256,384]{2,1,0:T(8,128)(2,1)S(1)} collective-permute-done((bf16[4,256,384]{2,1,0:T(8,128)(2,1)S(1)}, bf16[4,256,384]{2,1,0:T(8,128)(2,1)S(1)}, u32[]{:S(2)}, u32[]{:S(2)}) %collective-permute-start.5) | collective-permute-done | bytes 786464 | tf_op jit(solution)/shard_map/ppermute | solution.py:48
  67.5 7.7 %forward.1 = (bf16[12,2,160,320]{3,2,1,0:T(8,128)(2,1)}, bf16[512,320]{1,0:T(8,128)(2,1)}, f32[512,320]{1,0:T(8,128)S(1)}, f32[4,4,2,16,320]{4,3,2,1,0:T(8,128)S(1)}, f32[4,4,2,16,320]{4,3,2,1,0:T(8,128)S(1)}) custom-call(s32[4]{0:T(128)S(1)} %pad_add_fusion.place, bf16[4,304,384]{2,1,0:T(8,128)(2,1)} %bitcast.5.own_m, ...), custom_call_target="tpu_custom_call" | custom-call | flops 10000000 | bytes 1000000 | tf_op jit(solution)/shard_map/forward/pallas_call | solution.py:211
  75.2 2.3 %collective-permute-start.6 = (f32[4,4,2,16,320]{4,3,2,1,0:T(8,128)S(1)}, f32[4,4,2,16,320]{4,3,2,1,0:T(8,128)S(1)}, u32[]{:S(2)}, u32[]{:S(2)}) collective-permute-start(f32[4,4,2,16,320]{4,3,2,1,0:T(8,128)S(1)} %get-tuple-element.41), channel_id=1, source_target_pairs={{0,1},{1,0},{2,3},{3,2},{4,5},{5,4},{6,7},{7,6},{8,9},{9,8},{10,11... | collective-permute-start | bytes 1966088 | tf_op jit(solution)/shard_map/ppermute | solution.py:48
  77.5 1.9 %collective-permute-done.6 = f32[4,4,2,16,320]{4,3,2,1,0:T(8,128)S(1)} collective-permute-done((f32[4,4,2,16,320]{4,3,2,1,0:T(8,128)S(1)}, f32[4,4,2,16,320]{4,3,2,1,0:T(8,128)S(1)}, u32[]{:S(2)}, u32[]{:S(2)}) %collective-permute-start.6) | collective-permute-done | bytes 655392 | tf_op jit(solution)/shard_map/ppermute | solution.py:48
  79.4 1.0 add.18
  80.3 7.3 %all-to-all-start = ((f32[16,2,16,320]{3,2,1,0:T(8,128)}), f32[16,2,16,320]{3,2,1,0:T(8,128)S(1)}, u32[]{:S(2)}, u32[]{:S(2)}) async-start(f32[16,2,16,320]{3,2,1,0:T(8,128)} %bitcast.9), calls=%async_computation | async-start | bytes 1572864 | tf_op jit(solution)/shard_map/all_to_all | solution.py:260
  87.6 1.4 collective-permute-start.10
  89.0 1.3 collective-permute-start.9
  90.3 5.3 %collective-permute-start.8 = (bf16[512,320]{1,0:T(8,128)(2,1)}, bf16[512,320]{1,0:T(8,128)(2,1)}, u32[]{:S(2)}, u32[]{:S(2)}) collective-permute-start(bf16[512,320]{1,0:T(8,128)(2,1)} %get-tuple-element.45.hidden_h), channel_id=1, source_target_pairs={{0,16},{16,32},{32,48},{48,64},{64,80},{80,96},{96,112},{128,144},... | collective-permute-start | bytes 983048 | tf_op jit(solution)/shard_map/ppermute | solution.py:261
  95.6 5.8 %all-to-all-done.parts = f32[16,2,16,320]{3,2,1,0:T(8,128)S(1)} async-done(((f32[16,2,16,320]{3,2,1,0:T(8,128)}), f32[16,2,16,320]{3,2,1,0:T(8,128)S(1)}, u32[]{:S(2)}, u32[]{:S(2)}) %all-to-all-start) | async-done | bytes 655392 | tf_op jit(solution)/shard_map/all_to_all | solution.py:260
  102.0 3.3 %collective-permute-start.7 = (f32[16,320]{1,0:T(8,128)S(1)}, f32[16,320]{1,0:T(8,128)S(1)}, u32[]{:S(2)}, u32[]{:S(2)}) collective-permute-start(f32[16,320]{1,0:T(8,128)S(1)} %get-tuple-element.43), channel_id=1, source_target_pairs={{0,72},{16,88},{32,104},{48,120},{64,8},{80,24},{96,40},{112,56},{... | collective-permute-start | bytes 61448 | tf_op jit(solution)/shard_map/ppermute | solution.py:44
  105.3 6.4 %collective-permute-done.7 = f32[16,320]{1,0:T(8,128)S(1)} collective-permute-done((f32[16,320]{1,0:T(8,128)S(1)}, f32[16,320]{1,0:T(8,128)S(1)}, u32[]{:S(2)}, u32[]{:S(2)}) %collective-permute-start.7) | collective-permute-done | bytes 20512 | tf_op jit(solution)/shard_map/ppermute | solution.py:44
  112.5 8.3 %all-to-all-start.1 = ((f32[8,16,320]{2,1,0:T(8,128)}), f32[8,16,320]{2,1,0:T(8,128)S(1)}, u32[]{:S(2)}, u32[]{:S(2)}) async-start(f32[8,16,320]{2,1,0:T(8,128)} %broadcast_in_dim.4), calls=%async_computation.1 | async-start | bytes 393216 | tf_op jit(solution)/shard_map/all_to_all | solution.py:53
  120.7 7.5 %backward.1 = f32[512,320]{1,0:T(8,128)} custom-call(s32[4]{0:T(128)} %copy-done.3, bf16[12,2,160,320]{3,2,1,0:T(8,128)(2,1)} %get-tuple-element.39.w_h, f32[512,320]{1,0:T(8,128)} %copy-done.4, f32[512,320]{1,0:T(8,128)} %bitcast.17, bf16[512,320]{1,0:T(8,128)(2,1)} %copy-done.1, bf16[512,320]{1,0:T(8,128)(2,1)} %copy-done.2, bf16[512,320]{1,0:T(8,128)(2,1)} %copy-done), custom_call_target="tpu_custom_call" | custom-call | flops 5000000000 | bytes 1000000 | tf_op jit(solution)/shard_map/backward/pallas_call | solution.py:211
  128.3 5.5 %all-to-all-done.1 = f32[8,16,320]{2,1,0:T(8,128)S(1)} async-done(((f32[8,16,320]{2,1,0:T(8,128)}), f32[8,16,320]{2,1,0:T(8,128)S(1)}, u32[]{:S(2)}, u32[]{:S(2)}) %all-to-all-start.1) | async-done | bytes 163872 | tf_op jit(solution)/shard_map/all_to_all | solution.py:53
  134.4 8.8 %all-to-all-start.2 = ((f32[4,16,320]{2,1,0:T(8,128)}), f32[4,16,320]{2,1,0:T(8,128)S(1)}, u32[]{:S(2)}, u32[]{:S(2)}) async-start(f32[4,16,320]{2,1,0:T(8,128)} %broadcast_in_dim.5), calls=%async_computation.2 | async-start | bytes 196608 | tf_op jit(solution)/shard_map/all_to_all | solution.py:53
  143.3 4.3 %output.1 = f32[512,320]{1,0:T(8,128)} custom-call(s32[4]{0:T(128)} %copy-done.3, bf16[12,2,160,320]{3,2,1,0:T(8,128)(2,1)} %get-tuple-element.39.w_h, f32[512,320]{1,0:T(8,128)} %bitcast.19, bf16[512,320]{1,0:T(8,128)(2,1)} %get-tuple-element.45.hidden_h, bf16[512,320]{1,0:T(8,128)(2,1)} %collective-permute-done.8.prev_h, ...), custom_call_target="tpu_custom_call" | custom-call | flops 3000000000 | bytes 1000000 | tf_op jit(solution)/shard_map/output/pallas_call | solution.py:211
  147.6 1.5 %all-to-all-done.2 = f32[4,16,320]{2,1,0:T(8,128)S(1)} async-done(((f32[4,16,320]{2,1,0:T(8,128)}), f32[4,16,320]{2,1,0:T(8,128)S(1)}, u32[]{:S(2)}, u32[]{:S(2)}) %all-to-all-start.2) | async-done | bytes 81952 | tf_op jit(solution)/shard_map/all_to_all | solution.py:53
  (34 shorter events, 3.7 us)
Async XLA Ops:
  2.4 17.5 %collective-permute-start = (bf16[64,384]{1,0:T(8,128)(2,1)S(1)}, bf16[64,384]{1,0:T(8,128)(2,1)S(1)}, u32[]{:S(2)}, u32[]{:S(2)}) collective-permute-start(bf16[64,384]{1,0:T(8,128)(2,1)S(1)} %pad.8), channel_id=1, source_target_pairs={{0,72},{16,88},{32,104},{48,120},{64,8},{80,24},{96,40},{112,56},{... | collective-permute-start | bytes 147464 | tf_op jit(solution)/shard_map/ppermute | solution.py:44
  17.3 48.3 %copy-start.5 = (f32[320]{0:T(512)S(1)}, f32[320]{0:T(512)}, u32[]{:S(2)}) copy-start(f32[320]{0:T(512)} %param.7) | copy-start | bytes 3844
  20.0 21.7 %collective-permute-start.3 = (bf16[512,320]{1,0:T(8,128)(2,1)S(1)}, bf16[512,320]{1,0:T(8,128)(2,1)S(1)}, u32[]{:S(2)}, u32[]{:S(2)}) collective-permute-start(bf16[512,320]{1,0:T(8,128)(2,1)S(1)} %bitcast_convert_fusion), channel_id=1, source_target_pairs={{112,128},{128,112},{240,256},{256,240},{368,384},{384,368},{113,1... | collective-permute-start | bytes 983048 | tf_op jit(solution)/shard_map/ppermute | solution.py:241
  20.7 21.1 %collective-permute-start.2 = (bf16[512,320]{1,0:T(8,128)(2,1)S(1)}, bf16[512,320]{1,0:T(8,128)(2,1)S(1)}, u32[]{:S(2)}, u32[]{:S(2)}) collective-permute-start(bf16[512,320]{1,0:T(8,128)(2,1)S(1)} %bitcast_convert_fusion), channel_id=1, source_target_pairs={{0,16},{16,32},{32,48},{48,64},{64,80},{80,96},{96,112},{128,144},... | collective-permute-start | bytes 983048 | tf_op jit(solution)/shard_map/ppermute | solution.py:240
  23.6 20.6 %collective-permute-start.1 = (bf16[512,320]{1,0:T(8,128)(2,1)S(1)}, bf16[512,320]{1,0:T(8,128)(2,1)S(1)}, u32[]{:S(2)}, u32[]{:S(2)}) collective-permute-start(bf16[512,320]{1,0:T(8,128)(2,1)S(1)} %bitcast_convert_fusion), channel_id=1, source_target_pairs={{16,0},{32,16},{48,32},{64,48},{80,64},{96,80},{112,96},{144,128},... | collective-permute-start | bytes 983048 | tf_op jit(solution)/shard_map/ppermute | solution.py:239
  41.7 33.4 %copy-start = (bf16[512,320]{1,0:T(8,128)(2,1)}, bf16[512,320]{1,0:T(8,128)(2,1)S(1)}, u32[]{:S(2)}) copy-start(bf16[512,320]{1,0:T(8,128)(2,1)S(1)} %collective-permute-done.3.far.far_h) | copy-start | bytes 983044
  41.7 33.4 %copy-start.1 = (bf16[512,320]{1,0:T(8,128)(2,1)}, bf16[512,320]{1,0:T(8,128)(2,1)S(1)}, u32[]{:S(2)}) copy-start(bf16[512,320]{1,0:T(8,128)(2,1)S(1)} %collective-permute-done.2.cot_prev.prev_h) | copy-start | bytes 983044
  44.2 30.9 %copy-start.2 = (bf16[512,320]{1,0:T(8,128)(2,1)}, bf16[512,320]{1,0:T(8,128)(2,1)S(1)}, u32[]{:S(2)}) copy-start(bf16[512,320]{1,0:T(8,128)(2,1)S(1)} %collective-permute-done.1.cot_next.next_h) | copy-start | bytes 983044
  61.2 6.2 %collective-permute-start.4 = (bf16[4,304,384]{2,1,0:T(8,128)(2,1)}, bf16[4,304,384]{2,1,0:T(8,128)(2,1)}, u32[]{:S(2)}, u32[]{:S(2)}) collective-permute-start(bf16[4,304,384]{2,1,0:T(8,128)(2,1)} %bitcast.5.own_m), channel_id=1, source_target_pairs={{0,1},{1,0},{2,3},{3,2},{4,5},{5,4},{6,7},{7,6},{8,9},{9,8},{10,11... | collective-permute-start | bytes 2801672 | tf_op jit(solution)/shard_map/ppermute | solution.py:48
  63.2 4.3 %collective-permute-start.5 = (bf16[4,256,384]{2,1,0:T(8,128)(2,1)S(1)}, bf16[4,256,384]{2,1,0:T(8,128)(2,1)S(1)}, u32[]{:S(2)}, u32[]{:S(2)}) collective-permute-start(bf16[4,256,384]{2,1,0:T(8,128)(2,1)S(1)} %bitcast.14), channel_id=1, source_target_pairs={{0,1},{1,0},{2,3},{3,2},{4,5},{5,4},{6,7},{7,6},{8,9},{9,8},{10,11... | collective-permute-start | bytes 2359304 | tf_op jit(solution)/shard_map/ppermute | solution.py:48
  65.7 35.7 %copy-start.3 = (s32[4]{0:T(128)}, s32[4]{0:T(128)S(1)}, u32[]{:S(2)}) copy-start(s32[4]{0:T(128)S(1)} %pad_add_fusion.place) | copy-start | bytes 52
  75.2 5.2 %copy-start.4 = (f32[512,320]{1,0:T(8,128)}, f32[512,320]{1,0:T(8,128)S(1)}, u32[]{:S(2)}) copy-start(f32[512,320]{1,0:T(8,128)S(1)} %get-tuple-element.47.slope_h) | copy-start | bytes 1966084
  75.2 4.2 %collective-permute-start.6 = (f32[4,4,2,16,320]{4,3,2,1,0:T(8,128)S(1)}, f32[4,4,2,16,320]{4,3,2,1,0:T(8,128)S(1)}, u32[]{:S(2)}, u32[]{:S(2)}) collective-permute-start(f32[4,4,2,16,320]{4,3,2,1,0:T(8,128)S(1)} %get-tuple-element.41), channel_id=1, source_target_pairs={{0,1},{1,0},{2,3},{3,2},{4,5},{5,4},{6,7},{7,6},{8,9},{9,8},{10,11... | collective-permute-start | bytes 1966088 | tf_op jit(solution)/shard_map/ppermute | solution.py:48
  80.3 21.1 %all-to-all-start = ((f32[16,2,16,320]{3,2,1,0:T(8,128)}), f32[16,2,16,320]{3,2,1,0:T(8,128)S(1)}, u32[]{:S(2)}, u32[]{:S(2)}) async-start(f32[16,2,16,320]{3,2,1,0:T(8,128)} %bitcast.9), calls=%async_computation | async-start | bytes 1572864 | tf_op jit(solution)/shard_map/all_to_all | solution.py:260
  87.6 24.0 %collective-permute-start.10 = (bf16[512,320]{1,0:T(8,128)(2,1)}, bf16[512,320]{1,0:T(8,128)(2,1)}, u32[]{:S(2)}, u32[]{:S(2)}) collective-permute-start(bf16[512,320]{1,0:T(8,128)(2,1)} %get-tuple-element.45.hidden_h), channel_id=1, source_target_pairs={{112,128},{128,112},{240,256},{256,240},{368,384},{384,368},{113,1... | collective-permute-start | bytes 983048 | tf_op jit(solution)/shard_map/ppermute | solution.py:263
  89.0 22.8 %collective-permute-start.9 = (bf16[512,320]{1,0:T(8,128)(2,1)}, bf16[512,320]{1,0:T(8,128)(2,1)}, u32[]{:S(2)}, u32[]{:S(2)}) collective-permute-start(bf16[512,320]{1,0:T(8,128)(2,1)} %get-tuple-element.45.hidden_h), channel_id=1, source_target_pairs={{16,0},{32,16},{48,32},{64,48},{80,64},{96,80},{112,96},{144,128},... | collective-permute-start | bytes 983048 | tf_op jit(solution)/shard_map/ppermute | solution.py:262
  90.3 21.5 %collective-permute-start.8 = (bf16[512,320]{1,0:T(8,128)(2,1)}, bf16[512,320]{1,0:T(8,128)(2,1)}, u32[]{:S(2)}, u32[]{:S(2)}) collective-permute-start(bf16[512,320]{1,0:T(8,128)(2,1)} %get-tuple-element.45.hidden_h), channel_id=1, source_target_pairs={{0,16},{16,32},{32,48},{48,64},{64,80},{80,96},{96,112},{128,144},... | collective-permute-start | bytes 983048 | tf_op jit(solution)/shard_map/ppermute | solution.py:261
  102.0 9.6 %collective-permute-start.7 = (f32[16,320]{1,0:T(8,128)S(1)}, f32[16,320]{1,0:T(8,128)S(1)}, u32[]{:S(2)}, u32[]{:S(2)}) collective-permute-start(f32[16,320]{1,0:T(8,128)S(1)} %get-tuple-element.43), channel_id=1, source_target_pairs={{0,72},{16,88},{32,104},{48,120},{64,8},{80,24},{96,40},{112,56},{... | collective-permute-start | bytes 61448 | tf_op jit(solution)/shard_map/ppermute | solution.py:44
  112.5 21.3 %all-to-all-start.1 = ((f32[8,16,320]{2,1,0:T(8,128)}), f32[8,16,320]{2,1,0:T(8,128)S(1)}, u32[]{:S(2)}, u32[]{:S(2)}) async-start(f32[8,16,320]{2,1,0:T(8,128)} %broadcast_in_dim.4), calls=%async_computation.1 | async-start | bytes 393216 | tf_op jit(solution)/shard_map/all_to_all | solution.py:53
  134.4 14.7 %all-to-all-start.2 = ((f32[4,16,320]{2,1,0:T(8,128)}), f32[4,16,320]{2,1,0:T(8,128)S(1)}, u32[]{:S(2)}, u32[]{:S(2)}) async-start(f32[4,16,320]{2,1,0:T(8,128)} %broadcast_in_dim.5), calls=%async_computation.2 | async-start | bytes 196608 | tf_op jit(solution)/shard_map/all_to_all | solution.py:53

commit v6 on v5

--- a/solution.py
+++ b/solution.py
@@ -108,10 +108,13 @@
     return started
 
 
-def prepare_kernel(video, out, windows, sems):
+def prepare_kernel(video, windows):
     fill_windows(windows, video[...])
-    for one in copies(sems, (windows, out)):
-        one.wait()
+
+
+def apart_kernel(gathered, out):
+    for y in range(4):
+        out[y * SLOT : (y + 1) * SLOT, :] = gathered[y, TAPS * OWN : TAPS * OWN + SLOT, :]
 
 
 def forward_kernel(
@@ -151,9 +154,9 @@
 
 def split_kernel(place, parts, keep_ref, give_ref):
     h = place[1]
-    total = parts[0]
+    total = parts[0].astype(F32)
     for i in range(1, 16):
-        total = total + parts[i]
+        total = total + parts[i].astype(F32)
     keep_ref[...] = jnp.where(h == 0, total[0], total[1])
     give_ref[...] = jnp.where(h == 0, total[1], total[0])
 
@@ -239,12 +242,14 @@
     cot_next = lax.ppermute(cot_b, TM, FRAMES_DOWN)
     cot_prev = lax.ppermute(cot_b, TM, FRAMES_UP)
     far = lax.ppermute(cot_b, TM, FRAMES_FAR)
-    own_m = lax.all_gather(jnp.concatenate([w, other], axis=0), "y")
-    oth_m = own_m[:, TAPS * OWN :].reshape(4 * SLOT, WIDE)
+    own_m = to_all(jnp.concatenate([w, other], axis=0), "y")
+    (oth_m,) = kernel_call(
+        apart_kernel, [(own_m, "v")], [(((4 * SLOT, WIDE), BF), "v")], [], 0, 1000, "apart", 8,
+    )
+    oth_m = lax.all_gather(oth_m, "x")
+    oth_m, own_m, video_w = tie((oth_m, own_m, video_f))
     oth_m, cot_next, cot_prev, far = tie((oth_m, cot_next, cot_prev, far))
-    oth_m = lax.all_gather(oth_m, "x")
-    (windows,) = kernel_call(prepare_kernel, [(video_f, "v")], [(WINDOWS, "h")], [WINDOWS], 1, 0.01, "prepare")
-    oth_m, own_m, windows = tie((oth_m, own_m, windows))
+    (windows,) = kernel_call(prepare_kernel, [(video_w, "v")], [(WINDOWS, "v")], [], 0, 0.01, "prepare", 16)
     own_t, oth_t = core_swap(own_m), core_swap(oth_m)
 
     w_all, hidden, slope, mine, theirs = kernel_call(
@@ -256,7 +261,7 @@
         [(WEIGHTS, "h"), (FRAME_B, "v"), (FRAME_F, "v"), (SUMS, "v"), (SUMS, "v")],
         [WEIGHTS], 1, 0.01, "forward", LIMIT,
     )
-    part = mine + core_swap(theirs)
+    part = (mine + core_swap(theirs)).astype(BF)
     part = lax.all_to_all(part.reshape(16, 2, 16, C), PLANE, 0, 0, tiled=True)
     prev = lax.ppermute(hidden, TM, FRAMES_UP)
     after = lax.ppermute(hidden, TM, FRAMES_DOWN)
@@ -264,25 +269,27 @@
     keep, give = kernel_call(
         split_kernel, [(place, "s"), (part, "v")], [(SHARE, "v"), (SHARE, "v")], [], 0, 1000, "split", 8,
     )
-    part = keep + across(give)
-    part, slope, prev, after, hidden_far = tie((part, slope, prev, after, hidden_far))
-    part = to_all(part, Z_LO)
+    give, slope = tie((give, slope))
+    other = across(give)
     (grad_video,) = kernel_call(
         backward_kernel,
         [(place, "s"), (w_all, "h"), (slope, "h"), (cot_f, "h"), (cot_prev, "h"), (cot_next, "h"), (far, "h")],
         [(FRAME_F, "v")],
         [WEIGHTS, FRAME_F, FRAME_F, FRAME_B, FRAME_B, FRAME_B, WINDOWS], 7, 5, "backward",
     )
-    part, grad_video = tie((part, grad_video))
-    part = jnp.sum(part, axis=0)
-    part, video_f = tie((part, video_f))
-    part = to_all(part, "x").reshape(4 * 16, C)
+    other, grad_video = tie((other, grad_video))
+    part = keep + other
+    part, video_f, prev, after, hidden_far = tie((part, video_f, prev, after, hidden_far))
+    part = to_all(part, Z_LO)
     (output,) = kernel_call(
         output_kernel,
         [(place, "s"), (w_all, "h"), (video_f, "h"), (hidden, "h"), (prev, "h"), (after, "h"), (hidden_far, "h")],
         [(FRAME_F, "v")],
         [((3, 2, HALF, C), BF), FRAME_F, FRAME_B, FRAME_B, FRAME_B, FRAME_B], 6, 3, "output",
     )
+    part, output = tie((part, output))
+    part = jnp.sum(part, axis=0)
+    part = to_all(part, "x").reshape(4 * 16, C)
     total_rows = ROWS * lax.axis_size(TM) * lax.axis_size(CLIP)
     grad_temporal = part[: 3 * OWN].reshape(3, OWN, C) * (1.0 / math.sqrt(total_rows))
     return output.reshape(shape), grad_video.reshape(shape), grad_temporal

time: 151 us -> 141 us (0.934)
  starting transfers between devices: 59.9 us -> 55.9 us
  waiting for transfers between devices: 25.5 us -> 21.8 us
  Pallas kernels: 22.5 us -> 20.1 us
    all_gather x1 -> x0, blocking collectives: 15.8 us -> none  [on_device(): own_m = lax.all_gather(jnp.concatenate([w, other], axis=0), 'y')]
    all_to_all x0 -> x1, blocking collectives: none -> 15.4 us  [to_all(): lax.all_to_all(jnp.broadcast_to(a[None], (n, *a.shape)), axes, 0, 0, tile...]
    all_to_all x2, waiting for transfers between devices: 7.02 us -> 14 us  [to_all(): lax.all_to_all(jnp.broadcast_to(a[None], (n, *a.shape)), axes, 0, 0, tile...]
    ppermute x2, waiting for transfers between devices: 6.37 us -> 1.18 us  [across(): return lax.ppermute(a, ('m', 'k', 'h'), ACROSS)]
    all_to_all x1, waiting for transfers between devices: 5.79 us -> 0.81 us  [on_device(): part = lax.all_to_all(part.reshape(16, 2, 16, C), PLANE, 0, 0, tiled=True)]
    ppermute x1, waiting for transfers between devices: 0.14 us -> 3.56 us  [on_device(): after = lax.ppermute(hidden, TM, FRAMES_DOWN)]
    all_to_all x2, starting transfers between devices: 17.1 us -> 13.9 us  [to_all(): lax.all_to_all(jnp.broadcast_to(a[None], (n, *a.shape)), axes, 0, 0, tile...]
    ppermute x1, waiting for transfers between devices: 2.49 us -> 0.01 us  [on_device(): cot_next = lax.ppermute(cot_b, TM, FRAMES_DOWN)]
  transfers between devices with their start and end apart: 14 -> 14, of which waited for: 8 -> 7; matrix products, arithmetic and copies ran while one was open for 2% -> 2% of each run, Pallas kernels for 10% -> 9%
where the time goes in v6:
time: 141 us; the launch traced here: 140 us
  starting transfers between devices  55.9 us (40%)
  blocking collectives  32.1 us (23%)
  waiting for transfers between devices  21.8 us (15%)
  Pallas kernels  20.1 us (14%)
  other arithmetic  5.63 us (4%)
  local copies, waits for them, and re-layouts  3.59 us (3%)
    pallas_call x6, Pallas kernels, kernel_call(): pl.pallas_call(body, out_shape=tuple((jax.ShapeDtypeStruct(*o[0]) for o i...  20.1 us
    all_gather x1, blocking collectives, on_device(): oth_m = lax.all_gather(oth_m, 'x')  16.7 us
    ppermute x2, starting transfers between devices, across(): return lax.ppermute(a, ('m', 'k', 'h'), ACROSS)  16.4 us
    all_to_all x1, blocking collectives, to_all(): lax.all_to_all(jnp.broadcast_to(a[None], (n, *a.shape)), axes, 0, 0, tile...  15.4 us
    all_to_all x2, waiting for transfers between devices, to_all(): lax.all_to_all(jnp.broadcast_to(a[None], (n, *a.shape)), axes, 0, 0, tile...  14 us
    all_to_all x2, starting transfers between devices, to_all(): lax.all_to_all(jnp.broadcast_to(a[None], (n, *a.shape)), axes, 0, 0, tile...  13.9 us
    ppermute x3, starting transfers between devices, core_swap(): return lax.ppermute(a, 'c', [(0, 1), (1, 0)])  6.59 us
    all_to_all x1, starting transfers between devices, on_device(): part = lax.all_to_all(part.reshape(16, 2, 16, C), PLANE, 0, 0, tiled=True)  5.72 us
  transfers between devices with their start and end apart: 14, of which 7 were waited for; matrix products, arithmetic and copies ran while one was open for 2% of the time, Pallas kernels for 9%

profile of v6, /device:TPU:8, one launch (start us, length us, event | category | flops | bytes accessed | tf_op | source)
XLA Modules:
  0.0 140.1 jit_solution(8975820833664418284)
XLA Ops:
  0.6 0.9 convert_element_type.14
  1.5 0.8 fusion
  2.4 12.7 %collective-permute-start = (bf16[64,384]{1,0:T(8,128)(2,1)S(1)}, bf16[64,384]{1,0:T(8,128)(2,1)S(1)}, u32[]{:S(2)}, u32[]{:S(2)}) collective-permute-start(bf16[64,384]{1,0:T(8,128)(2,1)S(1)} %pad.8), channel_id=1, source_target_pairs={{0,72},{16,88},{32,104},{48,120},{64,8},{80,24},{96,40},{112,56},{... | collective-permute-start | bytes 147464 | tf_op jit(solution)/shard_map/ppermute | solution.py:44
  15.2 1.9 %bitcast_convert_fusion = bf16[512,320]{1,0:T(8,128)(2,1)} fusion(f32[1,1,16,32,320]{4,3,2,1,0:T(8,128)} %param.9), kind=kLoop, calls=%fused_computation.8 | loop fusion | flops 163840 | bytes 983040 | tf_op jit(solution)/shard_map/convert_element_type | solution.py:236
  17.1 1.0 pad_maximum_fusion
  18.2 1.2 collective-permute-done
  19.4 1.0 broadcast_in_dim.6
  20.4 4.9 %all-to-all-start = ((bf16[4,304,384]{2,1,0:T(8,128)(2,1)}), bf16[4,304,384]{2,1,0:T(8,128)(2,1)S(1)}, u32[]{:S(2)}, u32[]{:S(2)}) async-start(bf16[4,304,384]{2,1,0:T(8,128)(2,1)} %broadcast_in_dim.6), calls=%async_computation | async-start | bytes 1867776 | tf_op jit(solution)/shard_map/all_to_all | solution.py:53
  25.3 1.4 %collective-permute-start.4 = (bf16[512,320]{1,0:T(8,128)(2,1)}, bf16[512,320]{1,0:T(8,128)(2,1)}, u32[]{:S(2)}, u32[]{:S(2)}) collective-permute-start(bf16[512,320]{1,0:T(8,128)(2,1)} %bitcast_convert_fusion), channel_id=1, source_target_pairs={{112,128},{128,112},{240,256},{256,240},{368,384},{384,368},{113,1... | collective-permute-start | bytes 983048 | tf_op jit(solution)/shard_map/ppermute | solution.py:244
  26.7 2.7 %collective-permute-start.3 = (bf16[512,320]{1,0:T(8,128)(2,1)}, bf16[512,320]{1,0:T(8,128)(2,1)}, u32[]{:S(2)}, u32[]{:S(2)}) collective-permute-start(bf16[512,320]{1,0:T(8,128)(2,1)} %bitcast_convert_fusion), channel_id=1, source_target_pairs={{0,16},{16,32},{32,48},{48,64},{64,80},{80,96},{96,112},{128,144},... | collective-permute-start | bytes 983048 | tf_op jit(solution)/shard_map/ppermute | solution.py:243
  29.4 1.3 collective-permute-start.2
  30.7 5.6 %all-to-all-done.gathered.own_m = bf16[4,304,384]{2,1,0:T(8,128)(2,1)S(1)} async-done(((bf16[4,304,384]{2,1,0:T(8,128)(2,1)}), bf16[4,304,384]{2,1,0:T(8,128)(2,1)S(1)}, u32[]{:S(2)}, u32[]{:S(2)}) %all-to-all-start) | async-done | bytes 933920 | tf_op jit(solution)/shard_map/all_to_all | solution.py:53
  36.3 16.7 %all-gather = bf16[1024,384]{1,0:T(8,128)(2,1)S(1)} all-gather(bf16[256,384]{1,0:T(8,128)(2,1)S(1)} %apart.1), channel_id=2, replica_groups=mesh['x'=4,'m'=2,'k'=4,'h'=2,'y'=4,'c'=2] {'x'}, dimensions={0}, use_global_device_ids=true | all-gather | bytes 983040 | tf_op jit(solution)/shard_map/all_gather | solution.py:249
  53.0 1.9 %collective-permute-start.1 = (bf16[4,304,384]{2,1,0:T(8,128)(2,1)S(1)}, bf16[4,304,384]{2,1,0:T(8,128)(2,1)}, u32[]{:S(2)}, u32[]{:S(2)}) collective-permute-start(bf16[4,304,384]{2,1,0:T(8,128)(2,1)S(1)} %all-to-all-done.gathered.own_m), channel_id=1, source_target_pairs={{0,1},{1,0},{2,3},{3,2},{4,5},{5,4},{6,7},{7,6},{8,9},{9,8},{10,11... | collective-permute-start | bytes 2801672 | tf_op jit(solution)/shard_map/ppermute | solution.py:48
  55.0 2.4 %collective-permute-start.5 = (bf16[4,256,384]{2,1,0:T(8,128)(2,1)S(1)}, bf16[4,256,384]{2,1,0:T(8,128)(2,1)S(1)}, u32[]{:S(2)}, u32[]{:S(2)}) collective-permute-start(bf16[4,256,384]{2,1,0:T(8,128)(2,1)S(1)} %bitcast.12), channel_id=1, source_target_pairs={{0,1},{1,0},{2,3},{3,2},{4,5},{5,4},{6,7},{7,6},{8,9},{9,8},{10,11... | collective-permute-start | bytes 2359304 | tf_op jit(solution)/shard_map/ppermute | solution.py:48
  57.9 1.1 copy-done
  59.3 7.4 %forward.1 = (bf16[12,2,160,320]{3,2,1,0:T(8,128)(2,1)}, bf16[512,320]{1,0:T(8,128)(2,1)}, f32[512,320]{1,0:T(8,128)S(1)}, f32[4,4,2,16,320]{4,3,2,1,0:T(8,128)S(1)}, f32[4,4,2,16,320]{4,3,2,1,0:T(8,128)S(1)}) custom-call(s32[4]{0:T(128)S(1)} %pad_add_fusion.place, bf16[4,304,384]{2,1,0:T(8,128)(2,1)} %copy-done.1, ...), custom_call_target="tpu_custom_call" | custom-call | flops 10000000 | bytes 1000000 | tf_op jit(solution)/shard_map/forward/pallas_call | solution.py:214
  66.8 2.3 %collective-permute-start.6 = (f32[4,4,2,16,320]{4,3,2,1,0:T(8,128)S(1)}, f32[4,4,2,16,320]{4,3,2,1,0:T(8,128)S(1)}, u32[]{:S(2)}, u32[]{:S(2)}) collective-permute-start(f32[4,4,2,16,320]{4,3,2,1,0:T(8,128)S(1)} %get-tuple-element.42), channel_id=1, source_target_pairs={{0,1},{1,0},{2,3},{3,2},{4,5},{5,4},{6,7},{7,6},{8,9},{9,8},{10,11... | collective-permute-start | bytes 1966088 | tf_op jit(solution)/shard_map/ppermute | solution.py:48
  69.0 1.9 %collective-permute-done.6 = f32[4,4,2,16,320]{4,3,2,1,0:T(8,128)S(1)} collective-permute-done((f32[4,4,2,16,320]{4,3,2,1,0:T(8,128)S(1)}, f32[4,4,2,16,320]{4,3,2,1,0:T(8,128)S(1)}, u32[]{:S(2)}, u32[]{:S(2)}) %collective-permute-start.6) | collective-permute-done | bytes 655392 | tf_op jit(solution)/shard_map/ppermute | solution.py:48
  70.9 0.8 add_convert_fusion
  71.8 5.7 %all-to-all-start.1 = ((bf16[16,2,16,320]{3,2,1,0:T(8,128)(2,1)}), bf16[16,2,16,320]{3,2,1,0:T(8,128)(2,1)S(1)}, u32[]{:S(2)}, u32[]{:S(2)}) async-start(bf16[16,2,16,320]{3,2,1,0:T(8,128)(2,1)} %bitcast.7), calls=%async_computation.1 | async-start | bytes 786432 | tf_op jit(solution)/shard_map/all_to_all | solution.py:265
  77.5 1.4 collective-permute-start.10
  78.9 1.3 collective-permute-start.9
  80.2 5.3 %collective-permute-start.8 = (bf16[512,320]{1,0:T(8,128)(2,1)}, bf16[512,320]{1,0:T(8,128)(2,1)}, u32[]{:S(2)}, u32[]{:S(2)}) collective-permute-start(bf16[512,320]{1,0:T(8,128)(2,1)} %get-tuple-element.50.hidden_h), channel_id=1, source_target_pairs={{0,16},{16,32},{32,48},{48,64},{64,80},{80,96},{96,112},{128,144},... | collective-permute-start | bytes 983048 | tf_op jit(solution)/shard_map/ppermute | solution.py:266
  85.5 0.8 all-to-all-done.1.parts
  86.9 3.6 %collective-permute-start.7 = (f32[16,320]{1,0:T(8,128)S(1)}, f32[16,320]{1,0:T(8,128)S(1)}, u32[]{:S(2)}, u32[]{:S(2)}) collective-permute-start(f32[16,320]{1,0:T(8,128)S(1)} %get-tuple-element.46), channel_id=1, source_target_pairs={{0,72},{16,88},{32,104},{48,120},{64,8},{80,24},{96,40},{112,56},{... | collective-permute-start | bytes 61448 | tf_op jit(solution)/shard_map/ppermute | solution.py:44
  90.6 7.5 %backward.1 = f32[512,320]{1,0:T(8,128)} custom-call(s32[4]{0:T(128)} %copy-done.3, bf16[12,2,160,320]{3,2,1,0:T(8,128)(2,1)} %get-tuple-element.47.w_h, f32[512,320]{1,0:T(8,128)} %copy-done.4, f32[512,320]{1,0:T(8,128)} %bitcast.17, bf16[512,320]{1,0:T(8,128)(2,1)} %collective-permute-done.3.cot_prev.prev_h, ...), custom_call_target="tpu_custom_call" | custom-call | flops 5000000000 | bytes 1000000 | tf_op jit(solution)/shard_map/backward/pallas_call | solution.py:214
  98.1 3.6 %collective-permute-done.9.after_h = bf16[512,320]{1,0:T(8,128)(2,1)} collective-permute-done((bf16[512,320]{1,0:T(8,128)(2,1)}, bf16[512,320]{1,0:T(8,128)(2,1)}, u32[]{:S(2)}, u32[]{:S(2)}) %collective-permute-start.9) | collective-permute-done | bytes 327712 | tf_op jit(solution)/shard_map/ppermute | solution.py:267
  102.4 9.0 %all-to-all-start.2 = ((f32[8,16,320]{2,1,0:T(8,128)}), f32[8,16,320]{2,1,0:T(8,128)S(1)}, u32[]{:S(2)}, u32[]{:S(2)}) async-start(f32[8,16,320]{2,1,0:T(8,128)} %broadcast_in_dim.7), calls=%async_computation.2 | async-start | bytes 393216 | tf_op jit(solution)/shard_map/all_to_all | solution.py:53
  111.4 4.3 %output.1 = f32[512,320]{1,0:T(8,128)} custom-call(s32[4]{0:T(128)} %copy-done.3, bf16[12,2,160,320]{3,2,1,0:T(8,128)(2,1)} %get-tuple-element.47.w_h, f32[512,320]{1,0:T(8,128)} %bitcast.14, bf16[512,320]{1,0:T(8,128)(2,1)} %get-tuple-element.50.hidden_h, bf16[512,320]{1,0:T(8,128)(2,1)} %collective-permute-done.8.prev_h, ...), custom_call_target="tpu_custom_call" | custom-call | flops 3000000000 | bytes 1000000 | tf_op jit(solution)/shard_map/output/pallas_call | solution.py:214
  115.7 8.4 %all-to-all-done.2 = f32[8,16,320]{2,1,0:T(8,128)S(1)} async-done(((f32[8,16,320]{2,1,0:T(8,128)}), f32[8,16,320]{2,1,0:T(8,128)S(1)}, u32[]{:S(2)}, u32[]{:S(2)}) %all-to-all-start.2) | async-done | bytes 163872 | tf_op jit(solution)/shard_map/all_to_all | solution.py:53
  124.1 15.4 %all_to_all.20 = f32[4,16,320]{2,1,0:T(8,128)S(1)} all-to-all(f32[4,16,320]{2,1,0:T(8,128)S(1)} %broadcast_in_dim.8), channel_id=1, replica_groups=mesh['x'=4,'m'=2,'k'=4,'h'=2,'y'=4,'c'=2] {'x'}, dimensions={0} | all-to-all | bytes 163840 | tf_op jit(solution)/shard_map/all_to_all | solution.py:53
  (35 shorter events, 3.0 us)
Async XLA Ops:
  2.4 16.9 %collective-permute-start = (bf16[64,384]{1,0:T(8,128)(2,1)S(1)}, bf16[64,384]{1,0:T(8,128)(2,1)S(1)}, u32[]{:S(2)}, u32[]{:S(2)}) collective-permute-start(bf16[64,384]{1,0:T(8,128)(2,1)S(1)} %pad.8), channel_id=1, source_target_pairs={{0,72},{16,88},{32,104},{48,120},{64,8},{80,24},{96,40},{112,56},{... | collective-permute-start | bytes 147464 | tf_op jit(solution)/shard_map/ppermute | solution.py:44
  20.4 15.9 %all-to-all-start = ((bf16[4,304,384]{2,1,0:T(8,128)(2,1)}), bf16[4,304,384]{2,1,0:T(8,128)(2,1)S(1)}, u32[]{:S(2)}, u32[]{:S(2)}) async-start(bf16[4,304,384]{2,1,0:T(8,128)(2,1)} %broadcast_in_dim.6), calls=%async_computation | async-start | bytes 1867776 | tf_op jit(solution)/shard_map/all_to_all | solution.py:53
  25.3 29.6 %collective-permute-start.4 = (bf16[512,320]{1,0:T(8,128)(2,1)}, bf16[512,320]{1,0:T(8,128)(2,1)}, u32[]{:S(2)}, u32[]{:S(2)}) collective-permute-start(bf16[512,320]{1,0:T(8,128)(2,1)} %bitcast_convert_fusion), channel_id=1, source_target_pairs={{112,128},{128,112},{240,256},{256,240},{368,384},{384,368},{113,1... | collective-permute-start | bytes 983048 | tf_op jit(solution)/shard_map/ppermute | solution.py:244
  26.7 28.2 %collective-permute-start.3 = (bf16[512,320]{1,0:T(8,128)(2,1)}, bf16[512,320]{1,0:T(8,128)(2,1)}, u32[]{:S(2)}, u32[]{:S(2)}) collective-permute-start(bf16[512,320]{1,0:T(8,128)(2,1)} %bitcast_convert_fusion), channel_id=1, source_target_pairs={{0,16},{16,32},{32,48},{48,64},{64,80},{80,96},{96,112},{128,144},... | collective-permute-start | bytes 983048 | tf_op jit(solution)/shard_map/ppermute | solution.py:243
  29.4 25.6 %collective-permute-start.2 = (bf16[512,320]{1,0:T(8,128)(2,1)}, bf16[512,320]{1,0:T(8,128)(2,1)}, u32[]{:S(2)}, u32[]{:S(2)}) collective-permute-start(bf16[512,320]{1,0:T(8,128)(2,1)} %bitcast_convert_fusion), channel_id=1, source_target_pairs={{16,0},{32,16},{48,32},{64,48},{80,64},{96,80},{112,96},{144,128},... | collective-permute-start | bytes 983048 | tf_op jit(solution)/shard_map/ppermute | solution.py:242
  36.3 16.8 %copy-start.1 = (bf16[4,304,384]{2,1,0:T(8,128)(2,1)}, bf16[4,304,384]{2,1,0:T(8,128)(2,1)S(1)}, u32[]{:S(2)}) copy-start(bf16[4,304,384]{2,1,0:T(8,128)(2,1)S(1)} %all-to-all-done.gathered.own_m) | copy-start | bytes 2801668
  36.3 21.2 %copy-start.5 = (f32[320]{0:T(512)S(1)}, f32[320]{0:T(512)}, u32[]{:S(2)}) copy-start(f32[320]{0:T(512)} %param.7) | copy-start | bytes 3844
  36.3 21.3 %copy-start.2 = (f32[1,1,16,32,320]{4,3,2,1,0:T(8,128)S(1)}, f32[1,1,16,32,320]{4,3,2,1,0:T(8,128)}, u32[]{:S(2)}) copy-start(f32[1,1,16,32,320]{4,3,2,1,0:T(8,128)} %param.5) | copy-start | bytes 1966084
  53.0 6.3 %collective-permute-start.1 = (bf16[4,304,384]{2,1,0:T(8,128)(2,1)S(1)}, bf16[4,304,384]{2,1,0:T(8,128)(2,1)}, u32[]{:S(2)}, u32[]{:S(2)}) collective-permute-start(bf16[4,304,384]{2,1,0:T(8,128)(2,1)S(1)} %all-to-all-done.gathered.own_m), channel_id=1, source_target_pairs={{0,1},{1,0},{2,3},{3,2},{4,5},{5,4},{6,7},{7,6},{8,9},{9,8},{10,11... | collective-permute-start | bytes 2801672 | tf_op jit(solution)/shard_map/ppermute | solution.py:48
  55.0 4.3 %collective-permute-start.5 = (bf16[4,256,384]{2,1,0:T(8,128)(2,1)S(1)}, bf16[4,256,384]{2,1,0:T(8,128)(2,1)S(1)}, u32[]{:S(2)}, u32[]{:S(2)}) collective-permute-start(bf16[4,256,384]{2,1,0:T(8,128)(2,1)S(1)} %bitcast.12), channel_id=1, source_target_pairs={{0,1},{1,0},{2,3},{3,2},{4,5},{5,4},{6,7},{7,6},{8,9},{9,8},{10,11... | collective-permute-start | bytes 2359304 | tf_op jit(solution)/shard_map/ppermute | solution.py:48
  57.5 28.8 %copy-start.3 = (s32[4]{0:T(128)}, s32[4]{0:T(128)S(1)}, u32[]{:S(2)}) copy-start(s32[4]{0:T(128)S(1)} %pad_add_fusion.place) | copy-start | bytes 52
  57.8 1.1 copy-start
  66.8 5.0 %copy-start.4 = (f32[512,320]{1,0:T(8,128)}, f32[512,320]{1,0:T(8,128)S(1)}, u32[]{:S(2)}) copy-start(f32[512,320]{1,0:T(8,128)S(1)} %get-tuple-element.48.slope_h) | copy-start | bytes 1966084
  66.8 4.2 %collective-permute-start.6 = (f32[4,4,2,16,320]{4,3,2,1,0:T(8,128)S(1)}, f32[4,4,2,16,320]{4,3,2,1,0:T(8,128)S(1)}, u32[]{:S(2)}, u32[]{:S(2)}) collective-permute-start(f32[4,4,2,16,320]{4,3,2,1,0:T(8,128)S(1)} %get-tuple-element.42), channel_id=1, source_target_pairs={{0,1},{1,0},{2,3},{3,2},{4,5},{5,4},{6,7},{7,6},{8,9},{9,8},{10,11... | collective-permute-start | bytes 1966088 | tf_op jit(solution)/shard_map/ppermute | solution.py:48
  71.8 14.5 %all-to-all-start.1 = ((bf16[16,2,16,320]{3,2,1,0:T(8,128)(2,1)}), bf16[16,2,16,320]{3,2,1,0:T(8,128)(2,1)S(1)}, u32[]{:S(2)}, u32[]{:S(2)}) async-start(bf16[16,2,16,320]{3,2,1,0:T(8,128)(2,1)} %bitcast.7), calls=%async_computation.1 | async-start | bytes 786432 | tf_op jit(solution)/shard_map/all_to_all | solution.py:265
  77.5 20.6 %collective-permute-start.10 = (bf16[512,320]{1,0:T(8,128)(2,1)}, bf16[512,320]{1,0:T(8,128)(2,1)}, u32[]{:S(2)}, u32[]{:S(2)}) collective-permute-start(bf16[512,320]{1,0:T(8,128)(2,1)} %get-tuple-element.50.hidden_h), channel_id=1, source_target_pairs={{112,128},{128,112},{240,256},{256,240},{368,384},{384,368},{113,1... | collective-permute-start | bytes 983048 | tf_op jit(solution)/shard_map/ppermute | solution.py:268
  78.9 22.8 %collective-permute-start.9 = (bf16[512,320]{1,0:T(8,128)(2,1)}, bf16[512,320]{1,0:T(8,128)(2,1)}, u32[]{:S(2)}, u32[]{:S(2)}) collective-permute-start(bf16[512,320]{1,0:T(8,128)(2,1)} %get-tuple-element.50.hidden_h), channel_id=1, source_target_pairs={{16,0},{32,16},{48,32},{64,48},{80,64},{96,80},{112,96},{144,128},... | collective-permute-start | bytes 983048 | tf_op jit(solution)/shard_map/ppermute | solution.py:267
  80.2 21.5 %collective-permute-start.8 = (bf16[512,320]{1,0:T(8,128)(2,1)}, bf16[512,320]{1,0:T(8,128)(2,1)}, u32[]{:S(2)}, u32[]{:S(2)}) collective-permute-start(bf16[512,320]{1,0:T(8,128)(2,1)} %get-tuple-element.50.hidden_h), channel_id=1, source_target_pairs={{0,16},{16,32},{32,48},{48,64},{64,80},{80,96},{96,112},{128,144},... | collective-permute-start | bytes 983048 | tf_op jit(solution)/shard_map/ppermute | solution.py:266
  86.9 11.2 %collective-permute-start.7 = (f32[16,320]{1,0:T(8,128)S(1)}, f32[16,320]{1,0:T(8,128)S(1)}, u32[]{:S(2)}, u32[]{:S(2)}) collective-permute-start(f32[16,320]{1,0:T(8,128)S(1)} %get-tuple-element.46), channel_id=1, source_target_pairs={{0,72},{16,88},{32,104},{48,120},{64,8},{80,24},{96,40},{112,56},{... | collective-permute-start | bytes 61448 | tf_op jit(solution)/shard_map/ppermute | solution.py:44
  102.4 21.7 %all-to-all-start.2 = ((f32[8,16,320]{2,1,0:T(8,128)}), f32[8,16,320]{2,1,0:T(8,128)S(1)}, u32[]{:S(2)}, u32[]{:S(2)}) async-start(f32[8,16,320]{2,1,0:T(8,128)} %broadcast_in_dim.7), calls=%async_computation.2 | async-start | bytes 393216 | tf_op jit(solution)/shard_map/all_to_all | solution.py:53

commit v7 on v6

--- a/solution.py
+++ b/solution.py
@@ -61,11 +61,17 @@
     return lax.dot_general(a, b, (((1,), (1,)), ((), ())), preferred_element_type=F32)
 
 
-def dot_tn(a, b):
-    return lax.dot_general(a, b, (((0,), (0,)), ((), ())), preferred_element_type=F32)
-
-
 def fill_windows(windows, value):
+    col = lax.broadcasted_iota(jnp.int32, (ROWS, 1), 0) % W
+    edge = jnp.zeros((W, 3 * C), BF)
+    windows[0:W, :] = edge
+    windows[W + ROWS : 2 * W + ROWS, :] = edge
+    left = jnp.where(col == 0, 0.0, pltpu.roll(value, 1, 0))
+    right = jnp.where(col == W - 1, 0.0, pltpu.roll(value, ROWS - 1, 0))
+    windows[W : W + ROWS, :] = jnp.concatenate([a.astype(BF) for a in (left, value, right)], axis=1)
+
+
+def fill_shifts(windows, value):
     col = lax.broadcasted_iota(jnp.int32, (ROWS, 1), 0) % W
     edge = jnp.zeros((W, C), BF)
     for d in range(3):
@@ -96,8 +102,7 @@
 def conv(windows, w_ref, bias):
     acc = jnp.zeros((ROWS, C), F32) + bias
     for a in range(3):
-        for b in range(3):
-            acc = acc + dot(windows[b, a * W : a * W + ROWS, :], tap(w_ref, 3 * a + b))
+        acc = acc + dot(windows[a * W : a * W + ROWS, :], w_ref[3 * a : 3 * a + 3].reshape(3 * C, C))
     return acc
 
 
@@ -110,6 +115,25 @@
 
 def prepare_kernel(video, windows):
     fill_windows(windows, video[...])
+
+
+def cast_kernel(cot, video, cot_out, both):
+    cot_b = cot[...].astype(BF)
+    cot_out[...] = cot_b
+    both[0:ROWS, 0:C] = cot_b
+    both[ROWS:, 0:C] = video[...].astype(BF)
+    both[:, C:WIDE] = jnp.zeros((2 * ROWS, WIDE - C), BF)
+
+
+def pack_kernel(spatial, temporal, other, out):
+    for t in range(TAPS):
+        rows = spatial[t] if t < SPACE else temporal[t - SPACE].astype(BF)
+        for y in range(4):
+            out[y, t * OWN : (t + 1) * OWN, 0:C] = rows
+    side = jnp.zeros((TAPS * OWN, WIDE - C), BF)
+    for y in range(4):
+        out[y, 0 : TAPS * OWN, C:WIDE] = side
+        out[y, TAPS * OWN :, :] = other[...]
 
 
 def apart_kernel(gathered, out):
@@ -134,8 +158,9 @@
     hidden = (spatial * sig).astype(BF)
     hidden_ref[...] = hidden
     slope_ref[...] = sig * (1.0 + spatial * (1.0 - sig))
-    before, after = sides(place, cot_prev[...], cot_next[...], far[...])
-    grads = [dot_tn(hidden, other) for other in (after, cot[...].astype(BF), before)]
+    before, after = sides(place, cot_prev[...], cot_next[...], far[0:ROWS, 0:C])
+    turned = hidden.T
+    grads = [dot(turned, other) for other in (after, cot[...].astype(BF), before)]
     pad = jnp.zeros((4, C), F32)
     for half in range(2):
         for y in range(4):
@@ -167,23 +192,35 @@
 ):
     arrive = copies(
         sems, (w_h.at[SPACE:TAPS], w_ref.at[SPACE:TAPS]), (cot_h, cot), (prev_h, cot_prev), (next_h, cot_next),
-        (far_h, far), (slope_h, slope), (w_h.at[0:SPACE], w_ref.at[0:SPACE]),
+        (far_h.at[0:ROWS, :], far), (slope_h, slope), (w_h.at[0:SPACE], w_ref.at[0:SPACE]),
     )
     for one in arrive[:5]:
         one.wait()
-    before, after = sides(place, cot_prev[...], cot_next[...], far[...])
+    before, after = sides(place, cot_prev[...], cot_next[...], far[0:ROWS, 0:C])
     gh = dot_nt(after, tap(w_ref, 9))
     gh = gh + dot_nt(cot[...].astype(BF), tap(w_ref, 10))
     gh = gh + dot_nt(before, tap(w_ref, 11))
     arrive[5].wait()
     gs = (gh * slope[...]).astype(BF).astype(F32)
-    fill_windows(windows, gs)
+    fill_shifts(windows, gs)
     arrive[6].wait()
     acc = cot[...]
     for a in range(3):
         for b in range(3):
             acc = acc + dot_nt(windows[2 - b, (2 - a) * W : (2 - a) * W + ROWS, :], tap(w_ref, 3 * a + b))
     grad_ref[...] = acc
+
+
+def far_kernel(place, w_h, far_h, bias, hidden_h, w_ref, far, hidden_ref, windows, sems):
+    arrive = copies(sems, (far_h.at[ROWS : 2 * ROWS, :], far), (w_h.at[0:SPACE], w_ref))
+    arrive[0].wait()
+    fill_windows(windows, far[:, 0:C].astype(F32))
+    arrive[1].wait()
+    spatial = conv(windows, w_ref, bias[...])
+    hidden = (spatial * jax.nn.sigmoid(spatial)).astype(BF)
+    hidden_ref[...] = jnp.where(place[3] == 1, hidden, jnp.zeros_like(hidden))
+    for one in copies(sems, (hidden_ref, hidden_h)):
+        one.wait()
 
 
 def output_kernel(
@@ -202,7 +239,8 @@
 
 FRAME_B = (ROWS, C), BF
 FRAME_F = (ROWS, C), F32
-WINDOWS = (3, ROWS + 2 * W, C), BF
+WINDOWS = (ROWS + 2 * W, 3 * C), BF
+SHIFTS = (3, ROWS + 2 * W, C), BF
 WEIGHTS = (TAPS, 2, HALF, C), BF
 SUMS = (4, 4, 2, 16, C), F32
 SHARE = (16, C), F32
@@ -233,16 +271,21 @@
     cot_f = cotangent.reshape(ROWS, C)
     bias = spatial_b.reshape(1, C)
 
-    cot_b = cot_f.astype(BF)
     w = jnp.concatenate([spatial_w, temporal_w.astype(BF)], axis=0)
     quarter = lax.dynamic_slice_in_dim(w, 3 * x, 3, 0).reshape(3 * OWN, C)
     other = across(jnp.pad(quarter, ((0, SLOT - 3 * OWN), (0, WIDE - C))))
-    w = jnp.pad(w.reshape(TAPS * OWN, C), ((0, 0), (0, WIDE - C)))
-    other, cot_b, w = tie((other, cot_b, w))
+    other, cot_w, video_w = tie((other, cot_f, video_f))
+    cot_b, both = kernel_call(
+        cast_kernel, [(cot_w, "v"), (video_w, "v")], [(FRAME_B, "v"), (((2 * ROWS, WIDE), BF), "v")], [], 0, 0.01, "cast", 8,
+    )
     cot_next = lax.ppermute(cot_b, TM, FRAMES_DOWN)
     cot_prev = lax.ppermute(cot_b, TM, FRAMES_UP)
-    far = lax.ppermute(cot_b, TM, FRAMES_FAR)
-    own_m = to_all(jnp.concatenate([w, other], axis=0), "y")
+    far = lax.ppermute(both, TM, FRAMES_FAR)
+    (packed,) = kernel_call(
+        pack_kernel, [(spatial_w, "v"), (temporal_w, "v"), (other, "v")], [(((4, TAPS * OWN + SLOT, WIDE), BF), "v")],
+        [], 0, 0.01, "pack", 8,
+    )
+    own_m = lax.all_to_all(packed, "y", 0, 0, tiled=True)
     (oth_m,) = kernel_call(
         apart_kernel, [(own_m, "v")], [(((4 * SLOT, WIDE), BF), "v")], [], 0, 1000, "apart", 8,
     )
@@ -265,7 +308,11 @@
     part = lax.all_to_all(part.reshape(16, 2, 16, C), PLANE, 0, 0, tiled=True)
     prev = lax.ppermute(hidden, TM, FRAMES_UP)
     after = lax.ppermute(hidden, TM, FRAMES_DOWN)
-    hidden_far = lax.ppermute(hidden, TM, FRAMES_FAR)
+    (hidden_far,) = kernel_call(
+        far_kernel, [(place, "s"), (w_all, "h"), (far, "h"), (bias, "v")], [(FRAME_B, "h")],
+        [((SPACE, 2, HALF, C), BF), ((ROWS, WIDE), BF), FRAME_B, WINDOWS], 2, 0.01, "far",
+    )
+    part, hidden_far = tie((part, hidden_far))
     keep, give = kernel_call(
         split_kernel, [(place, "s"), (part, "v")], [(SHARE, "v"), (SHARE, "v")], [], 0, 1000, "split", 8,
     )
@@ -275,7 +322,7 @@
         backward_kernel,
         [(place, "s"), (w_all, "h"), (slope, "h"), (cot_f, "h"), (cot_prev, "h"), (cot_next, "h"), (far, "h")],
         [(FRAME_F, "v")],
-        [WEIGHTS, FRAME_F, FRAME_F, FRAME_B, FRAME_B, FRAME_B, WINDOWS], 7, 5, "backward",
+        [WEIGHTS, FRAME_F, FRAME_F, FRAME_B, FRAME_B, ((ROWS, WIDE), BF), SHIFTS], 7, 5, "backward",
     )
     other, grad_video = tie((other, grad_video))
     part = keep + other

time: 141 us -> 151 us (1.071)
  blocking collectives: 32.1 us -> 43 us
  Pallas kernels: 20.1 us -> 26.4 us
  waiting for transfers between devices: 21.8 us -> 18.6 us
  other arithmetic: 5.63 us -> 2.83 us
  starting transfers between devices: 55.9 us -> 53.6 us
    all_gather x1, blocking collectives: 16.7 us -> 33.2 us  [on_device(): oth_m = lax.all_gather(oth_m, 'x')]
    pallas_call x6 -> x9, Pallas kernels: 20.1 us -> 26.4 us  [kernel_call(): pl.pallas_call(body, out_shape=tuple((jax.ShapeDtypeStruct(*o[0]) for o i...]
    all_to_all x1, blocking collectives: 15.4 us -> 9.84 us  [to_all(): lax.all_to_all(jnp.broadcast_to(a[None], (n, *a.shape)), axes, 0, 0, tile...]
    all_to_all x2 -> x1, starting transfers between devices: 13.9 us -> 8.63 us  [to_all(): lax.all_to_all(jnp.broadcast_to(a[None], (n, *a.shape)), axes, 0, 0, tile...]
    all_to_all x2 -> x1, waiting for transfers between devices: 14 us -> 8.72 us  [to_all(): lax.all_to_all(jnp.broadcast_to(a[None], (n, *a.shape)), axes, 0, 0, tile...]
    all_to_all x0 -> x1, starting transfers between devices: none -> 4.91 us  [on_device(): own_m = lax.all_to_all(packed, 'y', 0, 0, tiled=True)]
    ppermute x1, waiting for transfers between devices: 3.56 us -> 0.01 us  [on_device(): after = lax.ppermute(hidden, TM, FRAMES_DOWN)]
    ppermute x2, waiting for transfers between devices: 1.18 us -> 4.33 us  [across(): return lax.ppermute(a, ('m', 'k', 'h'), ACROSS)]
  transfers between devices with their start and end apart: 14 -> 13, of which waited for: 7 -> 6; matrix products, arithmetic and copies ran while one was open for 2% -> 0% of each run, Pallas kernels for 9% -> 13%
where the time goes in v7:
time: 151 us; the launch traced here: 150 us
  starting transfers between devices  53.6 us (35%)
  blocking collectives  43 us (28%)
  Pallas kernels  26.4 us (17%)
  waiting for transfers between devices  18.6 us (12%)
  local copies, waits for them, and re-layouts  4.28 us (3%)
  other arithmetic  2.83 us (2%)
    all_gather x1, blocking collectives, on_device(): oth_m = lax.all_gather(oth_m, 'x')  33.2 us
    pallas_call x9, Pallas kernels, kernel_call(): pl.pallas_call(body, out_shape=tuple((jax.ShapeDtypeStruct(*o[0]) for o i...  26.4 us
    ppermute x2, starting transfers between devices, across(): return lax.ppermute(a, ('m', 'k', 'h'), ACROSS)  14.7 us
    all_to_all x1, blocking collectives, to_all(): lax.all_to_all(jnp.broadcast_to(a[None], (n, *a.shape)), axes, 0, 0, tile...  9.84 us
    all_to_all x1, waiting for transfers between devices, to_all(): lax.all_to_all(jnp.broadcast_to(a[None], (n, *a.shape)), axes, 0, 0, tile...  8.72 us
    all_to_all x1, starting transfers between devices, to_all(): lax.all_to_all(jnp.broadcast_to(a[None], (n, *a.shape)), axes, 0, 0, tile...  8.63 us
    all_to_all x1, starting transfers between devices, on_device(): part = lax.all_to_all(part.reshape(16, 2, 16, C), PLANE, 0, 0, tiled=True)  6.69 us
    ppermute x3, starting transfers between devices, core_swap(): return lax.ppermute(a, 'c', [(0, 1), (1, 0)])  6.6 us
  transfers between devices with their start and end apart: 13, of which 6 were waited for; matrix products, arithmetic and copies ran while one was open for 0% of the time, Pallas kernels for 13%

profile of v7, /device:TPU:8, one launch (start us, length us, event | category | flops | bytes accessed | tf_op | source)
XLA Modules:
  0.0 149.6 jit_solution(1485633780050151292)
XLA Ops:
  0.7 1.0 convert_element_type.9
  1.7 0.8 fusion
  2.6 12.7 %collective-permute-start = (bf16[64,384]{1,0:T(8,128)(2,1)S(1)}, bf16[64,384]{1,0:T(8,128)(2,1)S(1)}, u32[]{:S(2)}, u32[]{:S(2)}) collective-permute-start(bf16[64,384]{1,0:T(8,128)(2,1)S(1)} %pad.4), channel_id=1, source_target_pairs={{0,72},{16,88},{32,104},{48,120},{64,8},{80,24},{96,40},{112,56},{... | collective-permute-start | bytes 147464 | tf_op jit(solution)/shard_map/ppermute | solution.py:44
  15.3 4.2 %collective-permute-done.other = bf16[64,384]{1,0:T(8,128)(2,1)S(1)} collective-permute-done((bf16[64,384]{1,0:T(8,128)(2,1)S(1)}, bf16[64,384]{1,0:T(8,128)(2,1)S(1)}, u32[]{:S(2)}, u32[]{:S(2)}) %collective-permute-start) | collective-permute-done | bytes 49184 | tf_op jit(solution)/shard_map/ppermute | solution.py:44
  19.5 0.9 copy-done.5
  20.4 0.9 copy-done.6
  21.3 1.1 pack.1
  22.4 4.9 %all-to-all-start = ((bf16[4,304,384]{2,1,0:T(8,128)(2,1)}), bf16[4,304,384]{2,1,0:T(8,128)(2,1)S(1)}, u32[]{:S(2)}, u32[]{:S(2)}) async-start(bf16[4,304,384]{2,1,0:T(8,128)(2,1)} %pack.1), calls=%async_computation | async-start | bytes 1867776 | tf_op jit(solution)/shard_map/all_to_all | solution.py:288
  27.3 1.1 cast.1
  28.4 2.7 %collective-permute-start.3 = (bf16[512,320]{1,0:T(8,128)(2,1)}, bf16[512,320]{1,0:T(8,128)(2,1)}, u32[]{:S(2)}, u32[]{:S(2)}) collective-permute-start(bf16[512,320]{1,0:T(8,128)(2,1)} %get-tuple-element.40), channel_id=1, source_target_pairs={{0,16},{16,32},{32,48},{48,64},{64,80},{80,96},{96,112},{128,144},... | collective-permute-start | bytes 983048 | tf_op jit(solution)/shard_map/ppermute | solution.py:282
  31.1 1.3 collective-permute-start.2
  32.4 1.6 %collective-permute-start.4 = (bf16[1024,384]{1,0:T(8,128)(2,1)}, bf16[1024,384]{1,0:T(8,128)(2,1)}, u32[]{:S(2)}, u32[]{:S(2)}) collective-permute-start(bf16[1024,384]{1,0:T(8,128)(2,1)} %get-tuple-element.41), channel_id=1, source_target_pairs={{112,128},{128,112},{240,256},{256,240},{368,384},{384,368},{113,1... | collective-permute-start | bytes 2359304 | tf_op jit(solution)/shard_map/ppermute | solution.py:283
  34.0 3.0 %all-to-all-done.gathered.own_m = bf16[4,304,384]{2,1,0:T(8,128)(2,1)S(1)} async-done(((bf16[4,304,384]{2,1,0:T(8,128)(2,1)}), bf16[4,304,384]{2,1,0:T(8,128)(2,1)S(1)}, u32[]{:S(2)}, u32[]{:S(2)}) %all-to-all-start) | async-done | bytes 933920 | tf_op jit(solution)/shard_map/all_to_all | solution.py:288
  37.0 33.2 %all-gather = bf16[1024,384]{1,0:T(8,128)(2,1)S(1)} all-gather(bf16[256,384]{1,0:T(8,128)(2,1)S(1)} %apart.1), channel_id=2, replica_groups=mesh['x'=4,'m'=2,'k'=4,'h'=2,'y'=4,'c'=2] {'x'}, dimensions={0}, use_global_device_ids=true | all-gather | bytes 983040 | tf_op jit(solution)/shard_map/all_gather | solution.py:292
  70.2 1.9 %collective-permute-start.1 = (bf16[4,304,384]{2,1,0:T(8,128)(2,1)S(1)}, bf16[4,304,384]{2,1,0:T(8,128)(2,1)}, u32[]{:S(2)}, u32[]{:S(2)}) collective-permute-start(bf16[4,304,384]{2,1,0:T(8,128)(2,1)S(1)} %all-to-all-done.gathered.own_m), channel_id=1, source_target_pairs={{0,1},{1,0},{2,3},{3,2},{4,5},{5,4},{6,7},{7,6},{8,9},{9,8},{10,11... | collective-permute-start | bytes 2801672 | tf_op jit(solution)/shard_map/ppermute | solution.py:48
  72.2 2.4 %collective-permute-start.5 = (bf16[4,256,384]{2,1,0:T(8,128)(2,1)S(1)}, bf16[4,256,384]{2,1,0:T(8,128)(2,1)}, u32[]{:S(2)}, u32[]{:S(2)}) collective-permute-start(bf16[4,256,384]{2,1,0:T(8,128)(2,1)S(1)} %bitcast.14), channel_id=1, source_target_pairs={{0,1},{1,0},{2,3},{3,2},{4,5},{5,4},{6,7},{7,6},{8,9},{9,8},{10,11... | collective-permute-start | bytes 2359304 | tf_op jit(solution)/shard_map/ppermute | solution.py:48
  75.0 1.0 copy-done
  76.6 6.5 %forward.1 = (bf16[12,2,160,320]{3,2,1,0:T(8,128)(2,1)}, bf16[512,320]{1,0:T(8,128)(2,1)}, f32[512,320]{1,0:T(8,128)S(1)}, f32[4,4,2,16,320]{4,3,2,1,0:T(8,128)S(1)}, f32[4,4,2,16,320]{4,3,2,1,0:T(8,128)S(1)}) custom-call(s32[4]{0:T(128)S(1)} %pad_add_fusion.place, bf16[4,304,384]{2,1,0:T(8,128)(2,1)} %copy-done.1, ...), custom_call_target="tpu_custom_call" | custom-call | flops 10000000 | bytes 1000000 | tf_op jit(solution)/shard_map/forward/pallas_call | solution.py:252
  83.1 2.3 %collective-permute-start.6 = (f32[4,4,2,16,320]{4,3,2,1,0:T(8,128)S(1)}, f32[4,4,2,16,320]{4,3,2,1,0:T(8,128)S(1)}, u32[]{:S(2)}, u32[]{:S(2)}) collective-permute-start(f32[4,4,2,16,320]{4,3,2,1,0:T(8,128)S(1)} %get-tuple-element.48), channel_id=1, source_target_pairs={{0,1},{1,0},{2,3},{3,2},{4,5},{5,4},{6,7},{7,6},{8,9},{9,8},{10,11... | collective-permute-start | bytes 1966088 | tf_op jit(solution)/shard_map/ppermute | solution.py:48
  85.4 1.9 %collective-permute-done.6 = f32[4,4,2,16,320]{4,3,2,1,0:T(8,128)S(1)} collective-permute-done((f32[4,4,2,16,320]{4,3,2,1,0:T(8,128)S(1)}, f32[4,4,2,16,320]{4,3,2,1,0:T(8,128)S(1)}, u32[]{:S(2)}, u32[]{:S(2)}) %collective-permute-start.6) | collective-permute-done | bytes 655392 | tf_op jit(solution)/shard_map/ppermute | solution.py:48
  87.3 0.8 add_convert_fusion
  88.2 6.7 %all-to-all-start.1 = ((bf16[16,2,16,320]{3,2,1,0:T(8,128)(2,1)}), bf16[16,2,16,320]{3,2,1,0:T(8,128)(2,1)S(1)}, u32[]{:S(2)}, u32[]{:S(2)}) async-start(bf16[16,2,16,320]{3,2,1,0:T(8,128)(2,1)} %bitcast.7), calls=%async_computation.1 | async-start | bytes 786432 | tf_op jit(solution)/shard_map/all_to_all | solution.py:308
  94.8 1.3 collective-permute-start.9
  96.1 5.3 %collective-permute-start.8 = (bf16[512,320]{1,0:T(8,128)(2,1)}, bf16[512,320]{1,0:T(8,128)(2,1)}, u32[]{:S(2)}, u32[]{:S(2)}) collective-permute-start(bf16[512,320]{1,0:T(8,128)(2,1)} %get-tuple-element.57.hidden_h), channel_id=1, source_target_pairs={{0,16},{16,32},{32,48},{48,64},{64,80},{80,96},{96,112},{128,144},... | collective-permute-start | bytes 983048 | tf_op jit(solution)/shard_map/ppermute | solution.py:309
  101.4 5.0 %far.1.far_h = bf16[512,320]{1,0:T(8,128)(2,1)} custom-call(s32[4]{0:T(128)} %copy-done.8, bf16[12,2,160,320]{3,2,1,0:T(8,128)(2,1)} %get-tuple-element.49.w_h, bf16[1024,384]{1,0:T(8,128)(2,1)} %collective-permute-done.4.far.far_h, f32[1,320]{1,0:T(1,128)} %copy-done.7), custom_call_target="tpu_custom_call" | custom-call | flops 10000000 | bytes 1000000 | tf_op jit(solution)/shard_map/far/pallas_call | solution.py:252
  107.1 1.9 %collective-permute-start.7 = (f32[16,320]{1,0:T(8,128)S(1)}, f32[16,320]{1,0:T(8,128)S(1)}, u32[]{:S(2)}, u32[]{:S(2)}) collective-permute-start(f32[16,320]{1,0:T(8,128)S(1)} %get-tuple-element.54), channel_id=1, source_target_pairs={{0,72},{16,88},{32,104},{48,120},{64,8},{80,24},{96,40},{112,56},{... | collective-permute-start | bytes 61448 | tf_op jit(solution)/shard_map/ppermute | solution.py:44
  109.0 7.5 %backward.1 = f32[512,320]{1,0:T(8,128)} custom-call(s32[4]{0:T(128)} %copy-done.8, bf16[12,2,160,320]{3,2,1,0:T(8,128)(2,1)} %get-tuple-element.49.w_h, f32[512,320]{1,0:T(8,128)} %copy-done.10, f32[512,320]{1,0:T(8,128)} %bitcast.11, bf16[512,320]{1,0:T(8,128)(2,1)} %collective-permute-done.3.cot_prev.prev_h, ...), custom_call_target="tpu_custom_call" | custom-call | flops 5000000000 | bytes 1000000 | tf_op jit(solution)/shard_map/backward/pallas_call | solution.py:252
  116.7 0.7 broadcast_in_dim.4
  117.4 8.6 %all-to-all-start.2 = ((f32[8,16,320]{2,1,0:T(8,128)}), f32[8,16,320]{2,1,0:T(8,128)S(1)}, u32[]{:S(2)}, u32[]{:S(2)}) async-start(f32[8,16,320]{2,1,0:T(8,128)} %broadcast_in_dim.4), calls=%async_computation.2 | async-start | bytes 393216 | tf_op jit(solution)/shard_map/all_to_all | solution.py:53
  126.1 4.3 %output.1 = f32[512,320]{1,0:T(8,128)} custom-call(s32[4]{0:T(128)} %copy-done.8, bf16[12,2,160,320]{3,2,1,0:T(8,128)(2,1)} %get-tuple-element.49.w_h, f32[512,320]{1,0:T(8,128)} %bitcast.16, bf16[512,320]{1,0:T(8,128)(2,1)} %get-tuple-element.57.hidden_h, bf16[512,320]{1,0:T(8,128)(2,1)} %collective-permute-done.8.prev_h, ...), custom_call_target="tpu_custom_call" | custom-call | flops 3000000000 | bytes 1000000 | tf_op jit(solution)/shard_map/output/pallas_call | solution.py:252
  130.4 8.7 %all-to-all-done.2 = f32[8,16,320]{2,1,0:T(8,128)S(1)} async-done(((f32[8,16,320]{2,1,0:T(8,128)}), f32[8,16,320]{2,1,0:T(8,128)S(1)}, u32[]{:S(2)}, u32[]{:S(2)}) %all-to-all-start.2) | async-done | bytes 163872 | tf_op jit(solution)/shard_map/all_to_all | solution.py:53
  139.1 9.8 %all_to_all.20 = f32[4,16,320]{2,1,0:T(8,128)S(1)} all-to-all(f32[4,16,320]{2,1,0:T(8,128)S(1)} %broadcast_in_dim.5), channel_id=1, replica_groups=mesh['x'=4,'m'=2,'k'=4,'h'=2,'y'=4,'c'=2] {'x'}, dimensions={0} | all-to-all | bytes 163840 | tf_op jit(solution)/shard_map/all_to_all | solution.py:53
  (42 shorter events, 2.5 us)
Async XLA Ops:
  0.6 26.7 %copy-start.2 = (f32[1,1,16,32,320]{4,3,2,1,0:T(8,128)S(1)}, f32[1,1,16,32,320]{4,3,2,1,0:T(8,128)}, u32[]{:S(2)}) copy-start(f32[1,1,16,32,320]{4,3,2,1,0:T(8,128)} %param.9) | copy-start | bytes 1966084
  0.6 26.7 %copy-start.3 = (f32[1,1,16,32,320]{4,3,2,1,0:T(8,128)S(1)}, f32[1,1,16,32,320]{4,3,2,1,0:T(8,128)}, u32[]{:S(2)}) copy-start(f32[1,1,16,32,320]{4,3,2,1,0:T(8,128)} %param.5) | copy-start | bytes 1966084
  2.6 16.9 %collective-permute-start = (bf16[64,384]{1,0:T(8,128)(2,1)S(1)}, bf16[64,384]{1,0:T(8,128)(2,1)S(1)}, u32[]{:S(2)}, u32[]{:S(2)}) collective-permute-start(bf16[64,384]{1,0:T(8,128)(2,1)S(1)} %pad.4), channel_id=1, source_target_pairs={{0,72},{16,88},{32,104},{48,120},{64,8},{80,24},{96,40},{112,56},{... | collective-permute-start | bytes 147464 | tf_op jit(solution)/shard_map/ppermute | solution.py:44
  19.5 0.9 copy-start.5
  20.4 0.9 copy-start.6
  22.4 14.6 %all-to-all-start = ((bf16[4,304,384]{2,1,0:T(8,128)(2,1)}), bf16[4,304,384]{2,1,0:T(8,128)(2,1)S(1)}, u32[]{:S(2)}, u32[]{:S(2)}) async-start(bf16[4,304,384]{2,1,0:T(8,128)(2,1)} %pack.1), calls=%async_computation | async-start | bytes 1867776 | tf_op jit(solution)/shard_map/all_to_all | solution.py:288
  28.4 43.7 %collective-permute-start.3 = (bf16[512,320]{1,0:T(8,128)(2,1)}, bf16[512,320]{1,0:T(8,128)(2,1)}, u32[]{:S(2)}, u32[]{:S(2)}) collective-permute-start(bf16[512,320]{1,0:T(8,128)(2,1)} %get-tuple-element.40), channel_id=1, source_target_pairs={{0,16},{16,32},{32,48},{48,64},{64,80},{80,96},{96,112},{128,144},... | collective-permute-start | bytes 983048 | tf_op jit(solution)/shard_map/ppermute | solution.py:282
  31.1 41.0 %collective-permute-start.2 = (bf16[512,320]{1,0:T(8,128)(2,1)}, bf16[512,320]{1,0:T(8,128)(2,1)}, u32[]{:S(2)}, u32[]{:S(2)}) collective-permute-start(bf16[512,320]{1,0:T(8,128)(2,1)} %get-tuple-element.40), channel_id=1, source_target_pairs={{16,0},{32,16},{48,32},{64,48},{80,64},{96,80},{112,96},{144,128},... | collective-permute-start | bytes 983048 | tf_op jit(solution)/shard_map/ppermute | solution.py:281
  32.4 39.8 %collective-permute-start.4 = (bf16[1024,384]{1,0:T(8,128)(2,1)}, bf16[1024,384]{1,0:T(8,128)(2,1)}, u32[]{:S(2)}, u32[]{:S(2)}) collective-permute-start(bf16[1024,384]{1,0:T(8,128)(2,1)} %get-tuple-element.41), channel_id=1, source_target_pairs={{112,128},{128,112},{240,256},{256,240},{368,384},{384,368},{113,1... | collective-permute-start | bytes 2359304 | tf_op jit(solution)/shard_map/ppermute | solution.py:283
  37.0 33.2 %copy-start.1 = (bf16[4,304,384]{2,1,0:T(8,128)(2,1)}, bf16[4,304,384]{2,1,0:T(8,128)(2,1)S(1)}, u32[]{:S(2)}) copy-start(bf16[4,304,384]{2,1,0:T(8,128)(2,1)S(1)} %all-to-all-done.gathered.own_m) | copy-start | bytes 2801668
  37.0 37.6 %copy-start.11 = (f32[320]{0:T(512)S(1)}, f32[320]{0:T(512)}, u32[]{:S(2)}) copy-start(f32[320]{0:T(512)} %param.7) | copy-start | bytes 3844
  37.0 37.7 %copy-start.4 = (f32[1,1,16,32,320]{4,3,2,1,0:T(8,128)S(1)}, f32[1,1,16,32,320]{4,3,2,1,0:T(8,128)}, u32[]{:S(2)}) copy-start(f32[1,1,16,32,320]{4,3,2,1,0:T(8,128)} %param.5) | copy-start | bytes 1966084
  70.2 6.4 %collective-permute-start.1 = (bf16[4,304,384]{2,1,0:T(8,128)(2,1)S(1)}, bf16[4,304,384]{2,1,0:T(8,128)(2,1)}, u32[]{:S(2)}, u32[]{:S(2)}) collective-permute-start(bf16[4,304,384]{2,1,0:T(8,128)(2,1)S(1)} %all-to-all-done.gathered.own_m), channel_id=1, source_target_pairs={{0,1},{1,0},{2,3},{3,2},{4,5},{5,4},{6,7},{7,6},{8,9},{9,8},{10,11... | collective-permute-start | bytes 2801672 | tf_op jit(solution)/shard_map/ppermute | solution.py:48
  72.2 4.4 %collective-permute-start.5 = (bf16[4,256,384]{2,1,0:T(8,128)(2,1)S(1)}, bf16[4,256,384]{2,1,0:T(8,128)(2,1)}, u32[]{:S(2)}, u32[]{:S(2)}) collective-permute-start(bf16[4,256,384]{2,1,0:T(8,128)(2,1)S(1)} %bitcast.14), channel_id=1, source_target_pairs={{0,1},{1,0},{2,3},{3,2},{4,5},{5,4},{6,7},{7,6},{8,9},{9,8},{10,11... | collective-permute-start | bytes 2359304 | tf_op jit(solution)/shard_map/ppermute | solution.py:48
  74.6 8.4 %copy-start.7 = (f32[1,320]{1,0:T(1,128)}, f32[1,320]{1,0:T(1,128)S(1)}, u32[]{:S(2)}) copy-start(f32[1,320]{1,0:T(1,128)S(1)} %reshape.38.bias) | copy-start | bytes 3844
  74.7 8.4 %copy-start.8 = (s32[4]{0:T(128)}, s32[4]{0:T(128)S(1)}, u32[]{:S(2)}) copy-start(s32[4]{0:T(128)S(1)} %pad_add_fusion.place) | copy-start | bytes 52
  75.0 1.0 copy-start
  83.1 23.4 %copy-start.10 = (f32[512,320]{1,0:T(8,128)}, f32[512,320]{1,0:T(8,128)S(1)}, u32[]{:S(2)}) copy-start(f32[512,320]{1,0:T(8,128)S(1)} %get-tuple-element.55.slope_h) | copy-start | bytes 1966084
  83.1 4.2 %collective-permute-start.6 = (f32[4,4,2,16,320]{4,3,2,1,0:T(8,128)S(1)}, f32[4,4,2,16,320]{4,3,2,1,0:T(8,128)S(1)}, u32[]{:S(2)}, u32[]{:S(2)}) collective-permute-start(f32[4,4,2,16,320]{4,3,2,1,0:T(8,128)S(1)} %get-tuple-element.48), channel_id=1, source_target_pairs={{0,1},{1,0},{2,3},{3,2},{4,5},{5,4},{6,7},{7,6},{8,9},{9,8},{10,11... | collective-permute-start | bytes 1966088 | tf_op jit(solution)/shard_map/ppermute | solution.py:48
  88.2 18.3 %copy-start.9 = (s32[4]{0:T(128)S(1)}, s32[4]{0:T(128)}, u32[]{:S(2)}) copy-start(s32[4]{0:T(128)} %copy-done.8) | copy-start | bytes 52
  88.2 18.3 %all-to-all-start.1 = ((bf16[16,2,16,320]{3,2,1,0:T(8,128)(2,1)}), bf16[16,2,16,320]{3,2,1,0:T(8,128)(2,1)S(1)}, u32[]{:S(2)}, u32[]{:S(2)}) async-start(bf16[16,2,16,320]{3,2,1,0:T(8,128)(2,1)} %bitcast.7), calls=%async_computation.1 | async-start | bytes 786432 | tf_op jit(solution)/shard_map/all_to_all | solution.py:308
  94.8 21.9 %collective-permute-start.9 = (bf16[512,320]{1,0:T(8,128)(2,1)}, bf16[512,320]{1,0:T(8,128)(2,1)}, u32[]{:S(2)}, u32[]{:S(2)}) collective-permute-start(bf16[512,320]{1,0:T(8,128)(2,1)} %get-tuple-element.57.hidden_h), channel_id=1, source_target_pairs={{16,0},{32,16},{48,32},{64,48},{80,64},{96,80},{112,96},{144,128},... | collective-permute-start | bytes 983048 | tf_op jit(solution)/shard_map/ppermute | solution.py:310
  96.1 20.6 %collective-permute-start.8 = (bf16[512,320]{1,0:T(8,128)(2,1)}, bf16[512,320]{1,0:T(8,128)(2,1)}, u32[]{:S(2)}, u32[]{:S(2)}) collective-permute-start(bf16[512,320]{1,0:T(8,128)(2,1)} %get-tuple-element.57.hidden_h), channel_id=1, source_target_pairs={{0,16},{16,32},{32,48},{48,64},{64,80},{80,96},{96,112},{128,144},... | collective-permute-start | bytes 983048 | tf_op jit(solution)/shard_map/ppermute | solution.py:309
  107.1 9.6 %collective-permute-start.7 = (f32[16,320]{1,0:T(8,128)S(1)}, f32[16,320]{1,0:T(8,128)S(1)}, u32[]{:S(2)}, u32[]{:S(2)}) collective-permute-start(f32[16,320]{1,0:T(8,128)S(1)} %get-tuple-element.54), channel_id=1, source_target_pairs={{0,72},{16,88},{32,104},{48,120},{64,8},{80,24},{96,40},{112,56},{... | collective-permute-start | bytes 61448 | tf_op jit(solution)/shard_map/ppermute | solution.py:44
  117.4 21.6 %all-to-all-start.2 = ((f32[8,16,320]{2,1,0:T(8,128)}), f32[8,16,320]{2,1,0:T(8,128)S(1)}, u32[]{:S(2)}, u32[]{:S(2)}) async-start(f32[8,16,320]{2,1,0:T(8,128)} %broadcast_in_dim.4), calls=%async_computation.2 | async-start | bytes 393216 | tf_op jit(solution)/shard_map/all_to_all | solution.py:53

commit v8 on v6

--- a/solution.py
+++ b/solution.py
@@ -61,11 +61,17 @@
     return lax.dot_general(a, b, (((1,), (1,)), ((), ())), preferred_element_type=F32)
 
 
-def dot_tn(a, b):
-    return lax.dot_general(a, b, (((0,), (0,)), ((), ())), preferred_element_type=F32)
-
-
 def fill_windows(windows, value):
+    col = lax.broadcasted_iota(jnp.int32, (ROWS, 1), 0) % W
+    edge = jnp.zeros((W, 3 * C), BF)
+    windows[0:W, :] = edge
+    windows[W + ROWS : 2 * W + ROWS, :] = edge
+    left = jnp.where(col == 0, 0.0, pltpu.roll(value, 1, 0))
+    right = jnp.where(col == W - 1, 0.0, pltpu.roll(value, ROWS - 1, 0))
+    windows[W : W + ROWS, :] = jnp.concatenate([a.astype(BF) for a in (left, value, right)], axis=1)
+
+
+def fill_shifts(windows, value):
     col = lax.broadcasted_iota(jnp.int32, (ROWS, 1), 0) % W
     edge = jnp.zeros((W, C), BF)
     for d in range(3):
@@ -96,8 +102,7 @@
 def conv(windows, w_ref, bias):
     acc = jnp.zeros((ROWS, C), F32) + bias
     for a in range(3):
-        for b in range(3):
-            acc = acc + dot(windows[b, a * W : a * W + ROWS, :], tap(w_ref, 3 * a + b))
+        acc = acc + dot(windows[a * W : a * W + ROWS, :], w_ref[3 * a : 3 * a + 3].reshape(3 * C, C))
     return acc
 
 
@@ -135,7 +140,8 @@
     hidden_ref[...] = hidden
     slope_ref[...] = sig * (1.0 + spatial * (1.0 - sig))
     before, after = sides(place, cot_prev[...], cot_next[...], far[...])
-    grads = [dot_tn(hidden, other) for other in (after, cot[...].astype(BF), before)]
+    turned = hidden.T
+    grads = [dot(turned, other) for other in (after, cot[...].astype(BF), before)]
     pad = jnp.zeros((4, C), F32)
     for half in range(2):
         for y in range(4):
@@ -177,7 +183,7 @@
     gh = gh + dot_nt(before, tap(w_ref, 11))
     arrive[5].wait()
     gs = (gh * slope[...]).astype(BF).astype(F32)
-    fill_windows(windows, gs)
+    fill_shifts(windows, gs)
     arrive[6].wait()
     acc = cot[...]
     for a in range(3):
@@ -202,7 +208,8 @@
 
 FRAME_B = (ROWS, C), BF
 FRAME_F = (ROWS, C), F32
-WINDOWS = (3, ROWS + 2 * W, C), BF
+WINDOWS = (ROWS + 2 * W, 3 * C), BF
+SHIFTS = (3, ROWS + 2 * W, C), BF
 WEIGHTS = (TAPS, 2, HALF, C), BF
 SUMS = (4, 4, 2, 16, C), F32
 SHARE = (16, C), F32
@@ -239,16 +246,16 @@
     other = across(jnp.pad(quarter, ((0, SLOT - 3 * OWN), (0, WIDE - C))))
     w = jnp.pad(w.reshape(TAPS * OWN, C), ((0, 0), (0, WIDE - C)))
     other, cot_b, w = tie((other, cot_b, w))
+    far = lax.ppermute(cot_b, TM, FRAMES_FAR)
     cot_next = lax.ppermute(cot_b, TM, FRAMES_DOWN)
     cot_prev = lax.ppermute(cot_b, TM, FRAMES_UP)
-    far = lax.ppermute(cot_b, TM, FRAMES_FAR)
     own_m = to_all(jnp.concatenate([w, other], axis=0), "y")
     (oth_m,) = kernel_call(
         apart_kernel, [(own_m, "v")], [(((4 * SLOT, WIDE), BF), "v")], [], 0, 1000, "apart", 8,
     )
     oth_m = lax.all_gather(oth_m, "x")
     oth_m, own_m, video_w = tie((oth_m, own_m, video_f))
-    oth_m, cot_next, cot_prev, far = tie((oth_m, cot_next, cot_prev, far))
+    far, oth_m, cot_next, cot_prev = tie((far, oth_m, cot_next, cot_prev))
     (windows,) = kernel_call(prepare_kernel, [(video_w, "v")], [(WINDOWS, "v")], [], 0, 0.01, "prepare", 16)
     own_t, oth_t = core_swap(own_m), core_swap(oth_m)
 
@@ -263,9 +270,9 @@
     )
     part = (mine + core_swap(theirs)).astype(BF)
     part = lax.all_to_all(part.reshape(16, 2, 16, C), PLANE, 0, 0, tiled=True)
+    hidden_far = lax.ppermute(hidden, TM, FRAMES_FAR)
     prev = lax.ppermute(hidden, TM, FRAMES_UP)
     after = lax.ppermute(hidden, TM, FRAMES_DOWN)
-    hidden_far = lax.ppermute(hidden, TM, FRAMES_FAR)
     keep, give = kernel_call(
         split_kernel, [(place, "s"), (part, "v")], [(SHARE, "v"), (SHARE, "v")], [], 0, 1000, "split", 8,
     )
@@ -275,11 +282,11 @@
         backward_kernel,
         [(place, "s"), (w_all, "h"), (slope, "h"), (cot_f, "h"), (cot_prev, "h"), (cot_next, "h"), (far, "h")],
         [(FRAME_F, "v")],
-        [WEIGHTS, FRAME_F, FRAME_F, FRAME_B, FRAME_B, FRAME_B, WINDOWS], 7, 5, "backward",
+        [WEIGHTS, FRAME_F, FRAME_F, FRAME_B, FRAME_B, FRAME_B, SHIFTS], 7, 5, "backward",
     )
     other, grad_video = tie((other, grad_video))
     part = keep + other
-    part, video_f, prev, after, hidden_far = tie((part, video_f, prev, after, hidden_far))
+    hidden_far, part, video_f, prev, after = tie((hidden_far, part, video_f, prev, after))
     part = to_all(part, Z_LO)
     (output,) = kernel_call(
         output_kernel,

time: 141 us -> 143 us (1.014)
  the two profiles are of different devices: /device:TPU:8 before, /device:TPU:32 now
where the time goes in v8:
time: 143 us; the launch traced here: 142 us
  starting transfers between devices  72.4 us (51%)
  blocking collectives  22.8 us (16%)
  Pallas kernels  18.9 us (13%)
  waiting for transfers between devices  17.8 us (12%)
  other arithmetic  5.63 us (4%)
  local copies, waits for them, and re-layouts  3.57 us (2%)
    all_to_all x2, starting transfers between devices, to_all(): lax.all_to_all(jnp.broadcast_to(a[None], (n, *a.shape)), axes, 0, 0, tile...  24.8 us
    pallas_call x6, Pallas kernels, kernel_call(): pl.pallas_call(body, out_shape=tuple((jax.ShapeDtypeStruct(*o[0]) for o i...  18.9 us
    all_to_all x2, waiting for transfers between devices, to_all(): lax.all_to_all(jnp.broadcast_to(a[None], (n, *a.shape)), axes, 0, 0, tile...  15 us
    all_gather x1, blocking collectives, on_device(): oth_m = lax.all_gather(oth_m, 'x')  14.6 us
    ppermute x2, starting transfers between devices, across(): return lax.ppermute(a, ('m', 'k', 'h'), ACROSS)  13.8 us
    ppermute x1, starting transfers between devices, on_device(): after = lax.ppermute(hidden, TM, FRAMES_DOWN)  12.3 us
    all_to_all x1, blocking collectives, to_all(): lax.all_to_all(jnp.broadcast_to(a[None], (n, *a.shape)), axes, 0, 0, tile...  8.18 us
    ppermute x3, starting transfers between devices, core_swap(): return lax.ppermute(a, 'c', [(0, 1), (1, 0)])  6.6 us
  transfers between devices with their start and end apart: 14, of which 6 were waited for; matrix products, arithmetic and copies ran while one was open for 2% of the time, Pallas kernels for 9%

profile of v8, /device:TPU:32, one launch (start us, length us, event | category | flops | bytes accessed | tf_op | source)
XLA Modules:
  0.0 142.1 jit_solution(17773683584624324801)
XLA Ops:
  0.6 0.9 convert_element_type.14
  1.5 0.8 fusion
  2.4 11.8 %collective-permute-start = (bf16[64,384]{1,0:T(8,128)(2,1)S(1)}, bf16[64,384]{1,0:T(8,128)(2,1)S(1)}, u32[]{:S(2)}, u32[]{:S(2)}) collective-permute-start(bf16[64,384]{1,0:T(8,128)(2,1)S(1)} %pad.8), channel_id=1, source_target_pairs={{0,72},{16,88},{32,104},{48,120},{64,8},{80,24},{96,40},{112,56},{... | collective-permute-start | bytes 147464 | tf_op jit(solution)/shard_map/ppermute | solution.py:44
  14.3 1.9 %bitcast_convert_fusion = bf16[512,320]{1,0:T(8,128)(2,1)} fusion(f32[1,1,16,32,320]{4,3,2,1,0:T(8,128)} %param.9), kind=kLoop, calls=%fused_computation.8 | loop fusion | flops 163840 | bytes 983040 | tf_op jit(solution)/shard_map/convert_element_type | solution.py:243
  16.2 1.0 pad_maximum_fusion
  17.5 1.0 broadcast_in_dim.6
  18.5 4.5 %all-to-all-start = ((bf16[4,304,384]{2,1,0:T(8,128)(2,1)}), bf16[4,304,384]{2,1,0:T(8,128)(2,1)S(1)}, u32[]{:S(2)}, u32[]{:S(2)}) async-start(bf16[4,304,384]{2,1,0:T(8,128)(2,1)} %broadcast_in_dim.6), calls=%async_computation | async-start | bytes 1867776 | tf_op jit(solution)/shard_map/all_to_all | solution.py:53
  23.0 3.7 %collective-permute-start.4 = (bf16[512,320]{1,0:T(8,128)(2,1)}, bf16[512,320]{1,0:T(8,128)(2,1)}, u32[]{:S(2)}, u32[]{:S(2)}) collective-permute-start(bf16[512,320]{1,0:T(8,128)(2,1)} %bitcast_convert_fusion), channel_id=1, source_target_pairs={{0,16},{16,32},{32,48},{48,64},{64,80},{80,96},{96,112},{128,144},... | collective-permute-start | bytes 983048 | tf_op jit(solution)/shard_map/ppermute | solution.py:251
  26.7 2.9 %collective-permute-start.3 = (bf16[512,320]{1,0:T(8,128)(2,1)}, bf16[512,320]{1,0:T(8,128)(2,1)}, u32[]{:S(2)}, u32[]{:S(2)}) collective-permute-start(bf16[512,320]{1,0:T(8,128)(2,1)} %bitcast_convert_fusion), channel_id=1, source_target_pairs={{16,0},{32,16},{48,32},{64,48},{80,64},{96,80},{112,96},{144,128},... | collective-permute-start | bytes 983048 | tf_op jit(solution)/shard_map/ppermute | solution.py:250
  29.6 1.4 collective-permute-start.2
  31.0 5.4 %all-to-all-done.gathered.own_m = bf16[4,304,384]{2,1,0:T(8,128)(2,1)S(1)} async-done(((bf16[4,304,384]{2,1,0:T(8,128)(2,1)}), bf16[4,304,384]{2,1,0:T(8,128)(2,1)S(1)}, u32[]{:S(2)}, u32[]{:S(2)}) %all-to-all-start) | async-done | bytes 933920 | tf_op jit(solution)/shard_map/all_to_all | solution.py:53
  36.4 14.6 %all-gather = bf16[1024,384]{1,0:T(8,128)(2,1)S(1)} all-gather(bf16[256,384]{1,0:T(8,128)(2,1)S(1)} %apart.1), channel_id=2, replica_groups=mesh['x'=4,'m'=2,'k'=4,'h'=2,'y'=4,'c'=2] {'x'}, dimensions={0}, use_global_device_ids=true | all-gather | bytes 983040 | tf_op jit(solution)/shard_map/all_gather | solution.py:256
  51.0 1.9 %collective-permute-start.1 = (bf16[4,304,384]{2,1,0:T(8,128)(2,1)S(1)}, bf16[4,304,384]{2,1,0:T(8,128)(2,1)}, u32[]{:S(2)}, u32[]{:S(2)}) collective-permute-start(bf16[4,304,384]{2,1,0:T(8,128)(2,1)S(1)} %all-to-all-done.gathered.own_m), channel_id=1, source_target_pairs={{0,1},{1,0},{2,3},{3,2},{4,5},{5,4},{6,7},{7,6},{8,9},{9,8},{10,11... | collective-permute-start | bytes 2801672 | tf_op jit(solution)/shard_map/ppermute | solution.py:48
  53.0 2.4 %collective-permute-start.5 = (bf16[4,256,384]{2,1,0:T(8,128)(2,1)S(1)}, bf16[4,256,384]{2,1,0:T(8,128)(2,1)S(1)}, u32[]{:S(2)}, u32[]{:S(2)}) collective-permute-start(bf16[4,256,384]{2,1,0:T(8,128)(2,1)S(1)} %bitcast.12), channel_id=1, source_target_pairs={{0,1},{1,0},{2,3},{3,2},{4,5},{5,4},{6,7},{7,6},{8,9},{9,8},{10,11... | collective-permute-start | bytes 2359304 | tf_op jit(solution)/shard_map/ppermute | solution.py:48
  55.8 1.0 copy-done
  57.3 6.3 %forward.1 = (bf16[12,2,160,320]{3,2,1,0:T(8,128)(2,1)}, bf16[512,320]{1,0:T(8,128)(2,1)}, f32[512,320]{1,0:T(8,128)S(1)}, f32[4,4,2,16,320]{4,3,2,1,0:T(8,128)S(1)}, f32[4,4,2,16,320]{4,3,2,1,0:T(8,128)S(1)}) custom-call(s32[4]{0:T(128)S(1)} %pad_add_fusion.place, bf16[4,304,384]{2,1,0:T(8,128)(2,1)} %copy-done.1, ...), custom_call_target="tpu_custom_call" | custom-call | flops 10000000 | bytes 1000000 | tf_op jit(solution)/shard_map/forward/pallas_call | solution.py:221
  63.6 2.3 %collective-permute-start.7 = (f32[4,4,2,16,320]{4,3,2,1,0:T(8,128)S(1)}, f32[4,4,2,16,320]{4,3,2,1,0:T(8,128)S(1)}, u32[]{:S(2)}, u32[]{:S(2)}) collective-permute-start(f32[4,4,2,16,320]{4,3,2,1,0:T(8,128)S(1)} %get-tuple-element.43), channel_id=1, source_target_pairs={{0,1},{1,0},{2,3},{3,2},{4,5},{5,4},{6,7},{7,6},{8,9},{9,8},{10,11... | collective-permute-start | bytes 1966088 | tf_op jit(solution)/shard_map/ppermute | solution.py:48
  65.9 1.9 %collective-permute-done.7 = f32[4,4,2,16,320]{4,3,2,1,0:T(8,128)S(1)} collective-permute-done((f32[4,4,2,16,320]{4,3,2,1,0:T(8,128)S(1)}, f32[4,4,2,16,320]{4,3,2,1,0:T(8,128)S(1)}, u32[]{:S(2)}, u32[]{:S(2)}) %collective-permute-start.7) | collective-permute-done | bytes 655392 | tf_op jit(solution)/shard_map/ppermute | solution.py:48
  67.8 0.8 add_convert_fusion
  68.6 3.6 %all-to-all-start.1 = ((bf16[16,2,16,320]{3,2,1,0:T(8,128)(2,1)}), bf16[16,2,16,320]{3,2,1,0:T(8,128)(2,1)S(1)}, u32[]{:S(2)}, u32[]{:S(2)}) async-start(bf16[16,2,16,320]{3,2,1,0:T(8,128)(2,1)} %bitcast.7), calls=%async_computation.1 | async-start | bytes 786432 | tf_op jit(solution)/shard_map/all_to_all | solution.py:272
  72.3 12.3 %collective-permute-start.10 = (bf16[512,320]{1,0:T(8,128)(2,1)}, bf16[512,320]{1,0:T(8,128)(2,1)}, u32[]{:S(2)}, u32[]{:S(2)}) collective-permute-start(bf16[512,320]{1,0:T(8,128)(2,1)} %get-tuple-element.41.hidden_h), channel_id=1, source_target_pairs={{16,0},{32,16},{48,32},{64,48},{80,64},{96,80},{112,96},{144,128},... | collective-permute-start | bytes 983048 | tf_op jit(solution)/shard_map/ppermute | solution.py:275
  84.6 1.9 %collective-permute-start.9 = (bf16[512,320]{1,0:T(8,128)(2,1)}, bf16[512,320]{1,0:T(8,128)(2,1)}, u32[]{:S(2)}, u32[]{:S(2)}) collective-permute-start(bf16[512,320]{1,0:T(8,128)(2,1)} %get-tuple-element.41.hidden_h), channel_id=1, source_target_pairs={{0,16},{16,32},{32,48},{48,64},{64,80},{80,96},{96,112},{128,144},... | collective-permute-start | bytes 983048 | tf_op jit(solution)/shard_map/ppermute | solution.py:274
  86.5 1.4 collective-permute-start.6
  87.9 0.6 split.1
  88.5 1.9 %collective-permute-start.8 = (f32[16,320]{1,0:T(8,128)S(1)}, f32[16,320]{1,0:T(8,128)S(1)}, u32[]{:S(2)}, u32[]{:S(2)}) collective-permute-start(f32[16,320]{1,0:T(8,128)S(1)} %get-tuple-element.47), channel_id=1, source_target_pairs={{0,72},{16,88},{32,104},{48,120},{64,8},{80,24},{96,40},{112,56},{... | collective-permute-start | bytes 61448 | tf_op jit(solution)/shard_map/ppermute | solution.py:44
  90.5 7.5 %backward.1 = f32[512,320]{1,0:T(8,128)} custom-call(s32[4]{0:T(128)} %copy-done.3, bf16[12,2,160,320]{3,2,1,0:T(8,128)(2,1)} %get-tuple-element.48.w_h, f32[512,320]{1,0:T(8,128)} %copy-done.4, f32[512,320]{1,0:T(8,128)} %bitcast.17, bf16[512,320]{1,0:T(8,128)(2,1)} %collective-permute-done.4.cot_prev.prev_h, ...), custom_call_target="tpu_custom_call" | custom-call | flops 5000000000 | bytes 1000000 | tf_op jit(solution)/shard_map/backward/pallas_call | solution.py:221
  98.3 0.7 broadcast_in_dim.7
  99.0 20.3 %all-to-all-start.2 = ((f32[8,16,320]{2,1,0:T(8,128)}), f32[8,16,320]{2,1,0:T(8,128)S(1)}, u32[]{:S(2)}, u32[]{:S(2)}) async-start(f32[8,16,320]{2,1,0:T(8,128)} %broadcast_in_dim.7), calls=%async_computation.2 | async-start | bytes 393216 | tf_op jit(solution)/shard_map/all_to_all | solution.py:53
  119.3 4.3 %output.1 = f32[512,320]{1,0:T(8,128)} custom-call(s32[4]{0:T(128)} %copy-done.3, bf16[12,2,160,320]{3,2,1,0:T(8,128)(2,1)} %get-tuple-element.48.w_h, f32[512,320]{1,0:T(8,128)} %bitcast.14, bf16[512,320]{1,0:T(8,128)(2,1)} %get-tuple-element.41.hidden_h, bf16[512,320]{1,0:T(8,128)(2,1)} %collective-permute-done.9.prev_h, ...), custom_call_target="tpu_custom_call" | custom-call | flops 3000000000 | bytes 1000000 | tf_op jit(solution)/shard_map/output/pallas_call | solution.py:221
  123.6 9.6 %all-to-all-done.2 = f32[8,16,320]{2,1,0:T(8,128)S(1)} async-done(((f32[8,16,320]{2,1,0:T(8,128)}), f32[8,16,320]{2,1,0:T(8,128)S(1)}, u32[]{:S(2)}, u32[]{:S(2)}) %all-to-all-start.2) | async-done | bytes 163872 | tf_op jit(solution)/shard_map/all_to_all | solution.py:53
  133.2 8.2 %all_to_all.20 = f32[4,16,320]{2,1,0:T(8,128)S(1)} all-to-all(f32[4,16,320]{2,1,0:T(8,128)S(1)} %broadcast_in_dim.8), channel_id=1, replica_groups=mesh['x'=4,'m'=2,'k'=4,'h'=2,'y'=4,'c'=2] {'x'}, dimensions={0} | all-to-all | bytes 163840 | tf_op jit(solution)/shard_map/all_to_all | solution.py:53
  141.4 0.7 mul.19
  (35 shorter events, 1.5 us)
Async XLA Ops:
  2.4 15.0 %collective-permute-start = (bf16[64,384]{1,0:T(8,128)(2,1)S(1)}, bf16[64,384]{1,0:T(8,128)(2,1)S(1)}, u32[]{:S(2)}, u32[]{:S(2)}) collective-permute-start(bf16[64,384]{1,0:T(8,128)(2,1)S(1)} %pad.8), channel_id=1, source_target_pairs={{0,72},{16,88},{32,104},{48,120},{64,8},{80,24},{96,40},{112,56},{... | collective-permute-start | bytes 147464 | tf_op jit(solution)/shard_map/ppermute | solution.py:44
  18.5 17.9 %all-to-all-start = ((bf16[4,304,384]{2,1,0:T(8,128)(2,1)}), bf16[4,304,384]{2,1,0:T(8,128)(2,1)S(1)}, u32[]{:S(2)}, u32[]{:S(2)}) async-start(bf16[4,304,384]{2,1,0:T(8,128)(2,1)} %broadcast_in_dim.6), calls=%async_computation | async-start | bytes 1867776 | tf_op jit(solution)/shard_map/all_to_all | solution.py:53
  23.0 30.0 %collective-permute-start.4 = (bf16[512,320]{1,0:T(8,128)(2,1)}, bf16[512,320]{1,0:T(8,128)(2,1)}, u32[]{:S(2)}, u32[]{:S(2)}) collective-permute-start(bf16[512,320]{1,0:T(8,128)(2,1)} %bitcast_convert_fusion), channel_id=1, source_target_pairs={{0,16},{16,32},{32,48},{48,64},{64,80},{80,96},{96,112},{128,144},... | collective-permute-start | bytes 983048 | tf_op jit(solution)/shard_map/ppermute | solution.py:251
  26.7 26.3 %collective-permute-start.3 = (bf16[512,320]{1,0:T(8,128)(2,1)}, bf16[512,320]{1,0:T(8,128)(2,1)}, u32[]{:S(2)}, u32[]{:S(2)}) collective-permute-start(bf16[512,320]{1,0:T(8,128)(2,1)} %bitcast_convert_fusion), channel_id=1, source_target_pairs={{16,0},{32,16},{48,32},{64,48},{80,64},{96,80},{112,96},{144,128},... | collective-permute-start | bytes 983048 | tf_op jit(solution)/shard_map/ppermute | solution.py:250
  29.6 23.4 %collective-permute-start.2 = (bf16[512,320]{1,0:T(8,128)(2,1)}, bf16[512,320]{1,0:T(8,128)(2,1)}, u32[]{:S(2)}, u32[]{:S(2)}) collective-permute-start(bf16[512,320]{1,0:T(8,128)(2,1)} %bitcast_convert_fusion), channel_id=1, source_target_pairs={{112,128},{128,112},{240,256},{256,240},{368,384},{384,368},{113,1... | collective-permute-start | bytes 983048 | tf_op jit(solution)/shard_map/ppermute | solution.py:249
  36.4 14.6 %copy-start.1 = (bf16[4,304,384]{2,1,0:T(8,128)(2,1)}, bf16[4,304,384]{2,1,0:T(8,128)(2,1)S(1)}, u32[]{:S(2)}) copy-start(bf16[4,304,384]{2,1,0:T(8,128)(2,1)S(1)} %all-to-all-done.gathered.own_m) | copy-start | bytes 2801668
  36.4 19.0 %copy-start.5 = (f32[320]{0:T(512)S(1)}, f32[320]{0:T(512)}, u32[]{:S(2)}) copy-start(f32[320]{0:T(512)} %param.7) | copy-start | bytes 3844
  36.4 19.1 %copy-start.2 = (f32[1,1,16,32,320]{4,3,2,1,0:T(8,128)S(1)}, f32[1,1,16,32,320]{4,3,2,1,0:T(8,128)}, u32[]{:S(2)}) copy-start(f32[1,1,16,32,320]{4,3,2,1,0:T(8,128)} %param.5) | copy-start | bytes 1966084
  51.0 6.3 %collective-permute-start.1 = (bf16[4,304,384]{2,1,0:T(8,128)(2,1)S(1)}, bf16[4,304,384]{2,1,0:T(8,128)(2,1)}, u32[]{:S(2)}, u32[]{:S(2)}) collective-permute-start(bf16[4,304,384]{2,1,0:T(8,128)(2,1)S(1)} %all-to-all-done.gathered.own_m), channel_id=1, source_target_pairs={{0,1},{1,0},{2,3},{3,2},{4,5},{5,4},{6,7},{7,6},{8,9},{9,8},{10,11... | collective-permute-start | bytes 2801672 | tf_op jit(solution)/shard_map/ppermute | solution.py:48
  53.0 4.3 %collective-permute-start.5 = (bf16[4,256,384]{2,1,0:T(8,128)(2,1)S(1)}, bf16[4,256,384]{2,1,0:T(8,128)(2,1)S(1)}, u32[]{:S(2)}, u32[]{:S(2)}) collective-permute-start(bf16[4,256,384]{2,1,0:T(8,128)(2,1)S(1)} %bitcast.12), channel_id=1, source_target_pairs={{0,1},{1,0},{2,3},{3,2},{4,5},{5,4},{6,7},{7,6},{8,9},{9,8},{10,11... | collective-permute-start | bytes 2359304 | tf_op jit(solution)/shard_map/ppermute | solution.py:48
  55.5 32.4 %copy-start.3 = (s32[4]{0:T(128)}, s32[4]{0:T(128)S(1)}, u32[]{:S(2)}) copy-start(s32[4]{0:T(128)S(1)} %pad_add_fusion.place) | copy-start | bytes 52
  55.8 1.0 copy-start
  63.6 5.0 %copy-start.4 = (f32[512,320]{1,0:T(8,128)}, f32[512,320]{1,0:T(8,128)S(1)}, u32[]{:S(2)}) copy-start(f32[512,320]{1,0:T(8,128)S(1)} %get-tuple-element.49.slope_h) | copy-start | bytes 1966084
  63.6 4.2 %collective-permute-start.7 = (f32[4,4,2,16,320]{4,3,2,1,0:T(8,128)S(1)}, f32[4,4,2,16,320]{4,3,2,1,0:T(8,128)S(1)}, u32[]{:S(2)}, u32[]{:S(2)}) collective-permute-start(f32[4,4,2,16,320]{4,3,2,1,0:T(8,128)S(1)} %get-tuple-element.43), channel_id=1, source_target_pairs={{0,1},{1,0},{2,3},{3,2},{4,5},{5,4},{6,7},{7,6},{8,9},{9,8},{10,11... | collective-permute-start | bytes 1966088 | tf_op jit(solution)/shard_map/ppermute | solution.py:48
  68.6 19.3 %all-to-all-start.1 = ((bf16[16,2,16,320]{3,2,1,0:T(8,128)(2,1)}), bf16[16,2,16,320]{3,2,1,0:T(8,128)(2,1)S(1)}, u32[]{:S(2)}, u32[]{:S(2)}) async-start(bf16[16,2,16,320]{3,2,1,0:T(8,128)(2,1)} %bitcast.7), calls=%async_computation.1 | async-start | bytes 786432 | tf_op jit(solution)/shard_map/all_to_all | solution.py:272
  72.3 26.0 %collective-permute-start.10 = (bf16[512,320]{1,0:T(8,128)(2,1)}, bf16[512,320]{1,0:T(8,128)(2,1)}, u32[]{:S(2)}, u32[]{:S(2)}) collective-permute-start(bf16[512,320]{1,0:T(8,128)(2,1)} %get-tuple-element.41.hidden_h), channel_id=1, source_target_pairs={{16,0},{32,16},{48,32},{64,48},{80,64},{96,80},{112,96},{144,128},... | collective-permute-start | bytes 983048 | tf_op jit(solution)/shard_map/ppermute | solution.py:275
  84.6 13.7 %collective-permute-start.9 = (bf16[512,320]{1,0:T(8,128)(2,1)}, bf16[512,320]{1,0:T(8,128)(2,1)}, u32[]{:S(2)}, u32[]{:S(2)}) collective-permute-start(bf16[512,320]{1,0:T(8,128)(2,1)} %get-tuple-element.41.hidden_h), channel_id=1, source_target_pairs={{0,16},{16,32},{32,48},{48,64},{64,80},{80,96},{96,112},{128,144},... | collective-permute-start | bytes 983048 | tf_op jit(solution)/shard_map/ppermute | solution.py:274
  86.5 11.8 %collective-permute-start.6 = (bf16[512,320]{1,0:T(8,128)(2,1)}, bf16[512,320]{1,0:T(8,128)(2,1)}, u32[]{:S(2)}, u32[]{:S(2)}) collective-permute-start(bf16[512,320]{1,0:T(8,128)(2,1)} %get-tuple-element.41.hidden_h), channel_id=1, source_target_pairs={{112,128},{128,112},{240,256},{256,240},{368,384},{384,368},{113,1... | collective-permute-start | bytes 983048 | tf_op jit(solution)/shard_map/ppermute | solution.py:273
  88.5 9.7 %collective-permute-start.8 = (f32[16,320]{1,0:T(8,128)S(1)}, f32[16,320]{1,0:T(8,128)S(1)}, u32[]{:S(2)}, u32[]{:S(2)}) collective-permute-start(f32[16,320]{1,0:T(8,128)S(1)} %get-tuple-element.47), channel_id=1, source_target_pairs={{0,72},{16,88},{32,104},{48,120},{64,8},{80,24},{96,40},{112,56},{... | collective-permute-start | bytes 61448 | tf_op jit(solution)/shard_map/ppermute | solution.py:44
  99.0 34.2 %all-to-all-start.2 = ((f32[8,16,320]{2,1,0:T(8,128)}), f32[8,16,320]{2,1,0:T(8,128)S(1)}, u32[]{:S(2)}, u32[]{:S(2)}) async-start(f32[8,16,320]{2,1,0:T(8,128)} %broadcast_in_dim.7), calls=%async_computation.2 | async-start | bytes 393216 | tf_op jit(solution)/shard_map/all_to_all | solution.py:53

commit v9 on v8

--- a/solution.py
+++ b/solution.py
@@ -192,17 +192,24 @@
     grad_ref[...] = acc
 
 
+def middle_kernel(w_h, video_h, hidden_h, out_h, w_ref, video, hidden, out, sems):
+    for one in copies(sems, (w_h.at[SPACE + 1], w_ref), (video_h, video), (hidden_h, hidden)):
+        one.wait()
+    out[...] = video[...] + dot(hidden[...], w_ref[...].reshape(C, C))
+    for one in copies(sems, (out, out_h)):
+        one.wait()
+
+
 def output_kernel(
-    place, w_h, video_h, hidden_h, prev_h, after_h, far_h, out_ref,
-    w_ref, video, hidden, prev, after, far, sems,
+    place, w_h, part_h, prev_h, after_h, far_h, out_ref,
+    w_ref, part, prev, after, far, sems,
 ):
     for one in copies(
-        sems, (w_h.at[SPACE:TAPS], w_ref), (video_h, video), (hidden_h, hidden), (prev_h, prev), (after_h, after), (far_h, far),
+        sems, (w_h.at[SPACE:TAPS], w_ref), (part_h, part), (prev_h, prev), (after_h, after), (far_h, far),
     ):
         one.wait()
     before, behind = sides(place, prev[...], after[...], far[...])
-    acc = video[...] + dot(hidden[...], tap(w_ref, 1))
-    acc = acc + dot(before, tap(w_ref, 0))
+    acc = part[...] + dot(before, tap(w_ref, 0))
     out_ref[...] = acc + dot(behind, tap(w_ref, 2))
 
 
@@ -255,7 +262,7 @@
     )
     oth_m = lax.all_gather(oth_m, "x")
     oth_m, own_m, video_w = tie((oth_m, own_m, video_f))
-    far, oth_m, cot_next, cot_prev = tie((far, oth_m, cot_next, cot_prev))
+    oth_m, cot_next, cot_prev, far = tie((oth_m, cot_next, cot_prev, far))
     (windows,) = kernel_call(prepare_kernel, [(video_w, "v")], [(WINDOWS, "v")], [], 0, 0.01, "prepare", 16)
     own_t, oth_t = core_swap(own_m), core_swap(oth_m)
 
@@ -270,31 +277,35 @@
     )
     part = (mine + core_swap(theirs)).astype(BF)
     part = lax.all_to_all(part.reshape(16, 2, 16, C), PLANE, 0, 0, tiled=True)
-    hidden_far = lax.ppermute(hidden, TM, FRAMES_FAR)
     prev = lax.ppermute(hidden, TM, FRAMES_UP)
     after = lax.ppermute(hidden, TM, FRAMES_DOWN)
     keep, give = kernel_call(
         split_kernel, [(place, "s"), (part, "v")], [(SHARE, "v"), (SHARE, "v")], [], 0, 1000, "split", 8,
     )
-    give, slope = tie((give, slope))
+    give, hidden = tie((give, hidden))
     other = across(give)
+    hidden_far = lax.ppermute(hidden, TM, FRAMES_FAR)
+    (middle,) = kernel_call(
+        middle_kernel, [(w_all, "h"), (video_f, "h"), (hidden, "h")], [(FRAME_F, "h")],
+        [((2, HALF, C), BF), FRAME_F, FRAME_B, FRAME_F], 3, 1000, "middle",
+    )
+    other, middle, prev, after, slope = tie((other, middle, prev, after, slope))
+    part = to_all((keep + other).astype(BF), Z_LO)
     (grad_video,) = kernel_call(
         backward_kernel,
         [(place, "s"), (w_all, "h"), (slope, "h"), (cot_f, "h"), (cot_prev, "h"), (cot_next, "h"), (far, "h")],
         [(FRAME_F, "v")],
-        [WEIGHTS, FRAME_F, FRAME_F, FRAME_B, FRAME_B, FRAME_B, SHIFTS], 7, 5, "backward",
-    )
-    other, grad_video = tie((other, grad_video))
-    part = keep + other
-    hidden_far, part, video_f, prev, after = tie((hidden_far, part, video_f, prev, after))
-    part = to_all(part, Z_LO)
+        [WEIGHTS, FRAME_F, FRAME_F, FRAME_B, FRAME_B, FRAME_B, SHIFTS], 7, 0.01, "backward",
+    )
+    middle, grad_video, hidden_far = tie((middle, grad_video, hidden_far))
     (output,) = kernel_call(
         output_kernel,
-        [(place, "s"), (w_all, "h"), (video_f, "h"), (hidden, "h"), (prev, "h"), (after, "h"), (hidden_far, "h")],
+        [(place, "s"), (w_all, "h"), (middle, "h"), (prev, "h"), (after, "h"), (hidden_far, "h")],
         [(FRAME_F, "v")],
-        [((3, 2, HALF, C), BF), FRAME_F, FRAME_B, FRAME_B, FRAME_B, FRAME_B], 6, 3, "output",
+        [((3, 2, HALF, C), BF), FRAME_F, FRAME_B, FRAME_B, FRAME_B], 5, 0.01, "output",
     )
     part, output = tie((part, output))
+    part = part.astype(F32)
     part = jnp.sum(part, axis=0)
     part = to_all(part, "x").reshape(4 * 16, C)
     total_rows = ROWS * lax.axis_size(TM) * lax.axis_size(CLIP)

time: 143 us -> 130 us (0.909)
  starting transfers between devices: 72.4 us -> 57.7 us
  waiting for transfers between devices: 17.8 us -> 13.9 us
  Pallas kernels: 18.9 us -> 21.8 us
    all_to_all x2, starting transfers between devices: 24.8 us -> 14 us  [to_all(): lax.all_to_all(jnp.broadcast_to(a[None], (n, *a.shape)), axes, 0, 0, tile...]
    all_to_all x2, waiting for transfers between devices: 15 us -> 5.43 us  [to_all(): lax.all_to_all(jnp.broadcast_to(a[None], (n, *a.shape)), axes, 0, 0, tile...]
    ppermute x1, starting transfers between devices: 12.3 us -> 4.03 us  [on_device(): after = lax.ppermute(hidden, TM, FRAMES_DOWN)]
    all_to_all x1, waiting for transfers between devices: 0.01 us -> 4.38 us  [on_device(): part = lax.all_to_all(part.reshape(16, 2, 16, C), PLANE, 0, 0, tiled=True)]
    pallas_call x6 -> x7, Pallas kernels: 18.9 us -> 21.8 us  [kernel_call(): pl.pallas_call(body, out_shape=tuple((jax.ShapeDtypeStruct(*o[0]) for o i...]
    ppermute x2, starting transfers between devices: 13.8 us -> 16.1 us  [across(): return lax.ppermute(a, ('m', 'k', 'h'), ACROSS)]
    all_to_all x1, starting transfers between devices: 3.64 us -> 5.63 us  [on_device(): part = lax.all_to_all(part.reshape(16, 2, 16, C), PLANE, 0, 0, tiled=True)]
  transfers between devices with their start and end apart: 14 -> 14, of which waited for: 6 -> 6; matrix products, arithmetic and copies ran while one was open for 2% -> 3% of each run, Pallas kernels for 9% -> 12%
where the time goes in v9:
time: 130 us; the launch traced here: 129 us
  starting transfers between devices  57.7 us (44%)
  blocking collectives  24.2 us (19%)
  Pallas kernels  21.8 us (17%)
  waiting for transfers between devices  13.9 us (11%)
  other arithmetic  6.38 us (5%)
  local copies, waits for them, and re-layouts  4.39 us (3%)
    pallas_call x7, Pallas kernels, kernel_call(): pl.pallas_call(body, out_shape=tuple((jax.ShapeDtypeStruct(*o[0]) for o i...  21.8 us
    ppermute x2, starting transfers between devices, across(): return lax.ppermute(a, ('m', 'k', 'h'), ACROSS)  16.1 us
    all_gather x1, blocking collectives, on_device(): oth_m = lax.all_gather(oth_m, 'x')  14.6 us
    all_to_all x2, starting transfers between devices, to_all(): lax.all_to_all(jnp.broadcast_to(a[None], (n, *a.shape)), axes, 0, 0, tile...  14 us
    all_to_all x1, blocking collectives, to_all(): lax.all_to_all(jnp.broadcast_to(a[None], (n, *a.shape)), axes, 0, 0, tile...  9.6 us
    ppermute x3, starting transfers between devices, core_swap(): return lax.ppermute(a, 'c', [(0, 1), (1, 0)])  6.59 us
    all_to_all x1, starting transfers between devices, on_device(): part = lax.all_to_all(part.reshape(16, 2, 16, C), PLANE, 0, 0, tiled=True)  5.63 us
    all_to_all x2, waiting for transfers between devices, to_all(): lax.all_to_all(jnp.broadcast_to(a[None], (n, *a.shape)), axes, 0, 0, tile...  5.43 us
  transfers between devices with their start and end apart: 14, of which 6 were waited for; matrix products, arithmetic and copies ran while one was open for 3% of the time, Pallas kernels for 12%

profile of v9, /device:TPU:32, one launch (start us, length us, event | category | flops | bytes accessed | tf_op | source)
XLA Modules:
  0.0 129.3 jit_solution(15909936550313282875)
XLA Ops:
  0.6 0.9 convert_element_type.20
  2.4 11.8 %collective-permute-start = (bf16[64,384]{1,0:T(8,128)(2,1)S(1)}, bf16[64,384]{1,0:T(8,128)(2,1)S(1)}, u32[]{:S(2)}, u32[]{:S(2)}) collective-permute-start(bf16[64,384]{1,0:T(8,128)(2,1)S(1)} %pad.8), channel_id=1, source_target_pairs={{0,72},{16,88},{32,104},{48,120},{64,8},{80,24},{96,40},{112,56},{... | collective-permute-start | bytes 147464 | tf_op jit(solution)/shard_map/ppermute | solution.py:44
  14.3 1.9 %bitcast_convert_fusion = bf16[512,320]{1,0:T(8,128)(2,1)} fusion(f32[1,1,16,32,320]{4,3,2,1,0:T(8,128)} %param.9), kind=kLoop, calls=%fused_computation.10 | loop fusion | flops 163840 | bytes 983040 | tf_op jit(solution)/shard_map/convert_element_type | solution.py:250
  16.2 1.0 pad_maximum_fusion
  17.5 1.0 broadcast_in_dim.6
  18.5 4.5 %all-to-all-start = ((bf16[4,304,384]{2,1,0:T(8,128)(2,1)}), bf16[4,304,384]{2,1,0:T(8,128)(2,1)S(1)}, u32[]{:S(2)}, u32[]{:S(2)}) async-start(bf16[4,304,384]{2,1,0:T(8,128)(2,1)} %broadcast_in_dim.6), calls=%async_computation | async-start | bytes 1867776 | tf_op jit(solution)/shard_map/all_to_all | solution.py:53
  23.0 1.4 %collective-permute-start.4 = (bf16[512,320]{1,0:T(8,128)(2,1)}, bf16[512,320]{1,0:T(8,128)(2,1)}, u32[]{:S(2)}, u32[]{:S(2)}) collective-permute-start(bf16[512,320]{1,0:T(8,128)(2,1)} %bitcast_convert_fusion), channel_id=1, source_target_pairs={{112,128},{128,112},{240,256},{256,240},{368,384},{384,368},{113,1... | collective-permute-start | bytes 983048 | tf_op jit(solution)/shard_map/ppermute | solution.py:256
  24.4 3.7 %collective-permute-start.3 = (bf16[512,320]{1,0:T(8,128)(2,1)}, bf16[512,320]{1,0:T(8,128)(2,1)}, u32[]{:S(2)}, u32[]{:S(2)}) collective-permute-start(bf16[512,320]{1,0:T(8,128)(2,1)} %bitcast_convert_fusion), channel_id=1, source_target_pairs={{0,16},{16,32},{32,48},{48,64},{64,80},{80,96},{96,112},{128,144},... | collective-permute-start | bytes 983048 | tf_op jit(solution)/shard_map/ppermute | solution.py:258
  28.1 2.9 %collective-permute-start.2 = (bf16[512,320]{1,0:T(8,128)(2,1)}, bf16[512,320]{1,0:T(8,128)(2,1)}, u32[]{:S(2)}, u32[]{:S(2)}) collective-permute-start(bf16[512,320]{1,0:T(8,128)(2,1)} %bitcast_convert_fusion), channel_id=1, source_target_pairs={{16,0},{32,16},{48,32},{64,48},{80,64},{96,80},{112,96},{144,128},... | collective-permute-start | bytes 983048 | tf_op jit(solution)/shard_map/ppermute | solution.py:257
  31.0 5.4 %all-to-all-done.gathered.own_m = bf16[4,304,384]{2,1,0:T(8,128)(2,1)S(1)} async-done(((bf16[4,304,384]{2,1,0:T(8,128)(2,1)}), bf16[4,304,384]{2,1,0:T(8,128)(2,1)S(1)}, u32[]{:S(2)}, u32[]{:S(2)}) %all-to-all-start) | async-done | bytes 933920 | tf_op jit(solution)/shard_map/all_to_all | solution.py:53
  36.4 14.6 %all-gather = bf16[1024,384]{1,0:T(8,128)(2,1)S(1)} all-gather(bf16[256,384]{1,0:T(8,128)(2,1)S(1)} %apart.1), channel_id=2, replica_groups=mesh['x'=4,'m'=2,'k'=4,'h'=2,'y'=4,'c'=2] {'x'}, dimensions={0}, use_global_device_ids=true | all-gather | bytes 983040 | tf_op jit(solution)/shard_map/all_gather | solution.py:263
  51.0 1.9 %collective-permute-start.1 = (bf16[4,304,384]{2,1,0:T(8,128)(2,1)S(1)}, bf16[4,304,384]{2,1,0:T(8,128)(2,1)}, u32[]{:S(2)}, u32[]{:S(2)}) collective-permute-start(bf16[4,304,384]{2,1,0:T(8,128)(2,1)S(1)} %all-to-all-done.gathered.own_m), channel_id=1, source_target_pairs={{0,1},{1,0},{2,3},{3,2},{4,5},{5,4},{6,7},{7,6},{8,9},{9,8},{10,11... | collective-permute-start | bytes 2801672 | tf_op jit(solution)/shard_map/ppermute | solution.py:48
  53.0 2.4 %collective-permute-start.5 = (bf16[4,256,384]{2,1,0:T(8,128)(2,1)S(1)}, bf16[4,256,384]{2,1,0:T(8,128)(2,1)S(1)}, u32[]{:S(2)}, u32[]{:S(2)}) collective-permute-start(bf16[4,256,384]{2,1,0:T(8,128)(2,1)S(1)} %bitcast.12), channel_id=1, source_target_pairs={{0,1},{1,0},{2,3},{3,2},{4,5},{5,4},{6,7},{7,6},{8,9},{9,8},{10,11... | collective-permute-start | bytes 2359304 | tf_op jit(solution)/shard_map/ppermute | solution.py:48
  55.8 1.0 copy-done
  57.3 6.3 %forward.1 = (bf16[12,2,160,320]{3,2,1,0:T(8,128)(2,1)}, bf16[512,320]{1,0:T(8,128)(2,1)}, f32[512,320]{1,0:T(8,128)S(1)}, f32[4,4,2,16,320]{4,3,2,1,0:T(8,128)S(1)}, f32[4,4,2,16,320]{4,3,2,1,0:T(8,128)S(1)}) custom-call(s32[4]{0:T(128)S(1)} %pad_add_fusion.place, bf16[4,304,384]{2,1,0:T(8,128)(2,1)} %copy-done.1, ...), custom_call_target="tpu_custom_call" | custom-call | flops 10000000 | bytes 1000000 | tf_op jit(solution)/shard_map/forward/pallas_call | solution.py:228
  63.6 0.9 copy-done.2
  64.4 2.3 %collective-permute-start.6 = (f32[4,4,2,16,320]{4,3,2,1,0:T(8,128)S(1)}, f32[4,4,2,16,320]{4,3,2,1,0:T(8,128)S(1)}, u32[]{:S(2)}, u32[]{:S(2)}) collective-permute-start(f32[4,4,2,16,320]{4,3,2,1,0:T(8,128)S(1)} %get-tuple-element.43), channel_id=1, source_target_pairs={{0,1},{1,0},{2,3},{3,2},{4,5},{5,4},{6,7},{7,6},{8,9},{9,8},{10,11... | collective-permute-start | bytes 1966088 | tf_op jit(solution)/shard_map/ppermute | solution.py:48
  66.7 1.9 %collective-permute-done.6 = f32[4,4,2,16,320]{4,3,2,1,0:T(8,128)S(1)} collective-permute-done((f32[4,4,2,16,320]{4,3,2,1,0:T(8,128)S(1)}, f32[4,4,2,16,320]{4,3,2,1,0:T(8,128)S(1)}, u32[]{:S(2)}, u32[]{:S(2)}) %collective-permute-start.6) | collective-permute-done | bytes 655392 | tf_op jit(solution)/shard_map/ppermute | solution.py:48
  68.6 0.8 add_convert_fusion
  69.5 5.6 %all-to-all-start.1 = ((bf16[16,2,16,320]{3,2,1,0:T(8,128)(2,1)}), bf16[16,2,16,320]{3,2,1,0:T(8,128)(2,1)S(1)}, u32[]{:S(2)}, u32[]{:S(2)}) async-start(bf16[16,2,16,320]{3,2,1,0:T(8,128)(2,1)} %bitcast.7), calls=%async_computation.1 | async-start | bytes 786432 | tf_op jit(solution)/shard_map/all_to_all | solution.py:279
  75.1 4.0 %collective-permute-start.9 = (bf16[512,320]{1,0:T(8,128)(2,1)}, bf16[512,320]{1,0:T(8,128)(2,1)}, u32[]{:S(2)}, u32[]{:S(2)}) collective-permute-start(bf16[512,320]{1,0:T(8,128)(2,1)} %get-tuple-element.49.hidden_h), channel_id=1, source_target_pairs={{16,0},{32,16},{48,32},{64,48},{80,64},{96,80},{112,96},{144,128},... | collective-permute-start | bytes 983048 | tf_op jit(solution)/shard_map/ppermute | solution.py:281
  79.1 1.9 %collective-permute-start.8 = (bf16[512,320]{1,0:T(8,128)(2,1)}, bf16[512,320]{1,0:T(8,128)(2,1)}, u32[]{:S(2)}, u32[]{:S(2)}) collective-permute-start(bf16[512,320]{1,0:T(8,128)(2,1)} %get-tuple-element.49.hidden_h), channel_id=1, source_target_pairs={{0,16},{16,32},{32,48},{48,64},{64,80},{80,96},{96,112},{128,144},... | collective-permute-start | bytes 983048 | tf_op jit(solution)/shard_map/ppermute | solution.py:280
  81.1 4.4 %all-to-all-done.1.parts = bf16[16,2,16,320]{3,2,1,0:T(8,128)(2,1)S(1)} async-done(((bf16[16,2,16,320]{3,2,1,0:T(8,128)(2,1)}), bf16[16,2,16,320]{3,2,1,0:T(8,128)(2,1)S(1)}, u32[]{:S(2)}, u32[]{:S(2)}) %all-to-all-start.1) | async-done | bytes 327712 | tf_op jit(solution)/shard_map/all_to_all | solution.py:279
  85.5 1.2 split.1
  86.7 4.3 %collective-permute-start.7 = (f32[16,320]{1,0:T(8,128)}, f32[16,320]{1,0:T(8,128)}, u32[]{:S(2)}, u32[]{:S(2)}) collective-permute-start(f32[16,320]{1,0:T(8,128)} %get-tuple-element.47), channel_id=1, source_target_pairs={{0,72},{16,88},{32,104},{48,120},{64,8},{80,24},{96,40},{112,56},{... | collective-permute-start | bytes 61448 | tf_op jit(solution)/shard_map/ppermute | solution.py:44
  90.9 1.4 %collective-permute-start.10 = (bf16[512,320]{1,0:T(8,128)(2,1)}, bf16[512,320]{1,0:T(8,128)(2,1)}, u32[]{:S(2)}, u32[]{:S(2)}) collective-permute-start(bf16[512,320]{1,0:T(8,128)(2,1)} %get-tuple-element.49.hidden_h), channel_id=1, source_target_pairs={{112,128},{128,112},{240,256},{256,240},{368,384},{384,368},{113,1... | collective-permute-start | bytes 983048 | tf_op jit(solution)/shard_map/ppermute | solution.py:287
  92.4 2.7 %middle.1.part_h = f32[512,320]{1,0:T(8,128)} custom-call(bf16[12,2,160,320]{3,2,1,0:T(8,128)(2,1)} %get-tuple-element.48.w_h, f32[512,320]{1,0:T(8,128)} %bitcast.14, bf16[512,320]{1,0:T(8,128)(2,1)} %get-tuple-element.49.hidden_h), custom_call_target="tpu_custom_call" | custom-call | flops 999999995904 | bytes 1000000 | tf_op jit(solution)/shard_map/middle/pallas_call | solution.py:228
  95.1 1.5 %collective-permute-done.7 = f32[16,320]{1,0:T(8,128)} collective-permute-done((f32[16,320]{1,0:T(8,128)}, f32[16,320]{1,0:T(8,128)}, u32[]{:S(2)}, u32[]{:S(2)}) %collective-permute-start.7) | collective-permute-done | bytes 20512 | tf_op jit(solution)/shard_map/ppermute | solution.py:44
  98.0 9.5 %all-to-all-start.2 = ((bf16[8,16,320]{2,1,0:T(8,128)(2,1)}), bf16[8,16,320]{2,1,0:T(8,128)(2,1)S(1)}, u32[]{:S(2)}, u32[]{:S(2)}) async-start(bf16[8,16,320]{2,1,0:T(8,128)(2,1)} %broadcast_in_dim.7), calls=%async_computation.2 | async-start | bytes 196608 | tf_op jit(solution)/shard_map/all_to_all | solution.py:53
  107.5 7.5 %backward.1 = f32[512,320]{1,0:T(8,128)} custom-call(s32[4]{0:T(128)} %copy-done.4, bf16[12,2,160,320]{3,2,1,0:T(8,128)(2,1)} %get-tuple-element.48.w_h, f32[512,320]{1,0:T(8,128)} %copy-done.2, f32[512,320]{1,0:T(8,128)} %bitcast.17, bf16[512,320]{1,0:T(8,128)(2,1)} %collective-permute-done.3.cot_prev.prev_h, ...), custom_call_target="tpu_custom_call" | custom-call | flops 10000000 | bytes 1000000 | tf_op jit(solution)/shard_map/backward/pallas_call | solution.py:228
  115.1 3.9 %output.1 = f32[512,320]{1,0:T(8,128)} custom-call(s32[4]{0:T(128)} %copy-done.4, bf16[12,2,160,320]{3,2,1,0:T(8,128)(2,1)} %get-tuple-element.48.w_h, f32[512,320]{1,0:T(8,128)} %middle.1.part_h, bf16[512,320]{1,0:T(8,128)(2,1)} %collective-permute-done.8.prev_h, bf16[512,320]{1,0:T(8,128)(2,1)} %collective-permute-done.9.after_h, ...), custom_call_target="tpu_custom_call" | custom-call | flops 10000000 | bytes 1000000 | tf_op jit(solution)/shard_map/output/pallas_call | solution.py:228
  119.0 9.6 %all_to_all.20 = f32[4,16,320]{2,1,0:T(8,128)S(1)} all-to-all(f32[4,16,320]{2,1,0:T(8,128)S(1)} %broadcast_in_dim.8), channel_id=1, replica_groups=mesh['x'=4,'m'=2,'k'=4,'h'=2,'y'=4,'c'=2] {'x'}, dimensions={0} | all-to-all | bytes 163840 | tf_op jit(solution)/shard_map/all_to_all | solution.py:53
  (36 shorter events, 4.1 us)
Async XLA Ops:
  2.4 15.0 %collective-permute-start = (bf16[64,384]{1,0:T(8,128)(2,1)S(1)}, bf16[64,384]{1,0:T(8,128)(2,1)S(1)}, u32[]{:S(2)}, u32[]{:S(2)}) collective-permute-start(bf16[64,384]{1,0:T(8,128)(2,1)S(1)} %pad.8), channel_id=1, source_target_pairs={{0,72},{16,88},{32,104},{48,120},{64,8},{80,24},{96,40},{112,56},{... | collective-permute-start | bytes 147464 | tf_op jit(solution)/shard_map/ppermute | solution.py:44
  18.5 17.9 %all-to-all-start = ((bf16[4,304,384]{2,1,0:T(8,128)(2,1)}), bf16[4,304,384]{2,1,0:T(8,128)(2,1)S(1)}, u32[]{:S(2)}, u32[]{:S(2)}) async-start(bf16[4,304,384]{2,1,0:T(8,128)(2,1)} %broadcast_in_dim.6), calls=%async_computation | async-start | bytes 1867776 | tf_op jit(solution)/shard_map/all_to_all | solution.py:53
  23.0 30.0 %collective-permute-start.4 = (bf16[512,320]{1,0:T(8,128)(2,1)}, bf16[512,320]{1,0:T(8,128)(2,1)}, u32[]{:S(2)}, u32[]{:S(2)}) collective-permute-start(bf16[512,320]{1,0:T(8,128)(2,1)} %bitcast_convert_fusion), channel_id=1, source_target_pairs={{112,128},{128,112},{240,256},{256,240},{368,384},{384,368},{113,1... | collective-permute-start | bytes 983048 | tf_op jit(solution)/shard_map/ppermute | solution.py:256
  24.4 28.6 %collective-permute-start.3 = (bf16[512,320]{1,0:T(8,128)(2,1)}, bf16[512,320]{1,0:T(8,128)(2,1)}, u32[]{:S(2)}, u32[]{:S(2)}) collective-permute-start(bf16[512,320]{1,0:T(8,128)(2,1)} %bitcast_convert_fusion), channel_id=1, source_target_pairs={{0,16},{16,32},{32,48},{48,64},{64,80},{80,96},{96,112},{128,144},... | collective-permute-start | bytes 983048 | tf_op jit(solution)/shard_map/ppermute | solution.py:258
  28.1 24.9 %collective-permute-start.2 = (bf16[512,320]{1,0:T(8,128)(2,1)}, bf16[512,320]{1,0:T(8,128)(2,1)}, u32[]{:S(2)}, u32[]{:S(2)}) collective-permute-start(bf16[512,320]{1,0:T(8,128)(2,1)} %bitcast_convert_fusion), channel_id=1, source_target_pairs={{16,0},{32,16},{48,32},{64,48},{80,64},{96,80},{112,96},{144,128},... | collective-permute-start | bytes 983048 | tf_op jit(solution)/shard_map/ppermute | solution.py:257
  36.4 14.6 %copy-start.1 = (bf16[4,304,384]{2,1,0:T(8,128)(2,1)}, bf16[4,304,384]{2,1,0:T(8,128)(2,1)S(1)}, u32[]{:S(2)}) copy-start(bf16[4,304,384]{2,1,0:T(8,128)(2,1)S(1)} %all-to-all-done.gathered.own_m) | copy-start | bytes 2801668
  36.4 19.0 %copy-start.5 = (f32[320]{0:T(512)S(1)}, f32[320]{0:T(512)}, u32[]{:S(2)}) copy-start(f32[320]{0:T(512)} %param.7) | copy-start | bytes 3844
  36.4 19.1 %copy-start.3 = (f32[1,1,16,32,320]{4,3,2,1,0:T(8,128)S(1)}, f32[1,1,16,32,320]{4,3,2,1,0:T(8,128)}, u32[]{:S(2)}) copy-start(f32[1,1,16,32,320]{4,3,2,1,0:T(8,128)} %param.5) | copy-start | bytes 1966084
  51.0 6.3 %collective-permute-start.1 = (bf16[4,304,384]{2,1,0:T(8,128)(2,1)S(1)}, bf16[4,304,384]{2,1,0:T(8,128)(2,1)}, u32[]{:S(2)}, u32[]{:S(2)}) collective-permute-start(bf16[4,304,384]{2,1,0:T(8,128)(2,1)S(1)} %all-to-all-done.gathered.own_m), channel_id=1, source_target_pairs={{0,1},{1,0},{2,3},{3,2},{4,5},{5,4},{6,7},{7,6},{8,9},{9,8},{10,11... | collective-permute-start | bytes 2801672 | tf_op jit(solution)/shard_map/ppermute | solution.py:48
  53.0 4.3 %collective-permute-start.5 = (bf16[4,256,384]{2,1,0:T(8,128)(2,1)S(1)}, bf16[4,256,384]{2,1,0:T(8,128)(2,1)S(1)}, u32[]{:S(2)}, u32[]{:S(2)}) collective-permute-start(bf16[4,256,384]{2,1,0:T(8,128)(2,1)S(1)} %bitcast.12), channel_id=1, source_target_pairs={{0,1},{1,0},{2,3},{3,2},{4,5},{5,4},{6,7},{7,6},{8,9},{9,8},{10,11... | collective-permute-start | bytes 2359304 | tf_op jit(solution)/shard_map/ppermute | solution.py:48
  55.5 29.9 %copy-start.4 = (s32[4]{0:T(128)}, s32[4]{0:T(128)S(1)}, u32[]{:S(2)}) copy-start(s32[4]{0:T(128)S(1)} %pad_add_fusion.place) | copy-start | bytes 52
  55.8 1.0 copy-start
  63.6 0.9 copy-start.2
  64.4 4.2 %collective-permute-start.6 = (f32[4,4,2,16,320]{4,3,2,1,0:T(8,128)S(1)}, f32[4,4,2,16,320]{4,3,2,1,0:T(8,128)S(1)}, u32[]{:S(2)}, u32[]{:S(2)}) collective-permute-start(f32[4,4,2,16,320]{4,3,2,1,0:T(8,128)S(1)} %get-tuple-element.43), channel_id=1, source_target_pairs={{0,1},{1,0},{2,3},{3,2},{4,5},{5,4},{6,7},{7,6},{8,9},{9,8},{10,11... | collective-permute-start | bytes 1966088 | tf_op jit(solution)/shard_map/ppermute | solution.py:48
  69.5 16.0 %all-to-all-start.1 = ((bf16[16,2,16,320]{3,2,1,0:T(8,128)(2,1)}), bf16[16,2,16,320]{3,2,1,0:T(8,128)(2,1)S(1)}, u32[]{:S(2)}, u32[]{:S(2)}) async-start(bf16[16,2,16,320]{3,2,1,0:T(8,128)(2,1)} %bitcast.7), calls=%async_computation.1 | async-start | bytes 786432 | tf_op jit(solution)/shard_map/all_to_all | solution.py:279
  75.1 20.0 %collective-permute-start.9 = (bf16[512,320]{1,0:T(8,128)(2,1)}, bf16[512,320]{1,0:T(8,128)(2,1)}, u32[]{:S(2)}, u32[]{:S(2)}) collective-permute-start(bf16[512,320]{1,0:T(8,128)(2,1)} %get-tuple-element.49.hidden_h), channel_id=1, source_target_pairs={{16,0},{32,16},{48,32},{64,48},{80,64},{96,80},{112,96},{144,128},... | collective-permute-start | bytes 983048 | tf_op jit(solution)/shard_map/ppermute | solution.py:281
  79.1 15.9 %collective-permute-start.8 = (bf16[512,320]{1,0:T(8,128)(2,1)}, bf16[512,320]{1,0:T(8,128)(2,1)}, u32[]{:S(2)}, u32[]{:S(2)}) collective-permute-start(bf16[512,320]{1,0:T(8,128)(2,1)} %get-tuple-element.49.hidden_h), channel_id=1, source_target_pairs={{0,16},{16,32},{32,48},{48,64},{64,80},{80,96},{96,112},{128,144},... | collective-permute-start | bytes 983048 | tf_op jit(solution)/shard_map/ppermute | solution.py:280
  86.7 10.0 %collective-permute-start.7 = (f32[16,320]{1,0:T(8,128)}, f32[16,320]{1,0:T(8,128)}, u32[]{:S(2)}, u32[]{:S(2)}) collective-permute-start(f32[16,320]{1,0:T(8,128)} %get-tuple-element.47), channel_id=1, source_target_pairs={{0,72},{16,88},{32,104},{48,120},{64,8},{80,24},{96,40},{112,56},{... | collective-permute-start | bytes 61448 | tf_op jit(solution)/shard_map/ppermute | solution.py:44
  90.9 24.1 %collective-permute-start.10 = (bf16[512,320]{1,0:T(8,128)(2,1)}, bf16[512,320]{1,0:T(8,128)(2,1)}, u32[]{:S(2)}, u32[]{:S(2)}) collective-permute-start(bf16[512,320]{1,0:T(8,128)(2,1)} %get-tuple-element.49.hidden_h), channel_id=1, source_target_pairs={{112,128},{128,112},{240,256},{256,240},{368,384},{384,368},{113,1... | collective-permute-start | bytes 983048 | tf_op jit(solution)/shard_map/ppermute | solution.py:287
  98.0 20.9 %all-to-all-start.2 = ((bf16[8,16,320]{2,1,0:T(8,128)(2,1)}), bf16[8,16,320]{2,1,0:T(8,128)(2,1)S(1)}, u32[]{:S(2)}, u32[]{:S(2)}) async-start(bf16[8,16,320]{2,1,0:T(8,128)(2,1)} %broadcast_in_dim.7), calls=%async_computation.2 | async-start | bytes 196608 | tf_op jit(solution)/shard_map/all_to_all | solution.py:53

commit v10 on v9

--- a/solution.py
+++ b/solution.py
@@ -279,6 +279,13 @@
     part = lax.all_to_all(part.reshape(16, 2, 16, C), PLANE, 0, 0, tiled=True)
     prev = lax.ppermute(hidden, TM, FRAMES_UP)
     after = lax.ppermute(hidden, TM, FRAMES_DOWN)
+    (grad_video,) = kernel_call(
+        backward_kernel,
+        [(place, "s"), (w_all, "h"), (slope, "h"), (cot_f, "h"), (cot_prev, "h"), (cot_next, "h"), (far, "h")],
+        [(FRAME_F, "v")],
+        [WEIGHTS, FRAME_F, FRAME_F, FRAME_B, FRAME_B, FRAME_B, SHIFTS], 7, 0.01, "backward", 44,
+    )
+    part, grad_video = tie((part, grad_video))
     keep, give = kernel_call(
         split_kernel, [(place, "s"), (part, "v")], [(SHARE, "v"), (SHARE, "v")], [], 0, 1000, "split", 8,
     )
@@ -289,15 +296,8 @@
         middle_kernel, [(w_all, "h"), (video_f, "h"), (hidden, "h")], [(FRAME_F, "h")],
         [((2, HALF, C), BF), FRAME_F, FRAME_B, FRAME_F], 3, 1000, "middle",
     )
-    other, middle, prev, after, slope = tie((other, middle, prev, after, slope))
+    other, middle, prev, after = tie((other, middle, prev, after))
     part = to_all((keep + other).astype(BF), Z_LO)
-    (grad_video,) = kernel_call(
-        backward_kernel,
-        [(place, "s"), (w_all, "h"), (slope, "h"), (cot_f, "h"), (cot_prev, "h"), (cot_next, "h"), (far, "h")],
-        [(FRAME_F, "v")],
-        [WEIGHTS, FRAME_F, FRAME_F, FRAME_B, FRAME_B, FRAME_B, SHIFTS], 7, 0.01, "backward",
-    )
-    middle, grad_video, hidden_far = tie((middle, grad_video, hidden_far))
     (output,) = kernel_call(
         output_kernel,
         [(place, "s"), (w_all, "h"), (middle, "h"), (prev, "h"), (after, "h"), (hidden_far, "h")],

time: 130 us -> 136 us (1.046)
  the two profiles are of different devices: /device:TPU:32 before, /device:TPU:8 now
where the time goes in v10:
time: 136 us; the launch traced here: 135 us
  starting transfers between devices  54.7 us (40%)
  blocking collectives  26.2 us (19%)
  Pallas kernels  21.6 us (16%)
  waiting for transfers between devices  19.4 us (14%)
  other arithmetic  6.39 us (5%)
  local copies, waits for them, and re-layouts  5.35 us (4%)
    pallas_call x7, Pallas kernels, kernel_call(): pl.pallas_call(body, out_shape=tuple((jax.ShapeDtypeStruct(*o[0]) for o i...  21.6 us
    all_gather x1, blocking collectives, on_device(): oth_m = lax.all_gather(oth_m, 'x')  16.7 us
    ppermute x2, starting transfers between devices, across(): return lax.ppermute(a, ('m', 'k', 'h'), ACROSS)  15.5 us
    all_to_all x2, starting transfers between devices, to_all(): lax.all_to_all(jnp.broadcast_to(a[None], (n, *a.shape)), axes, 0, 0, tile...  13.2 us
    all_to_all x2, waiting for transfers between devices, to_all(): lax.all_to_all(jnp.broadcast_to(a[None], (n, *a.shape)), axes, 0, 0, tile...  12.9 us
    all_to_all x1, blocking collectives, to_all(): lax.all_to_all(jnp.broadcast_to(a[None], (n, *a.shape)), axes, 0, 0, tile...  9.55 us
    ppermute x3, starting transfers between devices, core_swap(): return lax.ppermute(a, 'c', [(0, 1), (1, 0)])  6.73 us
    all_to_all x1, starting transfers between devices, on_device(): part = lax.all_to_all(part.reshape(16, 2, 16, C), PLANE, 0, 0, tiled=True)  5.88 us
  transfers between devices with their start and end apart: 14, of which 6 were waited for; matrix products, arithmetic and copies ran while one was open for 3% of the time, Pallas kernels for 11%

profile of v10, /device:TPU:8, one launch (start us, length us, event | category | flops | bytes accessed | tf_op | source)
XLA Modules:
  0.0 134.6 jit_solution(7844844530206214798)
XLA Ops:
  0.6 0.9 convert_element_type.20
  2.4 12.7 %collective-permute-start = (bf16[64,384]{1,0:T(8,128)(2,1)S(1)}, bf16[64,384]{1,0:T(8,128)(2,1)S(1)}, u32[]{:S(2)}, u32[]{:S(2)}) collective-permute-start(bf16[64,384]{1,0:T(8,128)(2,1)S(1)} %pad.8), channel_id=1, source_target_pairs={{0,72},{16,88},{32,104},{48,120},{64,8},{80,24},{96,40},{112,56},{... | collective-permute-start | bytes 147464 | tf_op jit(solution)/shard_map/ppermute | solution.py:44
  15.2 1.9 %bitcast_convert_fusion = bf16[512,320]{1,0:T(8,128)(2,1)} fusion(f32[1,1,16,32,320]{4,3,2,1,0:T(8,128)} %param.9), kind=kLoop, calls=%fused_computation.10 | loop fusion | flops 163840 | bytes 983040 | tf_op jit(solution)/shard_map/convert_element_type | solution.py:250
  17.1 1.0 pad_maximum_fusion
  18.2 1.2 collective-permute-done
  19.4 1.0 broadcast_in_dim.6
  20.4 4.9 %all-to-all-start = ((bf16[4,304,384]{2,1,0:T(8,128)(2,1)}), bf16[4,304,384]{2,1,0:T(8,128)(2,1)S(1)}, u32[]{:S(2)}, u32[]{:S(2)}) async-start(bf16[4,304,384]{2,1,0:T(8,128)(2,1)} %broadcast_in_dim.6), calls=%async_computation | async-start | bytes 1867776 | tf_op jit(solution)/shard_map/all_to_all | solution.py:53
  25.3 1.4 %collective-permute-start.4 = (bf16[512,320]{1,0:T(8,128)(2,1)}, bf16[512,320]{1,0:T(8,128)(2,1)}, u32[]{:S(2)}, u32[]{:S(2)}) collective-permute-start(bf16[512,320]{1,0:T(8,128)(2,1)} %bitcast_convert_fusion), channel_id=1, source_target_pairs={{112,128},{128,112},{240,256},{256,240},{368,384},{384,368},{113,1... | collective-permute-start | bytes 983048 | tf_op jit(solution)/shard_map/ppermute | solution.py:256
  26.7 2.7 %collective-permute-start.3 = (bf16[512,320]{1,0:T(8,128)(2,1)}, bf16[512,320]{1,0:T(8,128)(2,1)}, u32[]{:S(2)}, u32[]{:S(2)}) collective-permute-start(bf16[512,320]{1,0:T(8,128)(2,1)} %bitcast_convert_fusion), channel_id=1, source_target_pairs={{0,16},{16,32},{32,48},{48,64},{64,80},{80,96},{96,112},{128,144},... | collective-permute-start | bytes 983048 | tf_op jit(solution)/shard_map/ppermute | solution.py:258
  29.4 1.3 collective-permute-start.2
  30.7 5.6 %all-to-all-done.gathered.own_m = bf16[4,304,384]{2,1,0:T(8,128)(2,1)S(1)} async-done(((bf16[4,304,384]{2,1,0:T(8,128)(2,1)}), bf16[4,304,384]{2,1,0:T(8,128)(2,1)S(1)}, u32[]{:S(2)}, u32[]{:S(2)}) %all-to-all-start) | async-done | bytes 933920 | tf_op jit(solution)/shard_map/all_to_all | solution.py:53
  36.3 16.7 %all-gather = bf16[1024,384]{1,0:T(8,128)(2,1)S(1)} all-gather(bf16[256,384]{1,0:T(8,128)(2,1)S(1)} %apart.1), channel_id=2, replica_groups=mesh['x'=4,'m'=2,'k'=4,'h'=2,'y'=4,'c'=2] {'x'}, dimensions={0}, use_global_device_ids=true | all-gather | bytes 983040 | tf_op jit(solution)/shard_map/all_gather | solution.py:263
  53.0 1.9 %collective-permute-start.1 = (bf16[4,304,384]{2,1,0:T(8,128)(2,1)S(1)}, bf16[4,304,384]{2,1,0:T(8,128)(2,1)}, u32[]{:S(2)}, u32[]{:S(2)}) collective-permute-start(bf16[4,304,384]{2,1,0:T(8,128)(2,1)S(1)} %all-to-all-done.gathered.own_m), channel_id=1, source_target_pairs={{0,1},{1,0},{2,3},{3,2},{4,5},{5,4},{6,7},{7,6},{8,9},{9,8},{10,11... | collective-permute-start | bytes 2801672 | tf_op jit(solution)/shard_map/ppermute | solution.py:48
  54.9 2.4 %collective-permute-start.5 = (bf16[4,256,384]{2,1,0:T(8,128)(2,1)S(1)}, bf16[4,256,384]{2,1,0:T(8,128)(2,1)S(1)}, u32[]{:S(2)}, u32[]{:S(2)}) collective-permute-start(bf16[4,256,384]{2,1,0:T(8,128)(2,1)S(1)} %bitcast.14), channel_id=1, source_target_pairs={{0,1},{1,0},{2,3},{3,2},{4,5},{5,4},{6,7},{7,6},{8,9},{9,8},{10,11... | collective-permute-start | bytes 2359304 | tf_op jit(solution)/shard_map/ppermute | solution.py:48
  57.7 1.0 copy-done.2
  59.2 6.3 %forward.1 = (bf16[12,2,160,320]{3,2,1,0:T(8,128)(2,1)}, bf16[512,320]{1,0:T(8,128)(2,1)}, f32[512,320]{1,0:T(8,128)S(1)}, f32[4,4,2,16,320]{4,3,2,1,0:T(8,128)S(1)}, f32[4,4,2,16,320]{4,3,2,1,0:T(8,128)S(1)}) custom-call(s32[4]{0:T(128)S(1)} %pad_add_fusion.place, bf16[4,304,384]{2,1,0:T(8,128)(2,1)} %copy-done.3, ...), custom_call_target="tpu_custom_call" | custom-call | flops 10000000 | bytes 1000000 | tf_op jit(solution)/shard_map/forward/pallas_call | solution.py:228
  65.5 2.4 %collective-permute-start.6 = (f32[4,4,2,16,320]{4,3,2,1,0:T(8,128)S(1)}, f32[4,4,2,16,320]{4,3,2,1,0:T(8,128)S(1)}, u32[]{:S(2)}, u32[]{:S(2)}) collective-permute-start(f32[4,4,2,16,320]{4,3,2,1,0:T(8,128)S(1)} %get-tuple-element.41), channel_id=1, source_target_pairs={{0,1},{1,0},{2,3},{3,2},{4,5},{5,4},{6,7},{7,6},{8,9},{9,8},{10,11... | collective-permute-start | bytes 1966088 | tf_op jit(solution)/shard_map/ppermute | solution.py:48
  67.9 1.9 %collective-permute-done.6 = f32[4,4,2,16,320]{4,3,2,1,0:T(8,128)S(1)} collective-permute-done((f32[4,4,2,16,320]{4,3,2,1,0:T(8,128)S(1)}, f32[4,4,2,16,320]{4,3,2,1,0:T(8,128)S(1)}, u32[]{:S(2)}, u32[]{:S(2)}) %collective-permute-start.6) | collective-permute-done | bytes 655392 | tf_op jit(solution)/shard_map/ppermute | solution.py:48
  70.7 5.9 %all-to-all-start.1 = ((bf16[16,2,16,320]{3,2,1,0:T(8,128)(2,1)}), bf16[16,2,16,320]{3,2,1,0:T(8,128)(2,1)S(1)}, u32[]{:S(2)}, u32[]{:S(2)}) async-start(bf16[16,2,16,320]{3,2,1,0:T(8,128)(2,1)} %bitcast.7), calls=%async_computation.1 | async-start | bytes 786432 | tf_op jit(solution)/shard_map/all_to_all | solution.py:279
  76.6 1.3 collective-permute-start.9
  77.9 5.3 %collective-permute-start.8 = (bf16[512,320]{1,0:T(8,128)(2,1)}, bf16[512,320]{1,0:T(8,128)(2,1)}, u32[]{:S(2)}, u32[]{:S(2)}) collective-permute-start(bf16[512,320]{1,0:T(8,128)(2,1)} %get-tuple-element.49.hidden_h), channel_id=1, source_target_pairs={{0,16},{16,32},{32,48},{48,64},{64,80},{80,96},{96,112},{128,144},... | collective-permute-start | bytes 983048 | tf_op jit(solution)/shard_map/ppermute | solution.py:280
  83.2 1.8 %copy-done = bf16[12,2,160,320]{3,2,1,0:T(8,128)(2,1)S(1)} copy-done((bf16[12,2,160,320]{3,2,1,0:T(8,128)(2,1)S(1)}, bf16[12,2,160,320]{3,2,1,0:T(8,128)(2,1)}, u32[]{:S(2)}) %copy-start) | copy-done | bytes 2457624
  85.0 7.3 %backward.1 = f32[512,320]{1,0:T(8,128)} custom-call(s32[4]{0:T(128)S(1)} %pad_add_fusion.place, bf16[12,2,160,320]{3,2,1,0:T(8,128)(2,1)S(1)} %copy-done, f32[512,320]{1,0:T(8,128)S(1)} %get-tuple-element.43.slope_h, f32[512,320]{1,0:T(8,128)S(1)} %bitcast.13, bf16[512,320]{1,0:T(8,128)(2,1)} %collective-permute-done.3.cot_prev.prev_h, ...), custom_call_target="tpu_custom_call" | custom-call | flops 10000000 | bytes 1000000 | tf_op jit(solution)/shard_map/backward/pallas_call | solution.py:228
  92.3 1.2 split.1
  93.5 2.8 %collective-permute-start.7 = (f32[16,320]{1,0:T(8,128)}, f32[16,320]{1,0:T(8,128)}, u32[]{:S(2)}, u32[]{:S(2)}) collective-permute-start(f32[16,320]{1,0:T(8,128)} %get-tuple-element.48), channel_id=1, source_target_pairs={{0,72},{16,88},{32,104},{48,120},{64,8},{80,24},{96,40},{112,56},{... | collective-permute-start | bytes 61448 | tf_op jit(solution)/shard_map/ppermute | solution.py:44
  96.3 1.4 %collective-permute-start.10 = (bf16[512,320]{1,0:T(8,128)(2,1)}, bf16[512,320]{1,0:T(8,128)(2,1)}, u32[]{:S(2)}, u32[]{:S(2)}) collective-permute-start(bf16[512,320]{1,0:T(8,128)(2,1)} %get-tuple-element.49.hidden_h), channel_id=1, source_target_pairs={{112,128},{128,112},{240,256},{256,240},{368,384},{384,368},{113,1... | collective-permute-start | bytes 983048 | tf_op jit(solution)/shard_map/ppermute | solution.py:294
  97.8 2.7 %middle.1.part_h = f32[512,320]{1,0:T(8,128)} custom-call(bf16[12,2,160,320]{3,2,1,0:T(8,128)(2,1)} %get-tuple-element.42.w_h, f32[512,320]{1,0:T(8,128)} %bitcast.16, bf16[512,320]{1,0:T(8,128)(2,1)} %get-tuple-element.49.hidden_h), custom_call_target="tpu_custom_call" | custom-call | flops 999999995904 | bytes 1000000 | tf_op jit(solution)/shard_map/middle/pallas_call | solution.py:228
  100.4 3.0 %collective-permute-done.7 = f32[16,320]{1,0:T(8,128)} collective-permute-done((f32[16,320]{1,0:T(8,128)}, f32[16,320]{1,0:T(8,128)}, u32[]{:S(2)}, u32[]{:S(2)}) %collective-permute-start.7) | collective-permute-done | bytes 20512 | tf_op jit(solution)/shard_map/ppermute | solution.py:44
  104.8 8.3 %all-to-all-start.2 = ((bf16[8,16,320]{2,1,0:T(8,128)(2,1)}), bf16[8,16,320]{2,1,0:T(8,128)(2,1)S(1)}, u32[]{:S(2)}, u32[]{:S(2)}) async-start(bf16[8,16,320]{2,1,0:T(8,128)(2,1)} %broadcast_in_dim.7), calls=%async_computation.2 | async-start | bytes 196608 | tf_op jit(solution)/shard_map/all_to_all | solution.py:53
  113.2 3.9 %output.1 = f32[512,320]{1,0:T(8,128)} custom-call(s32[4]{0:T(128)} %copy-done.5, bf16[12,2,160,320]{3,2,1,0:T(8,128)(2,1)} %get-tuple-element.42.w_h, f32[512,320]{1,0:T(8,128)} %middle.1.part_h, bf16[512,320]{1,0:T(8,128)(2,1)} %collective-permute-done.8.prev_h, bf16[512,320]{1,0:T(8,128)(2,1)} %collective-permute-done.9.after_h, ...), custom_call_target="tpu_custom_call" | custom-call | flops 10000000 | bytes 1000000 | tf_op jit(solution)/shard_map/output/pallas_call | solution.py:228
  117.1 7.3 %all-to-all-done.2 = bf16[8,16,320]{2,1,0:T(8,128)(2,1)S(1)} async-done(((bf16[8,16,320]{2,1,0:T(8,128)(2,1)}), bf16[8,16,320]{2,1,0:T(8,128)(2,1)S(1)}, u32[]{:S(2)}, u32[]{:S(2)}) %all-to-all-start.2) | async-done | bytes 81952 | tf_op jit(solution)/shard_map/all_to_all | solution.py:53
  124.4 9.6 %all_to_all.20 = f32[4,16,320]{2,1,0:T(8,128)S(1)} all-to-all(f32[4,16,320]{2,1,0:T(8,128)S(1)} %broadcast_in_dim.8), channel_id=1, replica_groups=mesh['x'=4,'m'=2,'k'=4,'h'=2,'y'=4,'c'=2] {'x'}, dimensions={0} | all-to-all | bytes 163840 | tf_op jit(solution)/shard_map/all_to_all | solution.py:53
  (38 shorter events, 4.8 us)
Async XLA Ops:
  2.4 16.9 %collective-permute-start = (bf16[64,384]{1,0:T(8,128)(2,1)S(1)}, bf16[64,384]{1,0:T(8,128)(2,1)S(1)}, u32[]{:S(2)}, u32[]{:S(2)}) collective-permute-start(bf16[64,384]{1,0:T(8,128)(2,1)S(1)} %pad.8), channel_id=1, source_target_pairs={{0,72},{16,88},{32,104},{48,120},{64,8},{80,24},{96,40},{112,56},{... | collective-permute-start | bytes 147464 | tf_op jit(solution)/shard_map/ppermute | solution.py:44
  20.4 15.9 %all-to-all-start = ((bf16[4,304,384]{2,1,0:T(8,128)(2,1)}), bf16[4,304,384]{2,1,0:T(8,128)(2,1)S(1)}, u32[]{:S(2)}, u32[]{:S(2)}) async-start(bf16[4,304,384]{2,1,0:T(8,128)(2,1)} %broadcast_in_dim.6), calls=%async_computation | async-start | bytes 1867776 | tf_op jit(solution)/shard_map/all_to_all | solution.py:53
  25.3 29.6 %collective-permute-start.4 = (bf16[512,320]{1,0:T(8,128)(2,1)}, bf16[512,320]{1,0:T(8,128)(2,1)}, u32[]{:S(2)}, u32[]{:S(2)}) collective-permute-start(bf16[512,320]{1,0:T(8,128)(2,1)} %bitcast_convert_fusion), channel_id=1, source_target_pairs={{112,128},{128,112},{240,256},{256,240},{368,384},{384,368},{113,1... | collective-permute-start | bytes 983048 | tf_op jit(solution)/shard_map/ppermute | solution.py:256
  26.7 28.2 %collective-permute-start.3 = (bf16[512,320]{1,0:T(8,128)(2,1)}, bf16[512,320]{1,0:T(8,128)(2,1)}, u32[]{:S(2)}, u32[]{:S(2)}) collective-permute-start(bf16[512,320]{1,0:T(8,128)(2,1)} %bitcast_convert_fusion), channel_id=1, source_target_pairs={{0,16},{16,32},{32,48},{48,64},{64,80},{80,96},{96,112},{128,144},... | collective-permute-start | bytes 983048 | tf_op jit(solution)/shard_map/ppermute | solution.py:258
  29.4 25.5 %collective-permute-start.2 = (bf16[512,320]{1,0:T(8,128)(2,1)}, bf16[512,320]{1,0:T(8,128)(2,1)}, u32[]{:S(2)}, u32[]{:S(2)}) collective-permute-start(bf16[512,320]{1,0:T(8,128)(2,1)} %bitcast_convert_fusion), channel_id=1, source_target_pairs={{16,0},{32,16},{48,32},{64,48},{80,64},{96,80},{112,96},{144,128},... | collective-permute-start | bytes 983048 | tf_op jit(solution)/shard_map/ppermute | solution.py:257
  36.3 16.7 %copy-start.3 = (bf16[4,304,384]{2,1,0:T(8,128)(2,1)}, bf16[4,304,384]{2,1,0:T(8,128)(2,1)S(1)}, u32[]{:S(2)}) copy-start(bf16[4,304,384]{2,1,0:T(8,128)(2,1)S(1)} %all-to-all-done.gathered.own_m) | copy-start | bytes 2801668
  36.3 21.1 %copy-start.6 = (f32[320]{0:T(512)S(1)}, f32[320]{0:T(512)}, u32[]{:S(2)}) copy-start(f32[320]{0:T(512)} %param.7) | copy-start | bytes 3844
  36.3 21.2 %copy-start.4 = (f32[1,1,16,32,320]{4,3,2,1,0:T(8,128)S(1)}, f32[1,1,16,32,320]{4,3,2,1,0:T(8,128)}, u32[]{:S(2)}) copy-start(f32[1,1,16,32,320]{4,3,2,1,0:T(8,128)} %param.5) | copy-start | bytes 1966084
  53.0 6.3 %collective-permute-start.1 = (bf16[4,304,384]{2,1,0:T(8,128)(2,1)S(1)}, bf16[4,304,384]{2,1,0:T(8,128)(2,1)}, u32[]{:S(2)}, u32[]{:S(2)}) collective-permute-start(bf16[4,304,384]{2,1,0:T(8,128)(2,1)S(1)} %all-to-all-done.gathered.own_m), channel_id=1, source_target_pairs={{0,1},{1,0},{2,3},{3,2},{4,5},{5,4},{6,7},{7,6},{8,9},{9,8},{10,11... | collective-permute-start | bytes 2801672 | tf_op jit(solution)/shard_map/ppermute | solution.py:48
  54.9 4.3 %collective-permute-start.5 = (bf16[4,256,384]{2,1,0:T(8,128)(2,1)S(1)}, bf16[4,256,384]{2,1,0:T(8,128)(2,1)S(1)}, u32[]{:S(2)}, u32[]{:S(2)}) collective-permute-start(bf16[4,256,384]{2,1,0:T(8,128)(2,1)S(1)} %bitcast.14), channel_id=1, source_target_pairs={{0,1},{1,0},{2,3},{3,2},{4,5},{5,4},{6,7},{7,6},{8,9},{9,8},{10,11... | collective-permute-start | bytes 2359304 | tf_op jit(solution)/shard_map/ppermute | solution.py:48
  57.4 34.8 %copy-start.5 = (s32[4]{0:T(128)}, s32[4]{0:T(128)S(1)}, u32[]{:S(2)}) copy-start(s32[4]{0:T(128)S(1)} %pad_add_fusion.place) | copy-start | bytes 52
  57.7 1.0 copy-start.2
  65.5 17.7 %copy-start.1 = (f32[1,1,16,32,320]{4,3,2,1,0:T(8,128)S(1)}, f32[1,1,16,32,320]{4,3,2,1,0:T(8,128)}, u32[]{:S(2)}) copy-start(f32[1,1,16,32,320]{4,3,2,1,0:T(8,128)} %param.9) | copy-start | bytes 1966084
  65.5 4.3 %collective-permute-start.6 = (f32[4,4,2,16,320]{4,3,2,1,0:T(8,128)S(1)}, f32[4,4,2,16,320]{4,3,2,1,0:T(8,128)S(1)}, u32[]{:S(2)}, u32[]{:S(2)}) collective-permute-start(f32[4,4,2,16,320]{4,3,2,1,0:T(8,128)S(1)} %get-tuple-element.41), channel_id=1, source_target_pairs={{0,1},{1,0},{2,3},{3,2},{4,5},{5,4},{6,7},{7,6},{8,9},{9,8},{10,11... | collective-permute-start | bytes 1966088 | tf_op jit(solution)/shard_map/ppermute | solution.py:48
  70.7 21.6 %all-to-all-start.1 = ((bf16[16,2,16,320]{3,2,1,0:T(8,128)(2,1)}), bf16[16,2,16,320]{3,2,1,0:T(8,128)(2,1)S(1)}, u32[]{:S(2)}, u32[]{:S(2)}) async-start(bf16[16,2,16,320]{3,2,1,0:T(8,128)(2,1)} %bitcast.7), calls=%async_computation.1 | async-start | bytes 786432 | tf_op jit(solution)/shard_map/all_to_all | solution.py:279
  76.6 23.8 %collective-permute-start.9 = (bf16[512,320]{1,0:T(8,128)(2,1)}, bf16[512,320]{1,0:T(8,128)(2,1)}, u32[]{:S(2)}, u32[]{:S(2)}) collective-permute-start(bf16[512,320]{1,0:T(8,128)(2,1)} %get-tuple-element.49.hidden_h), channel_id=1, source_target_pairs={{16,0},{32,16},{48,32},{64,48},{80,64},{96,80},{112,96},{144,128},... | collective-permute-start | bytes 983048 | tf_op jit(solution)/shard_map/ppermute | solution.py:281
  77.9 22.6 %collective-permute-start.8 = (bf16[512,320]{1,0:T(8,128)(2,1)}, bf16[512,320]{1,0:T(8,128)(2,1)}, u32[]{:S(2)}, u32[]{:S(2)}) collective-permute-start(bf16[512,320]{1,0:T(8,128)(2,1)} %get-tuple-element.49.hidden_h), channel_id=1, source_target_pairs={{0,16},{16,32},{32,48},{48,64},{64,80},{80,96},{96,112},{128,144},... | collective-permute-start | bytes 983048 | tf_op jit(solution)/shard_map/ppermute | solution.py:280
  83.2 1.8 %copy-start = (bf16[12,2,160,320]{3,2,1,0:T(8,128)(2,1)S(1)}, bf16[12,2,160,320]{3,2,1,0:T(8,128)(2,1)}, u32[]{:S(2)}) copy-start(bf16[12,2,160,320]{3,2,1,0:T(8,128)(2,1)} %get-tuple-element.42.w_h) | copy-start | bytes 7372804
  93.5 9.9 %collective-permute-start.7 = (f32[16,320]{1,0:T(8,128)}, f32[16,320]{1,0:T(8,128)}, u32[]{:S(2)}, u32[]{:S(2)}) collective-permute-start(f32[16,320]{1,0:T(8,128)} %get-tuple-element.48), channel_id=1, source_target_pairs={{0,72},{16,88},{32,104},{48,120},{64,8},{80,24},{96,40},{112,56},{... | collective-permute-start | bytes 61448 | tf_op jit(solution)/shard_map/ppermute | solution.py:44
  96.3 16.8 %collective-permute-start.10 = (bf16[512,320]{1,0:T(8,128)(2,1)}, bf16[512,320]{1,0:T(8,128)(2,1)}, u32[]{:S(2)}, u32[]{:S(2)}) collective-permute-start(bf16[512,320]{1,0:T(8,128)(2,1)} %get-tuple-element.49.hidden_h), channel_id=1, source_target_pairs={{112,128},{128,112},{240,256},{256,240},{368,384},{384,368},{113,1... | collective-permute-start | bytes 983048 | tf_op jit(solution)/shard_map/ppermute | solution.py:294
  104.8 19.5 %all-to-all-start.2 = ((bf16[8,16,320]{2,1,0:T(8,128)(2,1)}), bf16[8,16,320]{2,1,0:T(8,128)(2,1)S(1)}, u32[]{:S(2)}, u32[]{:S(2)}) async-start(bf16[8,16,320]{2,1,0:T(8,128)(2,1)} %broadcast_in_dim.7), calls=%async_computation.2 | async-start | bytes 196608 | tf_op jit(solution)/shard_map/all_to_all | solution.py:53

commit v11 on v8

--- a/solution.py
+++ b/solution.py
@@ -158,13 +158,16 @@
         one.wait()
 
 
-def split_kernel(place, parts, keep_ref, give_ref):
-    h = place[1]
+def split_kernel(place, parts, total_ref, give_ref):
     total = parts[0].astype(F32)
     for i in range(1, 16):
         total = total + parts[i].astype(F32)
-    keep_ref[...] = jnp.where(h == 0, total[0], total[1])
-    give_ref[...] = jnp.where(h == 0, total[1], total[0])
+    total_ref[...] = total
+    give_ref[...] = jnp.where(place[1] == 0, total[1], total[0])
+
+
+def keep_kernel(place, total, keep_ref):
+    keep_ref[...] = jnp.where(place[1] == 0, total[0], total[1])
 
 
 def backward_kernel(
@@ -255,7 +258,7 @@
     )
     oth_m = lax.all_gather(oth_m, "x")
     oth_m, own_m, video_w = tie((oth_m, own_m, video_f))
-    far, oth_m, cot_next, cot_prev = tie((far, oth_m, cot_next, cot_prev))
+    oth_m, cot_next, cot_prev, far = tie((oth_m, cot_next, cot_prev, far))
     (windows,) = kernel_call(prepare_kernel, [(video_w, "v")], [(WINDOWS, "v")], [], 0, 0.01, "prepare", 16)
     own_t, oth_t = core_swap(own_m), core_swap(oth_m)
 
@@ -270,31 +273,32 @@
     )
     part = (mine + core_swap(theirs)).astype(BF)
     part = lax.all_to_all(part.reshape(16, 2, 16, C), PLANE, 0, 0, tiled=True)
-    hidden_far = lax.ppermute(hidden, TM, FRAMES_FAR)
     prev = lax.ppermute(hidden, TM, FRAMES_UP)
     after = lax.ppermute(hidden, TM, FRAMES_DOWN)
-    keep, give = kernel_call(
-        split_kernel, [(place, "s"), (part, "v")], [(SHARE, "v"), (SHARE, "v")], [], 0, 1000, "split", 8,
-    )
-    give, slope = tie((give, slope))
+    total, give = kernel_call(
+        split_kernel, [(place, "s"), (part, "v")], [(((2, 16, C), F32), "v"), (SHARE, "v")], [], 0, 1000, "split", 8,
+    )
+    give, total, hidden = tie((give, total, hidden))
     other = across(give)
+    hidden_far = lax.ppermute(hidden, TM, FRAMES_FAR)
+    (keep,) = kernel_call(keep_kernel, [(place, "s"), (total, "v")], [(SHARE, "v")], [], 0, 1000, "keep", 8)
+    other, keep, prev, after, slope, video_f = tie((other, keep, prev, after, slope, video_f))
+    part = to_all((keep + other).astype(BF), Z_LO)
     (grad_video,) = kernel_call(
         backward_kernel,
         [(place, "s"), (w_all, "h"), (slope, "h"), (cot_f, "h"), (cot_prev, "h"), (cot_next, "h"), (far, "h")],
         [(FRAME_F, "v")],
-        [WEIGHTS, FRAME_F, FRAME_F, FRAME_B, FRAME_B, FRAME_B, SHIFTS], 7, 5, "backward",
-    )
-    other, grad_video = tie((other, grad_video))
-    part = keep + other
-    hidden_far, part, video_f, prev, after = tie((hidden_far, part, video_f, prev, after))
-    part = to_all(part, Z_LO)
+        [WEIGHTS, FRAME_F, FRAME_F, FRAME_B, FRAME_B, FRAME_B, SHIFTS], 7, 0.01, "backward",
+    )
+    video_f, grad_video, hidden_far = tie((video_f, grad_video, hidden_far))
     (output,) = kernel_call(
         output_kernel,
         [(place, "s"), (w_all, "h"), (video_f, "h"), (hidden, "h"), (prev, "h"), (after, "h"), (hidden_far, "h")],
         [(FRAME_F, "v")],
-        [((3, 2, HALF, C), BF), FRAME_F, FRAME_B, FRAME_B, FRAME_B, FRAME_B], 6, 3, "output",
+        [((3, 2, HALF, C), BF), FRAME_F, FRAME_B, FRAME_B, FRAME_B, FRAME_B], 6, 0.01, "output",
     )
     part, output = tie((part, output))
+    part = part.astype(F32)
     part = jnp.sum(part, axis=0)
     part = to_all(part, "x").reshape(4 * 16, C)
     total_rows = ROWS * lax.axis_size(TM) * lax.axis_size(CLIP)

time: 143 us -> 129 us (0.902)
  starting transfers between devices: 72.4 us -> 56.4 us
  local copies, waits for them, and re-layouts: 3.57 us -> 5.11 us
    all_to_all x2, starting transfers between devices: 24.8 us -> 13.6 us  [to_all(): lax.all_to_all(jnp.broadcast_to(a[None], (n, *a.shape)), axes, 0, 0, tile...]
    all_to_all x2, waiting for transfers between devices: 15 us -> 5.46 us  [to_all(): lax.all_to_all(jnp.broadcast_to(a[None], (n, *a.shape)), axes, 0, 0, tile...]
    ppermute x1, starting transfers between devices: 12.3 us -> 3.86 us  [on_device(): after = lax.ppermute(hidden, TM, FRAMES_DOWN)]
    all_to_all x1, waiting for transfers between devices: 0.01 us -> 4.48 us  [on_device(): part = lax.all_to_all(part.reshape(16, 2, 16, C), PLANE, 0, 0, tiled=True)]
    ppermute x2, waiting for transfers between devices: 0.47 us -> 4.55 us  [across(): return lax.ppermute(a, ('m', 'k', 'h'), ACROSS)]
    ppermute x2, starting transfers between devices: 13.8 us -> 16.1 us  [across(): return lax.ppermute(a, ('m', 'k', 'h'), ACROSS)]
    all_to_all x1, starting transfers between devices: 3.64 us -> 5.62 us  [on_device(): part = lax.all_to_all(part.reshape(16, 2, 16, C), PLANE, 0, 0, tiled=True)]
    unnamed x12 -> x14, local copies, waits for them, and re-layouts: 1.06 us -> 2.65 us
  transfers between devices with their start and end apart: 14 -> 14, of which waited for: 6 -> 6; matrix products, arithmetic and copies ran while one was open for 2% -> 3% of each run, Pallas kernels for 9% -> 11%
where the time goes in v11:
time: 129 us
  starting transfers between devices  56.4 us (44%)
  blocking collectives  22.8 us (18%)
  Pallas kernels  20.1 us (16%)
  waiting for transfers between devices  16.9 us (13%)
  other arithmetic  6.37 us (5%)
  local copies, waits for them, and re-layouts  5.11 us (4%)
    pallas_call x7, Pallas kernels, kernel_call(): pl.pallas_call(body, out_shape=tuple((jax.ShapeDtypeStruct(*o[0]) for o i...  20.1 us
    ppermute x2, starting transfers between devices, across(): return lax.ppermute(a, ('m', 'k', 'h'), ACROSS)  16.1 us
    all_gather x1, blocking collectives, on_device(): oth_m = lax.all_gather(oth_m, 'x')  14.6 us
    all_to_all x2, starting transfers between devices, to_all(): lax.all_to_all(jnp.broadcast_to(a[None], (n, *a.shape)), axes, 0, 0, tile...  13.6 us
    all_to_all x1, blocking collectives, to_all(): lax.all_to_all(jnp.broadcast_to(a[None], (n, *a.shape)), axes, 0, 0, tile...  8.21 us
    ppermute x3, starting transfers between devices, core_swap(): return lax.ppermute(a, 'c', [(0, 1), (1, 0)])  6.59 us
    all_to_all x1, starting transfers between devices, on_device(): part = lax.all_to_all(part.reshape(16, 2, 16, C), PLANE, 0, 0, tiled=True)  5.62 us
    all_to_all x2, waiting for transfers between devices, to_all(): lax.all_to_all(jnp.broadcast_to(a[None], (n, *a.shape)), axes, 0, 0, tile...  5.46 us
  transfers between devices with their start and end apart: 14, of which 6 were waited for; matrix products, arithmetic and copies ran while one was open for 3% of the time, Pallas kernels for 11%

profile of v11, /device:TPU:32, one launch (start us, length us, event | category | flops | bytes accessed | tf_op | source)
XLA Modules:
  0.0 128.6 jit_solution(6769917438193396328)
XLA Ops:
  0.6 0.9 convert_element_type.20
  1.5 0.8 fusion
  2.4 11.8 %collective-permute-start = (bf16[64,384]{1,0:T(8,128)(2,1)S(1)}, bf16[64,384]{1,0:T(8,128)(2,1)S(1)}, u32[]{:S(2)}, u32[]{:S(2)}) collective-permute-start(bf16[64,384]{1,0:T(8,128)(2,1)S(1)} %pad.8), channel_id=1, source_target_pairs={{0,72},{16,88},{32,104},{48,120},{64,8},{80,24},{96,40},{112,56},{... | collective-permute-start | bytes 147464 | tf_op jit(solution)/shard_map/ppermute | solution.py:44
  14.3 1.9 %bitcast_convert_fusion = bf16[512,320]{1,0:T(8,128)(2,1)} fusion(f32[1,1,16,32,320]{4,3,2,1,0:T(8,128)} %param.9), kind=kLoop, calls=%fused_computation.10 | loop fusion | flops 163840 | bytes 983040 | tf_op jit(solution)/shard_map/convert_element_type | solution.py:246
  16.2 1.0 pad_maximum_fusion
  17.5 1.0 broadcast_in_dim.6
  18.5 4.5 %all-to-all-start = ((bf16[4,304,384]{2,1,0:T(8,128)(2,1)}), bf16[4,304,384]{2,1,0:T(8,128)(2,1)S(1)}, u32[]{:S(2)}, u32[]{:S(2)}) async-start(bf16[4,304,384]{2,1,0:T(8,128)(2,1)} %broadcast_in_dim.6), calls=%async_computation | async-start | bytes 1867776 | tf_op jit(solution)/shard_map/all_to_all | solution.py:53
  23.0 1.4 %collective-permute-start.4 = (bf16[512,320]{1,0:T(8,128)(2,1)}, bf16[512,320]{1,0:T(8,128)(2,1)}, u32[]{:S(2)}, u32[]{:S(2)}) collective-permute-start(bf16[512,320]{1,0:T(8,128)(2,1)} %bitcast_convert_fusion), channel_id=1, source_target_pairs={{112,128},{128,112},{240,256},{256,240},{368,384},{384,368},{113,1... | collective-permute-start | bytes 983048 | tf_op jit(solution)/shard_map/ppermute | solution.py:252
  24.4 3.7 %collective-permute-start.3 = (bf16[512,320]{1,0:T(8,128)(2,1)}, bf16[512,320]{1,0:T(8,128)(2,1)}, u32[]{:S(2)}, u32[]{:S(2)}) collective-permute-start(bf16[512,320]{1,0:T(8,128)(2,1)} %bitcast_convert_fusion), channel_id=1, source_target_pairs={{0,16},{16,32},{32,48},{48,64},{64,80},{80,96},{96,112},{128,144},... | collective-permute-start | bytes 983048 | tf_op jit(solution)/shard_map/ppermute | solution.py:254
  28.1 2.9 %collective-permute-start.2 = (bf16[512,320]{1,0:T(8,128)(2,1)}, bf16[512,320]{1,0:T(8,128)(2,1)}, u32[]{:S(2)}, u32[]{:S(2)}) collective-permute-start(bf16[512,320]{1,0:T(8,128)(2,1)} %bitcast_convert_fusion), channel_id=1, source_target_pairs={{16,0},{32,16},{48,32},{64,48},{80,64},{96,80},{112,96},{144,128},... | collective-permute-start | bytes 983048 | tf_op jit(solution)/shard_map/ppermute | solution.py:253
  30.9 5.5 %all-to-all-done.gathered.own_m = bf16[4,304,384]{2,1,0:T(8,128)(2,1)S(1)} async-done(((bf16[4,304,384]{2,1,0:T(8,128)(2,1)}), bf16[4,304,384]{2,1,0:T(8,128)(2,1)S(1)}, u32[]{:S(2)}, u32[]{:S(2)}) %all-to-all-start) | async-done | bytes 933920 | tf_op jit(solution)/shard_map/all_to_all | solution.py:53
  36.4 14.6 %all-gather = bf16[1024,384]{1,0:T(8,128)(2,1)S(1)} all-gather(bf16[256,384]{1,0:T(8,128)(2,1)S(1)} %apart.1), channel_id=2, replica_groups=mesh['x'=4,'m'=2,'k'=4,'h'=2,'y'=4,'c'=2] {'x'}, dimensions={0}, use_global_device_ids=true | all-gather | bytes 983040 | tf_op jit(solution)/shard_map/all_gather | solution.py:259
  51.0 1.9 %collective-permute-start.1 = (bf16[4,304,384]{2,1,0:T(8,128)(2,1)S(1)}, bf16[4,304,384]{2,1,0:T(8,128)(2,1)}, u32[]{:S(2)}, u32[]{:S(2)}) collective-permute-start(bf16[4,304,384]{2,1,0:T(8,128)(2,1)S(1)} %all-to-all-done.gathered.own_m), channel_id=1, source_target_pairs={{0,1},{1,0},{2,3},{3,2},{4,5},{5,4},{6,7},{7,6},{8,9},{9,8},{10,11... | collective-permute-start | bytes 2801672 | tf_op jit(solution)/shard_map/ppermute | solution.py:48
  53.0 2.4 %collective-permute-start.5 = (bf16[4,256,384]{2,1,0:T(8,128)(2,1)S(1)}, bf16[4,256,384]{2,1,0:T(8,128)(2,1)S(1)}, u32[]{:S(2)}, u32[]{:S(2)}) collective-permute-start(bf16[4,256,384]{2,1,0:T(8,128)(2,1)S(1)} %bitcast.14), channel_id=1, source_target_pairs={{0,1},{1,0},{2,3},{3,2},{4,5},{5,4},{6,7},{7,6},{8,9},{9,8},{10,11... | collective-permute-start | bytes 2359304 | tf_op jit(solution)/shard_map/ppermute | solution.py:48
  55.8 1.0 copy-done
  57.3 6.3 %forward.1 = (bf16[12,2,160,320]{3,2,1,0:T(8,128)(2,1)}, bf16[512,320]{1,0:T(8,128)(2,1)}, f32[512,320]{1,0:T(8,128)S(1)}, f32[4,4,2,16,320]{4,3,2,1,0:T(8,128)S(1)}, f32[4,4,2,16,320]{4,3,2,1,0:T(8,128)S(1)}) custom-call(s32[4]{0:T(128)S(1)} %pad_add_fusion.place, bf16[4,304,384]{2,1,0:T(8,128)(2,1)} %copy-done.1, ...), custom_call_target="tpu_custom_call" | custom-call | flops 10000000 | bytes 1000000 | tf_op jit(solution)/shard_map/forward/pallas_call | solution.py:224
  63.6 0.9 copy-done.3
  64.4 2.3 %collective-permute-start.6 = (f32[4,4,2,16,320]{4,3,2,1,0:T(8,128)S(1)}, f32[4,4,2,16,320]{4,3,2,1,0:T(8,128)S(1)}, u32[]{:S(2)}, u32[]{:S(2)}) collective-permute-start(f32[4,4,2,16,320]{4,3,2,1,0:T(8,128)S(1)} %get-tuple-element.45), channel_id=1, source_target_pairs={{0,1},{1,0},{2,3},{3,2},{4,5},{5,4},{6,7},{7,6},{8,9},{9,8},{10,11... | collective-permute-start | bytes 1966088 | tf_op jit(solution)/shard_map/ppermute | solution.py:48
  66.7 1.9 %collective-permute-done.6 = f32[4,4,2,16,320]{4,3,2,1,0:T(8,128)S(1)} collective-permute-done((f32[4,4,2,16,320]{4,3,2,1,0:T(8,128)S(1)}, f32[4,4,2,16,320]{4,3,2,1,0:T(8,128)S(1)}, u32[]{:S(2)}, u32[]{:S(2)}) %collective-permute-start.6) | collective-permute-done | bytes 655392 | tf_op jit(solution)/shard_map/ppermute | solution.py:48
  68.6 0.8 add_convert_fusion
  69.5 5.6 %all-to-all-start.1 = ((bf16[16,2,16,320]{3,2,1,0:T(8,128)(2,1)}), bf16[16,2,16,320]{3,2,1,0:T(8,128)(2,1)S(1)}, u32[]{:S(2)}, u32[]{:S(2)}) async-start(bf16[16,2,16,320]{3,2,1,0:T(8,128)(2,1)} %bitcast.7), calls=%async_computation.1 | async-start | bytes 786432 | tf_op jit(solution)/shard_map/all_to_all | solution.py:275
  75.1 3.9 %collective-permute-start.9 = (bf16[512,320]{1,0:T(8,128)(2,1)}, bf16[512,320]{1,0:T(8,128)(2,1)}, u32[]{:S(2)}, u32[]{:S(2)}) collective-permute-start(bf16[512,320]{1,0:T(8,128)(2,1)} %get-tuple-element.57.hidden_h), channel_id=1, source_target_pairs={{16,0},{32,16},{48,32},{64,48},{80,64},{96,80},{112,96},{144,128},... | collective-permute-start | bytes 983048 | tf_op jit(solution)/shard_map/ppermute | solution.py:277
  78.9 2.0 %collective-permute-start.8 = (bf16[512,320]{1,0:T(8,128)(2,1)}, bf16[512,320]{1,0:T(8,128)(2,1)}, u32[]{:S(2)}, u32[]{:S(2)}) collective-permute-start(bf16[512,320]{1,0:T(8,128)(2,1)} %get-tuple-element.57.hidden_h), channel_id=1, source_target_pairs={{0,16},{16,32},{32,48},{48,64},{64,80},{80,96},{96,112},{128,144},... | collective-permute-start | bytes 983048 | tf_op jit(solution)/shard_map/ppermute | solution.py:276
  80.9 4.5 %all-to-all-done.1.parts = bf16[16,2,16,320]{3,2,1,0:T(8,128)(2,1)S(1)} async-done(((bf16[16,2,16,320]{3,2,1,0:T(8,128)(2,1)}), bf16[16,2,16,320]{3,2,1,0:T(8,128)(2,1)S(1)}, u32[]{:S(2)}, u32[]{:S(2)}) %all-to-all-start.1) | async-done | bytes 327712 | tf_op jit(solution)/shard_map/all_to_all | solution.py:275
  85.4 1.2 split.1
  86.6 4.3 %collective-permute-start.7 = (f32[16,320]{1,0:T(8,128)}, f32[16,320]{1,0:T(8,128)}, u32[]{:S(2)}, u32[]{:S(2)}) collective-permute-start(f32[16,320]{1,0:T(8,128)} %get-tuple-element.49), channel_id=1, source_target_pairs={{0,72},{16,88},{32,104},{48,120},{64,8},{80,24},{96,40},{112,56},{... | collective-permute-start | bytes 61448 | tf_op jit(solution)/shard_map/ppermute | solution.py:44
  92.2 4.4 %collective-permute-done.7 = f32[16,320]{1,0:T(8,128)} collective-permute-done((f32[16,320]{1,0:T(8,128)}, f32[16,320]{1,0:T(8,128)}, u32[]{:S(2)}, u32[]{:S(2)}) %collective-permute-start.7) | collective-permute-done | bytes 20512 | tf_op jit(solution)/shard_map/ppermute | solution.py:44
  96.6 0.7 add_convert_fusion.1
  98.0 9.1 %all-to-all-start.2 = ((bf16[8,16,320]{2,1,0:T(8,128)(2,1)}), bf16[8,16,320]{2,1,0:T(8,128)(2,1)S(1)}, u32[]{:S(2)}, u32[]{:S(2)}) async-start(bf16[8,16,320]{2,1,0:T(8,128)(2,1)} %broadcast_in_dim.7), calls=%async_computation.2 | async-start | bytes 196608 | tf_op jit(solution)/shard_map/all_to_all | solution.py:53
  107.1 7.5 %backward.1 = f32[512,320]{1,0:T(8,128)} custom-call(s32[4]{0:T(128)} %copy-done.4, bf16[12,2,160,320]{3,2,1,0:T(8,128)(2,1)} %get-tuple-element.54.w_h, f32[512,320]{1,0:T(8,128)} %copy-done.3, f32[512,320]{1,0:T(8,128)} %bitcast.17, bf16[512,320]{1,0:T(8,128)(2,1)} %collective-permute-done.3.cot_prev.prev_h, ...), custom_call_target="tpu_custom_call" | custom-call | flops 10000000 | bytes 1000000 | tf_op jit(solution)/shard_map/backward/pallas_call | solution.py:224
  115.3 4.3 %output.1 = f32[512,320]{1,0:T(8,128)} custom-call(s32[4]{0:T(128)} %copy-done.4, bf16[12,2,160,320]{3,2,1,0:T(8,128)(2,1)} %get-tuple-element.54.w_h, f32[512,320]{1,0:T(8,128)} %bitcast.12, bf16[512,320]{1,0:T(8,128)(2,1)} %get-tuple-element.57.hidden_h, bf16[512,320]{1,0:T(8,128)(2,1)} %collective-permute-done.8.prev_h, ...), custom_call_target="tpu_custom_call" | custom-call | flops 10000000 | bytes 1000000 | tf_op jit(solution)/shard_map/output/pallas_call | solution.py:224
  119.7 8.2 %all_to_all.20 = f32[4,16,320]{2,1,0:T(8,128)S(1)} all-to-all(f32[4,16,320]{2,1,0:T(8,128)S(1)} %broadcast_in_dim.8), channel_id=1, replica_groups=mesh['x'=4,'m'=2,'k'=4,'h'=2,'y'=4,'c'=2] {'x'}, dimensions={0} | all-to-all | bytes 163840 | tf_op jit(solution)/shard_map/all_to_all | solution.py:53
  (38 shorter events, 4.5 us)
Async XLA Ops:
  2.4 15.0 %collective-permute-start = (bf16[64,384]{1,0:T(8,128)(2,1)S(1)}, bf16[64,384]{1,0:T(8,128)(2,1)S(1)}, u32[]{:S(2)}, u32[]{:S(2)}) collective-permute-start(bf16[64,384]{1,0:T(8,128)(2,1)S(1)} %pad.8), channel_id=1, source_target_pairs={{0,72},{16,88},{32,104},{48,120},{64,8},{80,24},{96,40},{112,56},{... | collective-permute-start | bytes 147464 | tf_op jit(solution)/shard_map/ppermute | solution.py:44
  18.5 17.9 %all-to-all-start = ((bf16[4,304,384]{2,1,0:T(8,128)(2,1)}), bf16[4,304,384]{2,1,0:T(8,128)(2,1)S(1)}, u32[]{:S(2)}, u32[]{:S(2)}) async-start(bf16[4,304,384]{2,1,0:T(8,128)(2,1)} %broadcast_in_dim.6), calls=%async_computation | async-start | bytes 1867776 | tf_op jit(solution)/shard_map/all_to_all | solution.py:53
  23.0 30.0 %collective-permute-start.4 = (bf16[512,320]{1,0:T(8,128)(2,1)}, bf16[512,320]{1,0:T(8,128)(2,1)}, u32[]{:S(2)}, u32[]{:S(2)}) collective-permute-start(bf16[512,320]{1,0:T(8,128)(2,1)} %bitcast_convert_fusion), channel_id=1, source_target_pairs={{112,128},{128,112},{240,256},{256,240},{368,384},{384,368},{113,1... | collective-permute-start | bytes 983048 | tf_op jit(solution)/shard_map/ppermute | solution.py:252
  24.4 28.6 %collective-permute-start.3 = (bf16[512,320]{1,0:T(8,128)(2,1)}, bf16[512,320]{1,0:T(8,128)(2,1)}, u32[]{:S(2)}, u32[]{:S(2)}) collective-permute-start(bf16[512,320]{1,0:T(8,128)(2,1)} %bitcast_convert_fusion), channel_id=1, source_target_pairs={{0,16},{16,32},{32,48},{48,64},{64,80},{80,96},{96,112},{128,144},... | collective-permute-start | bytes 983048 | tf_op jit(solution)/shard_map/ppermute | solution.py:254
  28.1 24.9 %collective-permute-start.2 = (bf16[512,320]{1,0:T(8,128)(2,1)}, bf16[512,320]{1,0:T(8,128)(2,1)}, u32[]{:S(2)}, u32[]{:S(2)}) collective-permute-start(bf16[512,320]{1,0:T(8,128)(2,1)} %bitcast_convert_fusion), channel_id=1, source_target_pairs={{16,0},{32,16},{48,32},{64,48},{80,64},{96,80},{112,96},{144,128},... | collective-permute-start | bytes 983048 | tf_op jit(solution)/shard_map/ppermute | solution.py:253
  36.4 14.6 %copy-start.1 = (bf16[4,304,384]{2,1,0:T(8,128)(2,1)}, bf16[4,304,384]{2,1,0:T(8,128)(2,1)S(1)}, u32[]{:S(2)}) copy-start(bf16[4,304,384]{2,1,0:T(8,128)(2,1)S(1)} %all-to-all-done.gathered.own_m) | copy-start | bytes 2801668
  36.4 19.0 %copy-start.6 = (f32[320]{0:T(512)S(1)}, f32[320]{0:T(512)}, u32[]{:S(2)}) copy-start(f32[320]{0:T(512)} %param.7) | copy-start | bytes 3844
  36.4 19.1 %copy-start.2 = (f32[1,1,16,32,320]{4,3,2,1,0:T(8,128)S(1)}, f32[1,1,16,32,320]{4,3,2,1,0:T(8,128)}, u32[]{:S(2)}) copy-start(f32[1,1,16,32,320]{4,3,2,1,0:T(8,128)} %param.5) | copy-start | bytes 1966084
  51.0 6.3 %collective-permute-start.1 = (bf16[4,304,384]{2,1,0:T(8,128)(2,1)S(1)}, bf16[4,304,384]{2,1,0:T(8,128)(2,1)}, u32[]{:S(2)}, u32[]{:S(2)}) collective-permute-start(bf16[4,304,384]{2,1,0:T(8,128)(2,1)S(1)} %all-to-all-done.gathered.own_m), channel_id=1, source_target_pairs={{0,1},{1,0},{2,3},{3,2},{4,5},{5,4},{6,7},{7,6},{8,9},{9,8},{10,11... | collective-permute-start | bytes 2801672 | tf_op jit(solution)/shard_map/ppermute | solution.py:48
  53.0 4.3 %collective-permute-start.5 = (bf16[4,256,384]{2,1,0:T(8,128)(2,1)S(1)}, bf16[4,256,384]{2,1,0:T(8,128)(2,1)S(1)}, u32[]{:S(2)}, u32[]{:S(2)}) collective-permute-start(bf16[4,256,384]{2,1,0:T(8,128)(2,1)S(1)} %bitcast.14), channel_id=1, source_target_pairs={{0,1},{1,0},{2,3},{3,2},{4,5},{5,4},{6,7},{7,6},{8,9},{9,8},{10,11... | collective-permute-start | bytes 2359304 | tf_op jit(solution)/shard_map/ppermute | solution.py:48
  55.5 35.4 %copy-start.4 = (s32[4]{0:T(128)}, s32[4]{0:T(128)S(1)}, u32[]{:S(2)}) copy-start(s32[4]{0:T(128)S(1)} %pad_add_fusion.place) | copy-start | bytes 52
  55.8 1.0 copy-start
  63.6 0.9 copy-start.3
  64.4 4.2 %collective-permute-start.6 = (f32[4,4,2,16,320]{4,3,2,1,0:T(8,128)S(1)}, f32[4,4,2,16,320]{4,3,2,1,0:T(8,128)S(1)}, u32[]{:S(2)}, u32[]{:S(2)}) collective-permute-start(f32[4,4,2,16,320]{4,3,2,1,0:T(8,128)S(1)} %get-tuple-element.45), channel_id=1, source_target_pairs={{0,1},{1,0},{2,3},{3,2},{4,5},{5,4},{6,7},{7,6},{8,9},{9,8},{10,11... | collective-permute-start | bytes 1966088 | tf_op jit(solution)/shard_map/ppermute | solution.py:48
  69.5 16.0 %all-to-all-start.1 = ((bf16[16,2,16,320]{3,2,1,0:T(8,128)(2,1)}), bf16[16,2,16,320]{3,2,1,0:T(8,128)(2,1)S(1)}, u32[]{:S(2)}, u32[]{:S(2)}) async-start(bf16[16,2,16,320]{3,2,1,0:T(8,128)(2,1)} %bitcast.7), calls=%async_computation.1 | async-start | bytes 786432 | tf_op jit(solution)/shard_map/all_to_all | solution.py:275
  75.1 17.1 %collective-permute-start.9 = (bf16[512,320]{1,0:T(8,128)(2,1)}, bf16[512,320]{1,0:T(8,128)(2,1)}, u32[]{:S(2)}, u32[]{:S(2)}) collective-permute-start(bf16[512,320]{1,0:T(8,128)(2,1)} %get-tuple-element.57.hidden_h), channel_id=1, source_target_pairs={{16,0},{32,16},{48,32},{64,48},{80,64},{96,80},{112,96},{144,128},... | collective-permute-start | bytes 983048 | tf_op jit(solution)/shard_map/ppermute | solution.py:277
  78.9 13.3 %collective-permute-start.8 = (bf16[512,320]{1,0:T(8,128)(2,1)}, bf16[512,320]{1,0:T(8,128)(2,1)}, u32[]{:S(2)}, u32[]{:S(2)}) collective-permute-start(bf16[512,320]{1,0:T(8,128)(2,1)} %get-tuple-element.57.hidden_h), channel_id=1, source_target_pairs={{0,16},{16,32},{32,48},{48,64},{64,80},{80,96},{96,112},{128,144},... | collective-permute-start | bytes 983048 | tf_op jit(solution)/shard_map/ppermute | solution.py:276
  86.6 10.0 %collective-permute-start.7 = (f32[16,320]{1,0:T(8,128)}, f32[16,320]{1,0:T(8,128)}, u32[]{:S(2)}, u32[]{:S(2)}) collective-permute-start(f32[16,320]{1,0:T(8,128)} %get-tuple-element.49), channel_id=1, source_target_pairs={{0,72},{16,88},{32,104},{48,120},{64,8},{80,24},{96,40},{112,56},{... | collective-permute-start | bytes 61448 | tf_op jit(solution)/shard_map/ppermute | solution.py:44
  91.5 23.1 %collective-permute-start.10 = (bf16[512,320]{1,0:T(8,128)(2,1)}, bf16[512,320]{1,0:T(8,128)(2,1)S(1)}, u32[]{:S(2)}, u32[]{:S(2)}) collective-permute-start(bf16[512,320]{1,0:T(8,128)(2,1)} %get-tuple-element.57.hidden_h), channel_id=1, source_target_pairs={{112,128},{128,112},{240,256},{256,240},{368,384},{384,368},{113,1... | collective-permute-start | bytes 983048 | tf_op jit(solution)/shard_map/ppermute | solution.py:283
  98.0 21.7 %all-to-all-start.2 = ((bf16[8,16,320]{2,1,0:T(8,128)(2,1)}), bf16[8,16,320]{2,1,0:T(8,128)(2,1)S(1)}, u32[]{:S(2)}, u32[]{:S(2)}) async-start(bf16[8,16,320]{2,1,0:T(8,128)(2,1)} %broadcast_in_dim.7), calls=%async_computation.2 | async-start | bytes 196608 | tf_op jit(solution)/shard_map/all_to_all | solution.py:53
  114.6 0.7 copy-start.5

commit v12 on v11

--- a/solution.py
+++ b/solution.py
@@ -295,7 +295,7 @@
         output_kernel,
         [(place, "s"), (w_all, "h"), (video_f, "h"), (hidden, "h"), (prev, "h"), (after, "h"), (hidden_far, "h")],
         [(FRAME_F, "v")],
-        [((3, 2, HALF, C), BF), FRAME_F, FRAME_B, FRAME_B, FRAME_B, FRAME_B], 6, 0.01, "output",
+        [((3, 2, HALF, C), BF), FRAME_F, FRAME_B, FRAME_B, FRAME_B, FRAME_B], 6, 0.01, "output", 40,
     )
     part, output = tie((part, output))
     part = part.astype(F32)

time: 129 us -> 130 us (level)
    unnamed x14 -> x18, local copies, waits for them, and re-layouts: 2.65 us -> 2.49 us
where the time goes in v12:
time: 130 us; the launch traced here: 129 us
  starting transfers between devices  56.4 us (43%)
  blocking collectives  22.8 us (18%)
  Pallas kernels  20.2 us (16%)
  waiting for transfers between devices  16.8 us (13%)
  other arithmetic  7.27 us (6%)
  local copies, waits for them, and re-layouts  4.95 us (4%)
    pallas_call x7, Pallas kernels, kernel_call(): pl.pallas_call(body, out_shape=tuple((jax.ShapeDtypeStruct(*o[0]) for o i...  20.2 us
    ppermute x2, starting transfers between devices, across(): return lax.ppermute(a, ('m', 'k', 'h'), ACROSS)  16.1 us
    all_gather x1, blocking collectives, on_device(): oth_m = lax.all_gather(oth_m, 'x')  14.6 us
    all_to_all x2, starting transfers between devices, to_all(): lax.all_to_all(jnp.broadcast_to(a[None], (n, *a.shape)), axes, 0, 0, tile...  13.6 us
    all_to_all x1, blocking collectives, to_all(): lax.all_to_all(jnp.broadcast_to(a[None], (n, *a.shape)), axes, 0, 0, tile...  8.21 us
    ppermute x3, starting transfers between devices, core_swap(): return lax.ppermute(a, 'c', [(0, 1), (1, 0)])  6.59 us
    all_to_all x1, starting transfers between devices, on_device(): part = lax.all_to_all(part.reshape(16, 2, 16, C), PLANE, 0, 0, tiled=True)  5.62 us
    all_to_all x2, waiting for transfers between devices, to_all(): lax.all_to_all(jnp.broadcast_to(a[None], (n, *a.shape)), axes, 0, 0, tile...  5.44 us
  transfers between devices with their start and end apart: 14, of which 6 were waited for; matrix products, arithmetic and copies ran while one was open for 3% of the time, Pallas kernels for 11%

profile of v12, /device:TPU:32, one launch (start us, length us, event | category | flops | bytes accessed | tf_op | source)
XLA Modules:
  0.0 129.4 jit_solution(1261439819363325194)
XLA Ops:
  0.6 0.9 convert_element_type.20
  1.5 0.8 fusion
  2.4 11.8 %collective-permute-start = (bf16[64,384]{1,0:T(8,128)(2,1)S(1)}, bf16[64,384]{1,0:T(8,128)(2,1)S(1)}, u32[]{:S(2)}, u32[]{:S(2)}) collective-permute-start(bf16[64,384]{1,0:T(8,128)(2,1)S(1)} %pad.8), channel_id=1, source_target_pairs={{0,72},{16,88},{32,104},{48,120},{64,8},{80,24},{96,40},{112,56},{... | collective-permute-start | bytes 147464 | tf_op jit(solution)/shard_map/ppermute | solution.py:44
  14.3 1.9 %bitcast_convert_fusion = bf16[512,320]{1,0:T(8,128)(2,1)} fusion(f32[1,1,16,32,320]{4,3,2,1,0:T(8,128)} %param.9), kind=kLoop, calls=%fused_computation.10 | loop fusion | flops 163840 | bytes 983040 | tf_op jit(solution)/shard_map/convert_element_type | solution.py:246
  16.2 1.0 pad_maximum_fusion
  17.5 1.0 broadcast_in_dim.6
  18.5 4.5 %all-to-all-start = ((bf16[4,304,384]{2,1,0:T(8,128)(2,1)}), bf16[4,304,384]{2,1,0:T(8,128)(2,1)S(1)}, u32[]{:S(2)}, u32[]{:S(2)}) async-start(bf16[4,304,384]{2,1,0:T(8,128)(2,1)} %broadcast_in_dim.6), calls=%async_computation | async-start | bytes 1867776 | tf_op jit(solution)/shard_map/all_to_all | solution.py:53
  23.0 1.4 %collective-permute-start.4 = (bf16[512,320]{1,0:T(8,128)(2,1)}, bf16[512,320]{1,0:T(8,128)(2,1)}, u32[]{:S(2)}, u32[]{:S(2)}) collective-permute-start(bf16[512,320]{1,0:T(8,128)(2,1)} %bitcast_convert_fusion), channel_id=1, source_target_pairs={{112,128},{128,112},{240,256},{256,240},{368,384},{384,368},{113,1... | collective-permute-start | bytes 983048 | tf_op jit(solution)/shard_map/ppermute | solution.py:252
  24.4 3.7 %collective-permute-start.3 = (bf16[512,320]{1,0:T(8,128)(2,1)}, bf16[512,320]{1,0:T(8,128)(2,1)}, u32[]{:S(2)}, u32[]{:S(2)}) collective-permute-start(bf16[512,320]{1,0:T(8,128)(2,1)} %bitcast_convert_fusion), channel_id=1, source_target_pairs={{0,16},{16,32},{32,48},{48,64},{64,80},{80,96},{96,112},{128,144},... | collective-permute-start | bytes 983048 | tf_op jit(solution)/shard_map/ppermute | solution.py:254
  28.1 2.9 %collective-permute-start.2 = (bf16[512,320]{1,0:T(8,128)(2,1)}, bf16[512,320]{1,0:T(8,128)(2,1)}, u32[]{:S(2)}, u32[]{:S(2)}) collective-permute-start(bf16[512,320]{1,0:T(8,128)(2,1)} %bitcast_convert_fusion), channel_id=1, source_target_pairs={{16,0},{32,16},{48,32},{64,48},{80,64},{96,80},{112,96},{144,128},... | collective-permute-start | bytes 983048 | tf_op jit(solution)/shard_map/ppermute | solution.py:253
  30.9 5.4 %all-to-all-done.gathered.own_m = bf16[4,304,384]{2,1,0:T(8,128)(2,1)S(1)} async-done(((bf16[4,304,384]{2,1,0:T(8,128)(2,1)}), bf16[4,304,384]{2,1,0:T(8,128)(2,1)S(1)}, u32[]{:S(2)}, u32[]{:S(2)}) %all-to-all-start) | async-done | bytes 933920 | tf_op jit(solution)/shard_map/all_to_all | solution.py:53
  36.4 14.6 %all-gather = bf16[1024,384]{1,0:T(8,128)(2,1)S(1)} all-gather(bf16[256,384]{1,0:T(8,128)(2,1)S(1)} %apart.1), channel_id=2, replica_groups=mesh['x'=4,'m'=2,'k'=4,'h'=2,'y'=4,'c'=2] {'x'}, dimensions={0}, use_global_device_ids=true | all-gather | bytes 983040 | tf_op jit(solution)/shard_map/all_gather | solution.py:259
  51.0 1.9 %collective-permute-start.1 = (bf16[4,304,384]{2,1,0:T(8,128)(2,1)S(1)}, bf16[4,304,384]{2,1,0:T(8,128)(2,1)}, u32[]{:S(2)}, u32[]{:S(2)}) collective-permute-start(bf16[4,304,384]{2,1,0:T(8,128)(2,1)S(1)} %all-to-all-done.gathered.own_m), channel_id=1, source_target_pairs={{0,1},{1,0},{2,3},{3,2},{4,5},{5,4},{6,7},{7,6},{8,9},{9,8},{10,11... | collective-permute-start | bytes 2801672 | tf_op jit(solution)/shard_map/ppermute | solution.py:48
  53.0 2.4 %collective-permute-start.5 = (bf16[4,256,384]{2,1,0:T(8,128)(2,1)S(1)}, bf16[4,256,384]{2,1,0:T(8,128)(2,1)S(1)}, u32[]{:S(2)}, u32[]{:S(2)}) collective-permute-start(bf16[4,256,384]{2,1,0:T(8,128)(2,1)S(1)} %bitcast.14), channel_id=1, source_target_pairs={{0,1},{1,0},{2,3},{3,2},{4,5},{5,4},{6,7},{7,6},{8,9},{9,8},{10,11... | collective-permute-start | bytes 2359304 | tf_op jit(solution)/shard_map/ppermute | solution.py:48
  55.8 1.0 copy-done.1
  57.3 6.3 %forward.1 = (bf16[12,2,160,320]{3,2,1,0:T(8,128)(2,1)}, bf16[512,320]{1,0:T(8,128)(2,1)}, f32[512,320]{1,0:T(8,128)S(1)}, f32[4,4,2,16,320]{4,3,2,1,0:T(8,128)S(1)}, f32[4,4,2,16,320]{4,3,2,1,0:T(8,128)S(1)}) custom-call(s32[4]{0:T(128)S(1)} %pad_add_fusion.place, bf16[4,304,384]{2,1,0:T(8,128)(2,1)} %copy-done.2, ...), custom_call_target="tpu_custom_call" | custom-call | flops 10000000 | bytes 1000000 | tf_op jit(solution)/shard_map/forward/pallas_call | solution.py:224
  63.6 0.9 copy-done.5
  64.4 2.3 %collective-permute-start.6 = (f32[4,4,2,16,320]{4,3,2,1,0:T(8,128)S(1)}, f32[4,4,2,16,320]{4,3,2,1,0:T(8,128)S(1)}, u32[]{:S(2)}, u32[]{:S(2)}) collective-permute-start(f32[4,4,2,16,320]{4,3,2,1,0:T(8,128)S(1)} %get-tuple-element.45), channel_id=1, source_target_pairs={{0,1},{1,0},{2,3},{3,2},{4,5},{5,4},{6,7},{7,6},{8,9},{9,8},{10,11... | collective-permute-start | bytes 1966088 | tf_op jit(solution)/shard_map/ppermute | solution.py:48
  66.7 1.9 %collective-permute-done.6 = f32[4,4,2,16,320]{4,3,2,1,0:T(8,128)S(1)} collective-permute-done((f32[4,4,2,16,320]{4,3,2,1,0:T(8,128)S(1)}, f32[4,4,2,16,320]{4,3,2,1,0:T(8,128)S(1)}, u32[]{:S(2)}, u32[]{:S(2)}) %collective-permute-start.6) | collective-permute-done | bytes 655392 | tf_op jit(solution)/shard_map/ppermute | solution.py:48
  68.6 0.8 add_convert_fusion
  69.5 5.6 %all-to-all-start.1 = ((bf16[16,2,16,320]{3,2,1,0:T(8,128)(2,1)}), bf16[16,2,16,320]{3,2,1,0:T(8,128)(2,1)S(1)}, u32[]{:S(2)}, u32[]{:S(2)}) async-start(bf16[16,2,16,320]{3,2,1,0:T(8,128)(2,1)} %bitcast.7), calls=%async_computation.1 | async-start | bytes 786432 | tf_op jit(solution)/shard_map/all_to_all | solution.py:275
  75.1 3.9 %collective-permute-start.9 = (bf16[512,320]{1,0:T(8,128)(2,1)}, bf16[512,320]{1,0:T(8,128)(2,1)}, u32[]{:S(2)}, u32[]{:S(2)}) collective-permute-start(bf16[512,320]{1,0:T(8,128)(2,1)} %get-tuple-element.57.hidden_h), channel_id=1, source_target_pairs={{16,0},{32,16},{48,32},{64,48},{80,64},{96,80},{112,96},{144,128},... | collective-permute-start | bytes 983048 | tf_op jit(solution)/shard_map/ppermute | solution.py:277
  79.0 2.0 %collective-permute-start.8 = (bf16[512,320]{1,0:T(8,128)(2,1)}, bf16[512,320]{1,0:T(8,128)(2,1)}, u32[]{:S(2)}, u32[]{:S(2)}) collective-permute-start(bf16[512,320]{1,0:T(8,128)(2,1)} %get-tuple-element.57.hidden_h), channel_id=1, source_target_pairs={{0,16},{16,32},{32,48},{48,64},{64,80},{80,96},{96,112},{128,144},... | collective-permute-start | bytes 983048 | tf_op jit(solution)/shard_map/ppermute | solution.py:276
  81.0 4.5 %all-to-all-done.1.parts = bf16[16,2,16,320]{3,2,1,0:T(8,128)(2,1)S(1)} async-done(((bf16[16,2,16,320]{3,2,1,0:T(8,128)(2,1)}), bf16[16,2,16,320]{3,2,1,0:T(8,128)(2,1)S(1)}, u32[]{:S(2)}, u32[]{:S(2)}) %all-to-all-start.1) | async-done | bytes 327712 | tf_op jit(solution)/shard_map/all_to_all | solution.py:275
  85.4 1.2 split.1
  86.6 4.3 %collective-permute-start.7 = (f32[16,320]{1,0:T(8,128)}, f32[16,320]{1,0:T(8,128)}, u32[]{:S(2)}, u32[]{:S(2)}) collective-permute-start(f32[16,320]{1,0:T(8,128)} %get-tuple-element.49), channel_id=1, source_target_pairs={{0,72},{16,88},{32,104},{48,120},{64,8},{80,24},{96,40},{112,56},{... | collective-permute-start | bytes 61448 | tf_op jit(solution)/shard_map/ppermute | solution.py:44
  92.2 4.4 %collective-permute-done.7 = f32[16,320]{1,0:T(8,128)} collective-permute-done((f32[16,320]{1,0:T(8,128)}, f32[16,320]{1,0:T(8,128)}, u32[]{:S(2)}, u32[]{:S(2)}) %collective-permute-start.7) | collective-permute-done | bytes 20512 | tf_op jit(solution)/shard_map/ppermute | solution.py:44
  98.0 9.1 %all-to-all-start.2 = ((bf16[8,16,320]{2,1,0:T(8,128)(2,1)}), bf16[8,16,320]{2,1,0:T(8,128)(2,1)}, u32[]{:S(2)}, u32[]{:S(2)}) async-start(bf16[8,16,320]{2,1,0:T(8,128)(2,1)} %broadcast_in_dim.7), calls=%async_computation.2 | async-start | bytes 196608 | tf_op jit(solution)/shard_map/all_to_all | solution.py:53
  107.1 8.0 %backward.1 = f32[512,320]{1,0:T(8,128)} custom-call(s32[4]{0:T(128)} %copy-done.6, bf16[12,2,160,320]{3,2,1,0:T(8,128)(2,1)} %get-tuple-element.54.w_h, f32[512,320]{1,0:T(8,128)} %copy-done.5, f32[512,320]{1,0:T(8,128)} %bitcast.17, bf16[512,320]{1,0:T(8,128)(2,1)} %collective-permute-done.3.cot_prev.prev_h, ...), custom_call_target="tpu_custom_call" | custom-call | flops 10000000 | bytes 1000000 | tf_op jit(solution)/shard_map/backward/pallas_call | solution.py:224
  115.7 4.0 %output.1 = f32[512,320]{1,0:T(8,128)} custom-call(s32[4]{0:T(128)S(1)} %copy-done.7, bf16[12,2,160,320]{3,2,1,0:T(8,128)(2,1)S(1)} %copy-done, f32[512,320]{1,0:T(8,128)S(1)} %bitcast.13, bf16[512,320]{1,0:T(8,128)(2,1)} %get-tuple-element.57.hidden_h, bf16[512,320]{1,0:T(8,128)(2,1)} %collective-permute-done.8.prev_h, ...), custom_call_target="tpu_custom_call" | custom-call | flops 10000000 | bytes 1000000 | tf_op jit(solution)/shard_map/output/pallas_call | solution.py:224
  119.6 0.9 convert_reduce_fusion
  120.6 8.2 %all_to_all.20 = f32[4,16,320]{2,1,0:T(8,128)S(1)} all-to-all(f32[4,16,320]{2,1,0:T(8,128)S(1)} %broadcast_in_dim.8), channel_id=1, replica_groups=mesh['x'=4,'m'=2,'k'=4,'h'=2,'y'=4,'c'=2] {'x'}, dimensions={0} | all-to-all | bytes 163840 | tf_op jit(solution)/shard_map/all_to_all | solution.py:53
  (42 shorter events, 5.1 us)
Async XLA Ops:
  2.4 15.0 %collective-permute-start = (bf16[64,384]{1,0:T(8,128)(2,1)S(1)}, bf16[64,384]{1,0:T(8,128)(2,1)S(1)}, u32[]{:S(2)}, u32[]{:S(2)}) collective-permute-start(bf16[64,384]{1,0:T(8,128)(2,1)S(1)} %pad.8), channel_id=1, source_target_pairs={{0,72},{16,88},{32,104},{48,120},{64,8},{80,24},{96,40},{112,56},{... | collective-permute-start | bytes 147464 | tf_op jit(solution)/shard_map/ppermute | solution.py:44
  18.5 17.9 %all-to-all-start = ((bf16[4,304,384]{2,1,0:T(8,128)(2,1)}), bf16[4,304,384]{2,1,0:T(8,128)(2,1)S(1)}, u32[]{:S(2)}, u32[]{:S(2)}) async-start(bf16[4,304,384]{2,1,0:T(8,128)(2,1)} %broadcast_in_dim.6), calls=%async_computation | async-start | bytes 1867776 | tf_op jit(solution)/shard_map/all_to_all | solution.py:53
  23.0 30.0 %collective-permute-start.4 = (bf16[512,320]{1,0:T(8,128)(2,1)}, bf16[512,320]{1,0:T(8,128)(2,1)}, u32[]{:S(2)}, u32[]{:S(2)}) collective-permute-start(bf16[512,320]{1,0:T(8,128)(2,1)} %bitcast_convert_fusion), channel_id=1, source_target_pairs={{112,128},{128,112},{240,256},{256,240},{368,384},{384,368},{113,1... | collective-permute-start | bytes 983048 | tf_op jit(solution)/shard_map/ppermute | solution.py:252
  24.4 28.6 %collective-permute-start.3 = (bf16[512,320]{1,0:T(8,128)(2,1)}, bf16[512,320]{1,0:T(8,128)(2,1)}, u32[]{:S(2)}, u32[]{:S(2)}) collective-permute-start(bf16[512,320]{1,0:T(8,128)(2,1)} %bitcast_convert_fusion), channel_id=1, source_target_pairs={{0,16},{16,32},{32,48},{48,64},{64,80},{80,96},{96,112},{128,144},... | collective-permute-start | bytes 983048 | tf_op jit(solution)/shard_map/ppermute | solution.py:254
  28.1 24.9 %collective-permute-start.2 = (bf16[512,320]{1,0:T(8,128)(2,1)}, bf16[512,320]{1,0:T(8,128)(2,1)}, u32[]{:S(2)}, u32[]{:S(2)}) collective-permute-start(bf16[512,320]{1,0:T(8,128)(2,1)} %bitcast_convert_fusion), channel_id=1, source_target_pairs={{16,0},{32,16},{48,32},{64,48},{80,64},{96,80},{112,96},{144,128},... | collective-permute-start | bytes 983048 | tf_op jit(solution)/shard_map/ppermute | solution.py:253
  36.4 14.6 %copy-start.2 = (bf16[4,304,384]{2,1,0:T(8,128)(2,1)}, bf16[4,304,384]{2,1,0:T(8,128)(2,1)S(1)}, u32[]{:S(2)}) copy-start(bf16[4,304,384]{2,1,0:T(8,128)(2,1)S(1)} %all-to-all-done.gathered.own_m) | copy-start | bytes 2801668
  36.4 19.0 %copy-start.8 = (f32[320]{0:T(512)S(1)}, f32[320]{0:T(512)}, u32[]{:S(2)}) copy-start(f32[320]{0:T(512)} %param.7) | copy-start | bytes 3844
  36.4 19.1 %copy-start.3 = (f32[1,1,16,32,320]{4,3,2,1,0:T(8,128)S(1)}, f32[1,1,16,32,320]{4,3,2,1,0:T(8,128)}, u32[]{:S(2)}) copy-start(f32[1,1,16,32,320]{4,3,2,1,0:T(8,128)} %param.5) | copy-start | bytes 1966084
  51.0 6.3 %collective-permute-start.1 = (bf16[4,304,384]{2,1,0:T(8,128)(2,1)S(1)}, bf16[4,304,384]{2,1,0:T(8,128)(2,1)}, u32[]{:S(2)}, u32[]{:S(2)}) collective-permute-start(bf16[4,304,384]{2,1,0:T(8,128)(2,1)S(1)} %all-to-all-done.gathered.own_m), channel_id=1, source_target_pairs={{0,1},{1,0},{2,3},{3,2},{4,5},{5,4},{6,7},{7,6},{8,9},{9,8},{10,11... | collective-permute-start | bytes 2801672 | tf_op jit(solution)/shard_map/ppermute | solution.py:48
  53.0 4.3 %collective-permute-start.5 = (bf16[4,256,384]{2,1,0:T(8,128)(2,1)S(1)}, bf16[4,256,384]{2,1,0:T(8,128)(2,1)S(1)}, u32[]{:S(2)}, u32[]{:S(2)}) collective-permute-start(bf16[4,256,384]{2,1,0:T(8,128)(2,1)S(1)} %bitcast.14), channel_id=1, source_target_pairs={{0,1},{1,0},{2,3},{3,2},{4,5},{5,4},{6,7},{7,6},{8,9},{9,8},{10,11... | collective-permute-start | bytes 2359304 | tf_op jit(solution)/shard_map/ppermute | solution.py:48
  55.5 35.4 %copy-start.6 = (s32[4]{0:T(128)}, s32[4]{0:T(128)S(1)}, u32[]{:S(2)}) copy-start(s32[4]{0:T(128)S(1)} %pad_add_fusion.place) | copy-start | bytes 52
  55.8 1.0 copy-start.1
  63.6 0.9 copy-start.5
  64.4 4.2 %collective-permute-start.6 = (f32[4,4,2,16,320]{4,3,2,1,0:T(8,128)S(1)}, f32[4,4,2,16,320]{4,3,2,1,0:T(8,128)S(1)}, u32[]{:S(2)}, u32[]{:S(2)}) collective-permute-start(f32[4,4,2,16,320]{4,3,2,1,0:T(8,128)S(1)} %get-tuple-element.45), channel_id=1, source_target_pairs={{0,1},{1,0},{2,3},{3,2},{4,5},{5,4},{6,7},{7,6},{8,9},{9,8},{10,11... | collective-permute-start | bytes 1966088 | tf_op jit(solution)/shard_map/ppermute | solution.py:48
  69.5 16.0 %all-to-all-start.1 = ((bf16[16,2,16,320]{3,2,1,0:T(8,128)(2,1)}), bf16[16,2,16,320]{3,2,1,0:T(8,128)(2,1)S(1)}, u32[]{:S(2)}, u32[]{:S(2)}) async-start(bf16[16,2,16,320]{3,2,1,0:T(8,128)(2,1)} %bitcast.7), calls=%async_computation.1 | async-start | bytes 786432 | tf_op jit(solution)/shard_map/all_to_all | solution.py:275
  75.1 17.1 %collective-permute-start.9 = (bf16[512,320]{1,0:T(8,128)(2,1)}, bf16[512,320]{1,0:T(8,128)(2,1)}, u32[]{:S(2)}, u32[]{:S(2)}) collective-permute-start(bf16[512,320]{1,0:T(8,128)(2,1)} %get-tuple-element.57.hidden_h), channel_id=1, source_target_pairs={{16,0},{32,16},{48,32},{64,48},{80,64},{96,80},{112,96},{144,128},... | collective-permute-start | bytes 983048 | tf_op jit(solution)/shard_map/ppermute | solution.py:277
  79.0 13.3 %collective-permute-start.8 = (bf16[512,320]{1,0:T(8,128)(2,1)}, bf16[512,320]{1,0:T(8,128)(2,1)}, u32[]{:S(2)}, u32[]{:S(2)}) collective-permute-start(bf16[512,320]{1,0:T(8,128)(2,1)} %get-tuple-element.57.hidden_h), channel_id=1, source_target_pairs={{0,16},{16,32},{32,48},{48,64},{64,80},{80,96},{96,112},{128,144},... | collective-permute-start | bytes 983048 | tf_op jit(solution)/shard_map/ppermute | solution.py:276
  86.6 10.0 %collective-permute-start.7 = (f32[16,320]{1,0:T(8,128)}, f32[16,320]{1,0:T(8,128)}, u32[]{:S(2)}, u32[]{:S(2)}) collective-permute-start(f32[16,320]{1,0:T(8,128)} %get-tuple-element.49), channel_id=1, source_target_pairs={{0,72},{16,88},{32,104},{48,120},{64,8},{80,24},{96,40},{112,56},{... | collective-permute-start | bytes 61448 | tf_op jit(solution)/shard_map/ppermute | solution.py:44
  91.5 23.5 %collective-permute-start.10 = (bf16[512,320]{1,0:T(8,128)(2,1)}, bf16[512,320]{1,0:T(8,128)(2,1)S(1)}, u32[]{:S(2)}, u32[]{:S(2)}) collective-permute-start(bf16[512,320]{1,0:T(8,128)(2,1)} %get-tuple-element.57.hidden_h), channel_id=1, source_target_pairs={{112,128},{128,112},{240,256},{256,240},{368,384},{384,368},{113,1... | collective-permute-start | bytes 983048 | tf_op jit(solution)/shard_map/ppermute | solution.py:283
  98.0 21.6 %all-to-all-start.2 = ((bf16[8,16,320]{2,1,0:T(8,128)(2,1)}), bf16[8,16,320]{2,1,0:T(8,128)(2,1)}, u32[]{:S(2)}, u32[]{:S(2)}) async-start(bf16[8,16,320]{2,1,0:T(8,128)(2,1)} %broadcast_in_dim.7), calls=%async_computation.2 | async-start | bytes 196608 | tf_op jit(solution)/shard_map/all_to_all | solution.py:53
  107.1 8.0 %copy-start = (bf16[12,2,160,320]{3,2,1,0:T(8,128)(2,1)S(1)}, bf16[12,2,160,320]{3,2,1,0:T(8,128)(2,1)}, u32[]{:S(2)}) copy-start(bf16[12,2,160,320]{3,2,1,0:T(8,128)(2,1)} %get-tuple-element.54.w_h) | copy-start | bytes 7372804
  107.1 8.0 %copy-start.4 = (f32[1,1,16,32,320]{4,3,2,1,0:T(8,128)S(1)}, f32[1,1,16,32,320]{4,3,2,1,0:T(8,128)}, u32[]{:S(2)}) copy-start(f32[1,1,16,32,320]{4,3,2,1,0:T(8,128)} %param.5) | copy-start | bytes 1966084
  115.1 0.6 copy-start.7
